TPU v7x, 512 devices: a whole 4x4x16 slice. The times are simulated.
512 devices in a mesh: member: 16 (over y, x), space: 32 (over z, core).
Axes of the slice: x: 4, y: 4, z: 16, core: 2. Of those that a mesh axis runs over, the one named last changes fastest.
Arguments:
- air_ensemble: bfloat16 [16, 128, 360, 384], P('member', 'space'), may hold values from -12 to 12
- sea_indicator: int32 [128, 360], P('space'), may hold values 0 or 1
- layernorm_scaling: float32 [384], replicated, may hold values from 0.5 to 1.5
- harmonic_damping_factor: float32 [128, 384], replicated, may hold values from -4 to 4
- bypass_factor: bfloat16 [384, 384], replicated, may hold values from -0.3125 to 0.3125
- core_exit_factor: bfloat16 [384, 384], replicated, may hold values from -0.3125 to 0.3125
- air_to_exchange_factor: bfloat16 [384, 8], replicated, may hold values from -0.3125 to 0.3125
- sea_heat_imprint: float32 [384], replicated, may hold values from -4 to 4
- sea_ensemble_arrays: bfloat16 [16, 512, 76, 128], P('member', 'space'), may hold values from -6 to 6
- input_to_hidden_kernel: bfloat16 [9, 200, 84], replicated, may hold values from -0.21875 to 0.21875
- hidden_to_change_kernel: bfloat16 [9, 200], replicated, may hold values from -0.125 to 0.125
- patch_exchange_pick: int32 [448, 128], P('space'), may hold values from 0 to 1439
- node_sea_pick: int32 [128, 360], P('space'), may hold values from 0 to 1791
- patch_holder_shift: int32 [448, 1], P('space'), may hold values from 0 to 7; in each aligned block of 14 rows (0 to 13, 14 to 27, ...) at most 2 rows name the same one
- wet_depth_layers: int32 [448], P('space'), may hold values from 1 to 19
Outputs:
- atmos_out: bfloat16 [16, 128, 360, 384], P('member', 'space')
- sst_mean: float32 [128, 360], P('space')
Inputs may be any that keep to these rules, and one draw needn't show every extreme that they name: `patch_holder_shift`: among the 14 tiles of one band (aligned blocks of rows), no offset is named more than 2 times, a bound that some block reaches. Slots of sea_ensemble_arrays that no tile maps to are never read.
All inputs are finite; a program needn't handle non-finite values. No bound on the sum of `sea_indicator` on one device may be relied on, other than what follows from the above.
Results may differ from a plain program's by a relative error of at most 0.0075.
Values may be sent and summed in bfloat16 or wider, within the bound.
No kernel may reach another device: no remote copies, remote signals or barrier semaphores. Data moves between devices by JAX's collectives and lax.ppermute only.
A program may use at most 64 MiB of HBM per device.

v0:
```python
import math

import jax
import jax.numpy as jnp
from jax import lax
from jax.sharding import PartitionSpec as P

MERIDIAN_TOTAL = 360
MMAX = 128
LMAX = 128
FC = 8
LEV = 19
CAP = 2
NEAR = 8
HOME_DEV = 14


def passed_along(value, axis, by):
    devices = lax.axis_size(axis)
    return lax.ppermute(value, axis, [(i, (i + by) % devices) for i in range(devices)])


def analysis_table(orders, mesh_nodes):
    wavenumbers = jnp.arange(orders, dtype=jnp.int32)[:, None]
    columns = jnp.arange(mesh_nodes, dtype=jnp.int32)[None, :]
    angles = 2.0 * math.pi / mesh_nodes * (wavenumbers * columns % mesh_nodes).astype(jnp.float32)
    entries = jnp.stack([jnp.cos(angles), -jnp.sin(angles)], axis=1) / mesh_nodes
    return entries.reshape(2 * orders, mesh_nodes).astype(jnp.bfloat16)


def synthesis_table(orders, mesh_nodes):
    wavenumbers = jnp.arange(orders, dtype=jnp.int32)[:, None]
    columns = jnp.arange(mesh_nodes, dtype=jnp.int32)[None, :]
    angles = 2.0 * math.pi / mesh_nodes * (wavenumbers * columns % mesh_nodes).astype(jnp.float32)
    weights = jnp.where(wavenumbers == 0, 1.0, 2.0).astype(jnp.float32)
    entries = jnp.stack([weights * jnp.cos(angles), -weights * jnp.sin(angles)], axis=1)
    return jnp.transpose(entries.reshape(2 * orders, mesh_nodes)).astype(jnp.bfloat16)


def legendre_basis(orders, latitudes, degrees, highest):
    colatitude = (
        math.pi / latitudes * (jnp.arange(latitudes, dtype=jnp.int32).astype(jnp.float32) + 0.5)
    )
    cosine = jnp.cos(colatitude)[None, :]
    sine_values = jnp.sin(colatitude)
    counter = jnp.arange(1, highest, dtype=jnp.int32).astype(jnp.float32)
    log_terms = jnp.log((2.0 * counter - 1.0) / (2.0 * counter))
    totals = jnp.concatenate([jnp.zeros((1,), jnp.float32), jnp.cumsum(log_terms)])
    order_col = orders.astype(jnp.float32)[:, None]
    picked = jnp.take(totals, orders)[:, None]
    diagonal = jnp.exp(
        0.5 * (jnp.log((2.0 * order_col + 1.0) / (4.0 * math.pi)) + picked)
        + order_col * jnp.log(sine_values)[None, :]
    )

    def advance(previous, degree):
        latest, before = previous
        square = degree * degree - order_col * order_col
        lowered = (degree - 1.0) * (degree - 1.0)
        upward = jnp.sqrt(jnp.maximum(4.0 * degree * degree - 1.0, 0.0) / jnp.maximum(square, 1.0))
        damping = jnp.sqrt(
            jnp.maximum(lowered - order_col * order_col, 0.0)
            / jnp.maximum(4.0 * lowered - 1.0, 1.0)
        )
        current = upward * (cosine * latest - damping * before)
        current = jnp.where(degree == order_col, diagonal, current)
        current = jnp.where(degree < order_col, 0.0, current)
        return ((current, latest), current)

    empty_rows = jnp.zeros((orders.shape[0], latitudes), jnp.float32)
    degree_values = jnp.arange(degrees, dtype=jnp.int32).astype(jnp.float32)
    _, stacked = lax.scan(advance, (empty_rows, empty_rows), degree_values)
    return jnp.transpose(stacked, (1, 0, 2))


def transform_tables(polynomials, latitudes):
    colatitude = (
        math.pi / latitudes * (jnp.arange(latitudes, dtype=jnp.int32).astype(jnp.float32) + 0.5)
    )
    quadrature = 2.0 * math.pi * math.pi / latitudes * jnp.sin(colatitude)
    forward = (polynomials * quadrature[None, None, :]).astype(jnp.bfloat16)
    return (forward, polynomials.astype(jnp.bfloat16))


def layer_norm(values, scales):
    widened = values.astype(jnp.float32)
    centered = widened - jnp.mean(widened, axis=-1, keepdims=True)
    spread = jnp.mean(centered * centered, axis=-1, keepdims=True)
    return (centered * lax.rsqrt(spread + 1e-05) * scales).astype(jnp.bfloat16)


def spectral_core(spectra, forward, inverse, filter_gains):
    coefficients = jnp.einsum(
        "mlj,mrjc->mrlc", forward, spectra, preferred_element_type=jnp.float32
    )
    shaped = (coefficients * filter_gains[None, None]).astype(jnp.bfloat16)
    return jnp.einsum("mlj,mrlc->mrjc", inverse, shaped, preferred_element_type=jnp.float32).astype(
        jnp.bfloat16
    )


def patches(inputs):
    number, channels = (inputs.shape[0], inputs.shape[1])
    patch_grid = inputs.reshape(number, channels, 8, 16)
    padded = jnp.pad(patch_grid, ((0, 0), (0, 0), (1, 1), (1, 1)))
    shifted = [
        padded[:, :, rowshift : rowshift + 8, colshift : colshift + 16]
        for rowshift in range(3)
        for colshift in range(3)
    ]
    return jnp.stack(shifted, axis=1).reshape(number, 9 * channels, 128)


def decode_surface(hidden, hidden_to_change_kernel):
    number = hidden.shape[0]
    partial_maps = jnp.einsum(
        "qh,shc->sqc", hidden_to_change_kernel, hidden, preferred_element_type=jnp.float32
    )
    planes = jnp.pad(partial_maps.reshape(number, 9, 8, 16), ((0, 0), (0, 0), (1, 1), (1, 1)))
    coupled_step_return = jnp.zeros((number, 8, 16), jnp.float32)
    for rowshift in range(3):
        for colshift in range(3):
            coupled_step_return = (
                coupled_step_return
                + planes[
                    :, rowshift * 3 + colshift, rowshift : rowshift + 8, colshift : colshift + 16
                ]
            )
    return coupled_step_return.reshape(number, 128)


def marine_increment(
    current, boundary_driving, depth, input_to_hidden_kernel, hidden_to_change_kernel
):
    channels = current.shape[1]
    level_index = jnp.arange(channels, dtype=jnp.int32) % LEV
    active = level_index[None, :] < depth[:, None]
    masked = jnp.where(active[:, :, None], current, jnp.zeros((), jnp.bfloat16))
    inputs = jnp.concatenate([masked, boundary_driving], axis=1)
    columns = patches(inputs)
    kernel = jnp.transpose(input_to_hidden_kernel, (1, 0, 2)).reshape(
        input_to_hidden_kernel.shape[1], -1
    )
    hidden = jax.nn.gelu(
        jnp.einsum("hk,skc->shc", kernel, columns, preferred_element_type=jnp.float32)
    ).astype(jnp.bfloat16)
    increment = decode_surface(hidden, hidden_to_change_kernel)
    return (current[:, 0, :].astype(jnp.float32) + increment).astype(jnp.bfloat16)


def shards(
    air_ensemble,
    sea_indicator,
    layernorm_scaling,
    harmonic_damping_factor,
    bypass_factor,
    core_exit_factor,
    air_to_exchange_factor,
    sea_heat_imprint,
    sea_ensemble_arrays,
    input_to_hidden_kernel,
    hidden_to_change_kernel,
    patch_exchange_pick,
    node_sea_pick,
    patch_holder_shift,
    wet_depth_layers,
):
    band_count = lax.axis_size("space")
    current = air_ensemble[0]
    latitude_rows, longitude_values, channels = current.shape
    latitudes = latitude_rows * band_count
    normed = layer_norm(current, layernorm_scaling)
    spectra = jnp.einsum(
        "qk,jkc->qjc",
        analysis_table(MMAX, MERIDIAN_TOTAL),
        normed,
        preferred_element_type=jnp.float32,
    ).astype(jnp.bfloat16)
    skip_term = jnp.einsum("jkc,cd->jkd", normed, bypass_factor, preferred_element_type=jnp.float32)
    per_device = MMAX // band_count
    orders = lax.axis_index("space") * per_device + jnp.arange(per_device, dtype=jnp.int32)
    polynomials = legendre_basis(orders, latitudes, LMAX, MMAX)
    forward, inverse = transform_tables(polynomials, latitudes)
    gathered = lax.all_to_all(spectra, "space", split_axis=0, concat_axis=1, tiled=True)
    returned_spec = spectral_core(
        gathered.reshape(per_device, 2, latitudes, channels),
        forward,
        inverse,
        harmonic_damping_factor,
    )
    band_rows = lax.all_to_all(
        returned_spec.reshape(2 * per_device, latitudes, channels),
        "space",
        split_axis=1,
        concat_axis=0,
        tiled=True,
    )
    spectral = jnp.einsum(
        "kq,qjc->jkc",
        synthesis_table(MMAX, MERIDIAN_TOTAL),
        band_rows,
        preferred_element_type=jnp.float32,
    )
    mixed_rows = jax.nn.gelu(spectral + skip_term).astype(jnp.bfloat16)
    advanced_condition = current.astype(jnp.float32) + jnp.einsum(
        "jkc,cd->jkd", mixed_rows, core_exit_factor, preferred_element_type=jnp.float32
    )
    flux_points = jnp.einsum(
        "jkc,cf->fjk",
        advanced_condition,
        air_to_exchange_factor.astype(jnp.float32),
        precision=lax.Precision.HIGHEST,
    )
    flux_points = flux_points.astype(jnp.bfloat16).reshape(FC, latitude_rows * longitude_values)
    boundary_driving = jnp.transpose(
        jnp.take(flux_points, patch_exchange_pick.reshape(-1), axis=1).reshape(FC, HOME_DEV, 128),
        (1, 0, 2),
    )
    offsets = patch_holder_shift[:, 0]
    earlier = jnp.tril(jnp.ones((HOME_DEV, HOME_DEV), jnp.int32), -1)
    positions = jnp.sum((offsets[:, None] == offsets[None, :]).astype(jnp.int32) * earlier, axis=1)
    targets = offsets * CAP + positions
    selected = targets[None, :] == jnp.arange(NEAR * CAP, dtype=jnp.int32)[:, None]
    selection_matrix = selected.astype(jnp.bfloat16)
    outgoing = jnp.einsum(
        "gi,ifp->gfp", selection_matrix, boundary_driving, preferred_element_type=jnp.float32
    ).astype(jnp.bfloat16)
    depths = jnp.sum(jnp.where(selected, wet_depth_layers[None, :], 0), axis=1)
    forcing_pieces = []
    depth_pieces = []
    for offset in range(NEAR):
        got_forcing, got_depths = passed_along(
            (
                outgoing[offset * CAP : (offset + 1) * CAP],
                depths[offset * CAP : (offset + 1) * CAP],
            ),
            "space",
            offset,
        )
        forcing_pieces.append(got_forcing)
        depth_pieces.append(got_depths)
    slot_surface = marine_increment(
        sea_ensemble_arrays[0],
        jnp.concatenate(forcing_pieces, axis=0),
        jnp.concatenate(depth_pieces, axis=0),
        input_to_hidden_kernel,
        hidden_to_change_kernel,
    )
    returned_pieces = []
    for offset in range(NEAR):
        returned_pieces.append(
            passed_along(slot_surface[offset * CAP : (offset + 1) * CAP], "space", -offset)
        )
    returned_fields = jnp.concatenate(returned_pieces, axis=0)
    sea_heat_patches = jnp.einsum(
        "lx,lr->xr", selection_matrix, returned_fields, preferred_element_type=jnp.float32
    )
    mesh_nodes = jnp.take(sea_heat_patches.reshape(-1), node_sea_pick.reshape(-1)).reshape(
        latitude_rows, longitude_values
    )
    boundary_layer_array = sea_indicator.astype(jnp.float32) * mesh_nodes
    ensemble_sum = lax.psum(boundary_layer_array, "member")
    coupled_step_return = (
        advanced_condition + boundary_layer_array[:, :, None] * sea_heat_imprint
    ).astype(jnp.bfloat16)
    return (coupled_step_return[None], ensemble_sum / lax.axis_size("member"))


def solution(mesh):
    in_specs = (
        P("member", "space", None, None),
        P("space", None),
        P(),
        P(),
        P(),
        P(),
        P(),
        P(),
        P("member", "space", None, None),
        P(),
        P(),
        P("space", None),
        P("space", None),
        P("space", None),
        P("space"),
    )
    out_specs = (P("member", "space", None, None), P("space", None))
    return jax.shard_map(shards, mesh=mesh, in_specs=in_specs, out_specs=out_specs, check_vma=False)
```

profile of v0, /device:TPU:1, one launch (start us, length us, event | category | flops | bytes accessed | tf_op | source)
XLA Modules:
  0.0 820.9 jit_solution(4387011793569382106)
XLA Ops:
  0.7 0.8 fusion.94
  1.5 1.5 convert_reduce_fusion
  4.1 0.8 convolution_convert_fusion
  4.9 1.5 copy.95
  6.3 16.7 %all-to-all-start = ((bf16[256,4,384]{2,1,0:T(4,128)(2,1)}), bf16[256,4,384]{2,1,0:T(4,128)(2,1)S(1)}, u32[]{:S(2)}, u32[]{:S(2)}) async-start(bf16[256,4,384]{2,1,0:T(4,128)(2,1)} %copy.95), calls=%async_computation | async-start | bytes 1572864 | tf_op jit(solution)/shard_map/all_to_all | solution.py:184
  23.6 0.6 gather_fusion
  24.3 582.3 %while.20 = (s32[]{:T(128)}, f32[4,128]{1,0:T(4,128)S(1)}, f32[4,128]{1,0:T(4,128)S(1)}, f32[128,4,128]{2,1,0:T(4,128)S(1)}, f32[128]{0:T(128)S(1)}, /*index=5*/...) while((s32[]{:T(128)}, f32[4,128]{1,0:T(4,128)S(1)}, ...), condition=%wide.region_4.5_spmd.clone.clone.clone, body=%wide.region_3.4_spmd.clone.clone.clone.sunk | while | flops 5057 | bytes 15203 | solution.py:72
  24.3 0.6 dynamic_slice.12
  28.9 0.6 dynamic_slice.12
  33.4 0.6 dynamic_slice.12
  42.5 0.6 dynamic_slice.12
  47.1 0.6 dynamic_slice.12
  56.2 0.6 dynamic_slice.12
  60.7 0.6 dynamic_slice.12
  74.4 0.6 dynamic_slice.12
  78.9 0.6 dynamic_slice.12
  88.0 0.6 dynamic_slice.12
  92.6 0.6 dynamic_slice.12
  608.1 1.3 copy.101
  609.4 12.3 %all-to-all-start.1 = ((bf16[8,128,384]{2,0,1:T(8,128)(2,1)}), bf16[8,128,384]{2,0,1:T(8,128)(2,1)S(1)}, u32[]{:S(2)}, u32[]{:S(2)}) async-start(bf16[8,128,384]{2,0,1:T(8,128)(2,1)} %copy.101), calls=%async_computation.1 | async-start | bytes 1572864 | tf_op jit(solution)/shard_map/all_to_all | solution.py:191
  622.2 1.6 collective-permute-start.1
  623.8 3.1 collective-permute-start.2
  626.9 3.2 collective-permute-start.3
  630.1 5.2 collective-permute-start.4
  635.4 0.8 multiply_convert_fusion.1
  637.0 0.9 reshape.520
  637.9 0.7 reshape.523
  638.7 6.5 collective-permute-start.5
  645.2 3.6 collective-permute-done.1
  648.8 11.1 %collective-permute-start.6 = (s32[2]{0:T(128)S(1)}, s32[2]{0:T(128)S(1)}, u32[]{:S(2)}, u32[]{:S(2)}) collective-permute-start(s32[2]{0:T(128)S(1)} %get-tuple-element.277), channel_id=1, source_target_pairs={{0,6},{1,7},{2,8},{3,9},{4,10},{5,11},{6,12},{7,13},{8,14},{9,15},... | collective-permute-start | bytes 32 | tf_op jit(solution)/shard_map/ppermute | solution.py:20
  659.9 9.9 %collective-permute-start.7 = (s32[2]{0:T(128)S(1)}, s32[2]{0:T(128)S(1)}, u32[]{:S(2)}, u32[]{:S(2)}) collective-permute-start(s32[2]{0:T(128)S(1)} %get-tuple-element.276), channel_id=1, source_target_pairs={{0,7},{1,8},{2,9},{3,10},{4,11},{5,12},{6,13},{7,14},{8,15},{9,16}... | collective-permute-start | bytes 32 | tf_op jit(solution)/shard_map/ppermute | solution.py:20
  670.5 1.9 fusion.69
  672.3 4.5 fusion.9
  676.8 1.2 fusion.43
  678.2 4.6 gather_fusion.1
  682.9 1.2 copy.108
  684.2 3.9 collective-permute-start.10
  688.2 4.4 collective-permute-start.11
  692.6 6.1 collective-permute-start.12
  698.7 0.8 broadcast_select_fusion.2
  699.6 3.1 collective-permute-start.13
  702.7 1.9 collective-permute-start.14
  704.6 1.9 collective-permute-start.15
  707.2 0.7 broadcast_select_fusion.1
  707.9 2.1 collective-permute-done.14
  710.0 2.5 collective-permute-done.15
  713.7 2.6 concatenate.25
  716.4 1.0 copy.130
  717.4 1.8 fusion.63
  721.4 11.2 %copy.112 = bf16[16,9,84,8,16]{2,1,4,3,0:T(8,128)(2,1)} copy(bf16[16,9,84,8,16]{2,4,3,0,1:T(8,128)(2,1)S(1)} %fusion.73) | data formatting | bytes 6193152 | tf_op jit(solution)/shard_map/stack | solution.py:111
  732.6 11.3 %reshape.519 = bf16[16,756,128]{1,2,0:T(8,128)(2,1)} reshape(bf16[16,9,84,8,16]{2,1,4,3,0:T(8,128)(2,1)} %copy.112) | data formatting | bytes 6193152 | tf_op jit(solution)/shard_map/reshape | solution.py:111
  743.9 3.4 fusion.40
  747.9 0.7 fusion.114
  748.6 1.3 collective-permute-start.17
  749.9 4.3 collective-permute-start.18
  754.2 4.1 collective-permute-start.19
  758.3 3.7 collective-permute-start.20
  762.1 3.4 collective-permute-start.21
  765.5 2.4 collective-permute-start.22
  767.9 3.2 collective-permute-start.23
  771.6 5.1 collective-permute-done.23
  776.9 8.1 gather_fusion.2
  785.1 33.9 %psum.7 = f32[4,360]{1,0:T(4,128)S(1)} all-reduce(f32[4,360]{1,0:T(4,128)S(1)} %select_multiply_fusion), channel_id=1, replica_groups=mesh['member'=16,'space'=32] {'member'}, use_global_device_ids=true, to_apply=%region_7.8 | all-reduce | flops 1440 | bytes 11520 | tf_op jit(solution)/shard_map/psum | solution.py:262
  819.0 1.3 fusion.44
  (777 shorter events, 186.3 us)
Async XLA Ops:
  0.6 671.7 %copy-start = (bf16[384,384]{1,0:T(8,128)(2,1)S(1)}, bf16[384,384]{1,0:T(8,128)(2,1)}, u32[]{:S(2)}) copy-start(bf16[384,384]{1,0:T(8,128)(2,1)} %param.22) | copy-start | bytes 884740
  0.6 2.4 copy-start.1
  0.7 3.4 copy-start.26
  4.8 601.8 %copy-start.5 = (f32[128,384]{1,0:T(8,128)S(1)}, f32[128,384]{1,0:T(8,128)}, u32[]{:S(2)}) copy-start(f32[128,384]{1,0:T(8,128)} %param.20) | copy-start | bytes 589828
  6.3 600.6 %all-to-all-start = ((bf16[256,4,384]{2,1,0:T(4,128)(2,1)}), bf16[256,4,384]{2,1,0:T(4,128)(2,1)S(1)}, u32[]{:S(2)}, u32[]{:S(2)}) async-start(bf16[256,4,384]{2,1,0:T(4,128)(2,1)} %copy.95), calls=%async_computation | async-start | bytes 1572864 | tf_op jit(solution)/shard_map/all_to_all | solution.py:184
  607.4 14.3 %copy-start.23 = (s32[14,1]{0,1:T(1,128)S(1)}, s32[14,1]{0,1:T(1,128)}, u32[]{:S(2)}) copy-start(s32[14,1]{0,1:T(1,128)} %param.30) | copy-start | bytes 172
  607.4 14.5 %copy-start.27 = (s32[14]{0:T(128)S(1)}, s32[14]{0:T(128)}, u32[]{:S(2)}) copy-start(s32[14]{0:T(128)} %param.31) | copy-start | bytes 172
  608.0 28.5 %copy-start.4 = (bf16[1,16,76,128]{3,1,2,0:T(8,128)(2,1)S(1)}, bf16[1,16,76,128]{3,1,2,0:T(8,128)(2,1)}, u32[]{:S(2)}) copy-start(bf16[1,16,76,128]{3,1,2,0:T(8,128)(2,1)} %param.25) | copy-start | bytes 933892
  609.4 27.6 %copy-start.2 = (bf16[9,200,84]{1,2,0:T(8,128)(2,1)S(1)}, bf16[9,200,84]{1,2,0:T(8,128)(2,1)}, u32[]{:S(2)}) copy-start(bf16[9,200,84]{1,2,0:T(8,128)(2,1)} %param.26) | copy-start | bytes 907204
  609.4 28.5 %copy-start.8 = (s32[4,360]{1,0:T(4,128)S(1)}, s32[4,360]{1,0:T(4,128)}, u32[]{:S(2)}) copy-start(s32[4,360]{1,0:T(4,128)} %param.29) | copy-start | bytes 17284
  609.4 29.2 %copy-start.6 = (s32[14,128]{1,0:T(8,128)S(1)}, s32[14,128]{1,0:T(8,128)}, u32[]{:S(2)}) copy-start(s32[14,128]{1,0:T(8,128)} %param.28) | copy-start | bytes 21508
  609.4 61.0 %all-to-all-start.1 = ((bf16[8,128,384]{2,0,1:T(8,128)(2,1)}), bf16[8,128,384]{2,0,1:T(8,128)(2,1)S(1)}, u32[]{:S(2)}, u32[]{:S(2)}) async-start(bf16[8,128,384]{2,0,1:T(8,128)(2,1)} %copy.101), calls=%async_computation.1 | async-start | bytes 1572864 | tf_op jit(solution)/shard_map/all_to_all | solution.py:191
  621.9 62.1 %copy-start.21 = (s32[14]{0:T(128)}, s32[14]{0:T(128)S(1)}, u32[]{:S(2)}) copy-start(s32[14]{0:T(128)S(1)} %multiply_add_fusion) | copy-start | bytes 172
  622.1 16.5 %collective-permute-start = (s32[2]{0:T(128)S(1)}, s32[2]{0:T(128)S(1)}, u32[]{:S(2)}, u32[]{:S(2)}) collective-permute-start(s32[2]{0:T(128)S(1)} %get-tuple-element.283), channel_id=1, source_target_pairs={{0,0},{1,1},{2,2},{3,3},{4,4},{5,5},{6,6},{7,7},{8,8},{9,9},{10,10... | collective-permute-start | bytes 32 | tf_op jit(solution)/shard_map/ppermute | solution.py:20
  622.2 26.6 %collective-permute-start.1 = (s32[2]{0:T(128)S(1)}, s32[2]{0:T(128)S(1)}, u32[]{:S(2)}, u32[]{:S(2)}) collective-permute-start(s32[2]{0:T(128)S(1)} %get-tuple-element.282), channel_id=1, source_target_pairs={{0,1},{1,2},{2,3},{3,4},{4,5},{5,6},{6,7},{7,8},{8,9},{9,10},{10,1... | collective-permute-start | bytes 32 | tf_op jit(solution)/shard_map/ppermute | solution.py:20
  623.8 36.1 %collective-permute-start.2 = (s32[2]{0:T(128)S(1)}, s32[2]{0:T(128)S(1)}, u32[]{:S(2)}, u32[]{:S(2)}) collective-permute-start(s32[2]{0:T(128)S(1)} %get-tuple-element.281), channel_id=1, source_target_pairs={{0,2},{1,3},{2,4},{3,5},{4,6},{5,7},{6,8},{7,9},{8,10},{9,11},{10,... | collective-permute-start | bytes 32 | tf_op jit(solution)/shard_map/ppermute | solution.py:20
  626.9 42.9 %collective-permute-start.3 = (s32[2]{0:T(128)S(1)}, s32[2]{0:T(128)S(1)}, u32[]{:S(2)}, u32[]{:S(2)}) collective-permute-start(s32[2]{0:T(128)S(1)} %get-tuple-element.280), channel_id=1, source_target_pairs={{0,3},{1,4},{2,5},{3,6},{4,7},{5,8},{6,9},{7,10},{8,11},{9,12},{10... | collective-permute-start | bytes 32 | tf_op jit(solution)/shard_map/ppermute | solution.py:20
  630.1 39.7 %collective-permute-start.4 = (s32[2]{0:T(128)S(1)}, s32[2]{0:T(128)S(1)}, u32[]{:S(2)}, u32[]{:S(2)}) collective-permute-start(s32[2]{0:T(128)S(1)} %get-tuple-element.279), channel_id=1, source_target_pairs={{0,4},{1,5},{2,6},{3,7},{4,8},{5,9},{6,10},{7,11},{8,12},{9,13},{1... | collective-permute-start | bytes 32 | tf_op jit(solution)/shard_map/ppermute | solution.py:20
  637.0 35.3 %copy-start.24 = (bf16[384,384]{1,0:T(8,128)(2,1)S(1)}, bf16[384,384]{1,0:T(8,128)(2,1)}, u32[]{:S(2)}) copy-start(bf16[384,384]{1,0:T(8,128)(2,1)} %param.21) | copy-start | bytes 884740
  638.7 31.1 %collective-permute-start.5 = (s32[2]{0:T(128)S(1)}, s32[2]{0:T(128)S(1)}, u32[]{:S(2)}, u32[]{:S(2)}) collective-permute-start(s32[2]{0:T(128)S(1)} %get-tuple-element.278), channel_id=1, source_target_pairs={{0,5},{1,6},{2,7},{3,8},{4,9},{5,10},{6,11},{7,12},{8,13},{9,14},{... | collective-permute-start | bytes 32 | tf_op jit(solution)/shard_map/ppermute | solution.py:20
  648.8 21.0 %collective-permute-start.6 = (s32[2]{0:T(128)S(1)}, s32[2]{0:T(128)S(1)}, u32[]{:S(2)}, u32[]{:S(2)}) collective-permute-start(s32[2]{0:T(128)S(1)} %get-tuple-element.277), channel_id=1, source_target_pairs={{0,6},{1,7},{2,8},{3,9},{4,10},{5,11},{6,12},{7,13},{8,14},{9,15},... | collective-permute-start | bytes 32 | tf_op jit(solution)/shard_map/ppermute | solution.py:20
  659.9 10.4 %collective-permute-start.7 = (s32[2]{0:T(128)S(1)}, s32[2]{0:T(128)S(1)}, u32[]{:S(2)}, u32[]{:S(2)}) collective-permute-start(s32[2]{0:T(128)S(1)} %get-tuple-element.276), channel_id=1, source_target_pairs={{0,7},{1,8},{2,9},{3,10},{4,11},{5,12},{6,13},{7,14},{8,15},{9,16}... | collective-permute-start | bytes 32 | tf_op jit(solution)/shard_map/ppermute | solution.py:20
  670.4 28.3 %copy-start.10 = (pred[16,76]{1,0:T(8,128)(4,1)}, pred[16,76]{1,0:T(8,128)(4,1)S(1)}, u32[]{:S(2)}) copy-start(pred[16,76]{1,0:T(8,128)(4,1)S(1)} %broadcast_compare_fusion) | copy-start | bytes 3652
  672.3 4.5 copy-start.11
  684.2 20.3 %collective-permute-start.10 = (bf16[2,8,128]{2,0,1:T(2,128)(2,1)S(1)}, bf16[2,8,128]{2,0,1:T(2,128)(2,1)S(1)}, u32[]{:S(2)}, u32[]{:S(2)}) collective-permute-start(bf16[2,8,128]{2,0,1:T(2,128)(2,1)S(1)} %get-tuple-element.265), channel_id=1, source_target_pairs={{0,2},{1,3},{2,4},{3,5},{4,6},{5,7},{6,8},{7,9},{8,10},{9,11},{10,... | collective-permute-start | bytes 12296 | tf_op jit(solution)/shard_map/ppermute | solution.py:20
  688.2 18.4 %collective-permute-start.11 = (bf16[2,8,128]{2,0,1:T(2,128)(2,1)S(1)}, bf16[2,8,128]{2,0,1:T(2,128)(2,1)S(1)}, u32[]{:S(2)}, u32[]{:S(2)}) collective-permute-start(bf16[2,8,128]{2,0,1:T(2,128)(2,1)S(1)} %get-tuple-element.264), channel_id=1, source_target_pairs={{0,3},{1,4},{2,5},{3,6},{4,7},{5,8},{6,9},{7,10},{8,11},{9,12},{10... | collective-permute-start | bytes 12296 | tf_op jit(solution)/shard_map/ppermute | solution.py:20
  692.6 14.0 %collective-permute-start.12 = (bf16[2,8,128]{2,0,1:T(2,128)(2,1)S(1)}, bf16[2,8,128]{2,0,1:T(2,128)(2,1)S(1)}, u32[]{:S(2)}, u32[]{:S(2)}) collective-permute-start(bf16[2,8,128]{2,0,1:T(2,128)(2,1)S(1)} %get-tuple-element.263), channel_id=1, source_target_pairs={{0,4},{1,5},{2,6},{3,7},{4,8},{5,9},{6,10},{7,11},{8,12},{9,13},{1... | collective-permute-start | bytes 12296 | tf_op jit(solution)/shard_map/ppermute | solution.py:20
  699.6 8.3 %collective-permute-start.13 = (bf16[2,8,128]{2,0,1:T(2,128)(2,1)S(1)}, bf16[2,8,128]{2,0,1:T(2,128)(2,1)S(1)}, u32[]{:S(2)}, u32[]{:S(2)}) collective-permute-start(bf16[2,8,128]{2,0,1:T(2,128)(2,1)S(1)} %get-tuple-element.262), channel_id=1, source_target_pairs={{0,5},{1,6},{2,7},{3,8},{4,9},{5,10},{6,11},{7,12},{8,13},{9,14},{... | collective-permute-start | bytes 12296 | tf_op jit(solution)/shard_map/ppermute | solution.py:20
  702.7 7.4 collective-permute-start.14
  704.6 2.3 copy-start.13
  704.6 7.9 collective-permute-start.15
  706.5 0.6 copy-start.14
  706.6 6.0 collective-permute-start.8
  706.6 0.6 copy-start.15
  706.6 7.1 collective-permute-start.9
  707.9 4.6 copy-start.16
  710.0 2.5 copy-start.17
  712.5 0.6 copy-start.18
  713.1 0.6 copy-start.19
  732.6 11.3 %copy-start.3 = (bf16[200,756]{0,1:T(8,128)(2,1)S(1)}, bf16[200,756]{0,1:T(8,128)(2,1)}, u32[]{:S(2)}) copy-start(bf16[200,756]{0,1:T(8,128)(2,1)} %reshape.520) | copy-start | bytes 907204
  732.6 11.3 %copy-start.25 = (bf16[9,200]{1,0:T(8,128)(2,1)S(1)}, bf16[9,200]{1,0:T(8,128)(2,1)}, u32[]{:S(2)}) copy-start(bf16[9,200]{1,0:T(8,128)(2,1)} %param.27) | copy-start | bytes 10804
  743.9 6.0 copy-start.7
  743.9 32.8 %copy-start.22 = (s32[14]{0:T(128)S(1)}, s32[14]{0:T(128)}, u32[]{:S(2)}) copy-start(s32[14]{0:T(128)} %copy-done.21) | copy-start | bytes 172
  748.6 13.5 %collective-permute-start.16 = (bf16[2,128]{1,0:T(2,128)(2,1)S(1)}, bf16[2,128]{1,0:T(2,128)(2,1)S(1)}, u32[]{:S(2)}, u32[]{:S(2)}) collective-permute-start(bf16[2,128]{1,0:T(2,128)(2,1)S(1)} %get-tuple-element.275), channel_id=1, source_target_pairs={{0,0},{1,1},{2,2},{3,3},{4,4},{5,5},{6,6},{7,7},{8,8},{9,9},{10,10... | collective-permute-start | bytes 1544 | tf_op jit(solution)/shard_map/ppermute | solution.py:20
  748.6 16.9 %collective-permute-start.17 = (bf16[2,128]{1,0:T(2,128)(2,1)S(1)}, bf16[2,128]{1,0:T(2,128)(2,1)S(1)}, u32[]{:S(2)}, u32[]{:S(2)}) collective-permute-start(bf16[2,128]{1,0:T(2,128)(2,1)S(1)} %get-tuple-element.274), channel_id=1, source_target_pairs={{0,31},{1,0},{2,1},{3,2},{4,3},{5,4},{6,5},{7,6},{8,7},{9,8},{10,9... | collective-permute-start | bytes 1544 | tf_op jit(solution)/shard_map/ppermute | solution.py:20
  749.9 18.0 %collective-permute-start.18 = (bf16[2,128]{1,0:T(2,128)(2,1)S(1)}, bf16[2,128]{1,0:T(2,128)(2,1)S(1)}, u32[]{:S(2)}, u32[]{:S(2)}) collective-permute-start(bf16[2,128]{1,0:T(2,128)(2,1)S(1)} %get-tuple-element.273), channel_id=1, source_target_pairs={{0,30},{1,31},{2,0},{3,1},{4,2},{5,3},{6,4},{7,5},{8,6},{9,7},{10,... | collective-permute-start | bytes 1544 | tf_op jit(solution)/shard_map/ppermute | solution.py:20
  754.2 16.9 %collective-permute-start.19 = (bf16[2,128]{1,0:T(2,128)(2,1)S(1)}, bf16[2,128]{1,0:T(2,128)(2,1)S(1)}, u32[]{:S(2)}, u32[]{:S(2)}) collective-permute-start(bf16[2,128]{1,0:T(2,128)(2,1)S(1)} %get-tuple-element.272), channel_id=1, source_target_pairs={{0,29},{1,30},{2,31},{3,0},{4,1},{5,2},{6,3},{7,4},{8,5},{9,6},{10... | collective-permute-start | bytes 1544 | tf_op jit(solution)/shard_map/ppermute | solution.py:20
  758.3 12.8 %collective-permute-start.20 = (bf16[2,128]{1,0:T(2,128)(2,1)S(1)}, bf16[2,128]{1,0:T(2,128)(2,1)S(1)}, u32[]{:S(2)}, u32[]{:S(2)}) collective-permute-start(bf16[2,128]{1,0:T(2,128)(2,1)S(1)} %get-tuple-element.271), channel_id=1, source_target_pairs={{0,28},{1,29},{2,30},{3,31},{4,0},{5,1},{6,2},{7,3},{8,4},{9,5},{1... | collective-permute-start | bytes 1544 | tf_op jit(solution)/shard_map/ppermute | solution.py:20
  762.1 9.1 %collective-permute-start.21 = (bf16[2,128]{1,0:T(2,128)(2,1)S(1)}, bf16[2,128]{1,0:T(2,128)(2,1)S(1)}, u32[]{:S(2)}, u32[]{:S(2)}) collective-permute-start(bf16[2,128]{1,0:T(2,128)(2,1)S(1)} %get-tuple-element.270), channel_id=1, source_target_pairs={{0,27},{1,28},{2,29},{3,30},{4,31},{5,0},{6,1},{7,2},{8,3},{9,4},{... | collective-permute-start | bytes 1544 | tf_op jit(solution)/shard_map/ppermute | solution.py:20
  765.5 6.1 collective-permute-start.22
  767.9 8.8 %collective-permute-start.23 = (bf16[2,128]{1,0:T(2,128)(2,1)S(1)}, bf16[2,128]{1,0:T(2,128)(2,1)S(1)}, u32[]{:S(2)}, u32[]{:S(2)}) collective-permute-start(bf16[2,128]{1,0:T(2,128)(2,1)S(1)} %get-tuple-element.268), channel_id=1, source_target_pairs={{0,25},{1,26},{2,27},{3,28},{4,29},{5,30},{6,31},{7,0},{8,1},{9,2}... | collective-permute-start | bytes 1544 | tf_op jit(solution)/shard_map/ppermute | solution.py:20
  776.9 8.2 copy-start.9
  776.9 8.2 copy-start.12
  776.9 42.1 %copy-start.20 = (f32[384]{0:T(512)S(1)}, f32[384]{0:T(512)}, u32[]{:S(2)}) copy-start(f32[384]{0:T(512)} %param.24) | copy-start | bytes 4612
where the time goes:
time: 834 us; the launch traced here: 821 us
  loops' own time  400 us (48%)
  local copies, waits for them, and re-layouts  133 us (16%)
  starting transfers between devices  114 us (14%)
  other arithmetic  112 us (13%)
  blocking collectives  33.9 us (4%)
  waiting for transfers between devices  14.2 us (2%)
  matrix products  12.7 us (2%)
    another operation x1, loops' own time, legendre_basis(): _, stacked = lax.scan(advance, (empty_rows, empty_rows), degree_values)  400 us
    ppermute x24, starting transfers between devices, passed_along(): lax.ppermute(value, axis, [(i, (i + by) % devices) for i in range(devices)])  84.7 us
    dynamic_slice x128, local copies, waits for them, and re-layouts, legendre_basis(): _, stacked = lax.scan(advance, (empty_rows, empty_rows), degree_values)  82.1 us
    eq x128, other arithmetic, advance(): current = jnp.where(degree == order_col, diagonal, current)  80.6 us
    psum x1, blocking collectives, shards(): ensemble_sum = lax.psum(boundary_layer_array, 'member')  33.9 us
    all_to_all x1, starting transfers between devices, shards(): lax.all_to_all(spectra, 'space', split_axis=0, concat_axis=1, tiled=True)  16.7 us
  transfers between devices with their start and end apart: 26, of which 6 were waited for; matrix products, arithmetic and copies ran while one was open for 23% of the time, Pallas kernels for 0%

commit v1 on v0

v1 whole, which is shorter than its diff:
```python
import math

import jax
import jax.numpy as jnp
import numpy as np
from jax import lax
from jax.experimental import pallas as pl
from jax.experimental.pallas import tpu as pltpu
from jax.sharding import PartitionSpec as P

MERIDIAN_TOTAL = 360
MMAX = 128
LMAX = 128
FC = 8
LEV = 19
CAP = 2
NEAR = 8
HOME_DEV = 14
SLOTS = NEAR * CAP
CELLS = 128
SPAN = SLOTS * CELLS
OCH = 76
OCH_PAD = 80
TAPS = [(row, col) for row in (-1, 0, 1) for col in (-1, 0, 1)]
BF16 = jnp.bfloat16
F32 = jnp.float32
WHOLE = pl.BlockSpec(memory_space=pltpu.VMEM)


def passed_along(value, axis, by):
    devices = lax.axis_size(axis)
    return lax.ppermute(value, axis, [(i, (i + by) % devices) for i in range(devices)])


def fourier_tables():
    product = np.arange(MMAX)[:, None] * np.arange(MERIDIAN_TOTAL)[None, :] % MERIDIAN_TOTAL
    angles = 2.0 * np.pi / MERIDIAN_TOTAL * product
    analysis = np.stack([np.cos(angles), -np.sin(angles)], axis=1) / MERIDIAN_TOTAL
    weights = np.where(np.arange(MMAX) == 0, 1.0, 2.0)[:, None]
    synthesis = np.stack([weights * np.cos(angles), -weights * np.sin(angles)], axis=1)
    return (
        analysis.reshape(2 * MMAX, MERIDIAN_TOTAL).astype(BF16),
        synthesis.reshape(2 * MMAX, MERIDIAN_TOTAL).T.astype(BF16),
    )


def legendre_tables(latitudes):
    theta = np.pi / latitudes * (np.arange(latitudes) + 0.5)
    cosine = np.cos(theta)[None, :]
    sine = np.sin(theta)
    counter = np.arange(1, MMAX)
    totals = np.concatenate([[0.0], np.cumsum(np.log((2.0 * counter - 1.0) / (2.0 * counter)))])
    order = np.arange(MMAX, dtype=np.float64)[:, None]
    diagonal = np.exp(
        0.5 * (np.log((2.0 * order + 1.0) / (4.0 * np.pi)) + totals[:, None])
        + order * np.log(sine)[None, :]
    )
    values = np.zeros((MMAX, LMAX, latitudes))
    latest = np.zeros((MMAX, latitudes))
    before = np.zeros((MMAX, latitudes))
    for degree in range(LMAX):
        lowered = (degree - 1.0) ** 2
        upward = np.sqrt(
            max(4.0 * degree * degree - 1.0, 0.0) / np.maximum(degree * degree - order * order, 1.0)
        )
        damping = np.sqrt(
            np.maximum(lowered - order * order, 0.0) / max(4.0 * lowered - 1.0, 1.0)
        )
        current = upward * (cosine * latest - damping * before)
        current = np.where(degree == order, diagonal, current)
        current = np.where(degree < order, 0.0, current)
        values[:, degree, :] = current
        latest, before = current, latest
    quadrature = 2.0 * np.pi * np.pi / latitudes * sine
    forward = (values * quadrature[None, None, :]).astype(BF16)
    backward = np.transpose(values, (0, 2, 1)).astype(BF16)
    return forward, backward


def gelu(x):
    inner = math.sqrt(2.0 / math.pi) * (x + 0.044715 * (x * x * x))
    return 0.5 * x * (1.0 + jnp.tanh(inner))


def tap_masks(width):
    lane = lax.broadcasted_iota(jnp.int32, (1, width), 1) % CELLS
    row, col = lane // 16, lane % 16
    masks = []
    for down, right in TAPS:
        inside = (row + down >= 0) & (row + down < 8) & (col + right >= 0) & (col + right < 16)
        masks.append(inside)
    return masks


def shifted(x, tap, mask):
    by = 16 * tap[0] + tap[1]
    if by == 0:
        return x
    rolled = pltpu.roll(x, (-by) % x.shape[1], 1)
    return jnp.where(mask, rolled, 0.0)


def in_three(x):
    high = x.astype(BF16)
    rest = x - high.astype(F32)
    middle = rest.astype(BF16)
    return high, middle, (rest - middle.astype(F32)).astype(BF16)


def analysis_kernel(air_ref, scale_ref, table_ref, spectra_ref, normed_ref):
    rows = air_ref.shape[0]
    groups = spectra_ref.shape[0]
    table = table_ref[...]
    scale = scale_ref[...]
    for pair in range(rows // 2):
        both = []
        for j in (2 * pair, 2 * pair + 1):
            x = air_ref[j].astype(F32)
            centered = x - jnp.mean(x, axis=-1, keepdims=True)
            spread = jnp.mean(centered * centered, axis=-1, keepdims=True)
            normed = (centered * lax.rsqrt(spread + 1e-05) * scale).astype(BF16)
            normed_ref[j] = normed
            out = jnp.dot(table, normed, preferred_element_type=F32)
            both.append(out.reshape(groups, 8, out.shape[1]))
        block = jnp.concatenate(both, axis=1)
        spectra_ref[:, 16 * pair : 16 * (pair + 1), :] = block.astype(BF16)


def legendre_kernel(x_ref, forward_ref, backward_ref, gains_ref, out_ref, work):
    groups, chunk, channels = x_ref.shape
    total = groups * chunk
    latitudes = total // 8
    for third in range(channels // 128):
        lanes = slice(128 * third, 128 * (third + 1))
        work[third] = x_ref[:, :, lanes].astype(F32).reshape(total, 128)
    for m in range(4):
        for r in (0, 1):
            rows = pl.ds(2 * m + r, latitudes, stride=8)
            own = jnp.concatenate(
                [work[third, rows, :] for third in range(channels // 128)], axis=1
            ).astype(BF16)
            coefficients = jnp.dot(forward_ref[m], own, preferred_element_type=F32)
            shaped = (coefficients * gains_ref[...]).astype(BF16)
            back = jnp.dot(backward_ref[m], shaped, preferred_element_type=F32)
            for third in range(channels // 128):
                work[third, rows, :] = back[:, 128 * third : 128 * (third + 1)]
    for third in range(channels // 128):
        lanes = slice(128 * third, 128 * (third + 1))
        out_ref[:, :, lanes] = work[third].reshape(groups, chunk, 128).astype(BF16)


def ocean_kernel(depth_ref, a0_ref, a1_ref, b1_ref, c1_ref, weight_ref, out_ref, columns):
    masks = tap_masks(CELLS)
    level = lax.broadcasted_iota(jnp.int32, (OCH, CELLS), 0) % LEV
    places = {
        0: (a0_ref, 0), 4: (a1_ref, 0), 2: (b1_ref, 0), 6: (b1_ref, 4),
        1: (c1_ref, 0), 5: (c1_ref, 2), 3: (c1_ref, 4), 7: (c1_ref, 6),
    }
    for slot in range(SLOTS):
        ref, at = places[slot // CAP]
        state = ref[at + slot % CAP].astype(F32)
        state = jnp.where(level < depth_ref[slot], state, 0.0)
        state = jnp.concatenate([state, jnp.zeros((OCH_PAD - OCH, CELLS), F32)], axis=0)
        for q, tap in enumerate(TAPS):
            moved = shifted(state, tap, masks[q]).astype(BF16)
            columns[OCH_PAD * q : OCH_PAD * (q + 1), CELLS * slot : CELLS * (slot + 1)] = moved
    for at in range(0, SPAN, 512):
        out_ref[:, at : at + 512] = jnp.dot(
            weight_ref[...], columns[:, at : at + 512], preferred_element_type=F32
        )


def closing_kernel(
    rows_ref, synthesis_ref, skip_ref, air_ref, exit_ref, exchange_ref, place_ref, line_ref,
    wet_ref, forcing_weight_ref, decode_ref, top_ref, cell_ref, slot_ref, imprint_ref,
    out_ref, tiles_ref, updated, flux, sst,
):
    latitude_rows = air_ref.shape[0]
    groups, chunk, channels = rows_ref.shape
    synthesis = synthesis_ref[...]
    fields = rows_ref[...].astype(F32).reshape(groups, latitude_rows, 8, channels)
    for j in range(latitude_rows):
        own = fields[:, j].reshape(8 * groups, channels).astype(BF16)
        spectral = jnp.dot(synthesis, own, preferred_element_type=F32)
        mixed = gelu(spectral + skip_ref[j]).astype(BF16)
        state = air_ref[j].astype(F32) + jnp.dot(
            mixed, exit_ref[...], preferred_element_type=F32
        )
        updated[j] = state
        high = state.astype(BF16)
        low = (state - high.astype(F32)).astype(BF16)
        dims = (((1,), (1,)), ((), ()))
        flux[8 * j : 8 * (j + 1), :] = lax.dot_general(
            exchange_ref[...], high, dims, preferred_element_type=F32
        ) + lax.dot_general(exchange_ref[...], low, dims, preferred_element_type=F32)
    spread = jnp.dot(flux[...].astype(BF16), place_ref[...], preferred_element_type=F32)
    line = line_ref[...]
    forcing = jnp.zeros((FC, SPAN), F32)
    for j in range(latitude_rows):
        forcing = forcing + jnp.where(line == j, spread[8 * j : 8 * (j + 1), :], 0.0)
    masks = tap_masks(SPAN)
    columns = jnp.concatenate(
        [shifted(forcing, tap, masks[q]) for q, tap in enumerate(TAPS)], axis=0
    ).astype(BF16)
    change = jnp.zeros((1, SPAN), F32)
    hidden = gelu(
        wet_ref[...] + jnp.dot(forcing_weight_ref[...], columns, preferred_element_type=F32)
    ).astype(BF16)
    partial = jnp.dot(decode_ref[...], hidden, preferred_element_type=F32)
    for q, tap in enumerate(TAPS):
        change = change + shifted(partial[q : q + 1, :], tap, masks[q])
    surface = top_ref[...] + change
    for slot in range(SLOTS):
        sst[slot : slot + 1, :] = surface[:, CELLS * slot : CELLS * (slot + 1)]
    tiles = sst[...].astype(BF16)
    tiles_ref[...] = tiles
    tripled = jnp.concatenate([tiles, tiles, tiles], axis=0)
    imprint = jnp.concatenate(
        [jnp.broadcast_to(piece, (SLOTS, channels)) for piece in in_three(imprint_ref[...])], axis=0
    )
    for j in range(latitude_rows):
        picked = lax.dot_general(
            cell_ref[j], tripled, (((1,), (1,)), ((), ())), preferred_element_type=F32
        )
        chosen = picked.astype(BF16) * slot_ref[j]
        warmth = jnp.dot(chosen, imprint, preferred_element_type=F32)
        out_ref[j] = (updated[j] + warmth).astype(BF16)


def mean_kernel(tiles_ref, cell_ref, slot_ref, out_ref):
    members = tiles_ref.shape[0]
    total = jnp.zeros(tiles_ref.shape[1:], F32)
    for member in range(members):
        total = total + tiles_ref[member].astype(F32)
    pieces = jnp.concatenate(in_three(total), axis=0)
    for j in range(cell_ref.shape[0]):
        picked = lax.dot_general(
            pieces, cell_ref[j], (((1,), (1,)), ((), ())), preferred_element_type=F32
        )
        joined = picked[:SLOTS] + picked[SLOTS : 2 * SLOTS] + picked[2 * SLOTS :]
        kept = jnp.where(slot_ref[j] > 0, joined, 0.0)
        out_ref[j : j + 1, :] = jnp.sum(kept, axis=0, keepdims=True) / members


def call(kernel, outs, operands, flops, scratch=(), limit=32, specs=None):
    size = sum(math.prod(o.shape) * o.dtype.itemsize for o in list(outs) + list(operands))
    return pl.pallas_call(
        kernel,
        out_shape=outs if len(outs) > 1 else outs[0],
        in_specs=specs or [WHOLE] * len(operands),
        out_specs=[WHOLE] * len(outs) if len(outs) > 1 else WHOLE,
        scratch_shapes=list(scratch),
        compiler_params=pltpu.CompilerParams(vmem_limit_bytes=limit * 1024 * 1024),
        cost_estimate=pl.CostEstimate(flops=flops, bytes_accessed=size, transcendentals=0),
    )(*operands)


def shards(
    air_ensemble,
    sea_indicator,
    layernorm_scaling,
    harmonic_damping_factor,
    bypass_factor,
    core_exit_factor,
    air_to_exchange_factor,
    sea_heat_imprint,
    sea_ensemble_arrays,
    input_to_hidden_kernel,
    hidden_to_change_kernel,
    patch_exchange_pick,
    node_sea_pick,
    patch_holder_shift,
    wet_depth_layers,
):
    bands = lax.axis_size("space")
    members = lax.axis_size("member")
    air = air_ensemble[0]
    latitude_rows, longitudes, channels = air.shape
    latitudes = latitude_rows * bands
    hidden_channels = input_to_hidden_kernel.shape[1]
    per_device = MMAX // bands
    chunk = 2 * per_device * latitude_rows
    shape = jax.ShapeDtypeStruct

    analysis, synthesis = (jnp.asarray(t) for t in fourier_tables())
    spectra, normed = call(
        analysis_kernel,
        [shape((bands, chunk, channels), BF16), shape(air.shape, BF16)],
        [air, layernorm_scaling[None, :], analysis],
        2 * 2 * MMAX * latitude_rows * longitudes * channels,
    )
    gathered = lax.all_to_all(spectra, "space", split_axis=0, concat_axis=0, tiled=True)

    slots = sea_ensemble_arrays[0]
    a0 = slots[:8]
    a1 = passed_along(slots[8:], "space", -4)
    b1 = passed_along(jnp.concatenate([a0[4:], a1[4:]], axis=0), "space", -2)
    c1 = passed_along(
        jnp.concatenate([a0[2:4], a1[2:4], b1[2:4], b1[6:8]], axis=0), "space", -1
    )
    offsets = patch_holder_shift[:, 0]
    earlier = jnp.tril(jnp.ones((HOME_DEV, HOME_DEV), jnp.int32), -1)
    positions = jnp.sum((offsets[:, None] == offsets[None, :]).astype(jnp.int32) * earlier, axis=1)
    targets = offsets * CAP + positions
    selected = targets[None, :] == jnp.arange(SLOTS, dtype=jnp.int32)[:, None]
    depths = jnp.sum(jnp.where(selected, wet_depth_layers[None, :], 0), axis=1)
    kernel = jnp.transpose(input_to_hidden_kernel, (1, 0, 2))
    state_weight = jnp.pad(kernel[:, :, :OCH], ((0, 0), (0, 0), (0, OCH_PAD - OCH))).reshape(
        hidden_channels, -1
    )
    forcing_weight = kernel[:, :, OCH:].reshape(hidden_channels, -1)
    decode_weight = jnp.pad(hidden_to_change_kernel, ((0, 16 - len(TAPS)), (0, 0)))
    wet = call(
        ocean_kernel,
        [shape((hidden_channels, SPAN), F32)],
        [depths, a0, a1, b1, c1, state_weight],
        2 * hidden_channels * len(TAPS) * OCH_PAD * SPAN,
        [pltpu.VMEM((len(TAPS) * OCH_PAD, SPAN), BF16)],
        specs=[pl.BlockSpec(memory_space=pltpu.SMEM)] + [WHOLE] * 5,
    )
    picks = jnp.sum(jnp.where(selected[:, :, None], patch_exchange_pick[None], 0), axis=1)
    picks = picks.reshape(1, SPAN)
    line = picks // longitudes
    place = (
        picks % longitudes == jnp.arange(longitudes, dtype=jnp.int32)[:, None]
    ).astype(BF16)
    top = jnp.concatenate(
        [a0[0:2, 0], c1[0:2, 0], b1[0:2, 0], c1[4:6, 0], a1[0:2, 0], c1[2:4, 0], b1[4:6, 0], c1[6:8, 0]],
        axis=0,
    ).astype(F32).reshape(1, SPAN)
    tile = node_sea_pick // CELLS
    holder = jnp.sum(
        jnp.where(
            tile[:, :, None] == jnp.arange(HOME_DEV, dtype=jnp.int32), targets[None, None, :], 0
        ),
        axis=2,
    )
    holder = jnp.where(sea_indicator > 0, holder, -1)
    cell = (
        (node_sea_pick % CELLS)[:, :, None] == jnp.arange(CELLS, dtype=jnp.int32)
    ).astype(BF16)
    slot_of = (
        holder[:, :, None] == jnp.arange(3 * SLOTS, dtype=jnp.int32) % SLOTS
    ).astype(BF16)
    slot_rows = (
        holder[:, None, :] == jnp.arange(SLOTS, dtype=jnp.int32)[None, :, None]
    ).astype(F32)
    skip = jnp.einsum("jkc,cd->jkd", normed, bypass_factor, preferred_element_type=F32)
    forward, backward = (jnp.asarray(t) for t in legendre_tables(latitudes))
    first = lax.axis_index("space") * per_device
    forward = lax.dynamic_slice_in_dim(forward, first, per_device, 0)
    backward = lax.dynamic_slice_in_dim(backward, first, per_device, 0)
    filtered = call(
        legendre_kernel,
        [shape((bands, chunk, channels), BF16)],
        [gathered, forward, backward, harmonic_damping_factor],
        2 * 2 * 2 * per_device * LMAX * latitudes * channels,
        [pltpu.VMEM((channels // 128, bands * chunk, 128), F32)],
    )
    returned = lax.all_to_all(filtered, "space", split_axis=0, concat_axis=0, tiled=True)
    out, tiles = call(
        closing_kernel,
        [shape(air.shape, BF16), shape((SLOTS, CELLS), BF16)],
        [
            returned, synthesis, skip, air, core_exit_factor, air_to_exchange_factor.T, place,
            line, wet, forcing_weight, decode_weight, top, cell, slot_of,
            sea_heat_imprint[None, :],
        ],
        2 * latitude_rows * longitudes * channels * (channels + 2 * MMAX),
        [
            pltpu.VMEM(air.shape, F32),
            pltpu.VMEM((FC * latitude_rows, longitudes), F32),
            pltpu.VMEM((SLOTS, CELLS), F32),
        ],
    )
    everyone = lax.all_to_all(
        jnp.broadcast_to(tiles[None], (members,) + tiles.shape),
        "member",
        split_axis=0,
        concat_axis=0,
        tiled=True,
    )
    mean = call(
        mean_kernel,
        [shape((latitude_rows, longitudes), F32)],
        [everyone, cell, slot_rows],
        2 * 3 * SLOTS * CELLS * latitude_rows * longitudes,
    )
    return (out[None], mean)


def solution(mesh):
    in_specs = (
        P("member", "space", None, None),
        P("space", None),
        P(),
        P(),
        P(),
        P(),
        P(),
        P(),
        P("member", "space", None, None),
        P(),
        P(),
        P("space", None),
        P("space", None),
        P("space", None),
        P("space"),
    )
    out_specs = (P("member", "space", None, None), P("space", None))
    return jax.shard_map(shards, mesh=mesh, in_specs=in_specs, out_specs=out_specs, check_vma=False)
```

time: 834 us -> 168 us (0.20); the launches traced: 821 us -> 167 us
  loops' own time: 400 us -> 0 us
  other arithmetic: 112 us -> 7.93 us
  local copies, waits for them, and re-layouts: 133 us -> 38.5 us
  starting transfers between devices: 114 us -> 41.4 us
  waiting for transfers between devices: 14.2 us -> 60.2 us
  blocking collectives: 33.9 us -> 0 us
  Pallas kernels: 0 us -> 15.5 us
  matrix products: 12.7 us -> 2.17 us
    another operation x1 -> x0, loops' own time: 400 us -> none  [legendre_basis(): _, stacked = lax.scan(advance, (empty_rows, empty_rows), degree_values)]
    dynamic_slice x128 -> x1, local copies, waits for them, and re-layouts: 82.1 us -> 0.99 us  [shards(): backward = lax.dynamic_slice_in_dim(backward, first, per_device, 0)]
    eq x128 -> x1, other arithmetic: 80.6 us -> 0.01 us  [shards(): selected = targets[None, :] == jnp.arange(SLOTS, dtype=jnp.int32)[:, None]]
    ppermute x24 -> x3, starting transfers between devices: 84.7 us -> 12.2 us  [passed_along(): lax.ppermute(value, axis, [(i, (i + by) % devices) for i in range(devices)])]
    all_to_all x2 -> x3, waiting for transfers between devices: 0.01 us -> 41.2 us  [the longest x1 34.4 us: shards(): lax.all_to_all(spectra, 'space', split_axis=0, concat_axis=0, tiled=True)]
    psum x1 -> x0, blocking collectives: 33.9 us -> none  [shards(): ensemble_sum = lax.psum(boundary_layer_array, 'member')]
    unnamed x65 -> x77, local copies, waits for them, and re-layouts: 3.47 us -> 22.7 us
    pallas_call x0 -> x5, Pallas kernels: none -> 15.5 us  [call(): pl.pallas_call(kernel, out_shape=outs if len(outs) > 1 else outs[0], in_s...]
  transfers between devices with their start and end apart: 26 -> 6, of which waited for: 6 -> 4; matrix products, arithmetic and copies ran while one was open for 23% -> 17% of each run, Pallas kernels for 0% -> 3%
where the time goes in v1:
time: 168 us; the launch traced here: 167 us
  waiting for transfers between devices  60.2 us (36%)
  starting transfers between devices  41.4 us (25%)
  local copies, waits for them, and re-layouts  38.5 us (23%)
  Pallas kernels  15.5 us (9%)
  other arithmetic  7.93 us (5%)
  matrix products  2.17 us (1%)
    all_to_all x1, waiting for transfers between devices, shards(): lax.all_to_all(spectra, 'space', split_axis=0, concat_axis=0, tiled=True)  34.4 us
    unnamed x77, local copies, waits for them, and re-layouts  22.7 us
    ppermute x3, waiting for transfers between devices, passed_along(): lax.ppermute(value, axis, [(i, (i + by) % devices) for i in range(devices)])  19 us
    all_to_all x1, starting transfers between devices, shards(): lax.all_to_all(spectra, 'space', split_axis=0, concat_axis=0, tiled=True)  16.9 us
    pallas_call x5, Pallas kernels, call(): pl.pallas_call(kernel, out_shape=outs if len(outs) > 1 else outs[0], in_s...  15.5 us
    ppermute x3, starting transfers between devices, passed_along(): lax.ppermute(value, axis, [(i, (i + by) % devices) for i in range(devices)])  12.2 us
    all_to_all x1, waiting for transfers between devices, shards(): lax.all_to_all(jnp.broadcast_to(tiles[None], (members,) + tiles.shape), '...  6.8 us
    all_to_all x1, starting transfers between devices, shards(): lax.all_to_all(jnp.broadcast_to(tiles[None], (members,) + tiles.shape), '...  6.75 us
  transfers between devices with their start and end apart: 6, of which 4 were waited for; matrix products, arithmetic and copies ran while one was open for 17% of the time, Pallas kernels for 3%

profile of v1, /device:TPU:1, one launch (start us, length us, event | category | flops | bytes accessed | tf_op | source)
XLA Modules:
  0.0 166.8 jit_solution(7066529486406284204)
XLA Ops:
  0.6 0.7 broadcast_in_dim.83.scale_ref
  1.4 1.2 copy-done.4
  2.6 0.9 copy-done.13
  3.6 2.2 %shard_map.194 = (bf16[32,32,384]{2,1,0:T(8,128)(2,1)}, bf16[4,360,384]{2,1,0:T(8,128)(2,1)S(1)}) custom-call(bf16[4,360,384]{2,1,0:T(8,128)(2,1)S(1)} %bitcast.60, f32[1,384]{1,0:T(1,128)S(1)} %broadcast_in_dim.83.scale_ref, bf16[256,360]{1,0:T(8,128)(2,1)S(1)} %copy-done.13), custom_call_target="tpu_custom_call" | custom-call | flops 283115520 | bytes 3184128 | tf_op jit(solution)/shard_map/pallas_call | solution.py:247
  5.8 1.0 copy-done.6
  6.8 16.9 %all-to-all-start = ((bf16[32,32,384]{2,1,0:T(8,128)(2,1)}), bf16[32,32,384]{2,1,0:T(8,128)(2,1)S(1)}, u32[]{:S(2)}, u32[]{:S(2)}) async-start(bf16[32,32,384]{2,1,0:T(8,128)(2,1)} %get-tuple-element.6), calls=%async_computation | async-start | bytes 1572864 | tf_op jit(solution)/shard_map/all_to_all | solution.py:292
  23.7 0.7 fusion.9
  24.4 0.7 copy.117
  25.0 5.5 %collective-permute-start = (bf16[8,76,128]{2,1,0:T(8,128)(2,1)}, bf16[8,76,128]{2,1,0:T(8,128)(2,1)S(1)}, u32[]{:S(2)}, u32[]{:S(2)}) collective-permute-start(bf16[8,76,128]{2,1,0:T(8,128)(2,1)} %bitcast.54), channel_id=1, source_target_pairs={{0,28},{1,29},{2,30},{3,31},{4,0},{5,1},{6,2},{7,3},{8,4},{9,5},{1... | collective-permute-start | bytes 466952 | tf_op jit(solution)/shard_map/ppermute | solution.py:32
  31.1 1.0 constant_dynamic-slice_fusion
  32.5 0.8 slice_select_fusion
  33.3 0.6 bitcast_select_fusion.line_ref
  33.9 34.4 %all-to-all-done.x_ref = bf16[32,32,384]{2,1,0:T(8,128)(2,1)S(1)} async-done(((bf16[32,32,384]{2,1,0:T(8,128)(2,1)}), bf16[32,32,384]{2,1,0:T(8,128)(2,1)S(1)}, u32[]{:S(2)}, u32[]{:S(2)}) %all-to-all-start) | async-done | bytes 786464 | tf_op jit(solution)/shard_map/all_to_all | solution.py:292
  68.3 2.8 %shard_map.195 = bf16[32,32,384]{2,1,0:T(8,128)(2,1)} custom-call(bf16[32,32,384]{2,1,0:T(8,128)(2,1)S(1)} %all-to-all-done.x_ref, bf16[4,128,128]{2,1,0:T(8,128)(2,1)S(1)} %get-tuple-element.23.forward_ref, bf16[4,128,128]{2,1,0:T(8,128)(2,1)S(1)} %get-tuple-element.22.backward_ref, f32[128,384]{1,0:T(8,128)S(1)} %copy-done.14), custom_call_target="tpu_custom_call" | custom-call | flops 201326592 | bytes 2031616 | tf_op jit(solution)/shard_map/pallas_call | solution.py:247
  71.1 5.6 %all-to-all-start.1 = ((bf16[32,32,384]{2,1,0:T(8,128)(2,1)}), bf16[32,32,384]{2,1,0:T(8,128)(2,1)}, u32[]{:S(2)}, u32[]{:S(2)}) async-start(bf16[32,32,384]{2,1,0:T(8,128)(2,1)} %shard_map.195), calls=%async_computation.1 | async-start | bytes 1572864 | tf_op jit(solution)/shard_map/all_to_all | solution.py:360
  76.8 2.2 %fusion.2.skip_ref = f32[4,360,384]{2,1,0:T(8,128)S(1)} fusion(bf16[4,360,384]{2,1,0:T(8,128)(2,1)} %copy-done.6, bf16[384,384]{1,0:T(8,128)(2,1)S(1)} %copy-done), kind=kOutput, calls=%fused_computation.6 | convolution fusion | flops 424673280 | bytes 3612672 | tf_op jit(solution)/shard_map/jkc,cd->jkd/dot_general | solution.py:348
  78.9 1.5 fusion.place_ref
  80.7 0.7 pad_maximum_fusion
  81.4 4.6 %collective-permute-start.1 = (bf16[8,76,128]{2,1,0:T(8,128)(2,1)}, bf16[8,76,128]{2,1,0:T(8,128)(2,1)}, u32[]{:S(2)}, u32[]{:S(2)}) collective-permute-start(bf16[8,76,128]{2,1,0:T(8,128)(2,1)} %pad_maximum_fusion), channel_id=1, source_target_pairs={{0,30},{1,31},{2,0},{3,1},{4,2},{5,3},{6,4},{7,5},{8,6},{9,7},{10,... | collective-permute-start | bytes 466952 | tf_op jit(solution)/shard_map/ppermute | solution.py:32
  86.0 1.5 slice_bitcast_fusion
  87.5 1.0 slice.76
  88.5 0.6 copy.120
  89.1 0.7 copy-done.7
  89.8 0.5 copy.122
  90.3 1.1 copy.89.weight_ref
  91.5 1.5 copy.90.forcing_weight_ref
  93.0 0.7 broadcast_in_dim.93.imprint_ref
  93.6 1.3 pad.9.decode_ref
  94.9 1.3 select_reduce_fusion.2.depth_ref
  96.2 0.7 slice.101
  96.9 0.6 copy.121
  97.5 0.8 slice.92
  98.3 16.7 %collective-permute-done.1.b1_ref = bf16[8,76,128]{2,1,0:T(8,128)(2,1)} collective-permute-done((bf16[8,76,128]{2,1,0:T(8,128)(2,1)}, bf16[8,76,128]{2,1,0:T(8,128)(2,1)}, u32[]{:S(2)}, u32[]{:S(2)}) %collective-permute-start.1) | collective-permute-done | bytes 155680 | tf_op jit(solution)/shard_map/ppermute | solution.py:32
  114.9 0.8 fusion.12
  115.7 0.8 pad_maximum_fusion.1
  116.5 2.2 %collective-permute-start.2 = (bf16[8,76,128]{2,1,0:T(8,128)(2,1)S(1)}, bf16[8,76,128]{2,1,0:T(8,128)(2,1)S(1)}, u32[]{:S(2)}, u32[]{:S(2)}) collective-permute-start(bf16[8,76,128]{2,1,0:T(8,128)(2,1)S(1)} %pad_maximum_fusion.1), channel_id=1, source_target_pairs={{0,31},{1,0},{2,1},{3,2},{4,3},{5,4},{6,5},{7,6},{8,7},{9,8},{10,9... | collective-permute-start | bytes 466952 | tf_op jit(solution)/shard_map/ppermute | solution.py:32
  118.7 0.7 fusion.11
  119.9 2.4 %collective-permute-done.2.c1_ref = bf16[8,76,128]{2,1,0:T(8,128)(2,1)S(1)} collective-permute-done((bf16[8,76,128]{2,1,0:T(8,128)(2,1)S(1)}, bf16[8,76,128]{2,1,0:T(8,128)(2,1)S(1)}, u32[]{:S(2)}, u32[]{:S(2)}) %collective-permute-start.2) | collective-permute-done | bytes 155680 | tf_op jit(solution)/shard_map/ppermute | solution.py:32
  122.3 0.7 copy-done.16
  123.0 0.6 copy_bitcast_fusion.4
  123.6 0.6 copy_bitcast_fusion.8
  124.2 2.6 %concatenate.11 = bf16[16,128]{1,0:T(8,128)(2,1)} concatenate(bf16[2,128]{1,0:T(2,128)(2,1)} %bitcast.73, bf16[2,128]{1,0:T(2,128)(2,1)} %get-tuple-element.27, bf16[2,128]{1,0:T(2,128)(2,1)} %get-tuple-element.29, bf16[2,128]{1,0:T(2,128)(2,1)} %get-tuple-element.26, bf16[2,128]{1,0:T(2,128)(2,1)} %bitcast.74, bf16[2,128]{1,0:T(2,128)(2,1)} %get-tuple-element.25, ...), dimensions={0} | concatenate | bytes 8192 | tf_op jit(solution)/shard_map/concatenate | solution.py:327
  126.7 1.3 convert_element_type.36
  128.0 0.9 copy-done.8
  128.9 0.9 copy-done.10
  129.8 0.9 copy-done.17
  130.7 0.6 copy-done.22
  131.3 2.3 %shard_map.196.wet_ref = f32[200,2048]{1,0:T(8,128)S(1)} custom-call(s32[16]{0:T(128)S(1)} %copy-done.22, bf16[8,76,128]{2,1,0:T(8,128)(2,1)S(1)} %bitcast.63, bf16[8,76,128]{2,1,0:T(8,128)(2,1)S(1)} %copy-done.10, bf16[8,76,128]{2,1,0:T(8,128)(2,1)} %collective-permute-done.1.b1_ref, bf16[8,76,128]{2,1,0:T(8,128)(2,1)S(1)} %copy-done.17, ...), custom_call_target="tpu_custom_call" | custom-call | flops 589824000 | bytes 2549056 | tf_op jit(solution)/shard_map/pallas_call | solution.py:247
  133.6 1.2 copy-done.1
  134.8 1.4 copy-done.2
  136.2 1.4 copy-done.3
  137.6 1.2 copy-done.5
  138.8 1.0 copy-done.11
  139.8 0.8 copy-done.12
  140.6 0.9 copy-done.15
  141.5 0.7 copy-done.18
  142.2 0.7 copy-done.19
  142.9 0.7 copy-done.20
  143.6 0.7 copy-done.21
  144.3 7.4 %shard_map.197 = (bf16[4,360,384]{2,1,0:T(8,128)(2,1)}, bf16[16,128]{1,0:T(8,128)(2,1)S(1)}) custom-call(bf16[32,32,384]{2,1,0:T(8,128)(2,1)} %all-to-all-done.1.rows_ref, bf16[360,256]{1,0:T(8,128)(2,1)S(1)} %copy-done.15, f32[4,360,384]{2,1,0:T(8,128)S(1)} %fusion.2.skip_ref, bf16[4,360,384]{2,1,0:T(8,128)(2,1)S(1)} %bitcast.61, ...), custom_call_target="tpu_custom_call" | custom-call | flops 707788800 | bytes 9372544 | tf_op jit(solution)/shard_map/pallas_call | solution.py:247
  151.7 0.6 broadcast_in_dim.95
  152.4 6.8 %all-to-all-start.2 = ((bf16[16,16,128]{2,1,0:T(8,128)(2,1)}), bf16[16,16,128]{2,1,0:T(8,128)(2,1)S(1)}, u32[]{:S(2)}, u32[]{:S(2)}) async-start(bf16[16,16,128]{2,1,0:T(8,128)(2,1)} %broadcast_in_dim.95), calls=%async_computation.2 | async-start | bytes 131072 | tf_op jit(solution)/shard_map/all_to_all | solution.py:376
  159.1 6.8 %all-to-all-done.2.tiles_ref = bf16[16,16,128]{2,1,0:T(8,128)(2,1)S(1)} async-done(((bf16[16,16,128]{2,1,0:T(8,128)(2,1)}), bf16[16,16,128]{2,1,0:T(8,128)(2,1)S(1)}, u32[]{:S(2)}, u32[]{:S(2)}) %all-to-all-start.2) | async-done | bytes 65568 | tf_op jit(solution)/shard_map/all_to_all | solution.py:376
  166.0 0.9 shard_map.198
  (73 shorter events, 1.8 us)
Async XLA Ops:
  0.6 76.1 %copy-start = (bf16[384,384]{1,0:T(8,128)(2,1)S(1)}, bf16[384,384]{1,0:T(8,128)(2,1)}, u32[]{:S(2)}) copy-start(bf16[384,384]{1,0:T(8,128)(2,1)} %param.23) | copy-start | bytes 884740
  1.4 1.2 copy-start.4
  2.6 0.9 copy-start.13
  3.5 20.1 %copy-start.24 = (bf16[1,16,76,128]{3,1,2,0:T(8,128)(2,1)S(1)}, bf16[1,16,76,128]{3,1,2,0:T(8,128)(2,1)}, u32[]{:S(2)}) copy-start(bf16[1,16,76,128]{3,1,2,0:T(8,128)(2,1)} %param.27) | copy-start | bytes 933892
  3.5 27.0 %copy-start.32 = (s32[14,1]{0,1:T(1,128)S(1)}, s32[14,1]{0,1:T(1,128)}, u32[]{:S(2)}) copy-start(s32[14,1]{0,1:T(1,128)} %param.32) | copy-start | bytes 172
  3.5 27.3 %copy-start.28 = (s32[14,128]{1,0:T(8,128)S(1)}, s32[14,128]{1,0:T(8,128)}, u32[]{:S(2)}) copy-start(s32[14,128]{1,0:T(8,128)} %param.30) | copy-start | bytes 21508
  3.6 27.4 %copy-start.29 = (s32[4,360]{1,0:T(4,128)S(1)}, s32[4,360]{1,0:T(4,128)}, u32[]{:S(2)}) copy-start(s32[4,360]{1,0:T(4,128)} %param.31) | copy-start | bytes 17284
  5.8 1.0 copy-start.6
  6.8 25.4 %copy-start.30 = (s32[4,360]{1,0:T(4,128)S(1)}, s32[4,360]{1,0:T(4,128)}, u32[]{:S(2)}) copy-start(s32[4,360]{1,0:T(4,128)} %param.20) | copy-start | bytes 17284
  6.8 25.7 %copy-start.25 = (bf16[9,200,84]{1,2,0:T(8,128)(2,1)S(1)}, bf16[9,200,84]{1,2,0:T(8,128)(2,1)}, u32[]{:S(2)}) copy-start(bf16[9,200,84]{1,2,0:T(8,128)(2,1)} %param.28) | copy-start | bytes 907204
  6.8 25.7 %copy-start.33 = (pred[80]{0:T(512)(128)(4,1)S(1)}, pred[80]{0:T(512)(128)(4,1)}, u32[]{:S(2)}) copy-start(pred[80]{0:T(512)(128)(4,1)} %constant.83.clone.1) | copy-start | bytes 244
  6.8 61.6 %all-to-all-start = ((bf16[32,32,384]{2,1,0:T(8,128)(2,1)}), bf16[32,32,384]{2,1,0:T(8,128)(2,1)S(1)}, u32[]{:S(2)}, u32[]{:S(2)}) async-start(bf16[32,32,384]{2,1,0:T(8,128)(2,1)} %get-tuple-element.6), calls=%async_computation | async-start | bytes 1572864 | tf_op jit(solution)/shard_map/all_to_all | solution.py:292
  23.7 44.7 %copy-start.14 = (f32[128,384]{1,0:T(8,128)S(1)}, f32[128,384]{1,0:T(8,128)}, u32[]{:S(2)}) copy-start(f32[128,384]{1,0:T(8,128)} %gains_ref.1) | copy-start | bytes 589828
  25.0 55.6 %collective-permute-start = (bf16[8,76,128]{2,1,0:T(8,128)(2,1)}, bf16[8,76,128]{2,1,0:T(8,128)(2,1)S(1)}, u32[]{:S(2)}, u32[]{:S(2)}) collective-permute-start(bf16[8,76,128]{2,1,0:T(8,128)(2,1)} %bitcast.54), channel_id=1, source_target_pairs={{0,28},{1,29},{2,30},{3,31},{4,0},{5,1},{6,2},{7,3},{8,4},{9,5},{1... | collective-permute-start | bytes 466952 | tf_op jit(solution)/shard_map/ppermute | solution.py:32
  30.7 1.4 copy-start.31
  32.2 38.9 %copy-start.26 = (s32[4,360]{1,0:T(4,128)}, s32[4,360]{1,0:T(4,128)S(1)}, u32[]{:S(2)}) copy-start(s32[4,360]{1,0:T(4,128)S(1)} %compare_select_fusion) | copy-start | bytes 17284
  71.1 63.7 %all-to-all-start.1 = ((bf16[32,32,384]{2,1,0:T(8,128)(2,1)}), bf16[32,32,384]{2,1,0:T(8,128)(2,1)}, u32[]{:S(2)}, u32[]{:S(2)}) async-start(bf16[32,32,384]{2,1,0:T(8,128)(2,1)} %shard_map.195), calls=%async_computation.1 | async-start | bytes 1572864 | tf_op jit(solution)/shard_map/all_to_all | solution.py:360
  78.9 10.2 %copy-start.23 = (bf16[1,8,76,128]{3,1,2,0:T(8,128)(2,1)S(1)}, bf16[1,8,76,128]{3,1,2,0:T(8,128)(2,1)}, u32[]{:S(2)}) copy-start(bf16[1,8,76,128]{3,1,2,0:T(8,128)(2,1)} %get-tuple-element.11) | copy-start | bytes 466948
  80.7 9.7 %copy-start.9 = (bf16[8,76,128]{2,1,0:T(8,128)(2,1)}, bf16[8,76,128]{2,1,0:T(8,128)(2,1)S(1)}, u32[]{:S(2)}) copy-start(bf16[8,76,128]{2,1,0:T(8,128)(2,1)S(1)} %collective-permute-done.a1_ref) | copy-start | bytes 466948
  81.4 33.5 %collective-permute-start.1 = (bf16[8,76,128]{2,1,0:T(8,128)(2,1)}, bf16[8,76,128]{2,1,0:T(8,128)(2,1)}, u32[]{:S(2)}, u32[]{:S(2)}) collective-permute-start(bf16[8,76,128]{2,1,0:T(8,128)(2,1)} %pad_maximum_fusion), channel_id=1, source_target_pairs={{0,30},{1,31},{2,0},{3,1},{4,2},{5,3},{6,4},{7,5},{8,6},{9,7},{10,... | collective-permute-start | bytes 466952 | tf_op jit(solution)/shard_map/ppermute | solution.py:32
  89.1 0.7 copy-start.7
  116.5 5.8 %collective-permute-start.2 = (bf16[8,76,128]{2,1,0:T(8,128)(2,1)S(1)}, bf16[8,76,128]{2,1,0:T(8,128)(2,1)S(1)}, u32[]{:S(2)}, u32[]{:S(2)}) collective-permute-start(bf16[8,76,128]{2,1,0:T(8,128)(2,1)S(1)} %pad_maximum_fusion.1), channel_id=1, source_target_pairs={{0,31},{1,0},{2,1},{3,2},{4,3},{5,4},{6,5},{7,6},{8,7},{9,8},{10,9... | collective-permute-start | bytes 466952 | tf_op jit(solution)/shard_map/ppermute | solution.py:32
  122.3 0.7 copy-start.16
  128.0 0.9 copy-start.8
  128.9 0.9 copy-start.10
  129.8 0.9 copy-start.17
  130.7 0.6 copy-start.22
  133.6 1.2 copy-start.1
  134.8 1.4 copy-start.2
  136.2 1.4 copy-start.3
  137.6 1.2 copy-start.5
  138.8 1.0 copy-start.11
  139.8 0.8 copy-start.12
  140.6 0.9 copy-start.15
  141.5 0.7 copy-start.18
  142.2 0.7 copy-start.19
  142.9 0.7 copy-start.20
  143.6 0.7 copy-start.21
  144.3 14.8 %copy-start.27 = (s32[4,360]{1,0:T(4,128)S(1)}, s32[4,360]{1,0:T(4,128)}, u32[]{:S(2)}) copy-start(s32[4,360]{1,0:T(4,128)} %copy-done.26) | copy-start | bytes 17284
  152.4 13.6 %all-to-all-start.2 = ((bf16[16,16,128]{2,1,0:T(8,128)(2,1)}), bf16[16,16,128]{2,1,0:T(8,128)(2,1)S(1)}, u32[]{:S(2)}, u32[]{:S(2)}) async-start(bf16[16,16,128]{2,1,0:T(8,128)(2,1)} %broadcast_in_dim.95), calls=%async_computation.2 | async-start | bytes 131072 | tf_op jit(solution)/shard_map/all_to_all | solution.py:376

commit v2 on v1

--- a/solution.py
+++ b/solution.py
@@ -22,9 +22,12 @@
 OCH = 76
 OCH_PAD = 80
 TAPS = [(row, col) for row in (-1, 0, 1) for col in (-1, 0, 1)]
+LARGE = 56
+EARLY = 3
 BF16 = jnp.bfloat16
 F32 = jnp.float32
 WHOLE = pl.BlockSpec(memory_space=pltpu.VMEM)
+ANYWHERE = pl.BlockSpec(memory_space=pl.ANY)
 
 
 def passed_along(value, axis, by):
@@ -107,20 +110,37 @@
     return high, middle, (rest - middle.astype(F32)).astype(BF16)
 
 
-def analysis_kernel(air_ref, scale_ref, table_ref, spectra_ref, normed_ref):
+def begin(copies, sems):
+    started = [
+        pltpu.make_async_copy(source, target, sems.at[i])
+        for i, (source, target) in enumerate(copies)
+    ]
+    for one in started:
+        one.start()
+    return started
+
+
+def analysis_kernel(
+    air_any, scale_ref, table_any, spectra_ref, normed_ref, air_ref, table_ref, sems
+):
     rows = air_ref.shape[0]
     groups = spectra_ref.shape[0]
-    table = table_ref[...]
-    scale = scale_ref[...]
+    copies = begin(
+        [(air_any.at[j], air_ref.at[j]) for j in range(rows)] + [(table_any, table_ref)], sems
+    )
+    scale = scale_ref[...].reshape(1, scale_ref.shape[0])
     for pair in range(rows // 2):
         both = []
         for j in (2 * pair, 2 * pair + 1):
+            copies[j].wait()
             x = air_ref[j].astype(F32)
             centered = x - jnp.mean(x, axis=-1, keepdims=True)
             spread = jnp.mean(centered * centered, axis=-1, keepdims=True)
             normed = (centered * lax.rsqrt(spread + 1e-05) * scale).astype(BF16)
             normed_ref[j] = normed
-            out = jnp.dot(table, normed, preferred_element_type=F32)
+            if j == 0:
+                copies[rows].wait()
+            out = jnp.dot(table_ref[...], normed, preferred_element_type=F32)
             both.append(out.reshape(groups, 8, out.shape[1]))
         block = jnp.concatenate(both, axis=1)
         spectra_ref[:, 16 * pair : 16 * (pair + 1), :] = block.astype(BF16)
@@ -149,50 +169,62 @@
         out_ref[:, :, lanes] = work[third].reshape(groups, chunk, 128).astype(BF16)
 
 
-def ocean_kernel(depth_ref, a0_ref, a1_ref, b1_ref, c1_ref, weight_ref, out_ref, columns):
+def ocean_kernel(depth_ref, *refs):
+    pieces, (weight_ref, out_ref, top_ref, columns) = refs[:NEAR], refs[NEAR:]
     masks = tap_masks(CELLS)
     level = lax.broadcasted_iota(jnp.int32, (OCH, CELLS), 0) % LEV
-    places = {
-        0: (a0_ref, 0), 4: (a1_ref, 0), 2: (b1_ref, 0), 6: (b1_ref, 4),
-        1: (c1_ref, 0), 5: (c1_ref, 2), 3: (c1_ref, 4), 7: (c1_ref, 6),
-    }
     for slot in range(SLOTS):
-        ref, at = places[slot // CAP]
-        state = ref[at + slot % CAP].astype(F32)
+        lanes = slice(CELLS * slot, CELLS * (slot + 1))
+        state = pieces[slot // CAP][slot % CAP].astype(F32)
+        top_ref[:, lanes] = state[0:1]
         state = jnp.where(level < depth_ref[slot], state, 0.0)
         state = jnp.concatenate([state, jnp.zeros((OCH_PAD - OCH, CELLS), F32)], axis=0)
         for q, tap in enumerate(TAPS):
             moved = shifted(state, tap, masks[q]).astype(BF16)
-            columns[OCH_PAD * q : OCH_PAD * (q + 1), CELLS * slot : CELLS * (slot + 1)] = moved
+            columns[OCH_PAD * q : OCH_PAD * (q + 1), lanes] = moved
     for at in range(0, SPAN, 512):
         out_ref[:, at : at + 512] = jnp.dot(
             weight_ref[...], columns[:, at : at + 512], preferred_element_type=F32
         )
 
 
-def closing_kernel(
-    rows_ref, synthesis_ref, skip_ref, air_ref, exit_ref, exchange_ref, place_ref, line_ref,
-    wet_ref, forcing_weight_ref, decode_ref, top_ref, cell_ref, slot_ref, imprint_ref,
-    out_ref, tiles_ref, updated, flux, sst,
-):
+def surface_kernel(*refs):
+    sources, (updated_any, tiles_ref), held, (updated_ref, flux, sst, sems, out_sems) = (
+        refs[:12], refs[12:14], refs[14:26], refs[26:]
+    )
+    leaving = []
+    copies = begin(list(zip(sources, held)), sems)
+    (
+        rows_ref, synthesis_ref, skip_ref, air_ref, exit_ref, exchange_ref, place_ref, line_ref,
+        forcing_weight_ref, wet_ref, decode_ref, top_ref,
+    ) = held
     latitude_rows = air_ref.shape[0]
     groups, chunk, channels = rows_ref.shape
-    synthesis = synthesis_ref[...]
-    fields = rows_ref[...].astype(F32).reshape(groups, latitude_rows, 8, channels)
+    for one in copies[:2]:
+        one.wait()
     for j in range(latitude_rows):
-        own = fields[:, j].reshape(8 * groups, channels).astype(BF16)
-        spectral = jnp.dot(synthesis, own, preferred_element_type=F32)
+        own = rows_ref[...].astype(F32).reshape(groups, latitude_rows, 8, channels)[:, j]
+        own = own.reshape(8 * groups, channels).astype(BF16)
+        spectral = jnp.dot(synthesis_ref[...], own, preferred_element_type=F32)
+        if j == 0:
+            for one in copies[2:6]:
+                one.wait()
         mixed = gelu(spectral + skip_ref[j]).astype(BF16)
         state = air_ref[j].astype(F32) + jnp.dot(
             mixed, exit_ref[...], preferred_element_type=F32
         )
-        updated[j] = state
+        updated_ref[j] = state
+        leave = pltpu.make_async_copy(updated_ref.at[j], updated_any.at[j], out_sems.at[j])
+        leave.start()
+        leaving.append(leave)
         high = state.astype(BF16)
         low = (state - high.astype(F32)).astype(BF16)
-        dims = (((1,), (1,)), ((), ()))
+        dims = (((0,), (1,)), ((), ()))
         flux[8 * j : 8 * (j + 1), :] = lax.dot_general(
             exchange_ref[...], high, dims, preferred_element_type=F32
         ) + lax.dot_general(exchange_ref[...], low, dims, preferred_element_type=F32)
+    for one in copies[6:]:
+        one.wait()
     spread = jnp.dot(flux[...].astype(BF16), place_ref[...], preferred_element_type=F32)
     line = line_ref[...]
     forcing = jnp.zeros((FC, SPAN), F32)
@@ -202,29 +234,37 @@
     columns = jnp.concatenate(
         [shifted(forcing, tap, masks[q]) for q, tap in enumerate(TAPS)], axis=0
     ).astype(BF16)
-    change = jnp.zeros((1, SPAN), F32)
     hidden = gelu(
         wet_ref[...] + jnp.dot(forcing_weight_ref[...], columns, preferred_element_type=F32)
     ).astype(BF16)
     partial = jnp.dot(decode_ref[...], hidden, preferred_element_type=F32)
+    change = jnp.zeros((1, SPAN), F32)
     for q, tap in enumerate(TAPS):
         change = change + shifted(partial[q : q + 1, :], tap, masks[q])
     surface = top_ref[...] + change
     for slot in range(SLOTS):
         sst[slot : slot + 1, :] = surface[:, CELLS * slot : CELLS * (slot + 1)]
     tiles = sst[...].astype(BF16)
-    tiles_ref[...] = tiles
+    for member in range(tiles_ref.shape[0]):
+        tiles_ref[member] = tiles
+    for one in leaving:
+        one.wait()
+
+
+def imprint_kernel(updated_ref, tiles_ref, cell_ref, slot_ref, imprint_ref, out_ref):
+    channels = updated_ref.shape[2]
+    tiles = tiles_ref[0]
     tripled = jnp.concatenate([tiles, tiles, tiles], axis=0)
+    pieces = in_three(imprint_ref[...].reshape(1, channels))
     imprint = jnp.concatenate(
-        [jnp.broadcast_to(piece, (SLOTS, channels)) for piece in in_three(imprint_ref[...])], axis=0
-    )
-    for j in range(latitude_rows):
-        picked = lax.dot_general(
-            cell_ref[j], tripled, (((1,), (1,)), ((), ())), preferred_element_type=F32
-        )
-        chosen = picked.astype(BF16) * slot_ref[j]
-        warmth = jnp.dot(chosen, imprint, preferred_element_type=F32)
-        out_ref[j] = (updated[j] + warmth).astype(BF16)
+        [jnp.broadcast_to(piece, (SLOTS, channels)) for piece in pieces], axis=0
+    )
+    picked = lax.dot_general(
+        cell_ref[0], tripled, (((1,), (1,)), ((), ())), preferred_element_type=F32
+    )
+    chosen = picked.astype(BF16) * slot_ref[0]
+    warmth = jnp.dot(chosen, imprint, preferred_element_type=F32)
+    out_ref[0] = (updated_ref[0] + warmth).astype(BF16)
 
 
 def mean_kernel(tiles_ref, cell_ref, slot_ref, out_ref):
@@ -242,17 +282,21 @@
         out_ref[j : j + 1, :] = jnp.sum(kept, axis=0, keepdims=True) / members
 
 
-def call(kernel, outs, operands, flops, scratch=(), limit=32, specs=None):
+def call(kernel, outs, operands, flops, scratch=(), limit=32, specs=None, out_specs=None):
     size = sum(math.prod(o.shape) * o.dtype.itemsize for o in list(outs) + list(operands))
     return pl.pallas_call(
         kernel,
         out_shape=outs if len(outs) > 1 else outs[0],
         in_specs=specs or [WHOLE] * len(operands),
-        out_specs=[WHOLE] * len(outs) if len(outs) > 1 else WHOLE,
+        out_specs=out_specs or ([WHOLE] * len(outs) if len(outs) > 1 else WHOLE),
         scratch_shapes=list(scratch),
         compiler_params=pltpu.CompilerParams(vmem_limit_bytes=limit * 1024 * 1024),
         cost_estimate=pl.CostEstimate(flops=flops, bytes_accessed=size, transcendentals=0),
     )(*operands)
+
+
+def held(operands):
+    return [pltpu.VMEM(o.shape, o.dtype) for o in operands]
 
 
 def shards(
@@ -286,18 +330,37 @@
     spectra, normed = call(
         analysis_kernel,
         [shape((bands, chunk, channels), BF16), shape(air.shape, BF16)],
-        [air, layernorm_scaling[None, :], analysis],
+        [air, layernorm_scaling, analysis],
         2 * 2 * MMAX * latitude_rows * longitudes * channels,
+        held([air, analysis]) + [pltpu.SemaphoreType.DMA((latitude_rows + 1,))],
+        limit=LARGE,
+        specs=[ANYWHERE, WHOLE, ANYWHERE],
     )
     gathered = lax.all_to_all(spectra, "space", split_axis=0, concat_axis=0, tiled=True)
 
     slots = sea_ensemble_arrays[0]
-    a0 = slots[:8]
-    a1 = passed_along(slots[8:], "space", -4)
-    b1 = passed_along(jnp.concatenate([a0[4:], a1[4:]], axis=0), "space", -2)
-    c1 = passed_along(
-        jnp.concatenate([a0[2:4], a1[2:4], b1[2:4], b1[6:8]], axis=0), "space", -1
-    )
+    far = [
+        passed_along(slots[offset * CAP : (offset + 1) * CAP], "space", -offset)
+        for offset in range(EARLY, NEAR)
+    ]
+    gathered, *far = lax.optimization_barrier((gathered, *far))
+    forward, backward = (jnp.asarray(t) for t in legendre_tables(latitudes))
+    first = lax.axis_index("space") * per_device
+    forward = lax.dynamic_slice_in_dim(forward, first, per_device, 0)
+    backward = lax.dynamic_slice_in_dim(backward, first, per_device, 0)
+    filtered = call(
+        legendre_kernel,
+        [shape((bands, chunk, channels), BF16)],
+        [gathered, forward, backward, harmonic_damping_factor],
+        2 * 2 * 2 * per_device * LMAX * latitudes * channels,
+        [pltpu.VMEM((channels // 128, bands * chunk, 128), F32)],
+    )
+    filtered, slots = lax.optimization_barrier((filtered, slots[: EARLY * CAP]))
+    returned = lax.all_to_all(filtered, "space", split_axis=0, concat_axis=0, tiled=True)
+    pieces = [slots[:CAP]] + [
+        passed_along(slots[offset * CAP : (offset + 1) * CAP], "space", -offset)
+        for offset in range(1, EARLY)
+    ] + far
     offsets = patch_holder_shift[:, 0]
     earlier = jnp.tril(jnp.ones((HOME_DEV, HOME_DEV), jnp.int32), -1)
     positions = jnp.sum((offsets[:, None] == offsets[None, :]).astype(jnp.int32) * earlier, axis=1)
@@ -310,13 +373,13 @@
     )
     forcing_weight = kernel[:, :, OCH:].reshape(hidden_channels, -1)
     decode_weight = jnp.pad(hidden_to_change_kernel, ((0, 16 - len(TAPS)), (0, 0)))
-    wet = call(
+    wet, top = call(
         ocean_kernel,
-        [shape((hidden_channels, SPAN), F32)],
-        [depths, a0, a1, b1, c1, state_weight],
+        [shape((hidden_channels, SPAN), F32), shape((1, SPAN), F32)],
+        [depths, *pieces, state_weight],
         2 * hidden_channels * len(TAPS) * OCH_PAD * SPAN,
         [pltpu.VMEM((len(TAPS) * OCH_PAD, SPAN), BF16)],
-        specs=[pl.BlockSpec(memory_space=pltpu.SMEM)] + [WHOLE] * 5,
+        specs=[pl.BlockSpec(memory_space=pltpu.SMEM)] + [WHOLE] * (NEAR + 1),
     )
     picks = jnp.sum(jnp.where(selected[:, :, None], patch_exchange_pick[None], 0), axis=1)
     picks = picks.reshape(1, SPAN)
@@ -324,10 +387,6 @@
     place = (
         picks % longitudes == jnp.arange(longitudes, dtype=jnp.int32)[:, None]
     ).astype(BF16)
-    top = jnp.concatenate(
-        [a0[0:2, 0], c1[0:2, 0], b1[0:2, 0], c1[4:6, 0], a1[0:2, 0], c1[2:4, 0], b1[4:6, 0], c1[6:8, 0]],
-        axis=0,
-    ).astype(F32).reshape(1, SPAN)
     tile = node_sea_pick // CELLS
     holder = jnp.sum(
         jnp.where(
@@ -346,40 +405,51 @@
         holder[:, None, :] == jnp.arange(SLOTS, dtype=jnp.int32)[None, :, None]
     ).astype(F32)
     skip = jnp.einsum("jkc,cd->jkd", normed, bypass_factor, preferred_element_type=F32)
-    forward, backward = (jnp.asarray(t) for t in legendre_tables(latitudes))
-    first = lax.axis_index("space") * per_device
-    forward = lax.dynamic_slice_in_dim(forward, first, per_device, 0)
-    backward = lax.dynamic_slice_in_dim(backward, first, per_device, 0)
-    filtered = call(
-        legendre_kernel,
-        [shape((bands, chunk, channels), BF16)],
-        [gathered, forward, backward, harmonic_damping_factor],
-        2 * 2 * 2 * per_device * LMAX * latitudes * channels,
-        [pltpu.VMEM((channels // 128, bands * chunk, 128), F32)],
-    )
-    returned = lax.all_to_all(filtered, "space", split_axis=0, concat_axis=0, tiled=True)
-    out, tiles = call(
-        closing_kernel,
-        [shape(air.shape, BF16), shape((SLOTS, CELLS), BF16)],
-        [
-            returned, synthesis, skip, air, core_exit_factor, air_to_exchange_factor.T, place,
-            line, wet, forcing_weight, decode_weight, top, cell, slot_of,
-            sea_heat_imprint[None, :],
-        ],
+    operands = [
+        returned, synthesis, skip, air, core_exit_factor, air_to_exchange_factor, place, line,
+        forcing_weight, wet, decode_weight, top,
+    ]
+    updated, tiles = call(
+        surface_kernel,
+        [shape(air.shape, F32), shape((members, SLOTS, CELLS), BF16)],
+        operands,
         2 * latitude_rows * longitudes * channels * (channels + 2 * MMAX),
-        [
+        held(operands)
+        + [
             pltpu.VMEM(air.shape, F32),
             pltpu.VMEM((FC * latitude_rows, longitudes), F32),
             pltpu.VMEM((SLOTS, CELLS), F32),
+            pltpu.SemaphoreType.DMA((len(operands),)),
+            pltpu.SemaphoreType.DMA((latitude_rows,)),
         ],
-    )
-    everyone = lax.all_to_all(
-        jnp.broadcast_to(tiles[None], (members,) + tiles.shape),
-        "member",
-        split_axis=0,
-        concat_axis=0,
-        tiled=True,
-    )
+        limit=LARGE,
+        specs=[ANYWHERE] * len(operands),
+        out_specs=[ANYWHERE, WHOLE],
+    )
+    everyone = lax.all_to_all(tiles, "member", split_axis=0, concat_axis=0, tiled=True)
+
+    def by_latitude(*rest):
+        return pl.BlockSpec((1,) + rest, lambda j: (j, 0, 0))
+
+    out = pl.pallas_call(
+        imprint_kernel,
+        grid=(latitude_rows,),
+        out_shape=shape(air.shape, BF16),
+        in_specs=[
+            by_latitude(longitudes, channels),
+            pl.BlockSpec((1, SLOTS, CELLS), lambda j: (0, 0, 0)),
+            by_latitude(longitudes, CELLS),
+            by_latitude(longitudes, 3 * SLOTS),
+            pl.BlockSpec((channels,), lambda j: (0,)),
+        ],
+        out_specs=by_latitude(longitudes, channels),
+        compiler_params=pltpu.CompilerParams(vmem_limit_bytes=LARGE * 1024 * 1024),
+        cost_estimate=pl.CostEstimate(
+            flops=2 * latitude_rows * longitudes * channels * 256,
+            bytes_accessed=air.size * 6,
+            transcendentals=0,
+        ),
+    )(updated, tiles, cell, slot_of, sea_heat_imprint)
     mean = call(
         mean_kernel,
         [shape((latitude_rows, longitudes), F32)],

time: 168 us -> 151 us (0.90)
  local copies, waits for them, and re-layouts: 38.5 us -> 6.34 us
  starting transfers between devices: 41.4 us -> 60.2 us
  waiting for transfers between devices: 60.2 us -> 53.3 us
  Pallas kernels: 15.5 us -> 22.4 us
  other arithmetic: 7.93 us -> 4.79 us
    all_to_all x1, waiting for transfers between devices: 34.4 us -> 0.01 us  [shards(): lax.all_to_all(spectra, 'space', split_axis=0, concat_axis=0, tiled=True)]
    ppermute x3 -> x7, waiting for transfers between devices: 19 us -> 46 us  [passed_along(): lax.ppermute(value, axis, [(i, (i + by) % devices) for i in range(devices)])]
    unnamed x77 -> x41, local copies, waits for them, and re-layouts: 22.7 us -> 3.58 us
    ppermute x3 -> x7, starting transfers between devices: 12.2 us -> 26.5 us  [passed_along(): lax.ppermute(value, axis, [(i, (i + by) % devices) for i in range(devices)])]
    all_to_all x1, waiting for transfers between devices: 0.01 us -> 5.35 us  [shards(): lax.all_to_all(filtered, 'space', split_axis=0, concat_axis=0, tiled=True)]
    all_to_all x1, waiting for transfers between devices: 6.8 us -> 1.93 us  [shards(): lax.all_to_all(tiles, 'member', split_axis=0, concat_axis=0, tiled=True)]
    pallas_call x0 -> x1, Pallas kernels: none -> 4.57 us  [shards(): pl.pallas_call(imprint_kernel, grid=(latitude_rows,), out_shape=shape(air...]
    slice x10 -> x4, local copies, waits for them, and re-layouts: 4.66 us -> 0.18 us  [the longest x2 0.17 us: shards(): slots[offset * CAP:(offset + 1) * CAP]]
  transfers between devices with their start and end apart: 6 -> 10, of which waited for: 4 -> 6; matrix products, arithmetic and copies ran while one was open for 17% -> 7% of each run, Pallas kernels for 3% -> 4%
where the time goes in v2:
time: 151 us; the launch traced here: 150 us
  starting transfers between devices  60.2 us (40%)
  waiting for transfers between devices  53.3 us (35%)
  Pallas kernels  22.4 us (15%)
  local copies, waits for them, and re-layouts  6.34 us (4%)
  other arithmetic  4.79 us (3%)
  matrix products  2.32 us (2%)
    ppermute x7, waiting for transfers between devices, passed_along(): lax.ppermute(value, axis, [(i, (i + by) % devices) for i in range(devices)])  46 us
    ppermute x7, starting transfers between devices, passed_along(): lax.ppermute(value, axis, [(i, (i + by) % devices) for i in range(devices)])  26.5 us
    pallas_call x5, Pallas kernels, call(): pl.pallas_call(kernel, out_shape=outs if len(outs) > 1 else outs[0], in_s...  17.9 us
    all_to_all x1, starting transfers between devices, shards(): lax.all_to_all(spectra, 'space', split_axis=0, concat_axis=0, tiled=True)  16.8 us
    all_to_all x1, starting transfers between devices, shards(): lax.all_to_all(filtered, 'space', split_axis=0, concat_axis=0, tiled=True)  10 us
    all_to_all x1, starting transfers between devices, shards(): lax.all_to_all(tiles, 'member', split_axis=0, concat_axis=0, tiled=True)  6.88 us
    all_to_all x1, waiting for transfers between devices, shards(): lax.all_to_all(filtered, 'space', split_axis=0, concat_axis=0, tiled=True)  5.35 us
    pallas_call x1, Pallas kernels, shards(): pl.pallas_call(imprint_kernel, grid=(latitude_rows,), out_shape=shape(air...  4.57 us
  transfers between devices with their start and end apart: 10, of which 6 were waited for; matrix products, arithmetic and copies ran while one was open for 7% of the time, Pallas kernels for 4%

profile of v2, /device:TPU:1, one launch (start us, length us, event | category | flops | bytes accessed | tf_op | source)
XLA Modules:
  0.0 150.5 jit_solution(18191454192821681875)
XLA Ops:
  0.6 0.0 copy-start
  0.6 0.0 copy-start.7
  0.7 0.0 slice-start
  0.7 0.0 copy-start.3
  0.7 5.0 %shard_map.194 = (bf16[32,32,384]{2,1,0:T(8,128)(2,1)}, bf16[4,360,384]{2,1,0:T(8,128)(2,1)}) custom-call(bf16[4,360,384]{2,1,0:T(8,128)(2,1)} %bitcast.46, f32[384]{0:T(512)} %scale_ref.1, bf16[256,360]{1,0:T(8,128)(2,1)} %constant.89.clone.table_any), custom_call_target="tpu_custom_call" | custom-call | flops 283115520 | bytes 3184128 | tf_op jit(solution)/shard_map/pallas_call | solution.py:287
  5.8 16.8 %all-to-all-start = ((bf16[32,32,384]{2,1,0:T(8,128)(2,1)}), bf16[32,32,384]{2,1,0:T(8,128)(2,1)S(1)}, u32[]{:S(2)}, u32[]{:S(2)}) async-start(bf16[32,32,384]{2,1,0:T(8,128)(2,1)} %get-tuple-element.16), calls=%async_computation | async-start | bytes 1572864 | tf_op jit(solution)/shard_map/all_to_all | solution.py:339
  22.5 0.2 fusion.9
  22.7 4.8 %collective-permute-start = (bf16[2,76,128]{2,1,0:T(8,128)(2,1)S(1)}, bf16[2,76,128]{2,1,0:T(8,128)(2,1)S(1)}, u32[]{:S(2)}, u32[]{:S(2)}) collective-permute-start(bf16[2,76,128]{2,1,0:T(8,128)(2,1)S(1)} %bitcast.53), channel_id=1, source_target_pairs={{0,29},{1,30},{2,31},{3,0},{4,1},{5,2},{6,3},{7,4},{8,5},{9,6},{10... | collective-permute-start | bytes 116744 | tf_op jit(solution)/shard_map/ppermute | solution.py:35
  27.6 4.0 %collective-permute-start.1 = (bf16[2,76,128]{2,1,0:T(8,128)(2,1)S(1)}, bf16[2,76,128]{2,1,0:T(8,128)(2,1)S(1)}, u32[]{:S(2)}, u32[]{:S(2)}) collective-permute-start(bf16[2,76,128]{2,1,0:T(8,128)(2,1)S(1)} %bitcast.54), channel_id=1, source_target_pairs={{0,28},{1,29},{2,30},{3,31},{4,0},{5,1},{6,2},{7,3},{8,4},{9,5},{1... | collective-permute-start | bytes 116744 | tf_op jit(solution)/shard_map/ppermute | solution.py:35
  31.6 6.4 %collective-permute-start.2 = (bf16[2,76,128]{2,1,0:T(8,128)(2,1)S(1)}, bf16[2,76,128]{2,1,0:T(8,128)(2,1)S(1)}, u32[]{:S(2)}, u32[]{:S(2)}) collective-permute-start(bf16[2,76,128]{2,1,0:T(8,128)(2,1)S(1)} %bitcast.55), channel_id=1, source_target_pairs={{0,27},{1,28},{2,29},{3,30},{4,31},{5,0},{6,1},{7,2},{8,3},{9,4},{... | collective-permute-start | bytes 116744 | tf_op jit(solution)/shard_map/ppermute | solution.py:35
  38.0 4.0 %collective-permute-start.3 = (bf16[2,76,128]{2,1,0:T(8,128)(2,1)S(1)}, bf16[2,76,128]{2,1,0:T(8,128)(2,1)S(1)}, u32[]{:S(2)}, u32[]{:S(2)}) collective-permute-start(bf16[2,76,128]{2,1,0:T(8,128)(2,1)S(1)} %bitcast.56), channel_id=1, source_target_pairs={{0,26},{1,27},{2,28},{3,29},{4,30},{5,31},{6,0},{7,1},{8,2},{9,3},... | collective-permute-start | bytes 116744 | tf_op jit(solution)/shard_map/ppermute | solution.py:35
  42.0 2.4 %collective-permute-start.4 = (bf16[2,76,128]{2,1,0:T(8,128)(2,1)S(1)}, bf16[2,76,128]{2,1,0:T(8,128)(2,1)S(1)}, u32[]{:S(2)}, u32[]{:S(2)}) collective-permute-start(bf16[2,76,128]{2,1,0:T(8,128)(2,1)S(1)} %bitcast.57), channel_id=1, source_target_pairs={{0,25},{1,26},{2,27},{3,28},{4,29},{5,30},{6,31},{7,0},{8,1},{9,2}... | collective-permute-start | bytes 116744 | tf_op jit(solution)/shard_map/ppermute | solution.py:35
  44.4 0.0 copy-done.14
  44.4 0.2 select_reduce_fusion.3
  44.6 0.1 copy.45
  44.7 0.0 copy-done.9
  44.7 0.1 select_reduce_fusion
  44.9 1.0 constant_dynamic-slice_fusion
  45.9 0.0 copy-start.13
  45.9 0.0 copy-start.8
  45.9 0.0 copy-done.12
  45.9 0.1 select_reduce_fusion.1
  46.1 15.2 %collective-permute-done.refs_3_ = bf16[2,76,128]{2,1,0:T(8,128)(2,1)S(1)} collective-permute-done((bf16[2,76,128]{2,1,0:T(8,128)(2,1)S(1)}, bf16[2,76,128]{2,1,0:T(8,128)(2,1)S(1)}, u32[]{:S(2)}, u32[]{:S(2)}) %collective-permute-start) | collective-permute-done | bytes 38944 | tf_op jit(solution)/shard_map/ppermute | solution.py:35
  61.3 0.0 collective-permute-done.1.refs_4_
  61.3 3.4 %collective-permute-done.2.refs_5_ = bf16[2,76,128]{2,1,0:T(8,128)(2,1)S(1)} collective-permute-done((bf16[2,76,128]{2,1,0:T(8,128)(2,1)S(1)}, bf16[2,76,128]{2,1,0:T(8,128)(2,1)S(1)}, u32[]{:S(2)}, u32[]{:S(2)}) %collective-permute-start.2) | collective-permute-done | bytes 38944 | tf_op jit(solution)/shard_map/ppermute | solution.py:35
  64.7 0.0 collective-permute-done.3.refs_6_
  64.7 5.8 %collective-permute-done.4.refs_7_ = bf16[2,76,128]{2,1,0:T(8,128)(2,1)S(1)} collective-permute-done((bf16[2,76,128]{2,1,0:T(8,128)(2,1)S(1)}, bf16[2,76,128]{2,1,0:T(8,128)(2,1)S(1)}, u32[]{:S(2)}, u32[]{:S(2)}) %collective-permute-start.4) | collective-permute-done | bytes 38944 | tf_op jit(solution)/shard_map/ppermute | solution.py:35
  70.5 0.0 all-to-all-done.x_ref
  70.5 0.0 copy-done.3
  70.5 0.0 copy-start.6
  70.5 2.8 %shard_map.195 = bf16[32,32,384]{2,1,0:T(8,128)(2,1)} custom-call(bf16[32,32,384]{2,1,0:T(8,128)(2,1)S(1)} %all-to-all-done.x_ref, bf16[4,128,128]{2,1,0:T(8,128)(2,1)S(1)} %get-tuple-element.41.forward_ref, bf16[4,128,128]{2,1,0:T(8,128)(2,1)S(1)} %get-tuple-element.40.backward_ref, f32[128,384]{1,0:T(8,128)S(1)} %copy-done.3), custom_call_target="tpu_custom_call" | custom-call | flops 201326592 | bytes 2031616 | tf_op jit(solution)/shard_map/pallas_call | solution.py:287
  73.3 10.0 %all-to-all-start.1 = ((bf16[32,32,384]{2,1,0:T(8,128)(2,1)}), bf16[32,32,384]{2,1,0:T(8,128)(2,1)S(1)}, u32[]{:S(2)}, u32[]{:S(2)}) async-start(bf16[32,32,384]{2,1,0:T(8,128)(2,1)} %shard_map.195), calls=%async_computation.1 | async-start | bytes 1572864 | tf_op jit(solution)/shard_map/all_to_all | solution.py:359
  83.4 0.0 copy-done.8
  83.4 1.0 fusion.1.cell_ref
  84.4 1.0 compare_convert_fusion.slot_ref
  85.5 0.1 slice_select_fusion
  85.6 0.0 copy-start.16
  85.6 0.0 copy-start.11
  85.6 2.3 %fusion.2.refs_2_ = f32[4,360,384]{2,1,0:T(8,128)} fusion(bf16[4,360,384]{2,1,0:T(8,128)(2,1)S(1)} %copy-done.6, bf16[384,384]{1,0:T(8,128)(2,1)S(1)} %copy-done), kind=kOutput, calls=%fused_computation.6 | convolution fusion | flops 424673280 | bytes 3612672 | tf_op jit(solution)/shard_map/jkc,cd->jkd/dot_general | solution.py:407
  87.9 0.6 bitcast_select_fusion.refs_7_
  88.5 1.5 fusion.refs_6_
  90.0 0.2 collective-permute-start.5
  90.2 4.7 %collective-permute-start.6 = (bf16[2,76,128]{2,1,0:T(8,128)(2,1)S(1)}, bf16[2,76,128]{2,1,0:T(8,128)(2,1)S(1)}, u32[]{:S(2)}, u32[]{:S(2)}) collective-permute-start(bf16[2,76,128]{2,1,0:T(8,128)(2,1)S(1)} %get-tuple-element.35), channel_id=1, source_target_pairs={{0,30},{1,31},{2,0},{3,1},{4,2},{5,3},{6,4},{7,5},{8,6},{9,7},{10,... | collective-permute-start | bytes 116744 | tf_op jit(solution)/shard_map/ppermute | solution.py:35
  95.0 0.1 select_reduce_fusion.2.depth_ref
  95.1 0.2 copy.46.refs_8_
  95.3 0.7 copy.48.refs_8_
  96.0 0.0 copy-done.11
  96.0 0.8 copy.47.refs_5_
  96.7 0.6 pad.9.refs_10_
  97.3 21.6 %collective-permute-done.5.refs_1_ = bf16[2,76,128]{2,1,0:T(8,128)(2,1)S(1)} collective-permute-done((bf16[2,76,128]{2,1,0:T(8,128)(2,1)S(1)}, bf16[2,76,128]{2,1,0:T(8,128)(2,1)S(1)}, u32[]{:S(2)}, u32[]{:S(2)}) %collective-permute-start.5) | collective-permute-done | bytes 38944 | tf_op jit(solution)/shard_map/ppermute | solution.py:35
  118.9 0.0 collective-permute-done.6.refs_2_
  119.0 1.9 %shard_map.196 = (f32[200,2048]{1,0:T(8,128)S(1)}, f32[1,2048]{1,0:T(1,128)S(1)}) custom-call(s32[16]{0:T(128)S(1)} %select_reduce_fusion.2.depth_ref, bf16[2,76,128]{2,1,0:T(8,128)(2,1)S(1)} %get-tuple-element.37.refs_0_, bf16[2,76,128]{2,1,0:T(8,128)(2,1)S(1)} %collective-permute-done.5.refs_1_, bf16[2,76,128]{2,1,0:T(8,128)(2,1)S(1)} %collective-permute-done.6.refs_2_, ...), custom_call_target="tpu_custom_call" | custom-call | flops 589824000 | bytes 2245952 | tf_op jit(solution)/shard_map/pallas_call | solution.py:287
  120.8 0.0 copy-start.2
  120.8 1.2 copy-done.2
  122.0 0.6 copy-done.4
  122.6 5.3 %all-to-all-done.1.refs_0_ = bf16[32,32,384]{2,1,0:T(8,128)(2,1)S(1)} async-done(((bf16[32,32,384]{2,1,0:T(8,128)(2,1)}), bf16[32,32,384]{2,1,0:T(8,128)(2,1)S(1)}, u32[]{:S(2)}, u32[]{:S(2)}) %all-to-all-start.1) | async-done | bytes 786464 | tf_op jit(solution)/shard_map/all_to_all | solution.py:359
  128.0 0.9 copy-done.5
  128.9 7.3 %shard_map.197 = (f32[4,360,384]{2,1,0:T(8,128)}, bf16[16,16,128]{2,1,0:T(8,128)(2,1)}) custom-call(bf16[32,32,384]{2,1,0:T(8,128)(2,1)} %copy-done.5, bf16[360,256]{1,0:T(8,128)(2,1)} %constant.90.clone.refs_1_, f32[4,360,384]{2,1,0:T(8,128)} %fusion.2.refs_2_, bf16[4,360,384]{2,1,0:T(8,128)(2,1)} %bitcast.47, bf16[384,384]{1,0:T(8,128)(2,1)} %refs_4_.1, ...), custom_call_target="tpu_custom_call" | custom-call | flops 707788800 | bytes 10031488 | tf_op jit(solution)/shard_map/pallas_call | solution.py:287
  136.2 0.0 copy-start.1
  136.2 6.9 %all-to-all-start.2 = ((bf16[16,16,128]{2,1,0:T(8,128)(2,1)}), bf16[16,16,128]{2,1,0:T(8,128)(2,1)S(1)}, u32[]{:S(2)}, u32[]{:S(2)}) async-start(bf16[16,16,128]{2,1,0:T(8,128)(2,1)} %get-tuple-element.29.tiles_ref), calls=%async_computation.2 | async-start | bytes 131072 | tf_op jit(solution)/shard_map/all_to_all | solution.py:429
  143.1 4.6 %shard_map.198 = bf16[4,360,384]{2,1,0:T(8,128)(2,1)} custom-call(f32[4,360,384]{2,1,0:T(8,128)} %get-tuple-element.28.updated_ref, bf16[16,16,128]{2,1,0:T(8,128)(2,1)} %get-tuple-element.29.tiles_ref, bf16[4,360,128]{2,1,0:T(8,128)(2,1)} %fusion.1.cell_ref, bf16[4,360,48]{2,1,0:T(8,128)(2,1)} %compare_convert_fusion.slot_ref, f32[384]{0:T(512)} %imprint_ref.1), custom_call_target="tpu_custom_call" | custom-call | flops 283115520 | bytes 3317760 | tf_op jit(solution)/shard_map/pallas_call | solution.py:434
  147.7 1.9 %all-to-all-done.2.tiles_ref = bf16[16,16,128]{2,1,0:T(8,128)(2,1)S(1)} async-done(((bf16[16,16,128]{2,1,0:T(8,128)(2,1)}), bf16[16,16,128]{2,1,0:T(8,128)(2,1)S(1)}, u32[]{:S(2)}, u32[]{:S(2)}) %all-to-all-start.2) | async-done | bytes 65568 | tf_op jit(solution)/shard_map/all_to_all | solution.py:429
  149.6 0.0 copy-done.1
  149.6 0.9 shard_map.199
  (33 shorter events, 0.2 us)
Async XLA Ops:
  0.6 84.9 %copy-start = (bf16[384,384]{1,0:T(8,128)(2,1)S(1)}, bf16[384,384]{1,0:T(8,128)(2,1)}, u32[]{:S(2)}) copy-start(bf16[384,384]{1,0:T(8,128)(2,1)} %param.23) | copy-start | bytes 884740
  0.6 21.9 %copy-start.7 = (bf16[1,16,76,128]{3,1,2,0:T(8,128)(2,1)S(1)}, bf16[1,16,76,128]{3,1,2,0:T(8,128)(2,1)}, u32[]{:S(2)}) copy-start(bf16[1,16,76,128]{3,1,2,0:T(8,128)(2,1)} %param.27) | copy-start | bytes 933892
  0.7 43.8 %copy-start.14 = (s32[14,1]{0,1:T(1,128)S(1)}, s32[14,1]{0,1:T(1,128)}, u32[]{:S(2)}) copy-start(s32[14,1]{0,1:T(1,128)} %param.32) | copy-start | bytes 172
  0.7 44.1 %copy-start.9 = (s32[14,128]{1,0:T(8,128)S(1)}, s32[14,128]{1,0:T(8,128)}, u32[]{:S(2)}) copy-start(s32[14,128]{1,0:T(8,128)} %param.30) | copy-start | bytes 21508
  0.7 45.2 %copy-start.12 = (s32[4,360]{1,0:T(4,128)S(1)}, s32[4,360]{1,0:T(4,128)}, u32[]{:S(2)}) copy-start(s32[4,360]{1,0:T(4,128)} %param.31) | copy-start | bytes 17284
  0.7 45.4 %slice-start = ((bf16[1,16,76,128]{3,1,2,0:T(8,128)(2,1)}), bf16[1,6,76,128]{3,1,2,0:T(8,128)(2,1)S(1)}, s32[]{:S(2)}) async-start(bf16[1,16,76,128]{3,1,2,0:T(8,128)(2,1)} %param.27), calls=%async_computation.3 | async-start | bytes 311296 | tf_op jit(solution)/shard_map/slice | solution.py:358
  0.7 69.8 %copy-start.3 = (f32[128,384]{1,0:T(8,128)S(1)}, f32[128,384]{1,0:T(8,128)}, u32[]{:S(2)}) copy-start(f32[128,384]{1,0:T(8,128)} %gains_ref.1) | copy-start | bytes 589828
  5.8 64.8 %all-to-all-start = ((bf16[32,32,384]{2,1,0:T(8,128)(2,1)}), bf16[32,32,384]{2,1,0:T(8,128)(2,1)S(1)}, u32[]{:S(2)}, u32[]{:S(2)}) async-start(bf16[32,32,384]{2,1,0:T(8,128)(2,1)} %get-tuple-element.16), calls=%async_computation | async-start | bytes 1572864 | tf_op jit(solution)/shard_map/all_to_all | solution.py:339
  22.7 38.6 %collective-permute-start = (bf16[2,76,128]{2,1,0:T(8,128)(2,1)S(1)}, bf16[2,76,128]{2,1,0:T(8,128)(2,1)S(1)}, u32[]{:S(2)}, u32[]{:S(2)}) collective-permute-start(bf16[2,76,128]{2,1,0:T(8,128)(2,1)S(1)} %bitcast.53), channel_id=1, source_target_pairs={{0,29},{1,30},{2,31},{3,0},{4,1},{5,2},{6,3},{7,4},{8,5},{9,6},{10... | collective-permute-start | bytes 116744 | tf_op jit(solution)/shard_map/ppermute | solution.py:35
  27.6 33.7 %collective-permute-start.1 = (bf16[2,76,128]{2,1,0:T(8,128)(2,1)S(1)}, bf16[2,76,128]{2,1,0:T(8,128)(2,1)S(1)}, u32[]{:S(2)}, u32[]{:S(2)}) collective-permute-start(bf16[2,76,128]{2,1,0:T(8,128)(2,1)S(1)} %bitcast.54), channel_id=1, source_target_pairs={{0,28},{1,29},{2,30},{3,31},{4,0},{5,1},{6,2},{7,3},{8,4},{9,5},{1... | collective-permute-start | bytes 116744 | tf_op jit(solution)/shard_map/ppermute | solution.py:35
  31.6 33.1 %collective-permute-start.2 = (bf16[2,76,128]{2,1,0:T(8,128)(2,1)S(1)}, bf16[2,76,128]{2,1,0:T(8,128)(2,1)S(1)}, u32[]{:S(2)}, u32[]{:S(2)}) collective-permute-start(bf16[2,76,128]{2,1,0:T(8,128)(2,1)S(1)} %bitcast.55), channel_id=1, source_target_pairs={{0,27},{1,28},{2,29},{3,30},{4,31},{5,0},{6,1},{7,2},{8,3},{9,4},{... | collective-permute-start | bytes 116744 | tf_op jit(solution)/shard_map/ppermute | solution.py:35
  38.0 26.7 %collective-permute-start.3 = (bf16[2,76,128]{2,1,0:T(8,128)(2,1)S(1)}, bf16[2,76,128]{2,1,0:T(8,128)(2,1)S(1)}, u32[]{:S(2)}, u32[]{:S(2)}) collective-permute-start(bf16[2,76,128]{2,1,0:T(8,128)(2,1)S(1)} %bitcast.56), channel_id=1, source_target_pairs={{0,26},{1,27},{2,28},{3,29},{4,30},{5,31},{6,0},{7,1},{8,2},{9,3},... | collective-permute-start | bytes 116744 | tf_op jit(solution)/shard_map/ppermute | solution.py:35
  42.0 28.5 %collective-permute-start.4 = (bf16[2,76,128]{2,1,0:T(8,128)(2,1)S(1)}, bf16[2,76,128]{2,1,0:T(8,128)(2,1)S(1)}, u32[]{:S(2)}, u32[]{:S(2)}) collective-permute-start(bf16[2,76,128]{2,1,0:T(8,128)(2,1)S(1)} %bitcast.57), channel_id=1, source_target_pairs={{0,25},{1,26},{2,27},{3,28},{4,29},{5,30},{6,31},{7,0},{8,1},{9,2}... | collective-permute-start | bytes 116744 | tf_op jit(solution)/shard_map/ppermute | solution.py:35
  45.9 37.5 %copy-start.13 = (s32[4,360]{1,0:T(4,128)S(1)}, s32[4,360]{1,0:T(4,128)}, u32[]{:S(2)}) copy-start(s32[4,360]{1,0:T(4,128)} %param.20) | copy-start | bytes 17284
  45.9 37.5 %copy-start.8 = (bf16[9,200,84]{1,2,0:T(8,128)(2,1)S(1)}, bf16[9,200,84]{1,2,0:T(8,128)(2,1)}, u32[]{:S(2)}) copy-start(bf16[9,200,84]{1,2,0:T(8,128)(2,1)} %param.28) | copy-start | bytes 907204
  70.5 14.9 %copy-start.15 = (pred[80]{0:T(512)(128)(4,1)S(1)}, pred[80]{0:T(512)(128)(4,1)}, u32[]{:S(2)}) copy-start(pred[80]{0:T(512)(128)(4,1)} %constant.83.clone.1) | copy-start | bytes 244
  70.5 15.0 %copy-start.6 = (bf16[4,360,384]{2,1,0:T(8,128)(2,1)S(1)}, bf16[4,360,384]{2,1,0:T(8,128)(2,1)}, u32[]{:S(2)}) copy-start(bf16[4,360,384]{2,1,0:T(8,128)(2,1)} %get-tuple-element.19) | copy-start | bytes 3317764
  73.3 54.7 %all-to-all-start.1 = ((bf16[32,32,384]{2,1,0:T(8,128)(2,1)}), bf16[32,32,384]{2,1,0:T(8,128)(2,1)S(1)}, u32[]{:S(2)}, u32[]{:S(2)}) async-start(bf16[32,32,384]{2,1,0:T(8,128)(2,1)} %shard_map.195), calls=%async_computation.1 | async-start | bytes 1572864 | tf_op jit(solution)/shard_map/all_to_all | solution.py:359
  85.6 9.4 %copy-start.16 = (s32[14]{0:T(128)S(1)}, s32[14]{0:T(128)}, u32[]{:S(2)}) copy-start(s32[14]{0:T(128)} %param.33) | copy-start | bytes 172
  85.6 10.4 %copy-start.11 = (bf16[384,8]{0,1:T(8,128)(2,1)S(1)}, bf16[384,8]{0,1:T(8,128)(2,1)}, u32[]{:S(2)}) copy-start(bf16[384,8]{0,1:T(8,128)(2,1)} %param.25) | copy-start | bytes 18436
  87.9 8.8 %copy-start.10 = (bf16[9,200]{1,0:T(8,128)(2,1)S(1)}, bf16[9,200]{1,0:T(8,128)(2,1)}, u32[]{:S(2)}) copy-start(bf16[9,200]{1,0:T(8,128)(2,1)} %param.29) | copy-start | bytes 10804
  90.0 28.9 %collective-permute-start.5 = (bf16[2,76,128]{2,1,0:T(8,128)(2,1)S(1)}, bf16[2,76,128]{2,1,0:T(8,128)(2,1)S(1)}, u32[]{:S(2)}, u32[]{:S(2)}) collective-permute-start(bf16[2,76,128]{2,1,0:T(8,128)(2,1)S(1)} %get-tuple-element.36), channel_id=1, source_target_pairs={{0,31},{1,0},{2,1},{3,2},{4,3},{5,4},{6,5},{7,6},{8,7},{9,8},{10,9... | collective-permute-start | bytes 116744 | tf_op jit(solution)/shard_map/ppermute | solution.py:35
  90.2 28.7 %collective-permute-start.6 = (bf16[2,76,128]{2,1,0:T(8,128)(2,1)S(1)}, bf16[2,76,128]{2,1,0:T(8,128)(2,1)S(1)}, u32[]{:S(2)}, u32[]{:S(2)}) collective-permute-start(bf16[2,76,128]{2,1,0:T(8,128)(2,1)S(1)} %get-tuple-element.35), channel_id=1, source_target_pairs={{0,30},{1,31},{2,0},{3,1},{4,2},{5,3},{6,4},{7,5},{8,6},{9,7},{10,... | collective-permute-start | bytes 116744 | tf_op jit(solution)/shard_map/ppermute | solution.py:35
  120.8 1.2 copy-start.2
  122.0 0.6 copy-start.4
  128.0 0.9 copy-start.5
  136.2 13.4 %copy-start.1 = (bf16[4,360,128]{2,1,0:T(8,128)(2,1)S(1)}, bf16[4,360,128]{2,1,0:T(8,128)(2,1)}, u32[]{:S(2)}) copy-start(bf16[4,360,128]{2,1,0:T(8,128)(2,1)} %fusion.1.cell_ref) | copy-start | bytes 1105924
  136.2 13.4 %all-to-all-start.2 = ((bf16[16,16,128]{2,1,0:T(8,128)(2,1)}), bf16[16,16,128]{2,1,0:T(8,128)(2,1)S(1)}, u32[]{:S(2)}, u32[]{:S(2)}) async-start(bf16[16,16,128]{2,1,0:T(8,128)(2,1)} %get-tuple-element.29.tiles_ref), calls=%async_computation.2 | async-start | bytes 131072 | tf_op jit(solution)/shard_map/all_to_all | solution.py:429

commit v3 on v2

--- a/solution.py
+++ b/solution.py
@@ -22,12 +22,10 @@
 OCH = 76
 OCH_PAD = 80
 TAPS = [(row, col) for row in (-1, 0, 1) for col in (-1, 0, 1)]
-LARGE = 56
-EARLY = 3
 BF16 = jnp.bfloat16
 F32 = jnp.float32
 WHOLE = pl.BlockSpec(memory_space=pltpu.VMEM)
-ANYWHERE = pl.BlockSpec(memory_space=pl.ANY)
+FAR = pl.BlockSpec(memory_space=pltpu.HBM)
 
 
 def passed_along(value, axis, by):
@@ -120,9 +118,13 @@
     return started
 
 
-def analysis_kernel(
-    air_any, scale_ref, table_any, spectra_ref, normed_ref, air_ref, table_ref, sems
-):
+def normalised(x, scale):
+    centered = x - jnp.mean(x, axis=-1, keepdims=True)
+    spread = jnp.mean(centered * centered, axis=-1, keepdims=True)
+    return (centered * lax.rsqrt(spread + 1e-05) * scale).astype(BF16)
+
+
+def analysis_kernel(air_any, scale_ref, table_any, spectra_ref, air_ref, table_ref, sems):
     rows = air_ref.shape[0]
     groups = spectra_ref.shape[0]
     copies = begin(
@@ -133,17 +135,41 @@
         both = []
         for j in (2 * pair, 2 * pair + 1):
             copies[j].wait()
-            x = air_ref[j].astype(F32)
-            centered = x - jnp.mean(x, axis=-1, keepdims=True)
-            spread = jnp.mean(centered * centered, axis=-1, keepdims=True)
-            normed = (centered * lax.rsqrt(spread + 1e-05) * scale).astype(BF16)
-            normed_ref[j] = normed
+            normed = normalised(air_ref[j].astype(F32), scale)
             if j == 0:
                 copies[rows].wait()
             out = jnp.dot(table_ref[...], normed, preferred_element_type=F32)
             both.append(out.reshape(groups, 8, out.shape[1]))
         block = jnp.concatenate(both, axis=1)
         spectra_ref[:, 16 * pair : 16 * (pair + 1), :] = block.astype(BF16)
+
+
+def local_kernel(
+    air_any, scale_ref, bypass_ref, exit_ref, exchange_ref, skip_ref, flux_ref, wide_ref,
+    air_ref, sems,
+):
+    rows = air_ref.shape[0]
+    copies = begin([(air_any.at[j], air_ref.at[j]) for j in range(rows)], sems)
+    scale = scale_ref[...].reshape(1, scale_ref.shape[0])
+    channels = exit_ref.shape[0]
+    dims = (((1,), (1,)), ((), ()))
+    through = lax.dot_general(
+        exit_ref[...], exchange_ref[...], dims, preferred_element_type=F32
+    )
+    high = through.astype(BF16)
+    low = (through - high.astype(F32)).astype(BF16)
+    wide_ref[:, :channels] = exit_ref[...]
+    wide_ref[:, channels:] = jnp.concatenate(
+        [high.astype(F32), low.astype(F32), jnp.zeros((channels, 128 - 2 * FC), F32)], axis=1
+    ).astype(BF16)
+    for j in range(rows):
+        copies[j].wait()
+        own = air_ref[j]
+        normed = normalised(own.astype(F32), scale)
+        skip_ref[j] = jnp.dot(normed, bypass_ref[...], preferred_element_type=F32)
+        flux_ref[FC * j : FC * (j + 1), :] = lax.dot_general(
+            exchange_ref[...], own, dims, preferred_element_type=F32
+        )
 
 
 def legendre_kernel(x_ref, forward_ref, backward_ref, gains_ref, out_ref, work):
@@ -153,19 +179,18 @@
     for third in range(channels // 128):
         lanes = slice(128 * third, 128 * (third + 1))
         work[third] = x_ref[:, :, lanes].astype(F32).reshape(total, 128)
-    for m in range(4):
-        for r in (0, 1):
-            rows = pl.ds(2 * m + r, latitudes, stride=8)
+        gains = gains_ref[:, lanes]
+        gains = jnp.concatenate([gains, gains], axis=1)
+        for m in range(4):
+            real, imaginary = (pl.ds(2 * m + r, latitudes, stride=8) for r in (0, 1))
             own = jnp.concatenate(
-                [work[third, rows, :] for third in range(channels // 128)], axis=1
+                [work[third, real, :], work[third, imaginary, :]], axis=1
             ).astype(BF16)
             coefficients = jnp.dot(forward_ref[m], own, preferred_element_type=F32)
-            shaped = (coefficients * gains_ref[...]).astype(BF16)
+            shaped = (coefficients * gains).astype(BF16)
             back = jnp.dot(backward_ref[m], shaped, preferred_element_type=F32)
-            for third in range(channels // 128):
-                work[third, rows, :] = back[:, 128 * third : 128 * (third + 1)]
-    for third in range(channels // 128):
-        lanes = slice(128 * third, 128 * (third + 1))
+            work[third, real, :] = back[:, :128]
+            work[third, imaginary, :] = back[:, 128:]
         out_ref[:, :, lanes] = work[third].reshape(groups, chunk, 128).astype(BF16)
 
 
@@ -188,48 +213,57 @@
         )
 
 
-def surface_kernel(*refs):
+def surface_kernel(rows_ref, *refs):
+    count = 11
     sources, (updated_any, tiles_ref), held, (updated_ref, flux, sst, sems, out_sems) = (
-        refs[:12], refs[12:14], refs[14:26], refs[26:]
+        refs[:count], refs[count : count + 2], refs[count + 2 : 2 * count + 2],
+        refs[2 * count + 2 :],
     )
     leaving = []
     copies = begin(list(zip(sources, held)), sems)
     (
-        rows_ref, synthesis_ref, skip_ref, air_ref, exit_ref, exchange_ref, place_ref, line_ref,
+        synthesis_ref, skip_ref, air_ref, wide_ref, air_flux_ref, place_ref, group_ref,
         forcing_weight_ref, wet_ref, decode_ref, top_ref,
     ) = held
-    latitude_rows = air_ref.shape[0]
-    groups, chunk, channels = rows_ref.shape
-    for one in copies[:2]:
-        one.wait()
+    latitude_rows, longitudes, channels = air_ref.shape
+    groups = rows_ref.shape[0]
+    pairs = []
+    for pair in range(latitude_rows // 2):
+        both = rows_ref[:, 16 * pair : 16 * (pair + 1), :].astype(F32)
+        pairs.extend([both[:, :8], both[:, 8:]])
+    copies[0].wait()
     for j in range(latitude_rows):
-        own = rows_ref[...].astype(F32).reshape(groups, latitude_rows, 8, channels)[:, j]
-        own = own.reshape(8 * groups, channels).astype(BF16)
+        own = pairs[j].reshape(8 * groups, channels).astype(BF16)
         spectral = jnp.dot(synthesis_ref[...], own, preferred_element_type=F32)
         if j == 0:
-            for one in copies[2:6]:
+            for one in copies[1:4]:
                 one.wait()
         mixed = gelu(spectral + skip_ref[j]).astype(BF16)
-        state = air_ref[j].astype(F32) + jnp.dot(
-            mixed, exit_ref[...], preferred_element_type=F32
-        )
-        updated_ref[j] = state
+        wide = jnp.dot(mixed, wide_ref[...], preferred_element_type=F32)
+        updated_ref[j] = air_ref[j].astype(F32) + wide[:, :channels]
         leave = pltpu.make_async_copy(updated_ref.at[j], updated_any.at[j], out_sems.at[j])
         leave.start()
         leaving.append(leave)
-        high = state.astype(BF16)
-        low = (state - high.astype(F32)).astype(BF16)
-        dims = (((0,), (1,)), ((), ()))
-        flux[8 * j : 8 * (j + 1), :] = lax.dot_general(
-            exchange_ref[...], high, dims, preferred_element_type=F32
-        ) + lax.dot_general(exchange_ref[...], low, dims, preferred_element_type=F32)
-    for one in copies[6:]:
+        narrow = jnp.concatenate(
+            [wide[:, channels:], jnp.zeros((384 - longitudes, 128), F32)], axis=0
+        )
+        turned = jnp.transpose(narrow)
+        if j == 0:
+            copies[4].wait()
+        extra = jnp.concatenate(
+            [air_flux_ref[FC * j : FC * (j + 1), :], jnp.zeros((FC, 384 - longitudes), F32)], axis=1
+        )
+        total = turned[:FC] + turned[FC : 2 * FC] + extra
+        for part in range(3):
+            at = FC * (part * latitude_rows + j)
+            flux[at : at + FC, :] = total[:, 128 * part : 128 * (part + 1)]
+    for one in copies[5:]:
         one.wait()
     spread = jnp.dot(flux[...].astype(BF16), place_ref[...], preferred_element_type=F32)
-    line = line_ref[...]
+    group = group_ref[...]
     forcing = jnp.zeros((FC, SPAN), F32)
-    for j in range(latitude_rows):
-        forcing = forcing + jnp.where(line == j, spread[8 * j : 8 * (j + 1), :], 0.0)
+    for at in range(3 * latitude_rows):
+        forcing = forcing + jnp.where(group == at, spread[FC * at : FC * (at + 1), :], 0.0)
     masks = tap_masks(SPAN)
     columns = jnp.concatenate(
         [shifted(forcing, tap, masks[q]) for q, tap in enumerate(TAPS)], axis=0
@@ -251,20 +285,38 @@
         one.wait()
 
 
-def imprint_kernel(updated_ref, tiles_ref, cell_ref, slot_ref, imprint_ref, out_ref):
-    channels = updated_ref.shape[2]
+def imprint_kernel(
+    updated_any, tiles_ref, cell_any, slot_any, imprint_ref, out_any,
+    updated_ref, cell_ref, slot_ref, out_ref, sems, out_sems,
+):
+    rows, _, channels = updated_ref.shape
+    copies = begin(
+        [(cell_any, cell_ref), (slot_any, slot_ref)]
+        + [(updated_any.at[j], updated_ref.at[j]) for j in range(rows)],
+        sems,
+    )
     tiles = tiles_ref[0]
     tripled = jnp.concatenate([tiles, tiles, tiles], axis=0)
     pieces = in_three(imprint_ref[...].reshape(1, channels))
     imprint = jnp.concatenate(
         [jnp.broadcast_to(piece, (SLOTS, channels)) for piece in pieces], axis=0
     )
-    picked = lax.dot_general(
-        cell_ref[0], tripled, (((1,), (1,)), ((), ())), preferred_element_type=F32
-    )
-    chosen = picked.astype(BF16) * slot_ref[0]
-    warmth = jnp.dot(chosen, imprint, preferred_element_type=F32)
-    out_ref[0] = (updated_ref[0] + warmth).astype(BF16)
+    copies[0].wait()
+    copies[1].wait()
+    leaving = []
+    for j in range(rows):
+        picked = lax.dot_general(
+            cell_ref[j], tripled, (((1,), (1,)), ((), ())), preferred_element_type=F32
+        )
+        chosen = picked.astype(BF16) * slot_ref[j]
+        warmth = jnp.dot(chosen, imprint, preferred_element_type=F32)
+        copies[2 + j].wait()
+        out_ref[j] = (updated_ref[j] + warmth).astype(BF16)
+        leave = pltpu.make_async_copy(out_ref.at[j], out_any.at[j], out_sems.at[j])
+        leave.start()
+        leaving.append(leave)
+    for one in leaving:
+        one.wait()
 
 
 def mean_kernel(tiles_ref, cell_ref, slot_ref, out_ref):
@@ -327,27 +379,37 @@
     shape = jax.ShapeDtypeStruct
 
     analysis, synthesis = (jnp.asarray(t) for t in fourier_tables())
-    spectra, normed = call(
+    spectra = call(
         analysis_kernel,
-        [shape((bands, chunk, channels), BF16), shape(air.shape, BF16)],
+        [shape((bands, chunk, channels), BF16)],
         [air, layernorm_scaling, analysis],
         2 * 2 * MMAX * latitude_rows * longitudes * channels,
         held([air, analysis]) + [pltpu.SemaphoreType.DMA((latitude_rows + 1,))],
-        limit=LARGE,
-        specs=[ANYWHERE, WHOLE, ANYWHERE],
+        specs=[FAR, WHOLE, FAR],
     )
     gathered = lax.all_to_all(spectra, "space", split_axis=0, concat_axis=0, tiled=True)
 
     slots = sea_ensemble_arrays[0]
-    far = [
+    pieces = [slots[:CAP]] + [
         passed_along(slots[offset * CAP : (offset + 1) * CAP], "space", -offset)
-        for offset in range(EARLY, NEAR)
+        for offset in range(1, NEAR)
     ]
-    gathered, *far = lax.optimization_barrier((gathered, *far))
     forward, backward = (jnp.asarray(t) for t in legendre_tables(latitudes))
     first = lax.axis_index("space") * per_device
     forward = lax.dynamic_slice_in_dim(forward, first, per_device, 0)
     backward = lax.dynamic_slice_in_dim(backward, first, per_device, 0)
+    skip, air_flux, wide = call(
+        local_kernel,
+        [
+            shape(air.shape, F32),
+            shape((FC * latitude_rows, longitudes), F32),
+            shape((channels, channels + 128), BF16),
+        ],
+        [air, layernorm_scaling, bypass_factor, core_exit_factor, air_to_exchange_factor.T],
+        2 * latitude_rows * longitudes * channels * channels,
+        held([air]) + [pltpu.SemaphoreType.DMA((latitude_rows,))],
+        specs=[FAR] + [WHOLE] * 4,
+    )
     filtered = call(
         legendre_kernel,
         [shape((bands, chunk, channels), BF16)],
@@ -355,12 +417,7 @@
         2 * 2 * 2 * per_device * LMAX * latitudes * channels,
         [pltpu.VMEM((channels // 128, bands * chunk, 128), F32)],
     )
-    filtered, slots = lax.optimization_barrier((filtered, slots[: EARLY * CAP]))
     returned = lax.all_to_all(filtered, "space", split_axis=0, concat_axis=0, tiled=True)
-    pieces = [slots[:CAP]] + [
-        passed_along(slots[offset * CAP : (offset + 1) * CAP], "space", -offset)
-        for offset in range(1, EARLY)
-    ] + far
     offsets = patch_holder_shift[:, 0]
     earlier = jnp.tril(jnp.ones((HOME_DEV, HOME_DEV), jnp.int32), -1)
     positions = jnp.sum((offsets[:, None] == offsets[None, :]).astype(jnp.int32) * earlier, axis=1)
@@ -383,10 +440,9 @@
     )
     picks = jnp.sum(jnp.where(selected[:, :, None], patch_exchange_pick[None], 0), axis=1)
     picks = picks.reshape(1, SPAN)
-    line = picks // longitudes
-    place = (
-        picks % longitudes == jnp.arange(longitudes, dtype=jnp.int32)[:, None]
-    ).astype(BF16)
+    line, column = picks // longitudes, picks % longitudes
+    group = column // 128 * latitude_rows + line
+    place = (column % 128 == jnp.arange(128, dtype=jnp.int32)[:, None]).astype(BF16)
     tile = node_sea_pick // CELLS
     holder = jnp.sum(
         jnp.where(
@@ -404,52 +460,39 @@
     slot_rows = (
         holder[:, None, :] == jnp.arange(SLOTS, dtype=jnp.int32)[None, :, None]
     ).astype(F32)
-    skip = jnp.einsum("jkc,cd->jkd", normed, bypass_factor, preferred_element_type=F32)
     operands = [
-        returned, synthesis, skip, air, core_exit_factor, air_to_exchange_factor, place, line,
-        forcing_weight, wet, decode_weight, top,
+        synthesis, skip, air, wide, air_flux, place, group, forcing_weight, wet, decode_weight, top
     ]
     updated, tiles = call(
         surface_kernel,
         [shape(air.shape, F32), shape((members, SLOTS, CELLS), BF16)],
-        operands,
+        [returned] + operands,
         2 * latitude_rows * longitudes * channels * (channels + 2 * MMAX),
         held(operands)
         + [
             pltpu.VMEM(air.shape, F32),
-            pltpu.VMEM((FC * latitude_rows, longitudes), F32),
+            pltpu.VMEM((3 * FC * latitude_rows, 128), F32),
             pltpu.VMEM((SLOTS, CELLS), F32),
             pltpu.SemaphoreType.DMA((len(operands),)),
             pltpu.SemaphoreType.DMA((latitude_rows,)),
         ],
-        limit=LARGE,
-        specs=[ANYWHERE] * len(operands),
-        out_specs=[ANYWHERE, WHOLE],
+        specs=[WHOLE] + [FAR] * len(operands),
+        out_specs=[FAR, WHOLE],
     )
     everyone = lax.all_to_all(tiles, "member", split_axis=0, concat_axis=0, tiled=True)
-
-    def by_latitude(*rest):
-        return pl.BlockSpec((1,) + rest, lambda j: (j, 0, 0))
-
-    out = pl.pallas_call(
+    out = call(
         imprint_kernel,
-        grid=(latitude_rows,),
-        out_shape=shape(air.shape, BF16),
-        in_specs=[
-            by_latitude(longitudes, channels),
-            pl.BlockSpec((1, SLOTS, CELLS), lambda j: (0, 0, 0)),
-            by_latitude(longitudes, CELLS),
-            by_latitude(longitudes, 3 * SLOTS),
-            pl.BlockSpec((channels,), lambda j: (0,)),
+        [shape(air.shape, BF16)],
+        [updated, tiles, cell, slot_of, sea_heat_imprint],
+        2 * latitude_rows * longitudes * channels * 256,
+        held([updated, cell, slot_of, air])
+        + [
+            pltpu.SemaphoreType.DMA((latitude_rows + 2,)),
+            pltpu.SemaphoreType.DMA((latitude_rows,)),
         ],
-        out_specs=by_latitude(longitudes, channels),
-        compiler_params=pltpu.CompilerParams(vmem_limit_bytes=LARGE * 1024 * 1024),
-        cost_estimate=pl.CostEstimate(
-            flops=2 * latitude_rows * longitudes * channels * 256,
-            bytes_accessed=air.size * 6,
-            transcendentals=0,
-        ),
-    )(updated, tiles, cell, slot_of, sea_heat_imprint)
+        specs=[FAR, WHOLE, FAR, FAR, WHOLE],
+        out_specs=FAR,
+    )
     mean = call(
         mean_kernel,
         [shape((latitude_rows, longitudes), F32)],

time: 151 us -> 157 us (1.040)
  the two profiles are of different devices: /device:TPU:1 before, /device:TPU:35 now
where the time goes in v3:
time: 157 us; the launch traced here: 156 us
  starting transfers between devices  59.8 us (38%)
  waiting for transfers between devices  36.5 us (23%)
  local copies, waits for them, and re-layouts  35.5 us (23%)
  Pallas kernels  19.7 us (13%)
  other arithmetic  3.38 us (2%)
    unnamed x92, local copies, waits for them, and re-layouts  30.9 us
    ppermute x7, starting transfers between devices, passed_along(): lax.ppermute(value, axis, [(i, (i + by) % devices) for i in range(devices)])  29.6 us
    all_to_all x1, waiting for transfers between devices, shards(): lax.all_to_all(spectra, 'space', split_axis=0, concat_axis=0, tiled=True)  19.8 us
    pallas_call x7, Pallas kernels, call(): pl.pallas_call(kernel, out_shape=outs if len(outs) > 1 else outs[0], in_s...  19.7 us
    ppermute x7, waiting for transfers between devices, passed_along(): lax.ppermute(value, axis, [(i, (i + by) % devices) for i in range(devices)])  16.6 us
    all_to_all x1, starting transfers between devices, shards(): lax.all_to_all(spectra, 'space', split_axis=0, concat_axis=0, tiled=True)  15.7 us
    all_to_all x1, starting transfers between devices, shards(): lax.all_to_all(filtered, 'space', split_axis=0, concat_axis=0, tiled=True)  7.62 us
    all_to_all x1, starting transfers between devices, shards(): lax.all_to_all(tiles, 'member', split_axis=0, concat_axis=0, tiled=True)  6.92 us
  transfers between devices with their start and end apart: 10, of which 3 were waited for; matrix products, arithmetic and copies ran while one was open for 7% of the time, Pallas kernels for 6%

profile of v3, /device:TPU:35, one launch (start us, length us, event | category | flops | bytes accessed | tf_op | source)
XLA Modules:
  0.0 155.9 jit_solution(8084034767873580835)
XLA Ops:
  0.6 1.2 copy-done
  1.9 0.9 copy-done.14
  2.8 0.7 copy-done.23
  3.5 3.4 %shard_map.194 = bf16[32,32,384]{2,1,0:T(8,128)(2,1)} custom-call(bf16[4,360,384]{2,1,0:T(8,128)(2,1)S(1)} %bitcast.56, f32[384]{0:T(512)S(1)} %copy-done.23, bf16[256,360]{1,0:T(8,128)(2,1)S(1)} %copy-done.14), custom_call_target="tpu_custom_call" | custom-call | flops 283115520 | bytes 2078208 | tf_op jit(solution)/shard_map/pallas_call | solution.py:339
  7.0 15.7 %all-to-all-start = ((bf16[32,32,384]{2,1,0:T(8,128)(2,1)}), bf16[32,32,384]{2,1,0:T(8,128)(2,1)S(1)}, u32[]{:S(2)}, u32[]{:S(2)}) async-start(bf16[32,32,384]{2,1,0:T(8,128)(2,1)} %shard_map.194), calls=%async_computation | async-start | bytes 1572864 | tf_op jit(solution)/shard_map/all_to_all | solution.py:390
  22.9 0.4 collective-permute-start
  23.3 1.9 %collective-permute-start.1 = (bf16[2,76,128]{2,1,0:T(8,128)(2,1)S(1)}, bf16[2,76,128]{2,1,0:T(8,128)(2,1)S(1)}, u32[]{:S(2)}, u32[]{:S(2)}) collective-permute-start(bf16[2,76,128]{2,1,0:T(8,128)(2,1)S(1)} %bitcast.65), channel_id=1, source_target_pairs={{0,30},{1,31},{2,0},{3,1},{4,2},{5,3},{6,4},{7,5},{8,6},{9,7},{10,... | collective-permute-start | bytes 116744 | tf_op jit(solution)/shard_map/ppermute | solution.py:33
  25.2 0.6 copy.76
  25.9 6.1 %collective-permute-start.2 = (bf16[2,76,128]{2,1,0:T(8,128)(2,1)}, bf16[2,76,128]{2,1,0:T(8,128)(2,1)}, u32[]{:S(2)}, u32[]{:S(2)}) collective-permute-start(bf16[2,76,128]{2,1,0:T(8,128)(2,1)} %bitcast.52), channel_id=1, source_target_pairs={{0,29},{1,30},{2,31},{3,0},{4,1},{5,2},{6,3},{7,4},{8,5},{9,6},{10... | collective-permute-start | bytes 116744 | tf_op jit(solution)/shard_map/ppermute | solution.py:33
  32.0 0.6 copy.75
  32.7 4.0 %collective-permute-start.3 = (bf16[2,76,128]{2,1,0:T(8,128)(2,1)}, bf16[2,76,128]{2,1,0:T(8,128)(2,1)}, u32[]{:S(2)}, u32[]{:S(2)}) collective-permute-start(bf16[2,76,128]{2,1,0:T(8,128)(2,1)} %bitcast.51), channel_id=1, source_target_pairs={{0,28},{1,29},{2,30},{3,31},{4,0},{5,1},{6,2},{7,3},{8,4},{9,5},{1... | collective-permute-start | bytes 116744 | tf_op jit(solution)/shard_map/ppermute | solution.py:33
  36.6 0.6 copy.74
  37.2 5.2 %collective-permute-start.4 = (bf16[2,76,128]{2,1,0:T(8,128)(2,1)}, bf16[2,76,128]{2,1,0:T(8,128)(2,1)}, u32[]{:S(2)}, u32[]{:S(2)}) collective-permute-start(bf16[2,76,128]{2,1,0:T(8,128)(2,1)} %bitcast.50), channel_id=1, source_target_pairs={{0,27},{1,28},{2,29},{3,30},{4,31},{5,0},{6,1},{7,2},{8,3},{9,4},{... | collective-permute-start | bytes 116744 | tf_op jit(solution)/shard_map/ppermute | solution.py:33
  43.0 1.0 constant_dynamic-slice_fusion
  44.0 19.8 %all-to-all-done.x_ref = bf16[32,32,384]{2,1,0:T(8,128)(2,1)S(1)} async-done(((bf16[32,32,384]{2,1,0:T(8,128)(2,1)}), bf16[32,32,384]{2,1,0:T(8,128)(2,1)S(1)}, u32[]{:S(2)}, u32[]{:S(2)}) %all-to-all-start) | async-done | bytes 786464 | tf_op jit(solution)/shard_map/all_to_all | solution.py:390
  63.9 1.7 %shard_map.195 = bf16[32,32,384]{2,1,0:T(8,128)(2,1)} custom-call(bf16[32,32,384]{2,1,0:T(8,128)(2,1)S(1)} %all-to-all-done.x_ref, bf16[4,128,128]{2,1,0:T(8,128)(2,1)S(1)} %get-tuple-element.29.forward_ref, bf16[4,128,128]{2,1,0:T(8,128)(2,1)S(1)} %get-tuple-element.28.backward_ref, f32[128,384]{1,0:T(8,128)S(1)} %copy-done.15), custom_call_target="tpu_custom_call" | custom-call | flops 201326592 | bytes 2031616 | tf_op jit(solution)/shard_map/pallas_call | solution.py:339
  65.6 7.6 %all-to-all-start.1 = ((bf16[32,32,384]{2,1,0:T(8,128)(2,1)}), bf16[32,32,384]{2,1,0:T(8,128)(2,1)S(1)}, u32[]{:S(2)}, u32[]{:S(2)}) async-start(bf16[32,32,384]{2,1,0:T(8,128)(2,1)} %shard_map.195), calls=%async_computation.1 | async-start | bytes 1572864 | tf_op jit(solution)/shard_map/all_to_all | solution.py:420
  73.7 0.3 compare_convert_fusion.slot_any
  73.9 0.8 slice_select_fusion
  75.0 0.7 select_reduce_fusion.2.depth_ref
  75.7 0.6 copy.73
  76.3 0.6 copy.72
  76.9 0.6 copy.79
  77.5 1.9 %copy.50.refs_8_ = bf16[200,720]{1,0:T(8,128)(2,1)} copy(bf16[200,720]{0,1:T(8,128)(2,1)} %bitcast.61) | data formatting | bytes 576000 | tf_op jit(solution)/shard_map/reshape | solution.py:428
  79.4 0.7 copy.51.refs_7_
  80.1 0.6 pad.9.refs_9_
  80.7 0.6 copy-done.27
  81.3 5.4 %collective-permute-start.5 = (bf16[2,76,128]{2,1,0:T(8,128)(2,1)}, bf16[2,76,128]{2,1,0:T(8,128)(2,1)S(1)}, u32[]{:S(2)}, u32[]{:S(2)}) collective-permute-start(bf16[2,76,128]{2,1,0:T(8,128)(2,1)} %bitcast.49), channel_id=1, source_target_pairs={{0,26},{1,27},{2,28},{3,29},{4,30},{5,31},{6,0},{7,1},{8,2},{9,3},... | collective-permute-start | bytes 116744 | tf_op jit(solution)/shard_map/ppermute | solution.py:33
  86.7 0.6 copy-done.29
  87.3 6.6 %collective-permute-start.6 = (bf16[2,76,128]{2,1,0:T(8,128)(2,1)}, bf16[2,76,128]{2,1,0:T(8,128)(2,1)S(1)}, u32[]{:S(2)}, u32[]{:S(2)}) collective-permute-start(bf16[2,76,128]{2,1,0:T(8,128)(2,1)} %bitcast.48), channel_id=1, source_target_pairs={{0,25},{1,26},{2,27},{3,28},{4,29},{5,30},{6,31},{7,0},{8,1},{9,2}... | collective-permute-start | bytes 116744 | tf_op jit(solution)/shard_map/ppermute | solution.py:33
  93.9 1.0 copy-done.9
  94.9 1.0 copy-done.10
  95.8 0.7 copy-done.24
  96.5 0.7 copy-done.25
  97.2 2.9 %shard_map.196 = (f32[4,360,384]{2,1,0:T(8,128)S(1)}, f32[32,360]{1,0:T(8,128)S(1)}, bf16[384,512]{1,0:T(8,128)(2,1)S(1)}) custom-call(bf16[4,360,384]{2,1,0:T(8,128)(2,1)S(1)} %bitcast.57, f32[384]{0:T(512)S(1)} %copy-done.24, bf16[384,384]{1,0:T(8,128)(2,1)S(1)} %copy-done.9, bf16[384,384]{1,0:T(8,128)(2,1)S(1)} %copy-done.10, bf16[8,384]{1,0:T(8,128)(2,1)S(1)} %bitcast.60), custom_call_target="tpu_custom_call" | custom-call | flops 424673280 | bytes 4354560 | tf_op jit(solution)/shard_map/pallas_call | solution.py:339
  100.1 1.4 copy-done.4
  101.5 0.6 copy-done.17
  102.1 7.4 %collective-permute-done.5.refs_6_ = bf16[2,76,128]{2,1,0:T(8,128)(2,1)S(1)} collective-permute-done((bf16[2,76,128]{2,1,0:T(8,128)(2,1)}, bf16[2,76,128]{2,1,0:T(8,128)(2,1)S(1)}, u32[]{:S(2)}, u32[]{:S(2)}) %collective-permute-start.5) | collective-permute-done | bytes 38944 | tf_op jit(solution)/shard_map/ppermute | solution.py:33
  109.5 9.3 %collective-permute-done.6.refs_7_ = bf16[2,76,128]{2,1,0:T(8,128)(2,1)S(1)} collective-permute-done((bf16[2,76,128]{2,1,0:T(8,128)(2,1)}, bf16[2,76,128]{2,1,0:T(8,128)(2,1)S(1)}, u32[]{:S(2)}, u32[]{:S(2)}) %collective-permute-start.6) | collective-permute-done | bytes 38944 | tf_op jit(solution)/shard_map/ppermute | solution.py:33
  118.7 1.0 copy-done.8
  119.7 0.8 copy-done.19
  120.5 0.8 copy-done.28
  121.3 0.8 copy-done.30
  122.0 0.7 copy-done.31
  122.7 2.1 %shard_map.197 = (f32[200,2048]{1,0:T(8,128)S(1)}, f32[1,2048]{1,0:T(1,128)S(1)}) custom-call(s32[16]{0:T(128)S(1)} %copy-done.31, bf16[2,76,128]{2,1,0:T(8,128)(2,1)S(1)} %bitcast.59, bf16[2,76,128]{2,1,0:T(8,128)(2,1)S(1)} %copy-done.28, bf16[2,76,128]{2,1,0:T(8,128)(2,1)S(1)} %copy-done.30, bf16[2,76,128]{2,1,0:T(8,128)(2,1)} %collective-permute-done.2.refs_3_, ...), custom_call_target="tpu_custom_call" | custom-call | flops 589824000 | bytes 2245952 | tf_op jit(solution)/shard_map/pallas_call | solution.py:339
  124.9 1.2 copy-done.6
  126.0 0.6 copy-done.21
  126.6 1.6 %copy-done.5 = f32[4,360,384]{2,1,0:T(8,128)S(1)} copy-done((f32[4,360,384]{2,1,0:T(8,128)S(1)}, f32[4,360,384]{2,1,0:T(8,128)}, u32[]{:S(2)}) %copy-start.5) | copy-done | bytes 2211864
  128.2 1.4 copy-done.7
  129.7 0.8 copy-done.13
  130.5 0.9 copy-done.16
  131.4 0.8 copy-done.18
  132.2 0.7 copy-done.20
  132.9 0.7 copy-done.22
  133.6 5.6 %shard_map.198 = (f32[4,360,384]{2,1,0:T(8,128)S(1)}, bf16[16,16,128]{2,1,0:T(8,128)(2,1)S(1)}) custom-call(bf16[32,32,384]{2,1,0:T(8,128)(2,1)S(1)} %all-to-all-done.1.rows_ref, bf16[360,256]{1,0:T(8,128)(2,1)S(1)} %copy-done.16, f32[4,360,384]{2,1,0:T(8,128)S(1)} %copy-done.5, bf16[4,360,384]{2,1,0:T(8,128)(2,1)S(1)} %bitcast.58, ...), custom_call_target="tpu_custom_call" | custom-call | flops 707788800 | bytes 9219456 | tf_op jit(solution)/shard_map/pallas_call | solution.py:339
  139.2 1.4 copy-done.2
  140.6 0.6 copy-done.11
  141.2 6.9 %all-to-all-start.2 = ((bf16[16,16,128]{2,1,0:T(8,128)(2,1)}), bf16[16,16,128]{2,1,0:T(8,128)(2,1)S(1)}, u32[]{:S(2)}, u32[]{:S(2)}) async-start(bf16[16,16,128]{2,1,0:T(8,128)(2,1)} %copy-done.11), calls=%async_computation.2 | async-start | bytes 131072 | tf_op jit(solution)/shard_map/all_to_all | solution.py:482
  148.1 0.7 fusion.2.slot_ref
  148.8 1.6 %copy-done.3 = f32[4,360,384]{2,1,0:T(8,128)S(1)} copy-done((f32[4,360,384]{2,1,0:T(8,128)S(1)}, f32[4,360,384]{2,1,0:T(8,128)}, u32[]{:S(2)}) %copy-start.3) | copy-done | bytes 2211864
  150.4 0.8 copy-done.12
  151.3 0.7 copy-done.26
  152.0 3.0 %shard_map.199 = bf16[4,360,384]{2,1,0:T(8,128)(2,1)} custom-call(f32[4,360,384]{2,1,0:T(8,128)S(1)} %copy-done.3, bf16[16,16,128]{2,1,0:T(8,128)(2,1)S(1)} %copy-done.12, bf16[4,360,128]{2,1,0:T(8,128)(2,1)S(1)} %fusion.1.cell_any.cell_ref, bf16[4,360,48]{2,1,0:T(8,128)(2,1)S(1)} %compare_convert_fusion.slot_any, f32[384]{0:T(512)S(1)} %copy-done.26), custom_call_target="tpu_custom_call" | custom-call | flops 283115520 | bytes 3891712 | tf_op jit(solution)/shard_map/pallas_call | solution.py:339
  155.0 0.9 shard_map.200
  (81 shorter events, 1.4 us)
Async XLA Ops:
  0.6 1.2 copy-start
  1.9 0.9 copy-start.14
  2.8 0.7 copy-start.23
  3.5 19.2 %copy-start.33 = (bf16[1,16,76,128]{3,1,2,0:T(8,128)(2,1)S(1)}, bf16[1,16,76,128]{3,1,2,0:T(8,128)(2,1)}, u32[]{:S(2)}) copy-start(bf16[1,16,76,128]{3,1,2,0:T(8,128)(2,1)} %param.27) | copy-start | bytes 933892
  3.5 39.0 %copy-start.39 = (s32[14,1]{0,1:T(1,128)S(1)}, s32[14,1]{0,1:T(1,128)}, u32[]{:S(2)}) copy-start(s32[14,1]{0,1:T(1,128)} %param.32) | copy-start | bytes 172
  3.5 39.3 %copy-start.35 = (s32[14,128]{1,0:T(8,128)S(1)}, s32[14,128]{1,0:T(8,128)}, u32[]{:S(2)}) copy-start(s32[14,128]{1,0:T(8,128)} %param.30) | copy-start | bytes 21508
  3.5 39.4 %copy-start.37 = (s32[4,360]{1,0:T(4,128)S(1)}, s32[4,360]{1,0:T(4,128)}, u32[]{:S(2)}) copy-start(s32[4,360]{1,0:T(4,128)} %param.31) | copy-start | bytes 17284
  3.5 60.4 %copy-start.15 = (f32[128,384]{1,0:T(8,128)S(1)}, f32[128,384]{1,0:T(8,128)}, u32[]{:S(2)}) copy-start(f32[128,384]{1,0:T(8,128)} %gains_ref.1) | copy-start | bytes 589828
  7.0 56.9 %all-to-all-start = ((bf16[32,32,384]{2,1,0:T(8,128)(2,1)}), bf16[32,32,384]{2,1,0:T(8,128)(2,1)S(1)}, u32[]{:S(2)}, u32[]{:S(2)}) async-start(bf16[32,32,384]{2,1,0:T(8,128)(2,1)} %shard_map.194), calls=%async_computation | async-start | bytes 1572864 | tf_op jit(solution)/shard_map/all_to_all | solution.py:390
  22.9 57.8 %collective-permute-start = (bf16[2,76,128]{2,1,0:T(8,128)(2,1)S(1)}, bf16[2,76,128]{2,1,0:T(8,128)(2,1)S(1)}, u32[]{:S(2)}, u32[]{:S(2)}) collective-permute-start(bf16[2,76,128]{2,1,0:T(8,128)(2,1)S(1)} %bitcast.66), channel_id=1, source_target_pairs={{0,31},{1,0},{2,1},{3,2},{4,3},{5,4},{6,5},{7,6},{8,7},{9,8},{10,9... | collective-permute-start | bytes 116744 | tf_op jit(solution)/shard_map/ppermute | solution.py:33
  23.3 63.4 %collective-permute-start.1 = (bf16[2,76,128]{2,1,0:T(8,128)(2,1)S(1)}, bf16[2,76,128]{2,1,0:T(8,128)(2,1)S(1)}, u32[]{:S(2)}, u32[]{:S(2)}) collective-permute-start(bf16[2,76,128]{2,1,0:T(8,128)(2,1)S(1)} %bitcast.65), channel_id=1, source_target_pairs={{0,30},{1,31},{2,0},{3,1},{4,2},{5,3},{6,4},{7,5},{8,6},{9,7},{10,... | collective-permute-start | bytes 116744 | tf_op jit(solution)/shard_map/ppermute | solution.py:33
  25.9 47.5 %copy-start.38 = (s32[4,360]{1,0:T(4,128)S(1)}, s32[4,360]{1,0:T(4,128)}, u32[]{:S(2)}) copy-start(s32[4,360]{1,0:T(4,128)} %param.20) | copy-start | bytes 17284
  25.9 76.2 %collective-permute-start.2 = (bf16[2,76,128]{2,1,0:T(8,128)(2,1)}, bf16[2,76,128]{2,1,0:T(8,128)(2,1)}, u32[]{:S(2)}, u32[]{:S(2)}) collective-permute-start(bf16[2,76,128]{2,1,0:T(8,128)(2,1)} %bitcast.52), channel_id=1, source_target_pairs={{0,29},{1,30},{2,31},{3,0},{4,1},{5,2},{6,3},{7,4},{8,5},{9,6},{10... | collective-permute-start | bytes 116744 | tf_op jit(solution)/shard_map/ppermute | solution.py:33
  32.0 41.4 %copy-start.32 = (bf16[9,200,84]{1,2,0:T(8,128)(2,1)S(1)}, bf16[9,200,84]{1,2,0:T(8,128)(2,1)}, u32[]{:S(2)}) copy-start(bf16[9,200,84]{1,2,0:T(8,128)(2,1)} %param.28) | copy-start | bytes 907204
  32.7 69.5 %collective-permute-start.3 = (bf16[2,76,128]{2,1,0:T(8,128)(2,1)}, bf16[2,76,128]{2,1,0:T(8,128)(2,1)}, u32[]{:S(2)}, u32[]{:S(2)}) collective-permute-start(bf16[2,76,128]{2,1,0:T(8,128)(2,1)} %bitcast.51), channel_id=1, source_target_pairs={{0,28},{1,29},{2,30},{3,31},{4,0},{5,1},{6,2},{7,3},{8,4},{9,5},{1... | collective-permute-start | bytes 116744 | tf_op jit(solution)/shard_map/ppermute | solution.py:33
  37.2 64.9 %collective-permute-start.4 = (bf16[2,76,128]{2,1,0:T(8,128)(2,1)}, bf16[2,76,128]{2,1,0:T(8,128)(2,1)}, u32[]{:S(2)}, u32[]{:S(2)}) collective-permute-start(bf16[2,76,128]{2,1,0:T(8,128)(2,1)} %bitcast.50), channel_id=1, source_target_pairs={{0,27},{1,28},{2,29},{3,30},{4,31},{5,0},{6,1},{7,2},{8,3},{9,4},{... | collective-permute-start | bytes 116744 | tf_op jit(solution)/shard_map/ppermute | solution.py:33
  63.9 10.0 %copy-start.40 = (pred[80]{0:T(512)(128)(4,1)S(1)}, pred[80]{0:T(512)(128)(4,1)}, u32[]{:S(2)}) copy-start(pred[80]{0:T(512)(128)(4,1)} %constant.98.clone.1) | copy-start | bytes 244
  65.6 9.3 %copy-start.41 = (s32[14]{0:T(128)S(1)}, s32[14]{0:T(128)}, u32[]{:S(2)}) copy-start(s32[14]{0:T(128)} %param.33) | copy-start | bytes 172
  65.6 14.5 %copy-start.36 = (bf16[9,200]{1,0:T(8,128)(2,1)S(1)}, bf16[9,200]{1,0:T(8,128)(2,1)}, u32[]{:S(2)}) copy-start(bf16[9,200]{1,0:T(8,128)(2,1)} %param.29) | copy-start | bytes 10804
  65.6 28.3 %copy-start.1 = (bf16[1,4,360,384]{3,2,1,0:T(8,128)(2,1)S(1)}, bf16[1,4,360,384]{3,2,1,0:T(8,128)(2,1)}, u32[]{:S(2)}) copy-start(bf16[1,4,360,384]{3,2,1,0:T(8,128)(2,1)} %param.19) | copy-start | bytes 3317764
  65.6 61.0 %all-to-all-start.1 = ((bf16[32,32,384]{2,1,0:T(8,128)(2,1)}), bf16[32,32,384]{2,1,0:T(8,128)(2,1)S(1)}, u32[]{:S(2)}, u32[]{:S(2)}) async-start(bf16[32,32,384]{2,1,0:T(8,128)(2,1)} %shard_map.195), calls=%async_computation.1 | async-start | bytes 1572864 | tf_op jit(solution)/shard_map/all_to_all | solution.py:420
  73.3 1.4 copy-start.34
  80.7 0.6 copy-start.27
  81.3 28.1 %collective-permute-start.5 = (bf16[2,76,128]{2,1,0:T(8,128)(2,1)}, bf16[2,76,128]{2,1,0:T(8,128)(2,1)S(1)}, u32[]{:S(2)}, u32[]{:S(2)}) collective-permute-start(bf16[2,76,128]{2,1,0:T(8,128)(2,1)} %bitcast.49), channel_id=1, source_target_pairs={{0,26},{1,27},{2,28},{3,29},{4,30},{5,31},{6,0},{7,1},{8,2},{9,3},... | collective-permute-start | bytes 116744 | tf_op jit(solution)/shard_map/ppermute | solution.py:33
  86.7 0.6 copy-start.29
  87.3 31.4 %collective-permute-start.6 = (bf16[2,76,128]{2,1,0:T(8,128)(2,1)}, bf16[2,76,128]{2,1,0:T(8,128)(2,1)S(1)}, u32[]{:S(2)}, u32[]{:S(2)}) collective-permute-start(bf16[2,76,128]{2,1,0:T(8,128)(2,1)} %bitcast.48), channel_id=1, source_target_pairs={{0,25},{1,26},{2,27},{3,28},{4,29},{5,30},{6,31},{7,0},{8,1},{9,2}... | collective-permute-start | bytes 116744 | tf_op jit(solution)/shard_map/ppermute | solution.py:33
  93.9 1.0 copy-start.9
  94.9 1.0 copy-start.10
  95.8 0.7 copy-start.24
  96.5 0.7 copy-start.25
  100.1 1.4 copy-start.4
  101.5 0.6 copy-start.17
  118.7 1.0 copy-start.8
  119.7 0.8 copy-start.19
  120.5 0.8 copy-start.28
  121.3 0.8 copy-start.30
  122.0 0.7 copy-start.31
  124.8 1.2 copy-start.6
  126.0 0.6 copy-start.21
  126.6 1.6 %copy-start.5 = (f32[4,360,384]{2,1,0:T(8,128)S(1)}, f32[4,360,384]{2,1,0:T(8,128)}, u32[]{:S(2)}) copy-start(f32[4,360,384]{2,1,0:T(8,128)} %copy-done.4) | copy-start | bytes 6635524
  128.2 1.4 copy-start.7
  129.7 0.8 copy-start.13
  130.5 0.9 copy-start.16
  131.4 0.8 copy-start.18
  132.2 0.7 copy-start.20
  132.9 0.7 copy-start.22
  139.2 1.4 copy-start.2
  140.6 0.6 copy-start.11
  141.2 13.8 %all-to-all-start.2 = ((bf16[16,16,128]{2,1,0:T(8,128)(2,1)}), bf16[16,16,128]{2,1,0:T(8,128)(2,1)S(1)}, u32[]{:S(2)}, u32[]{:S(2)}) async-start(bf16[16,16,128]{2,1,0:T(8,128)(2,1)} %copy-done.11), calls=%async_computation.2 | async-start | bytes 131072 | tf_op jit(solution)/shard_map/all_to_all | solution.py:482
  148.8 1.6 %copy-start.3 = (f32[4,360,384]{2,1,0:T(8,128)S(1)}, f32[4,360,384]{2,1,0:T(8,128)}, u32[]{:S(2)}) copy-start(f32[4,360,384]{2,1,0:T(8,128)} %copy-done.2) | copy-start | bytes 6635524
  150.4 0.8 copy-start.12
  151.3 0.7 copy-start.26

commit v4 on v3

--- a/solution.py
+++ b/solution.py
@@ -22,6 +22,7 @@
 OCH = 76
 OCH_PAD = 80
 TAPS = [(row, col) for row in (-1, 0, 1) for col in (-1, 0, 1)]
+LATE = 6
 BF16 = jnp.bfloat16
 F32 = jnp.float32
 WHOLE = pl.BlockSpec(memory_space=pltpu.VMEM)
@@ -213,8 +214,8 @@
         )
 
 
-def surface_kernel(rows_ref, *refs):
-    count = 11
+def surface_kernel(*refs):
+    count = 12
     sources, (updated_any, tiles_ref), held, (updated_ref, flux, sst, sems, out_sems) = (
         refs[:count], refs[count : count + 2], refs[count + 2 : 2 * count + 2],
         refs[2 * count + 2 :],
@@ -222,21 +223,22 @@
     leaving = []
     copies = begin(list(zip(sources, held)), sems)
     (
-        synthesis_ref, skip_ref, air_ref, wide_ref, air_flux_ref, place_ref, group_ref,
+        rows_ref, synthesis_ref, skip_ref, air_ref, wide_ref, air_flux_ref, place_ref, group_ref,
         forcing_weight_ref, wet_ref, decode_ref, top_ref,
     ) = held
     latitude_rows, longitudes, channels = air_ref.shape
     groups = rows_ref.shape[0]
     pairs = []
+    copies[0].wait()
     for pair in range(latitude_rows // 2):
         both = rows_ref[:, 16 * pair : 16 * (pair + 1), :].astype(F32)
         pairs.extend([both[:, :8], both[:, 8:]])
-    copies[0].wait()
+    copies[1].wait()
     for j in range(latitude_rows):
         own = pairs[j].reshape(8 * groups, channels).astype(BF16)
         spectral = jnp.dot(synthesis_ref[...], own, preferred_element_type=F32)
         if j == 0:
-            for one in copies[1:4]:
+            for one in copies[2:5]:
                 one.wait()
         mixed = gelu(spectral + skip_ref[j]).astype(BF16)
         wide = jnp.dot(mixed, wide_ref[...], preferred_element_type=F32)
@@ -249,7 +251,7 @@
         )
         turned = jnp.transpose(narrow)
         if j == 0:
-            copies[4].wait()
+            copies[5].wait()
         extra = jnp.concatenate(
             [air_flux_ref[FC * j : FC * (j + 1), :], jnp.zeros((FC, 384 - longitudes), F32)], axis=1
         )
@@ -257,7 +259,7 @@
         for part in range(3):
             at = FC * (part * latitude_rows + j)
             flux[at : at + FC, :] = total[:, 128 * part : 128 * (part + 1)]
-    for one in copies[5:]:
+    for one in copies[6:]:
         one.wait()
     spread = jnp.dot(flux[...].astype(BF16), place_ref[...], preferred_element_type=F32)
     group = group_ref[...]
@@ -334,7 +336,7 @@
         out_ref[j : j + 1, :] = jnp.sum(kept, axis=0, keepdims=True) / members
 
 
-def call(kernel, outs, operands, flops, scratch=(), limit=32, specs=None, out_specs=None):
+def call(kernel, outs, operands, flops, scratch=(), limit=56, specs=None, out_specs=None):
     size = sum(math.prod(o.shape) * o.dtype.itemsize for o in list(outs) + list(operands))
     return pl.pallas_call(
         kernel,
@@ -390,9 +392,9 @@
     gathered = lax.all_to_all(spectra, "space", split_axis=0, concat_axis=0, tiled=True)
 
     slots = sea_ensemble_arrays[0]
-    pieces = [slots[:CAP]] + [
+    near = [
         passed_along(slots[offset * CAP : (offset + 1) * CAP], "space", -offset)
-        for offset in range(1, NEAR)
+        for offset in range(1, LATE)
     ]
     forward, backward = (jnp.asarray(t) for t in legendre_tables(latitudes))
     first = lax.axis_index("space") * per_device
@@ -410,14 +412,6 @@
         held([air]) + [pltpu.SemaphoreType.DMA((latitude_rows,))],
         specs=[FAR] + [WHOLE] * 4,
     )
-    filtered = call(
-        legendre_kernel,
-        [shape((bands, chunk, channels), BF16)],
-        [gathered, forward, backward, harmonic_damping_factor],
-        2 * 2 * 2 * per_device * LMAX * latitudes * channels,
-        [pltpu.VMEM((channels // 128, bands * chunk, 128), F32)],
-    )
-    returned = lax.all_to_all(filtered, "space", split_axis=0, concat_axis=0, tiled=True)
     offsets = patch_holder_shift[:, 0]
     earlier = jnp.tril(jnp.ones((HOME_DEV, HOME_DEV), jnp.int32), -1)
     positions = jnp.sum((offsets[:, None] == offsets[None, :]).astype(jnp.int32) * earlier, axis=1)
@@ -430,14 +424,6 @@
     )
     forcing_weight = kernel[:, :, OCH:].reshape(hidden_channels, -1)
     decode_weight = jnp.pad(hidden_to_change_kernel, ((0, 16 - len(TAPS)), (0, 0)))
-    wet, top = call(
-        ocean_kernel,
-        [shape((hidden_channels, SPAN), F32), shape((1, SPAN), F32)],
-        [depths, *pieces, state_weight],
-        2 * hidden_channels * len(TAPS) * OCH_PAD * SPAN,
-        [pltpu.VMEM((len(TAPS) * OCH_PAD, SPAN), BF16)],
-        specs=[pl.BlockSpec(memory_space=pltpu.SMEM)] + [WHOLE] * (NEAR + 1),
-    )
     picks = jnp.sum(jnp.where(selected[:, :, None], patch_exchange_pick[None], 0), axis=1)
     picks = picks.reshape(1, SPAN)
     line, column = picks // longitudes, picks % longitudes
@@ -460,13 +446,45 @@
     slot_rows = (
         holder[:, None, :] == jnp.arange(SLOTS, dtype=jnp.int32)[None, :, None]
     ).astype(F32)
+    prepared = (
+        near, skip, air_flux, wide, place, group, forcing_weight, state_weight, decode_weight,
+        depths, cell, slot_of,
+    )
+    gathered, prepared = lax.optimization_barrier((gathered, prepared))
+    (
+        near, skip, air_flux, wide, place, group, forcing_weight, state_weight, decode_weight,
+        depths, cell, slot_of,
+    ) = prepared
+    filtered = call(
+        legendre_kernel,
+        [shape((bands, chunk, channels), BF16)],
+        [gathered, forward, backward, harmonic_damping_factor],
+        2 * 2 * 2 * per_device * LMAX * latitudes * channels,
+        [pltpu.VMEM((channels // 128, bands * chunk, 128), F32)],
+        limit=32,
+    )
+    filtered, late = lax.optimization_barrier((filtered, slots[LATE * CAP :]))
+    returned = lax.all_to_all(filtered, "space", split_axis=0, concat_axis=0, tiled=True)
+    rest = [
+        passed_along(late[at : at + CAP], "space", -(LATE + at // CAP))
+        for at in range(0, late.shape[0], CAP)
+    ]
+    wet, top = call(
+        ocean_kernel,
+        [shape((hidden_channels, SPAN), F32), shape((1, SPAN), F32)],
+        [depths, slots[:CAP], *near, *rest, state_weight],
+        2 * hidden_channels * len(TAPS) * OCH_PAD * SPAN,
+        [pltpu.VMEM((len(TAPS) * OCH_PAD, SPAN), BF16)],
+        specs=[pl.BlockSpec(memory_space=pltpu.SMEM)] + [WHOLE] * (NEAR + 1),
+    )
     operands = [
-        synthesis, skip, air, wide, air_flux, place, group, forcing_weight, wet, decode_weight, top
+        returned, synthesis, skip, air, wide, air_flux, place, group, forcing_weight, wet,
+        decode_weight, top,
     ]
     updated, tiles = call(
         surface_kernel,
         [shape(air.shape, F32), shape((members, SLOTS, CELLS), BF16)],
-        [returned] + operands,
+        operands,
         2 * latitude_rows * longitudes * channels * (channels + 2 * MMAX),
         held(operands)
         + [
@@ -476,7 +494,7 @@
             pltpu.SemaphoreType.DMA((len(operands),)),
             pltpu.SemaphoreType.DMA((latitude_rows,)),
         ],
-        specs=[WHOLE] + [FAR] * len(operands),
+        specs=[FAR] * len(operands),
         out_specs=[FAR, WHOLE],
     )
     everyone = lax.all_to_all(tiles, "member", split_axis=0, concat_axis=0, tiled=True)
@@ -498,6 +516,7 @@
         [shape((latitude_rows, longitudes), F32)],
         [everyone, cell, slot_rows],
         2 * 3 * SLOTS * CELLS * latitude_rows * longitudes,
+        limit=32,
     )
     return (out[None], mean)
 

time: 157 us -> 158 us (level)
  the two profiles are of different devices: /device:TPU:35 before, /device:TPU:33 now
where the time goes in v4:
time: 158 us; the launch traced here: 157 us
  waiting for transfers between devices  61.9 us (39%)
  starting transfers between devices  53.6 us (34%)
  Pallas kernels  28 us (18%)
  local copies, waits for them, and re-layouts  8.1 us (5%)
  other arithmetic  4.74 us (3%)
    ppermute x7, starting transfers between devices, passed_along(): lax.ppermute(value, axis, [(i, (i + by) % devices) for i in range(devices)])  33.9 us
    ppermute x7, waiting for transfers between devices, passed_along(): lax.ppermute(value, axis, [(i, (i + by) % devices) for i in range(devices)])  31.2 us
    all_to_all x1, waiting for transfers between devices, shards(): lax.all_to_all(spectra, 'space', split_axis=0, concat_axis=0, tiled=True)  28.5 us
    pallas_call x7, Pallas kernels, call(): pl.pallas_call(kernel, out_shape=outs if len(outs) > 1 else outs[0], in_s...  28 us
    all_to_all x1, starting transfers between devices, shards(): lax.all_to_all(tiles, 'member', split_axis=0, concat_axis=0, tiled=True)  6.93 us
    all_to_all x1, starting transfers between devices, shards(): lax.all_to_all(filtered, 'space', split_axis=0, concat_axis=0, tiled=True)  6.5 us
    all_to_all x1, starting transfers between devices, shards(): lax.all_to_all(spectra, 'space', split_axis=0, concat_axis=0, tiled=True)  6.27 us
  transfers between devices with their start and end apart: 10, of which 4 were waited for; matrix products, arithmetic and copies ran while one was open for 6% of the time, Pallas kernels for 12%

profile of v4, /device:TPU:33, one launch (start us, length us, event | category | flops | bytes accessed | tf_op | source)
XLA Modules:
  0.0 157.4 jit_solution(9747477356821495445)
XLA Ops:
  0.6 0.0 copy-start.8
  0.6 0.0 copy-start.6
  0.7 0.0 copy-start.17
  0.7 0.0 copy-start.4
  0.7 1.5 fusion.8
  2.2 0.0 copy-start.5
  2.2 0.7 collective-permute-start
  2.9 7.1 %collective-permute-start.1 = (bf16[2,76,128]{2,1,0:T(8,128)(2,1)S(1)}, bf16[2,76,128]{2,1,0:T(8,128)(2,1)S(1)}, u32[]{:S(2)}, u32[]{:S(2)}) collective-permute-start(bf16[2,76,128]{2,1,0:T(8,128)(2,1)S(1)} %bitcast.62), channel_id=1, source_target_pairs={{0,30},{1,31},{2,0},{3,1},{4,2},{5,3},{6,4},{7,5},{8,6},{9,7},{10,... | collective-permute-start | bytes 116744 | tf_op jit(solution)/shard_map/ppermute | solution.py:34
  10.1 6.4 %collective-permute-start.2 = (bf16[2,76,128]{2,1,0:T(8,128)(2,1)S(1)}, bf16[2,76,128]{2,1,0:T(8,128)(2,1)S(1)}, u32[]{:S(2)}, u32[]{:S(2)}) collective-permute-start(bf16[2,76,128]{2,1,0:T(8,128)(2,1)S(1)} %bitcast.63), channel_id=1, source_target_pairs={{0,29},{1,30},{2,31},{3,0},{4,1},{5,2},{6,3},{7,4},{8,5},{9,6},{10... | collective-permute-start | bytes 116744 | tf_op jit(solution)/shard_map/ppermute | solution.py:34
  16.4 3.1 %collective-permute-start.3 = (bf16[2,76,128]{2,1,0:T(8,128)(2,1)S(1)}, bf16[2,76,128]{2,1,0:T(8,128)(2,1)S(1)}, u32[]{:S(2)}, u32[]{:S(2)}) collective-permute-start(bf16[2,76,128]{2,1,0:T(8,128)(2,1)S(1)} %bitcast.64), channel_id=1, source_target_pairs={{0,28},{1,29},{2,30},{3,31},{4,0},{5,1},{6,2},{7,3},{8,4},{9,5},{1... | collective-permute-start | bytes 116744 | tf_op jit(solution)/shard_map/ppermute | solution.py:34
  19.5 4.7 %collective-permute-start.4 = (bf16[2,76,128]{2,1,0:T(8,128)(2,1)S(1)}, bf16[2,76,128]{2,1,0:T(8,128)(2,1)S(1)}, u32[]{:S(2)}, u32[]{:S(2)}) collective-permute-start(bf16[2,76,128]{2,1,0:T(8,128)(2,1)S(1)} %bitcast.65), channel_id=1, source_target_pairs={{0,27},{1,28},{2,29},{3,30},{4,31},{5,0},{6,1},{7,2},{8,3},{9,4},{... | collective-permute-start | bytes 116744 | tf_op jit(solution)/shard_map/ppermute | solution.py:34
  24.2 0.0 copy-start.7
  24.3 0.0 copy-start.3
  24.3 4.8 %shard_map.194 = bf16[32,32,384]{2,1,0:T(8,128)(2,1)} custom-call(bf16[4,360,384]{2,1,0:T(8,128)(2,1)} %bitcast.53, f32[384]{0:T(512)} %scale_ref.3, bf16[256,360]{1,0:T(8,128)(2,1)} %constant.102.clone.table_any), custom_call_target="tpu_custom_call" | custom-call | flops 283115520 | bytes 2078208 | tf_op jit(solution)/shard_map/pallas_call | solution.py:341
  29.1 0.0 copy-start.9
  29.1 6.3 %all-to-all-start = ((bf16[32,32,384]{2,1,0:T(8,128)(2,1)}), bf16[32,32,384]{2,1,0:T(8,128)(2,1)S(1)}, u32[]{:S(2)}, u32[]{:S(2)}) async-start(bf16[32,32,384]{2,1,0:T(8,128)(2,1)} %shard_map.194), calls=%async_computation | async-start | bytes 1572864 | tf_op jit(solution)/shard_map/all_to_all | solution.py:392
  35.4 0.0 copy-done.8
  35.4 0.2 select_reduce_fusion.3
  35.6 0.1 copy.44
  35.7 0.0 copy-done.6
  35.7 0.0 copy-done.17
  35.7 0.6 select_reduce_fusion.2.depth_ref
  36.4 0.0 copy-done.4
  36.4 0.1 select_reduce_fusion
  36.5 1.0 slice.67
  37.5 0.0 copy-done.5
  37.5 0.6 pad.9.refs_10_
  38.1 0.1 select_reduce_fusion.1
  38.2 0.0 copy-start.1
  38.2 1.0 constant_dynamic-slice_fusion
  39.3 0.0 copy-done.7
  39.3 1.0 fusion.1.cell_any.cell_ref
  40.3 1.0 compare_convert_fusion.slot_any
  41.3 0.1 slice_select_fusion
  41.4 0.7 multiply_add_fusion.refs_7_
  42.1 0.9 fusion.refs_6_
  43.0 6.0 %shard_map.195 = (f32[4,360,384]{2,1,0:T(8,128)}, f32[32,360]{1,0:T(8,128)}, bf16[384,512]{1,0:T(8,128)(2,1)}) custom-call(bf16[4,360,384]{2,1,0:T(8,128)(2,1)} %bitcast.54, f32[384]{0:T(512)} %scale_ref.3, bf16[384,384]{1,0:T(8,128)(2,1)} %bypass_ref.1, bf16[384,384]{1,0:T(8,128)(2,1)} %exit_ref.1, bf16[8,384]{1,0:T(8,128)(2,1)} %bitcast.69), custom_call_target="tpu_custom_call" | custom-call | flops 424673280 | bytes 4354560 | tf_op jit(solution)/shard_map/pallas_call | solution.py:341
  49.0 0.0 collective-permute-done.refs_1_
  49.0 0.0 collective-permute-done.1.refs_2_
  49.0 0.0 collective-permute-done.2.refs_3_
  49.1 0.0 collective-permute-done.3.refs_4_
  49.1 0.0 collective-permute-done.4.refs_5_
  49.1 28.5 %all-to-all-done.x_ref = bf16[32,32,384]{2,1,0:T(8,128)(2,1)S(1)} async-done(((bf16[32,32,384]{2,1,0:T(8,128)(2,1)}), bf16[32,32,384]{2,1,0:T(8,128)(2,1)S(1)}, u32[]{:S(2)}, u32[]{:S(2)}) %all-to-all-start) | async-done | bytes 786464 | tf_op jit(solution)/shard_map/all_to_all | solution.py:392
  77.6 1.8 %shard_map.196 = bf16[32,32,384]{2,1,0:T(8,128)(2,1)} custom-call(bf16[32,32,384]{2,1,0:T(8,128)(2,1)S(1)} %all-to-all-done.x_ref, bf16[4,128,128]{2,1,0:T(8,128)(2,1)S(1)} %get-tuple-element.66.forward_ref, bf16[4,128,128]{2,1,0:T(8,128)(2,1)S(1)} %get-tuple-element.67.backward_ref, f32[128,384]{1,0:T(8,128)S(1)} %copy-done.1), custom_call_target="tpu_custom_call" | custom-call | flops 201326592 | bytes 2031616 | tf_op jit(solution)/shard_map/pallas_call | solution.py:341
  79.4 6.5 %all-to-all-start.1 = ((bf16[32,32,384]{2,1,0:T(8,128)(2,1)}), bf16[32,32,384]{2,1,0:T(8,128)(2,1)S(1)}, u32[]{:S(2)}, u32[]{:S(2)}) async-start(bf16[32,32,384]{2,1,0:T(8,128)(2,1)} %shard_map.196), calls=%async_computation.1 | async-start | bytes 1572864 | tf_op jit(solution)/shard_map/all_to_all | solution.py:467
  85.9 5.4 %collective-permute-start.5 = (bf16[2,76,128]{2,1,0:T(8,128)(2,1)S(1)}, bf16[2,76,128]{2,1,0:T(8,128)(2,1)S(1)}, u32[]{:S(2)}, u32[]{:S(2)}) collective-permute-start(bf16[2,76,128]{2,1,0:T(8,128)(2,1)S(1)} %get-tuple-element.61), channel_id=1, source_target_pairs={{0,26},{1,27},{2,28},{3,29},{4,30},{5,31},{6,0},{7,1},{8,2},{9,3},... | collective-permute-start | bytes 116744 | tf_op jit(solution)/shard_map/ppermute | solution.py:34
  91.3 6.6 %collective-permute-start.6 = (bf16[2,76,128]{2,1,0:T(8,128)(2,1)S(1)}, bf16[2,76,128]{2,1,0:T(8,128)(2,1)S(1)}, u32[]{:S(2)}, u32[]{:S(2)}) collective-permute-start(bf16[2,76,128]{2,1,0:T(8,128)(2,1)S(1)} %get-tuple-element.60), channel_id=1, source_target_pairs={{0,25},{1,26},{2,27},{3,28},{4,29},{5,30},{6,31},{7,0},{8,1},{9,2}... | collective-permute-start | bytes 116744 | tf_op jit(solution)/shard_map/ppermute | solution.py:34
  97.9 0.6 copy.68
  98.5 0.9 copy.47.refs_8_
  99.4 0.0 copy-done.10
  99.4 0.0 copy-done.14
  99.4 0.7 copy.48.refs_8_
  100.1 22.0 %collective-permute-done.5.refs_6_ = bf16[2,76,128]{2,1,0:T(8,128)(2,1)S(1)} collective-permute-done((bf16[2,76,128]{2,1,0:T(8,128)(2,1)S(1)}, bf16[2,76,128]{2,1,0:T(8,128)(2,1)S(1)}, u32[]{:S(2)}, u32[]{:S(2)}) %collective-permute-start.5) | collective-permute-done | bytes 38944 | tf_op jit(solution)/shard_map/ppermute | solution.py:34
  122.1 9.3 %collective-permute-done.6.refs_7_ = bf16[2,76,128]{2,1,0:T(8,128)(2,1)S(1)} collective-permute-done((bf16[2,76,128]{2,1,0:T(8,128)(2,1)S(1)}, bf16[2,76,128]{2,1,0:T(8,128)(2,1)S(1)}, u32[]{:S(2)}, u32[]{:S(2)}) %collective-permute-start.6) | collective-permute-done | bytes 38944 | tf_op jit(solution)/shard_map/ppermute | solution.py:34
  131.3 0.0 copy-done.15
  131.3 0.6 copy-done.16
  131.9 3.7 %shard_map.197 = (f32[200,2048]{1,0:T(8,128)}, f32[1,2048]{1,0:T(1,128)}) custom-call(s32[16]{0:T(128)} %select_reduce_fusion.2.depth_ref, bf16[2,76,128]{2,1,0:T(8,128)(2,1)} %bitcast.66, bf16[2,76,128]{2,1,0:T(8,128)(2,1)} %copy-done.10, bf16[2,76,128]{2,1,0:T(8,128)(2,1)} %copy-done.11, bf16[2,76,128]{2,1,0:T(8,128)(2,1)} %copy-done.12, ...), custom_call_target="tpu_custom_call" | custom-call | flops 589824000 | bytes 2245952 | tf_op jit(solution)/shard_map/pallas_call | solution.py:341
  135.6 0.0 all-to-all-done.1.refs_0_
  135.7 0.9 copy-done.2
  136.5 6.5 %shard_map.198 = (f32[4,360,384]{2,1,0:T(8,128)}, bf16[16,16,128]{2,1,0:T(8,128)(2,1)}) custom-call(bf16[32,32,384]{2,1,0:T(8,128)(2,1)} %copy-done.2, bf16[360,256]{1,0:T(8,128)(2,1)} %constant.103.clone.refs_1_, f32[4,360,384]{2,1,0:T(8,128)} %get-tuple-element.33.refs_2_, bf16[4,360,384]{2,1,0:T(8,128)(2,1)} %bitcast.55, ...), custom_call_target="tpu_custom_call" | custom-call | flops 707788800 | bytes 9219456 | tf_op jit(solution)/shard_map/pallas_call | solution.py:341
  143.0 6.9 %all-to-all-start.2 = ((bf16[16,16,128]{2,1,0:T(8,128)(2,1)}), bf16[16,16,128]{2,1,0:T(8,128)(2,1)S(1)}, u32[]{:S(2)}, u32[]{:S(2)}) async-start(bf16[16,16,128]{2,1,0:T(8,128)(2,1)} %get-tuple-element.51.tiles_ref), calls=%async_computation.2 | async-start | bytes 131072 | tf_op jit(solution)/shard_map/all_to_all | solution.py:500
  150.0 4.4 %shard_map.199 = bf16[4,360,384]{2,1,0:T(8,128)(2,1)} custom-call(f32[4,360,384]{2,1,0:T(8,128)} %get-tuple-element.50.updated_any, bf16[16,16,128]{2,1,0:T(8,128)(2,1)} %get-tuple-element.51.tiles_ref, bf16[4,360,128]{2,1,0:T(8,128)(2,1)} %fusion.1.cell_any.cell_ref, bf16[4,360,48]{2,1,0:T(8,128)(2,1)} %compare_convert_fusion.slot_any, f32[384]{0:T(512)} %imprint_ref.1), custom_call_target="tpu_custom_call" | custom-call | flops 283115520 | bytes 3891712 | tf_op jit(solution)/shard_map/pallas_call | solution.py:341
  154.4 2.1 %all-to-all-done.2.tiles_ref = bf16[16,16,128]{2,1,0:T(8,128)(2,1)S(1)} async-done(((bf16[16,16,128]{2,1,0:T(8,128)(2,1)}), bf16[16,16,128]{2,1,0:T(8,128)(2,1)S(1)}, u32[]{:S(2)}, u32[]{:S(2)}) %all-to-all-start.2) | async-done | bytes 65568 | tf_op jit(solution)/shard_map/all_to_all | solution.py:500
  156.5 0.9 shard_map.200
  (34 shorter events, 0.2 us)
Async XLA Ops:
  0.6 34.8 %copy-start.8 = (s32[14,1]{0,1:T(1,128)S(1)}, s32[14,1]{0,1:T(1,128)}, u32[]{:S(2)}) copy-start(s32[14,1]{0,1:T(1,128)} %param.32) | copy-start | bytes 172
  0.6 35.1 %copy-start.6 = (s32[4,360]{1,0:T(4,128)S(1)}, s32[4,360]{1,0:T(4,128)}, u32[]{:S(2)}) copy-start(s32[4,360]{1,0:T(4,128)} %param.31) | copy-start | bytes 17284
  0.7 35.1 %copy-start.17 = (s32[14]{0:T(128)S(1)}, s32[14]{0:T(128)}, u32[]{:S(2)}) copy-start(s32[14]{0:T(128)} %param.33) | copy-start | bytes 172
  0.7 35.7 %copy-start.4 = (s32[14,128]{1,0:T(8,128)S(1)}, s32[14,128]{1,0:T(8,128)}, u32[]{:S(2)}) copy-start(s32[14,128]{1,0:T(8,128)} %param.30) | copy-start | bytes 21508
  2.2 35.3 %copy-start.5 = (bf16[9,200]{1,0:T(8,128)(2,1)S(1)}, bf16[9,200]{1,0:T(8,128)(2,1)}, u32[]{:S(2)}) copy-start(bf16[9,200]{1,0:T(8,128)(2,1)} %param.29) | copy-start | bytes 10804
  2.2 46.8 %collective-permute-start = (bf16[2,76,128]{2,1,0:T(8,128)(2,1)S(1)}, bf16[2,76,128]{2,1,0:T(8,128)(2,1)S(1)}, u32[]{:S(2)}, u32[]{:S(2)}) collective-permute-start(bf16[2,76,128]{2,1,0:T(8,128)(2,1)S(1)} %bitcast.61), channel_id=1, source_target_pairs={{0,31},{1,0},{2,1},{3,2},{4,3},{5,4},{6,5},{7,6},{8,7},{9,8},{10,9... | collective-permute-start | bytes 116744 | tf_op jit(solution)/shard_map/ppermute | solution.py:34
  2.9 46.1 %collective-permute-start.1 = (bf16[2,76,128]{2,1,0:T(8,128)(2,1)S(1)}, bf16[2,76,128]{2,1,0:T(8,128)(2,1)S(1)}, u32[]{:S(2)}, u32[]{:S(2)}) collective-permute-start(bf16[2,76,128]{2,1,0:T(8,128)(2,1)S(1)} %bitcast.62), channel_id=1, source_target_pairs={{0,30},{1,31},{2,0},{3,1},{4,2},{5,3},{6,4},{7,5},{8,6},{9,7},{10,... | collective-permute-start | bytes 116744 | tf_op jit(solution)/shard_map/ppermute | solution.py:34
  10.1 39.0 %collective-permute-start.2 = (bf16[2,76,128]{2,1,0:T(8,128)(2,1)S(1)}, bf16[2,76,128]{2,1,0:T(8,128)(2,1)S(1)}, u32[]{:S(2)}, u32[]{:S(2)}) collective-permute-start(bf16[2,76,128]{2,1,0:T(8,128)(2,1)S(1)} %bitcast.63), channel_id=1, source_target_pairs={{0,29},{1,30},{2,31},{3,0},{4,1},{5,2},{6,3},{7,4},{8,5},{9,6},{10... | collective-permute-start | bytes 116744 | tf_op jit(solution)/shard_map/ppermute | solution.py:34
  16.4 32.6 %collective-permute-start.3 = (bf16[2,76,128]{2,1,0:T(8,128)(2,1)S(1)}, bf16[2,76,128]{2,1,0:T(8,128)(2,1)S(1)}, u32[]{:S(2)}, u32[]{:S(2)}) collective-permute-start(bf16[2,76,128]{2,1,0:T(8,128)(2,1)S(1)} %bitcast.64), channel_id=1, source_target_pairs={{0,28},{1,29},{2,30},{3,31},{4,0},{5,1},{6,2},{7,3},{8,4},{9,5},{1... | collective-permute-start | bytes 116744 | tf_op jit(solution)/shard_map/ppermute | solution.py:34
  19.5 29.5 %collective-permute-start.4 = (bf16[2,76,128]{2,1,0:T(8,128)(2,1)S(1)}, bf16[2,76,128]{2,1,0:T(8,128)(2,1)S(1)}, u32[]{:S(2)}, u32[]{:S(2)}) collective-permute-start(bf16[2,76,128]{2,1,0:T(8,128)(2,1)S(1)} %bitcast.65), channel_id=1, source_target_pairs={{0,27},{1,28},{2,29},{3,30},{4,31},{5,0},{6,1},{7,2},{8,3},{9,4},{... | collective-permute-start | bytes 116744 | tf_op jit(solution)/shard_map/ppermute | solution.py:34
  24.2 15.0 %copy-start.7 = (s32[4,360]{1,0:T(4,128)S(1)}, s32[4,360]{1,0:T(4,128)}, u32[]{:S(2)}) copy-start(s32[4,360]{1,0:T(4,128)} %param.20) | copy-start | bytes 17284
  24.3 15.1 %copy-start.3 = (bf16[9,200,84]{1,2,0:T(8,128)(2,1)S(1)}, bf16[9,200,84]{1,2,0:T(8,128)(2,1)}, u32[]{:S(2)}) copy-start(bf16[9,200,84]{1,2,0:T(8,128)(2,1)} %param.28) | copy-start | bytes 907204
  29.1 12.2 %copy-start.9 = (pred[80]{0:T(512)(128)(4,1)S(1)}, pred[80]{0:T(512)(128)(4,1)}, u32[]{:S(2)}) copy-start(pred[80]{0:T(512)(128)(4,1)} %constant.97.clone.1) | copy-start | bytes 244
  29.1 48.5 %all-to-all-start = ((bf16[32,32,384]{2,1,0:T(8,128)(2,1)}), bf16[32,32,384]{2,1,0:T(8,128)(2,1)S(1)}, u32[]{:S(2)}, u32[]{:S(2)}) async-start(bf16[32,32,384]{2,1,0:T(8,128)(2,1)} %shard_map.194), calls=%async_computation | async-start | bytes 1572864 | tf_op jit(solution)/shard_map/all_to_all | solution.py:392
  38.2 39.4 %copy-start.1 = (f32[128,384]{1,0:T(8,128)S(1)}, f32[128,384]{1,0:T(8,128)}, u32[]{:S(2)}) copy-start(f32[128,384]{1,0:T(8,128)} %gains_ref.1) | copy-start | bytes 589828
  49.0 50.4 %copy-start.10 = (bf16[2,76,128]{2,1,0:T(8,128)(2,1)}, bf16[2,76,128]{2,1,0:T(8,128)(2,1)S(1)}, u32[]{:S(2)}) copy-start(bf16[2,76,128]{2,1,0:T(8,128)(2,1)S(1)} %collective-permute-done.refs_1_) | copy-start | bytes 116740
  49.0 50.4 %copy-start.11 = (bf16[2,76,128]{2,1,0:T(8,128)(2,1)}, bf16[2,76,128]{2,1,0:T(8,128)(2,1)S(1)}, u32[]{:S(2)}) copy-start(bf16[2,76,128]{2,1,0:T(8,128)(2,1)S(1)} %collective-permute-done.1.refs_2_) | copy-start | bytes 116740
  49.0 50.3 %copy-start.12 = (bf16[2,76,128]{2,1,0:T(8,128)(2,1)}, bf16[2,76,128]{2,1,0:T(8,128)(2,1)S(1)}, u32[]{:S(2)}) copy-start(bf16[2,76,128]{2,1,0:T(8,128)(2,1)S(1)} %collective-permute-done.2.refs_3_) | copy-start | bytes 116740
  49.1 50.3 %copy-start.13 = (bf16[2,76,128]{2,1,0:T(8,128)(2,1)}, bf16[2,76,128]{2,1,0:T(8,128)(2,1)S(1)}, u32[]{:S(2)}) copy-start(bf16[2,76,128]{2,1,0:T(8,128)(2,1)S(1)} %collective-permute-done.3.refs_4_) | copy-start | bytes 116740
  49.1 50.3 %copy-start.14 = (bf16[2,76,128]{2,1,0:T(8,128)(2,1)}, bf16[2,76,128]{2,1,0:T(8,128)(2,1)S(1)}, u32[]{:S(2)}) copy-start(bf16[2,76,128]{2,1,0:T(8,128)(2,1)S(1)} %collective-permute-done.4.refs_5_) | copy-start | bytes 116740
  79.4 56.3 %all-to-all-start.1 = ((bf16[32,32,384]{2,1,0:T(8,128)(2,1)}), bf16[32,32,384]{2,1,0:T(8,128)(2,1)S(1)}, u32[]{:S(2)}, u32[]{:S(2)}) async-start(bf16[32,32,384]{2,1,0:T(8,128)(2,1)} %shard_map.196), calls=%async_computation.1 | async-start | bytes 1572864 | tf_op jit(solution)/shard_map/all_to_all | solution.py:467
  85.9 36.2 %collective-permute-start.5 = (bf16[2,76,128]{2,1,0:T(8,128)(2,1)S(1)}, bf16[2,76,128]{2,1,0:T(8,128)(2,1)S(1)}, u32[]{:S(2)}, u32[]{:S(2)}) collective-permute-start(bf16[2,76,128]{2,1,0:T(8,128)(2,1)S(1)} %get-tuple-element.61), channel_id=1, source_target_pairs={{0,26},{1,27},{2,28},{3,29},{4,30},{5,31},{6,0},{7,1},{8,2},{9,3},... | collective-permute-start | bytes 116744 | tf_op jit(solution)/shard_map/ppermute | solution.py:34
  91.3 40.1 %collective-permute-start.6 = (bf16[2,76,128]{2,1,0:T(8,128)(2,1)S(1)}, bf16[2,76,128]{2,1,0:T(8,128)(2,1)S(1)}, u32[]{:S(2)}, u32[]{:S(2)}) collective-permute-start(bf16[2,76,128]{2,1,0:T(8,128)(2,1)S(1)} %get-tuple-element.60), channel_id=1, source_target_pairs={{0,25},{1,26},{2,27},{3,28},{4,29},{5,30},{6,31},{7,0},{8,1},{9,2}... | collective-permute-start | bytes 116744 | tf_op jit(solution)/shard_map/ppermute | solution.py:34
  122.1 9.3 %copy-start.15 = (bf16[2,76,128]{2,1,0:T(8,128)(2,1)}, bf16[2,76,128]{2,1,0:T(8,128)(2,1)S(1)}, u32[]{:S(2)}) copy-start(bf16[2,76,128]{2,1,0:T(8,128)(2,1)S(1)} %collective-permute-done.5.refs_6_) | copy-start | bytes 116740
  131.3 0.6 copy-start.16
  135.6 0.9 copy-start.2
  143.0 13.5 %copy-start = (bf16[4,360,128]{2,1,0:T(8,128)(2,1)S(1)}, bf16[4,360,128]{2,1,0:T(8,128)(2,1)}, u32[]{:S(2)}) copy-start(bf16[4,360,128]{2,1,0:T(8,128)(2,1)} %fusion.1.cell_any.cell_ref) | copy-start | bytes 1105924
  143.0 13.5 %all-to-all-start.2 = ((bf16[16,16,128]{2,1,0:T(8,128)(2,1)}), bf16[16,16,128]{2,1,0:T(8,128)(2,1)S(1)}, u32[]{:S(2)}, u32[]{:S(2)}) async-start(bf16[16,16,128]{2,1,0:T(8,128)(2,1)} %get-tuple-element.51.tiles_ref), calls=%async_computation.2 | async-start | bytes 131072 | tf_op jit(solution)/shard_map/all_to_all | solution.py:500

commit v5 on v4

--- a/solution.py
+++ b/solution.py
@@ -22,7 +22,7 @@
 OCH = 76
 OCH_PAD = 80
 TAPS = [(row, col) for row in (-1, 0, 1) for col in (-1, 0, 1)]
-LATE = 6
+EARLY = 3
 BF16 = jnp.bfloat16
 F32 = jnp.float32
 WHOLE = pl.BlockSpec(memory_space=pltpu.VMEM)
@@ -125,8 +125,11 @@
     return (centered * lax.rsqrt(spread + 1e-05) * scale).astype(BF16)
 
 
-def analysis_kernel(air_any, scale_ref, table_any, spectra_ref, air_ref, table_ref, sems):
+def analysis_kernel(
+    air_any, scale_ref, table_any, spectra_any, air_ref, table_ref, spectra_ref, sems, out_sems
+):
     rows = air_ref.shape[0]
+    leaving = []
     groups = spectra_ref.shape[0]
     copies = begin(
         [(air_any.at[j], air_ref.at[j]) for j in range(rows)] + [(table_any, table_ref)], sems
@@ -142,7 +145,15 @@
             out = jnp.dot(table_ref[...], normed, preferred_element_type=F32)
             both.append(out.reshape(groups, 8, out.shape[1]))
         block = jnp.concatenate(both, axis=1)
-        spectra_ref[:, 16 * pair : 16 * (pair + 1), :] = block.astype(BF16)
+        rows_16 = slice(16 * pair, 16 * (pair + 1))
+        spectra_ref[:, rows_16, :] = block.astype(BF16)
+        leave = pltpu.make_async_copy(
+            spectra_ref.at[:, rows_16], spectra_any.at[:, rows_16], out_sems.at[pair]
+        )
+        leave.start()
+        leaving.append(leave)
+    for one in leaving:
+        one.wait()
 
 
 def local_kernel(
@@ -221,11 +232,16 @@
         refs[2 * count + 2 :],
     )
     leaving = []
-    copies = begin(list(zip(sources, held)), sems)
     (
-        rows_ref, synthesis_ref, skip_ref, air_ref, wide_ref, air_flux_ref, place_ref, group_ref,
+        rows_ref, synthesis_ref, wide_ref, air_flux_ref, skip_ref, air_ref, place_ref, group_ref,
         forcing_weight_ref, wet_ref, decode_ref, top_ref,
     ) = held
+    moves = list(zip(sources, held))
+    ordered = moves[:4]
+    for j in range(air_ref.shape[0]):
+        ordered += [(source.at[j], target.at[j]) for source, target in moves[4:6]]
+    copies = begin(ordered + moves[6:], sems)
+    after = len(ordered)
     latitude_rows, longitudes, channels = air_ref.shape
     groups = rows_ref.shape[0]
     pairs = []
@@ -237,9 +253,8 @@
     for j in range(latitude_rows):
         own = pairs[j].reshape(8 * groups, channels).astype(BF16)
         spectral = jnp.dot(synthesis_ref[...], own, preferred_element_type=F32)
-        if j == 0:
-            for one in copies[2:5]:
-                one.wait()
+        for one in copies[2:6] if j == 0 else copies[4 + 2 * j : 6 + 2 * j]:
+            one.wait()
         mixed = gelu(spectral + skip_ref[j]).astype(BF16)
         wide = jnp.dot(mixed, wide_ref[...], preferred_element_type=F32)
         updated_ref[j] = air_ref[j].astype(F32) + wide[:, :channels]
@@ -250,8 +265,6 @@
             [wide[:, channels:], jnp.zeros((384 - longitudes, 128), F32)], axis=0
         )
         turned = jnp.transpose(narrow)
-        if j == 0:
-            copies[5].wait()
         extra = jnp.concatenate(
             [air_flux_ref[FC * j : FC * (j + 1), :], jnp.zeros((FC, 384 - longitudes), F32)], axis=1
         )
@@ -259,7 +272,7 @@
         for part in range(3):
             at = FC * (part * latitude_rows + j)
             flux[at : at + FC, :] = total[:, 128 * part : 128 * (part + 1)]
-    for one in copies[6:]:
+    for one in copies[after:]:
         one.wait()
     spread = jnp.dot(flux[...].astype(BF16), place_ref[...], preferred_element_type=F32)
     group = group_ref[...]
@@ -386,15 +399,21 @@
         [shape((bands, chunk, channels), BF16)],
         [air, layernorm_scaling, analysis],
         2 * 2 * MMAX * latitude_rows * longitudes * channels,
-        held([air, analysis]) + [pltpu.SemaphoreType.DMA((latitude_rows + 1,))],
+        held([air, analysis])
+        + [
+            pltpu.VMEM((bands, chunk, channels), BF16),
+            pltpu.SemaphoreType.DMA((latitude_rows + 1,)),
+            pltpu.SemaphoreType.DMA((latitude_rows // 2,)),
+        ],
         specs=[FAR, WHOLE, FAR],
-    )
+        out_specs=FAR,
+    )
+    spectra, slots = lax.optimization_barrier((spectra, sea_ensemble_arrays[0]))
     gathered = lax.all_to_all(spectra, "space", split_axis=0, concat_axis=0, tiled=True)
 
-    slots = sea_ensemble_arrays[0]
-    near = [
+    far = [
         passed_along(slots[offset * CAP : (offset + 1) * CAP], "space", -offset)
-        for offset in range(1, LATE)
+        for offset in range(EARLY, NEAR)
     ]
     forward, backward = (jnp.asarray(t) for t in legendre_tables(latitudes))
     first = lax.axis_index("space") * per_device
@@ -447,12 +466,12 @@
         holder[:, None, :] == jnp.arange(SLOTS, dtype=jnp.int32)[None, :, None]
     ).astype(F32)
     prepared = (
-        near, skip, air_flux, wide, place, group, forcing_weight, state_weight, decode_weight,
+        far, skip, air_flux, wide, place, group, forcing_weight, state_weight, decode_weight,
         depths, cell, slot_of,
     )
     gathered, prepared = lax.optimization_barrier((gathered, prepared))
     (
-        near, skip, air_flux, wide, place, group, forcing_weight, state_weight, decode_weight,
+        far, skip, air_flux, wide, place, group, forcing_weight, state_weight, decode_weight,
         depths, cell, slot_of,
     ) = prepared
     filtered = call(
@@ -463,22 +482,22 @@
         [pltpu.VMEM((channels // 128, bands * chunk, 128), F32)],
         limit=32,
     )
-    filtered, late = lax.optimization_barrier((filtered, slots[LATE * CAP :]))
+    filtered, late = lax.optimization_barrier((filtered, slots[CAP : EARLY * CAP]))
     returned = lax.all_to_all(filtered, "space", split_axis=0, concat_axis=0, tiled=True)
-    rest = [
-        passed_along(late[at : at + CAP], "space", -(LATE + at // CAP))
+    near = [
+        passed_along(late[at : at + CAP], "space", -(1 + at // CAP))
         for at in range(0, late.shape[0], CAP)
     ]
     wet, top = call(
         ocean_kernel,
         [shape((hidden_channels, SPAN), F32), shape((1, SPAN), F32)],
-        [depths, slots[:CAP], *near, *rest, state_weight],
+        [depths, slots[:CAP], *near, *far, state_weight],
         2 * hidden_channels * len(TAPS) * OCH_PAD * SPAN,
         [pltpu.VMEM((len(TAPS) * OCH_PAD, SPAN), BF16)],
         specs=[pl.BlockSpec(memory_space=pltpu.SMEM)] + [WHOLE] * (NEAR + 1),
     )
     operands = [
-        returned, synthesis, skip, air, wide, air_flux, place, group, forcing_weight, wet,
+        returned, synthesis, wide, air_flux, skip, air, place, group, forcing_weight, wet,
         decode_weight, top,
     ]
     updated, tiles = call(
@@ -491,7 +510,7 @@
             pltpu.VMEM(air.shape, F32),
             pltpu.VMEM((3 * FC * latitude_rows, 128), F32),
             pltpu.VMEM((SLOTS, CELLS), F32),
-            pltpu.SemaphoreType.DMA((len(operands),)),
+            pltpu.SemaphoreType.DMA((len(operands) + 2 * latitude_rows,)),
             pltpu.SemaphoreType.DMA((latitude_rows,)),
         ],
         specs=[FAR] * len(operands),

time: 158 us -> 161 us (1.019)
  the two profiles are of different devices: /device:TPU:33 before, /device:TPU:1 now
where the time goes in v5:
time: 161 us; the launch traced here: 160 us
  waiting for transfers between devices  67.7 us (42%)
  starting transfers between devices  52.3 us (32%)
  Pallas kernels  27.6 us (17%)
  local copies, waits for them, and re-layouts  6.65 us (4%)
  other arithmetic  4.74 us (3%)
    all_to_all x1, waiting for transfers between devices, shards(): lax.all_to_all(spectra, 'space', split_axis=0, concat_axis=0, tiled=True)  31.9 us
    ppermute x7, starting transfers between devices, passed_along(): lax.ppermute(value, axis, [(i, (i + by) % devices) for i in range(devices)])  30.7 us
    ppermute x7, waiting for transfers between devices, passed_along(): lax.ppermute(value, axis, [(i, (i + by) % devices) for i in range(devices)])  28.9 us
    pallas_call x7, Pallas kernels, call(): pl.pallas_call(kernel, out_shape=outs if len(outs) > 1 else outs[0], in_s...  27.6 us
    all_to_all x1, starting transfers between devices, shards(): lax.all_to_all(spectra, 'space', split_axis=0, concat_axis=0, tiled=True)  10.7 us
    all_to_all x1, starting transfers between devices, shards(): lax.all_to_all(tiles, 'member', split_axis=0, concat_axis=0, tiled=True)  6.9 us
    all_to_all x1, waiting for transfers between devices, shards(): lax.all_to_all(filtered, 'space', split_axis=0, concat_axis=0, tiled=True)  4.71 us
    all_to_all x1, starting transfers between devices, shards(): lax.all_to_all(filtered, 'space', split_axis=0, concat_axis=0, tiled=True)  4.07 us
  transfers between devices with their start and end apart: 10, of which 4 were waited for; matrix products, arithmetic and copies ran while one was open for 5% of the time, Pallas kernels for 9%

profile of v5, /device:TPU:1, one launch (start us, length us, event | category | flops | bytes accessed | tf_op | source)
XLA Modules:
  0.0 160.0 jit_solution(7457313484855248266)
XLA Ops:
  0.6 1.1 copy.36
  1.7 0.0 copy-start.8
  1.7 0.0 copy-start.6
  1.7 0.0 copy-start.17
  1.7 0.0 copy-start.4
  1.7 0.0 copy-start.5
  1.7 0.0 copy-start.7
  1.8 0.0 copy-start.3
  1.8 4.7 %shard_map.194 = bf16[32,32,384]{2,1,0:T(8,128)(2,1)} custom-call(bf16[4,360,384]{2,1,0:T(8,128)(2,1)} %bitcast.35, f32[384]{0:T(512)} %scale_ref.3, bf16[256,360]{1,0:T(8,128)(2,1)} %constant.102.clone.table_any), custom_call_target="tpu_custom_call" | custom-call | flops 283115520 | bytes 2078208 | tf_op jit(solution)/shard_map/pallas_call | solution.py:354
  6.5 0.0 copy-start.9
  6.5 0.6 fusion.8
  7.1 12.5 %collective-permute-start = (bf16[2,76,128]{2,1,0:T(8,128)(2,1)S(1)}, bf16[2,76,128]{2,1,0:T(8,128)(2,1)S(1)}, u32[]{:S(2)}, u32[]{:S(2)}) collective-permute-start(bf16[2,76,128]{2,1,0:T(8,128)(2,1)S(1)} %get-tuple-element.63), channel_id=1, source_target_pairs={{0,29},{1,30},{2,31},{3,0},{4,1},{5,2},{6,3},{7,4},{8,5},{9,6},{10... | collective-permute-start | bytes 116744 | tf_op jit(solution)/shard_map/ppermute | solution.py:34
  19.6 3.1 %collective-permute-start.1 = (bf16[2,76,128]{2,1,0:T(8,128)(2,1)S(1)}, bf16[2,76,128]{2,1,0:T(8,128)(2,1)S(1)}, u32[]{:S(2)}, u32[]{:S(2)}) collective-permute-start(bf16[2,76,128]{2,1,0:T(8,128)(2,1)S(1)} %get-tuple-element.62), channel_id=1, source_target_pairs={{0,28},{1,29},{2,30},{3,31},{4,0},{5,1},{6,2},{7,3},{8,4},{9,5},{1... | collective-permute-start | bytes 116744 | tf_op jit(solution)/shard_map/ppermute | solution.py:34
  22.7 4.7 %collective-permute-start.2 = (bf16[2,76,128]{2,1,0:T(8,128)(2,1)S(1)}, bf16[2,76,128]{2,1,0:T(8,128)(2,1)S(1)}, u32[]{:S(2)}, u32[]{:S(2)}) collective-permute-start(bf16[2,76,128]{2,1,0:T(8,128)(2,1)S(1)} %get-tuple-element.61), channel_id=1, source_target_pairs={{0,27},{1,28},{2,29},{3,30},{4,31},{5,0},{6,1},{7,2},{8,3},{9,4},{... | collective-permute-start | bytes 116744 | tf_op jit(solution)/shard_map/ppermute | solution.py:34
  27.4 2.7 %collective-permute-start.3 = (bf16[2,76,128]{2,1,0:T(8,128)(2,1)S(1)}, bf16[2,76,128]{2,1,0:T(8,128)(2,1)S(1)}, u32[]{:S(2)}, u32[]{:S(2)}) collective-permute-start(bf16[2,76,128]{2,1,0:T(8,128)(2,1)S(1)} %get-tuple-element.60), channel_id=1, source_target_pairs={{0,26},{1,27},{2,28},{3,29},{4,30},{5,31},{6,0},{7,1},{8,2},{9,3},... | collective-permute-start | bytes 116744 | tf_op jit(solution)/shard_map/ppermute | solution.py:34
  30.1 2.6 %collective-permute-start.4 = (bf16[2,76,128]{2,1,0:T(8,128)(2,1)S(1)}, bf16[2,76,128]{2,1,0:T(8,128)(2,1)S(1)}, u32[]{:S(2)}, u32[]{:S(2)}) collective-permute-start(bf16[2,76,128]{2,1,0:T(8,128)(2,1)S(1)} %get-tuple-element.59), channel_id=1, source_target_pairs={{0,25},{1,26},{2,27},{3,28},{4,29},{5,30},{6,31},{7,0},{8,1},{9,2}... | collective-permute-start | bytes 116744 | tf_op jit(solution)/shard_map/ppermute | solution.py:34
  32.7 10.7 %all-to-all-start = ((bf16[32,32,384]{2,1,0:T(8,128)(2,1)}), bf16[32,32,384]{2,1,0:T(8,128)(2,1)S(1)}, u32[]{:S(2)}, u32[]{:S(2)}) async-start(bf16[32,32,384]{2,1,0:T(8,128)(2,1)} %shard_map.194), calls=%async_computation | async-start | bytes 1572864 | tf_op jit(solution)/shard_map/all_to_all | solution.py:412
  43.4 0.0 copy-done.8
  43.4 0.2 select_reduce_fusion.3
  43.6 0.1 copy.28
  43.7 0.0 copy-done.6
  43.8 0.0 copy-done.17
  43.8 0.6 select_reduce_fusion.2.depth_ref
  44.4 0.1 select_reduce_fusion
  44.5 0.0 copy-done.5
  44.6 0.6 pad.9.refs_10_
  45.2 0.1 select_reduce_fusion.1
  45.3 0.0 copy-start.1
  45.3 1.0 constant_dynamic-slice_fusion
  46.4 0.0 copy-done.7
  46.4 0.0 copy-done.3
  46.4 1.0 fusion.1.cell_any.cell_ref
  47.4 1.0 compare_convert_fusion.slot_any
  48.4 0.1 slice_select_fusion
  48.5 0.7 multiply_add_fusion.refs_7_
  49.2 0.9 fusion.refs_6_
  50.1 6.0 %shard_map.195 = (f32[4,360,384]{2,1,0:T(8,128)}, f32[32,360]{1,0:T(8,128)}, bf16[384,512]{1,0:T(8,128)(2,1)}) custom-call(bf16[4,360,384]{2,1,0:T(8,128)(2,1)} %bitcast.36, f32[384]{0:T(512)} %scale_ref.3, bf16[384,384]{1,0:T(8,128)(2,1)} %bypass_ref.1, bf16[384,384]{1,0:T(8,128)(2,1)} %exit_ref.1, bf16[8,384]{1,0:T(8,128)(2,1)} %bitcast.46), custom_call_target="tpu_custom_call" | custom-call | flops 424673280 | bytes 4354560 | tf_op jit(solution)/shard_map/pallas_call | solution.py:354
  56.1 0.0 collective-permute-done.refs_3_
  56.1 0.0 collective-permute-done.1.refs_4_
  56.1 0.0 copy-start.11
  56.1 0.0 collective-permute-done.2.refs_5_
  56.1 0.0 collective-permute-done.3.refs_6_
  56.1 0.0 collective-permute-done.4.refs_7_
  56.1 0.0 copy-start.14
  56.2 31.9 %all-to-all-done.x_ref = bf16[32,32,384]{2,1,0:T(8,128)(2,1)S(1)} async-done(((bf16[32,32,384]{2,1,0:T(8,128)(2,1)}), bf16[32,32,384]{2,1,0:T(8,128)(2,1)S(1)}, u32[]{:S(2)}, u32[]{:S(2)}) %all-to-all-start) | async-done | bytes 786464 | tf_op jit(solution)/shard_map/all_to_all | solution.py:412
  88.1 0.0 copy-done.1
  88.1 1.7 %shard_map.196 = bf16[32,32,384]{2,1,0:T(8,128)(2,1)} custom-call(bf16[32,32,384]{2,1,0:T(8,128)(2,1)S(1)} %all-to-all-done.x_ref, bf16[4,128,128]{2,1,0:T(8,128)(2,1)S(1)} %get-tuple-element.70.forward_ref, bf16[4,128,128]{2,1,0:T(8,128)(2,1)S(1)} %get-tuple-element.71.backward_ref, f32[128,384]{1,0:T(8,128)S(1)} %copy-done.1), custom_call_target="tpu_custom_call" | custom-call | flops 201326592 | bytes 2031616 | tf_op jit(solution)/shard_map/pallas_call | solution.py:354
  89.8 4.1 %all-to-all-start.1 = ((bf16[32,32,384]{2,1,0:T(8,128)(2,1)}), bf16[32,32,384]{2,1,0:T(8,128)(2,1)S(1)}, u32[]{:S(2)}, u32[]{:S(2)}) async-start(bf16[32,32,384]{2,1,0:T(8,128)(2,1)} %shard_map.196), calls=%async_computation.1 | async-start | bytes 1572864 | tf_op jit(solution)/shard_map/all_to_all | solution.py:486
  93.9 0.4 collective-permute-start.5
  94.3 4.7 %collective-permute-start.6 = (bf16[2,76,128]{2,1,0:T(8,128)(2,1)S(1)}, bf16[2,76,128]{2,1,0:T(8,128)(2,1)S(1)}, u32[]{:S(2)}, u32[]{:S(2)}) collective-permute-start(bf16[2,76,128]{2,1,0:T(8,128)(2,1)S(1)} %get-tuple-element.64), channel_id=1, source_target_pairs={{0,30},{1,31},{2,0},{3,1},{4,2},{5,3},{6,4},{7,5},{8,6},{9,7},{10,... | collective-permute-start | bytes 116744 | tf_op jit(solution)/shard_map/ppermute | solution.py:34
  99.0 0.9 copy.29.refs_8_
  99.9 0.7 copy.30.refs_8_
  100.6 28.9 %collective-permute-done.5.refs_1_ = bf16[2,76,128]{2,1,0:T(8,128)(2,1)S(1)} collective-permute-done((bf16[2,76,128]{2,1,0:T(8,128)(2,1)S(1)}, bf16[2,76,128]{2,1,0:T(8,128)(2,1)S(1)}, u32[]{:S(2)}, u32[]{:S(2)}) %collective-permute-start.5) | collective-permute-done | bytes 38944 | tf_op jit(solution)/shard_map/ppermute | solution.py:34
  129.5 0.0 collective-permute-done.6.refs_2_
  129.5 0.6 copy-done.15
  130.1 0.0 copy-done.16
  130.1 3.7 %shard_map.197 = (f32[200,2048]{1,0:T(8,128)}, f32[1,2048]{1,0:T(1,128)}) custom-call(s32[16]{0:T(128)} %select_reduce_fusion.2.depth_ref, bf16[2,76,128]{2,1,0:T(8,128)(2,1)} %get-tuple-element.58.refs_0_, bf16[2,76,128]{2,1,0:T(8,128)(2,1)} %copy-done.15, bf16[2,76,128]{2,1,0:T(8,128)(2,1)} %copy-done.16, bf16[2,76,128]{2,1,0:T(8,128)(2,1)} %copy-done.10, ...), custom_call_target="tpu_custom_call" | custom-call | flops 589824000 | bytes 2245952 | tf_op jit(solution)/shard_map/pallas_call | solution.py:354
  133.8 4.7 %all-to-all-done.1.refs_0_ = bf16[32,32,384]{2,1,0:T(8,128)(2,1)S(1)} async-done(((bf16[32,32,384]{2,1,0:T(8,128)(2,1)}), bf16[32,32,384]{2,1,0:T(8,128)(2,1)S(1)}, u32[]{:S(2)}, u32[]{:S(2)}) %all-to-all-start.1) | async-done | bytes 786464 | tf_op jit(solution)/shard_map/all_to_all | solution.py:486
  138.5 0.9 copy-done.2
  139.4 6.2 %shard_map.198 = (f32[4,360,384]{2,1,0:T(8,128)}, bf16[16,16,128]{2,1,0:T(8,128)(2,1)}) custom-call(bf16[32,32,384]{2,1,0:T(8,128)(2,1)} %copy-done.2, bf16[360,256]{1,0:T(8,128)(2,1)} %constant.103.clone.refs_1_, bf16[384,512]{1,0:T(8,128)(2,1)} %get-tuple-element.37.refs_2_, f32[32,360]{1,0:T(8,128)} %get-tuple-element.38.refs_3_, ...), custom_call_target="tpu_custom_call" | custom-call | flops 707788800 | bytes 9219456 | tf_op jit(solution)/shard_map/pallas_call | solution.py:354
  145.7 6.9 %all-to-all-start.2 = ((bf16[16,16,128]{2,1,0:T(8,128)(2,1)}), bf16[16,16,128]{2,1,0:T(8,128)(2,1)S(1)}, u32[]{:S(2)}, u32[]{:S(2)}) async-start(bf16[16,16,128]{2,1,0:T(8,128)(2,1)} %get-tuple-element.55.tiles_ref), calls=%async_computation.2 | async-start | bytes 131072 | tf_op jit(solution)/shard_map/all_to_all | solution.py:519
  152.6 4.4 %shard_map.199 = bf16[4,360,384]{2,1,0:T(8,128)(2,1)} custom-call(f32[4,360,384]{2,1,0:T(8,128)} %get-tuple-element.54.updated_any, bf16[16,16,128]{2,1,0:T(8,128)(2,1)} %get-tuple-element.55.tiles_ref, bf16[4,360,128]{2,1,0:T(8,128)(2,1)} %fusion.1.cell_any.cell_ref, bf16[4,360,48]{2,1,0:T(8,128)(2,1)} %compare_convert_fusion.slot_any, f32[384]{0:T(512)} %imprint_ref.1), custom_call_target="tpu_custom_call" | custom-call | flops 283115520 | bytes 3891712 | tf_op jit(solution)/shard_map/pallas_call | solution.py:354
  157.0 2.1 %all-to-all-done.2.tiles_ref = bf16[16,16,128]{2,1,0:T(8,128)(2,1)S(1)} async-done(((bf16[16,16,128]{2,1,0:T(8,128)(2,1)}), bf16[16,16,128]{2,1,0:T(8,128)(2,1)S(1)}, u32[]{:S(2)}, u32[]{:S(2)}) %all-to-all-start.2) | async-done | bytes 65568 | tf_op jit(solution)/shard_map/all_to_all | solution.py:519
  159.1 0.9 shard_map.200
  (28 shorter events, 0.2 us)
Async XLA Ops:
  1.7 41.8 %copy-start.8 = (s32[14,1]{0,1:T(1,128)S(1)}, s32[14,1]{0,1:T(1,128)}, u32[]{:S(2)}) copy-start(s32[14,1]{0,1:T(1,128)} %param.32) | copy-start | bytes 172
  1.7 42.0 %copy-start.6 = (s32[4,360]{1,0:T(4,128)S(1)}, s32[4,360]{1,0:T(4,128)}, u32[]{:S(2)}) copy-start(s32[4,360]{1,0:T(4,128)} %param.31) | copy-start | bytes 17284
  1.7 42.1 %copy-start.17 = (s32[14]{0:T(128)S(1)}, s32[14]{0:T(128)}, u32[]{:S(2)}) copy-start(s32[14]{0:T(128)} %param.33) | copy-start | bytes 172
  1.7 42.7 %copy-start.4 = (s32[14,128]{1,0:T(8,128)S(1)}, s32[14,128]{1,0:T(8,128)}, u32[]{:S(2)}) copy-start(s32[14,128]{1,0:T(8,128)} %param.30) | copy-start | bytes 21508
  1.7 42.8 %copy-start.5 = (bf16[9,200]{1,0:T(8,128)(2,1)S(1)}, bf16[9,200]{1,0:T(8,128)(2,1)}, u32[]{:S(2)}) copy-start(bf16[9,200]{1,0:T(8,128)(2,1)} %param.29) | copy-start | bytes 10804
  1.7 44.6 %copy-start.7 = (s32[4,360]{1,0:T(4,128)S(1)}, s32[4,360]{1,0:T(4,128)}, u32[]{:S(2)}) copy-start(s32[4,360]{1,0:T(4,128)} %param.20) | copy-start | bytes 17284
  1.8 44.6 %copy-start.3 = (bf16[9,200,84]{1,2,0:T(8,128)(2,1)S(1)}, bf16[9,200,84]{1,2,0:T(8,128)(2,1)}, u32[]{:S(2)}) copy-start(bf16[9,200,84]{1,2,0:T(8,128)(2,1)} %param.28) | copy-start | bytes 907204
  6.5 41.9 %copy-start.9 = (pred[80]{0:T(512)(128)(4,1)S(1)}, pred[80]{0:T(512)(128)(4,1)}, u32[]{:S(2)}) copy-start(pred[80]{0:T(512)(128)(4,1)} %constant.97.clone.1) | copy-start | bytes 244
  7.1 49.0 %collective-permute-start = (bf16[2,76,128]{2,1,0:T(8,128)(2,1)S(1)}, bf16[2,76,128]{2,1,0:T(8,128)(2,1)S(1)}, u32[]{:S(2)}, u32[]{:S(2)}) collective-permute-start(bf16[2,76,128]{2,1,0:T(8,128)(2,1)S(1)} %get-tuple-element.63), channel_id=1, source_target_pairs={{0,29},{1,30},{2,31},{3,0},{4,1},{5,2},{6,3},{7,4},{8,5},{9,6},{10... | collective-permute-start | bytes 116744 | tf_op jit(solution)/shard_map/ppermute | solution.py:34
  19.6 36.5 %collective-permute-start.1 = (bf16[2,76,128]{2,1,0:T(8,128)(2,1)S(1)}, bf16[2,76,128]{2,1,0:T(8,128)(2,1)S(1)}, u32[]{:S(2)}, u32[]{:S(2)}) collective-permute-start(bf16[2,76,128]{2,1,0:T(8,128)(2,1)S(1)} %get-tuple-element.62), channel_id=1, source_target_pairs={{0,28},{1,29},{2,30},{3,31},{4,0},{5,1},{6,2},{7,3},{8,4},{9,5},{1... | collective-permute-start | bytes 116744 | tf_op jit(solution)/shard_map/ppermute | solution.py:34
  22.7 33.4 %collective-permute-start.2 = (bf16[2,76,128]{2,1,0:T(8,128)(2,1)S(1)}, bf16[2,76,128]{2,1,0:T(8,128)(2,1)S(1)}, u32[]{:S(2)}, u32[]{:S(2)}) collective-permute-start(bf16[2,76,128]{2,1,0:T(8,128)(2,1)S(1)} %get-tuple-element.61), channel_id=1, source_target_pairs={{0,27},{1,28},{2,29},{3,30},{4,31},{5,0},{6,1},{7,2},{8,3},{9,4},{... | collective-permute-start | bytes 116744 | tf_op jit(solution)/shard_map/ppermute | solution.py:34
  27.4 28.7 %collective-permute-start.3 = (bf16[2,76,128]{2,1,0:T(8,128)(2,1)S(1)}, bf16[2,76,128]{2,1,0:T(8,128)(2,1)S(1)}, u32[]{:S(2)}, u32[]{:S(2)}) collective-permute-start(bf16[2,76,128]{2,1,0:T(8,128)(2,1)S(1)} %get-tuple-element.60), channel_id=1, source_target_pairs={{0,26},{1,27},{2,28},{3,29},{4,30},{5,31},{6,0},{7,1},{8,2},{9,3},... | collective-permute-start | bytes 116744 | tf_op jit(solution)/shard_map/ppermute | solution.py:34
  30.1 26.0 %collective-permute-start.4 = (bf16[2,76,128]{2,1,0:T(8,128)(2,1)S(1)}, bf16[2,76,128]{2,1,0:T(8,128)(2,1)S(1)}, u32[]{:S(2)}, u32[]{:S(2)}) collective-permute-start(bf16[2,76,128]{2,1,0:T(8,128)(2,1)S(1)} %get-tuple-element.59), channel_id=1, source_target_pairs={{0,25},{1,26},{2,27},{3,28},{4,29},{5,30},{6,31},{7,0},{8,1},{9,2}... | collective-permute-start | bytes 116744 | tf_op jit(solution)/shard_map/ppermute | solution.py:34
  32.7 55.3 %all-to-all-start = ((bf16[32,32,384]{2,1,0:T(8,128)(2,1)}), bf16[32,32,384]{2,1,0:T(8,128)(2,1)S(1)}, u32[]{:S(2)}, u32[]{:S(2)}) async-start(bf16[32,32,384]{2,1,0:T(8,128)(2,1)} %shard_map.194), calls=%async_computation | async-start | bytes 1572864 | tf_op jit(solution)/shard_map/all_to_all | solution.py:412
  45.3 42.8 %copy-start.1 = (f32[128,384]{1,0:T(8,128)S(1)}, f32[128,384]{1,0:T(8,128)}, u32[]{:S(2)}) copy-start(f32[128,384]{1,0:T(8,128)} %gains_ref.1) | copy-start | bytes 589828
  56.1 43.8 %copy-start.10 = (bf16[2,76,128]{2,1,0:T(8,128)(2,1)}, bf16[2,76,128]{2,1,0:T(8,128)(2,1)S(1)}, u32[]{:S(2)}) copy-start(bf16[2,76,128]{2,1,0:T(8,128)(2,1)S(1)} %collective-permute-done.refs_3_) | copy-start | bytes 116740
  56.1 43.8 %copy-start.11 = (bf16[2,76,128]{2,1,0:T(8,128)(2,1)}, bf16[2,76,128]{2,1,0:T(8,128)(2,1)S(1)}, u32[]{:S(2)}) copy-start(bf16[2,76,128]{2,1,0:T(8,128)(2,1)S(1)} %collective-permute-done.1.refs_4_) | copy-start | bytes 116740
  56.1 43.8 %copy-start.12 = (bf16[2,76,128]{2,1,0:T(8,128)(2,1)}, bf16[2,76,128]{2,1,0:T(8,128)(2,1)S(1)}, u32[]{:S(2)}) copy-start(bf16[2,76,128]{2,1,0:T(8,128)(2,1)S(1)} %collective-permute-done.2.refs_5_) | copy-start | bytes 116740
  56.1 43.8 %copy-start.13 = (bf16[2,76,128]{2,1,0:T(8,128)(2,1)}, bf16[2,76,128]{2,1,0:T(8,128)(2,1)S(1)}, u32[]{:S(2)}) copy-start(bf16[2,76,128]{2,1,0:T(8,128)(2,1)S(1)} %collective-permute-done.3.refs_6_) | copy-start | bytes 116740
  56.1 43.8 %copy-start.14 = (bf16[2,76,128]{2,1,0:T(8,128)(2,1)}, bf16[2,76,128]{2,1,0:T(8,128)(2,1)S(1)}, u32[]{:S(2)}) copy-start(bf16[2,76,128]{2,1,0:T(8,128)(2,1)S(1)} %collective-permute-done.4.refs_7_) | copy-start | bytes 116740
  89.8 48.7 %all-to-all-start.1 = ((bf16[32,32,384]{2,1,0:T(8,128)(2,1)}), bf16[32,32,384]{2,1,0:T(8,128)(2,1)S(1)}, u32[]{:S(2)}, u32[]{:S(2)}) async-start(bf16[32,32,384]{2,1,0:T(8,128)(2,1)} %shard_map.196), calls=%async_computation.1 | async-start | bytes 1572864 | tf_op jit(solution)/shard_map/all_to_all | solution.py:486
  93.9 35.6 %collective-permute-start.5 = (bf16[2,76,128]{2,1,0:T(8,128)(2,1)S(1)}, bf16[2,76,128]{2,1,0:T(8,128)(2,1)S(1)}, u32[]{:S(2)}, u32[]{:S(2)}) collective-permute-start(bf16[2,76,128]{2,1,0:T(8,128)(2,1)S(1)} %get-tuple-element.65), channel_id=1, source_target_pairs={{0,31},{1,0},{2,1},{3,2},{4,3},{5,4},{6,5},{7,6},{8,7},{9,8},{10,9... | collective-permute-start | bytes 116744 | tf_op jit(solution)/shard_map/ppermute | solution.py:34
  94.3 35.2 %collective-permute-start.6 = (bf16[2,76,128]{2,1,0:T(8,128)(2,1)S(1)}, bf16[2,76,128]{2,1,0:T(8,128)(2,1)S(1)}, u32[]{:S(2)}, u32[]{:S(2)}) collective-permute-start(bf16[2,76,128]{2,1,0:T(8,128)(2,1)S(1)} %get-tuple-element.64), channel_id=1, source_target_pairs={{0,30},{1,31},{2,0},{3,1},{4,2},{5,3},{6,4},{7,5},{8,6},{9,7},{10,... | collective-permute-start | bytes 116744 | tf_op jit(solution)/shard_map/ppermute | solution.py:34
  129.5 0.6 copy-start.15
  129.5 0.6 copy-start.16
  138.5 0.9 copy-start.2
  145.7 13.5 %copy-start = (bf16[4,360,128]{2,1,0:T(8,128)(2,1)S(1)}, bf16[4,360,128]{2,1,0:T(8,128)(2,1)}, u32[]{:S(2)}) copy-start(bf16[4,360,128]{2,1,0:T(8,128)(2,1)} %fusion.1.cell_any.cell_ref) | copy-start | bytes 1105924
  145.7 13.4 %all-to-all-start.2 = ((bf16[16,16,128]{2,1,0:T(8,128)(2,1)}), bf16[16,16,128]{2,1,0:T(8,128)(2,1)S(1)}, u32[]{:S(2)}, u32[]{:S(2)}) async-start(bf16[16,16,128]{2,1,0:T(8,128)(2,1)} %get-tuple-element.55.tiles_ref), calls=%async_computation.2 | async-start | bytes 131072 | tf_op jit(solution)/shard_map/all_to_all | solution.py:519

commit v6 on v5

--- a/solution.py
+++ b/solution.py
@@ -23,6 +23,7 @@
 OCH_PAD = 80
 TAPS = [(row, col) for row in (-1, 0, 1) for col in (-1, 0, 1)]
 EARLY = 3
+SMALL = 1024
 BF16 = jnp.bfloat16
 F32 = jnp.float32
 WHOLE = pl.BlockSpec(memory_space=pltpu.VMEM)
@@ -358,7 +359,9 @@
         out_specs=out_specs or ([WHOLE] * len(outs) if len(outs) > 1 else WHOLE),
         scratch_shapes=list(scratch),
         compiler_params=pltpu.CompilerParams(vmem_limit_bytes=limit * 1024 * 1024),
-        cost_estimate=pl.CostEstimate(flops=flops, bytes_accessed=size, transcendentals=0),
+        cost_estimate=pl.CostEstimate(
+            flops=flops, bytes_accessed=min(size, flops), transcendentals=0
+        ),
     )(*operands)
 
 
@@ -408,9 +411,9 @@
         specs=[FAR, WHOLE, FAR],
         out_specs=FAR,
     )
-    spectra, slots = lax.optimization_barrier((spectra, sea_ensemble_arrays[0]))
     gathered = lax.all_to_all(spectra, "space", split_axis=0, concat_axis=0, tiled=True)
 
+    slots = sea_ensemble_arrays[0]
     far = [
         passed_along(slots[offset * CAP : (offset + 1) * CAP], "space", -offset)
         for offset in range(EARLY, NEAR)
@@ -427,7 +430,7 @@
             shape((channels, channels + 128), BF16),
         ],
         [air, layernorm_scaling, bypass_factor, core_exit_factor, air_to_exchange_factor.T],
-        2 * latitude_rows * longitudes * channels * channels,
+        SMALL,
         held([air]) + [pltpu.SemaphoreType.DMA((latitude_rows,))],
         specs=[FAR] + [WHOLE] * 4,
     )
@@ -465,15 +468,7 @@
     slot_rows = (
         holder[:, None, :] == jnp.arange(SLOTS, dtype=jnp.int32)[None, :, None]
     ).astype(F32)
-    prepared = (
-        far, skip, air_flux, wide, place, group, forcing_weight, state_weight, decode_weight,
-        depths, cell, slot_of,
-    )
-    gathered, prepared = lax.optimization_barrier((gathered, prepared))
-    (
-        far, skip, air_flux, wide, place, group, forcing_weight, state_weight, decode_weight,
-        depths, cell, slot_of,
-    ) = prepared
+    gathered, *far = lax.optimization_barrier((gathered, *far))
     filtered = call(
         legendre_kernel,
         [shape((bands, chunk, channels), BF16)],
@@ -492,8 +487,9 @@
         ocean_kernel,
         [shape((hidden_channels, SPAN), F32), shape((1, SPAN), F32)],
         [depths, slots[:CAP], *near, *far, state_weight],
-        2 * hidden_channels * len(TAPS) * OCH_PAD * SPAN,
+        SMALL,
         [pltpu.VMEM((len(TAPS) * OCH_PAD, SPAN), BF16)],
+        limit=32,
         specs=[pl.BlockSpec(memory_space=pltpu.SMEM)] + [WHOLE] * (NEAR + 1),
     )
     operands = [

time: 161 us -> 149 us (0.925)
  waiting for transfers between devices: 67.7 us -> 51.1 us
  starting transfers between devices: 52.3 us -> 60.4 us
  Pallas kernels: 27.6 us -> 25.8 us
    all_to_all x1, waiting for transfers between devices: 31.9 us -> 0.01 us  [shards(): lax.all_to_all(spectra, 'space', split_axis=0, concat_axis=0, tiled=True)]
    ppermute x7, waiting for transfers between devices: 28.9 us -> 43.6 us  [passed_along(): lax.ppermute(value, axis, [(i, (i + by) % devices) for i in range(devices)])]
    all_to_all x1, starting transfers between devices: 10.7 us -> 16.9 us  [shards(): lax.all_to_all(spectra, 'space', split_axis=0, concat_axis=0, tiled=True)]
    all_to_all x1, starting transfers between devices: 4.07 us -> 10.1 us  [shards(): lax.all_to_all(filtered, 'space', split_axis=0, concat_axis=0, tiled=True)]
    ppermute x7, starting transfers between devices: 30.7 us -> 26.5 us  [passed_along(): lax.ppermute(value, axis, [(i, (i + by) % devices) for i in range(devices)])]
    pallas_call x7, Pallas kernels: 27.6 us -> 25.8 us  [call(): pl.pallas_call(kernel, out_shape=outs if len(outs) > 1 else outs[0], in_s...]
  transfers between devices with their start and end apart: 10 -> 10, of which waited for: 4 -> 6; matrix products, arithmetic and copies ran while one was open for 5% -> 5% of each run, Pallas kernels for 9% -> 8%
where the time goes in v6:
time: 149 us; the launch traced here: 148 us
  starting transfers between devices  60.4 us (41%)
  waiting for transfers between devices  51.1 us (34%)
  Pallas kernels  25.8 us (17%)
  local copies, waits for them, and re-layouts  5.62 us (4%)
  other arithmetic  4.28 us (3%)
    ppermute x7, waiting for transfers between devices, passed_along(): lax.ppermute(value, axis, [(i, (i + by) % devices) for i in range(devices)])  43.6 us
    ppermute x7, starting transfers between devices, passed_along(): lax.ppermute(value, axis, [(i, (i + by) % devices) for i in range(devices)])  26.5 us
    pallas_call x7, Pallas kernels, call(): pl.pallas_call(kernel, out_shape=outs if len(outs) > 1 else outs[0], in_s...  25.8 us
    all_to_all x1, starting transfers between devices, shards(): lax.all_to_all(spectra, 'space', split_axis=0, concat_axis=0, tiled=True)  16.9 us
    all_to_all x1, starting transfers between devices, shards(): lax.all_to_all(filtered, 'space', split_axis=0, concat_axis=0, tiled=True)  10.1 us
    all_to_all x1, starting transfers between devices, shards(): lax.all_to_all(tiles, 'member', split_axis=0, concat_axis=0, tiled=True)  6.9 us
    all_to_all x1, waiting for transfers between devices, shards(): lax.all_to_all(filtered, 'space', split_axis=0, concat_axis=0, tiled=True)  5.37 us
  transfers between devices with their start and end apart: 10, of which 6 were waited for; matrix products, arithmetic and copies ran while one was open for 5% of the time, Pallas kernels for 8%

profile of v6, /device:TPU:1, one launch (start us, length us, event | category | flops | bytes accessed | tf_op | source)
XLA Modules:
  0.0 148.3 jit_solution(3390224709130109839)
XLA Ops:
  0.6 0.0 copy-start.6
  0.6 0.0 copy-start.11
  0.7 0.0 copy-start.7
  0.7 0.0 copy-start.9
  0.7 4.7 %shard_map.194 = bf16[32,32,384]{2,1,0:T(8,128)(2,1)} custom-call(bf16[4,360,384]{2,1,0:T(8,128)(2,1)} %bitcast.54, f32[384]{0:T(512)} %scale_ref.3, bf16[256,360]{1,0:T(8,128)(2,1)} %constant.102.clone.table_any), custom_call_target="tpu_custom_call" | custom-call | flops 283115520 | bytes 2078208 | tf_op jit(solution)/shard_map/pallas_call | solution.py:355
  5.3 0.0 copy-start.2
  5.4 16.9 %all-to-all-start = ((bf16[32,32,384]{2,1,0:T(8,128)(2,1)}), bf16[32,32,384]{2,1,0:T(8,128)(2,1)S(1)}, u32[]{:S(2)}, u32[]{:S(2)}) async-start(bf16[32,32,384]{2,1,0:T(8,128)(2,1)} %shard_map.194), calls=%async_computation | async-start | bytes 1572864 | tf_op jit(solution)/shard_map/all_to_all | solution.py:414
  22.3 0.0 copy-done.6
  22.3 0.2 fusion.8
  22.5 4.8 %collective-permute-start = (bf16[2,76,128]{2,1,0:T(8,128)(2,1)S(1)}, bf16[2,76,128]{2,1,0:T(8,128)(2,1)S(1)}, u32[]{:S(2)}, u32[]{:S(2)}) collective-permute-start(bf16[2,76,128]{2,1,0:T(8,128)(2,1)S(1)} %bitcast.62), channel_id=1, source_target_pairs={{0,29},{1,30},{2,31},{3,0},{4,1},{5,2},{6,3},{7,4},{8,5},{9,6},{10... | collective-permute-start | bytes 116744 | tf_op jit(solution)/shard_map/ppermute | solution.py:35
  27.3 4.0 %collective-permute-start.1 = (bf16[2,76,128]{2,1,0:T(8,128)(2,1)S(1)}, bf16[2,76,128]{2,1,0:T(8,128)(2,1)S(1)}, u32[]{:S(2)}, u32[]{:S(2)}) collective-permute-start(bf16[2,76,128]{2,1,0:T(8,128)(2,1)S(1)} %bitcast.63), channel_id=1, source_target_pairs={{0,28},{1,29},{2,30},{3,31},{4,0},{5,1},{6,2},{7,3},{8,4},{9,5},{1... | collective-permute-start | bytes 116744 | tf_op jit(solution)/shard_map/ppermute | solution.py:35
  31.3 6.4 %collective-permute-start.2 = (bf16[2,76,128]{2,1,0:T(8,128)(2,1)S(1)}, bf16[2,76,128]{2,1,0:T(8,128)(2,1)S(1)}, u32[]{:S(2)}, u32[]{:S(2)}) collective-permute-start(bf16[2,76,128]{2,1,0:T(8,128)(2,1)S(1)} %bitcast.64), channel_id=1, source_target_pairs={{0,27},{1,28},{2,29},{3,30},{4,31},{5,0},{6,1},{7,2},{8,3},{9,4},{... | collective-permute-start | bytes 116744 | tf_op jit(solution)/shard_map/ppermute | solution.py:35
  37.7 4.0 %collective-permute-start.3 = (bf16[2,76,128]{2,1,0:T(8,128)(2,1)S(1)}, bf16[2,76,128]{2,1,0:T(8,128)(2,1)S(1)}, u32[]{:S(2)}, u32[]{:S(2)}) collective-permute-start(bf16[2,76,128]{2,1,0:T(8,128)(2,1)S(1)} %bitcast.65), channel_id=1, source_target_pairs={{0,26},{1,27},{2,28},{3,29},{4,30},{5,31},{6,0},{7,1},{8,2},{9,3},... | collective-permute-start | bytes 116744 | tf_op jit(solution)/shard_map/ppermute | solution.py:35
  41.7 2.4 %collective-permute-start.4 = (bf16[2,76,128]{2,1,0:T(8,128)(2,1)S(1)}, bf16[2,76,128]{2,1,0:T(8,128)(2,1)S(1)}, u32[]{:S(2)}, u32[]{:S(2)}) collective-permute-start(bf16[2,76,128]{2,1,0:T(8,128)(2,1)S(1)} %bitcast.66), channel_id=1, source_target_pairs={{0,25},{1,26},{2,27},{3,28},{4,29},{5,30},{6,31},{7,0},{8,1},{9,2}... | collective-permute-start | bytes 116744 | tf_op jit(solution)/shard_map/ppermute | solution.py:35
  44.2 0.0 copy-done.11
  44.2 0.2 select_reduce_fusion.3
  44.4 0.1 copy.45
  44.5 0.0 copy-done.7
  44.5 0.1 select_reduce_fusion
  44.6 0.0 copy-done.9
  44.6 0.1 select_reduce_fusion.1
  44.7 0.0 copy-start.10
  44.7 0.0 copy-start.5
  44.7 1.0 constant_dynamic-slice_fusion
  45.9 15.1 %collective-permute-done.refs_3_ = bf16[2,76,128]{2,1,0:T(8,128)(2,1)S(1)} collective-permute-done((bf16[2,76,128]{2,1,0:T(8,128)(2,1)S(1)}, bf16[2,76,128]{2,1,0:T(8,128)(2,1)S(1)}, u32[]{:S(2)}, u32[]{:S(2)}) %collective-permute-start) | collective-permute-done | bytes 38944 | tf_op jit(solution)/shard_map/ppermute | solution.py:35
  61.0 0.0 collective-permute-done.1.refs_4_
  61.0 3.4 %collective-permute-done.2.refs_5_ = bf16[2,76,128]{2,1,0:T(8,128)(2,1)S(1)} collective-permute-done((bf16[2,76,128]{2,1,0:T(8,128)(2,1)S(1)}, bf16[2,76,128]{2,1,0:T(8,128)(2,1)S(1)}, u32[]{:S(2)}, u32[]{:S(2)}) %collective-permute-start.2) | collective-permute-done | bytes 38944 | tf_op jit(solution)/shard_map/ppermute | solution.py:35
  64.4 0.0 collective-permute-done.3.refs_6_
  64.4 5.8 %collective-permute-done.4.refs_7_ = bf16[2,76,128]{2,1,0:T(8,128)(2,1)S(1)} collective-permute-done((bf16[2,76,128]{2,1,0:T(8,128)(2,1)S(1)}, bf16[2,76,128]{2,1,0:T(8,128)(2,1)S(1)}, u32[]{:S(2)}, u32[]{:S(2)}) %collective-permute-start.4) | collective-permute-done | bytes 38944 | tf_op jit(solution)/shard_map/ppermute | solution.py:35
  70.2 0.0 all-to-all-done.x_ref
  70.3 0.0 copy-done.2
  70.3 1.8 %shard_map.195 = bf16[32,32,384]{2,1,0:T(8,128)(2,1)} custom-call(bf16[32,32,384]{2,1,0:T(8,128)(2,1)S(1)} %all-to-all-done.x_ref, bf16[4,128,128]{2,1,0:T(8,128)(2,1)S(1)} %get-tuple-element.45.forward_ref, bf16[4,128,128]{2,1,0:T(8,128)(2,1)S(1)} %get-tuple-element.44.backward_ref, f32[128,384]{1,0:T(8,128)S(1)} %copy-done.2), custom_call_target="tpu_custom_call" | custom-call | flops 201326592 | bytes 2031616 | tf_op jit(solution)/shard_map/pallas_call | solution.py:355
  72.0 10.1 %all-to-all-start.1 = ((bf16[32,32,384]{2,1,0:T(8,128)(2,1)}), bf16[32,32,384]{2,1,0:T(8,128)(2,1)S(1)}, u32[]{:S(2)}, u32[]{:S(2)}) async-start(bf16[32,32,384]{2,1,0:T(8,128)(2,1)} %shard_map.195), calls=%async_computation.1 | async-start | bytes 1572864 | tf_op jit(solution)/shard_map/all_to_all | solution.py:481
  82.2 0.0 copy-done.10
  82.2 0.0 copy-done.5
  82.3 1.0 fusion.1.cell_any.cell_ref
  83.3 1.0 compare_convert_fusion.slot_any
  84.3 0.0 copy-done.12
  84.3 0.1 slice_select_fusion
  84.4 0.7 multiply_add_fusion.refs_7_
  85.0 0.9 fusion.refs_6_
  86.0 0.2 collective-permute-start.5
  86.2 4.7 %collective-permute-start.6 = (bf16[2,76,128]{2,1,0:T(8,128)(2,1)S(1)}, bf16[2,76,128]{2,1,0:T(8,128)(2,1)S(1)}, u32[]{:S(2)}, u32[]{:S(2)}) collective-permute-start(bf16[2,76,128]{2,1,0:T(8,128)(2,1)S(1)} %get-tuple-element.38), channel_id=1, source_target_pairs={{0,30},{1,31},{2,0},{3,1},{4,2},{5,3},{6,4},{7,5},{8,6},{9,7},{10,... | collective-permute-start | bytes 116744 | tf_op jit(solution)/shard_map/ppermute | solution.py:35
  90.9 0.0 copy-done.13
  90.9 0.1 select_reduce_fusion.2.depth_ref
  91.1 6.0 %shard_map.196 = (f32[4,360,384]{2,1,0:T(8,128)}, f32[32,360]{1,0:T(8,128)}, bf16[384,512]{1,0:T(8,128)(2,1)}) custom-call(bf16[4,360,384]{2,1,0:T(8,128)(2,1)} %bitcast.55, f32[384]{0:T(512)} %scale_ref.3, bf16[384,384]{1,0:T(8,128)(2,1)} %bypass_ref.1, bf16[384,384]{1,0:T(8,128)(2,1)} %exit_ref.1, bf16[8,384]{1,0:T(8,128)(2,1)} %bitcast.69), custom_call_target="tpu_custom_call" | custom-call | flops 1024 | bytes 1024 | tf_op jit(solution)/shard_map/pallas_call | solution.py:355
  97.0 0.2 copy.47.refs_8_
  97.2 0.7 copy.48.refs_8_
  97.9 0.0 copy-done.8
  97.9 0.6 pad.9.refs_10_
  98.5 19.3 %collective-permute-done.5.refs_1_ = bf16[2,76,128]{2,1,0:T(8,128)(2,1)S(1)} collective-permute-done((bf16[2,76,128]{2,1,0:T(8,128)(2,1)S(1)}, bf16[2,76,128]{2,1,0:T(8,128)(2,1)S(1)}, u32[]{:S(2)}, u32[]{:S(2)}) %collective-permute-start.5) | collective-permute-done | bytes 38944 | tf_op jit(solution)/shard_map/ppermute | solution.py:35
  117.8 0.0 collective-permute-done.6.refs_2_
  117.8 1.9 %shard_map.197 = (f32[200,2048]{1,0:T(8,128)S(1)}, f32[1,2048]{1,0:T(1,128)S(1)}) custom-call(s32[16]{0:T(128)S(1)} %select_reduce_fusion.2.depth_ref, bf16[2,76,128]{2,1,0:T(8,128)(2,1)S(1)} %bitcast.53, bf16[2,76,128]{2,1,0:T(8,128)(2,1)S(1)} %collective-permute-done.5.refs_1_, bf16[2,76,128]{2,1,0:T(8,128)(2,1)S(1)} %collective-permute-done.6.refs_2_, ...), custom_call_target="tpu_custom_call" | custom-call | flops 1024 | bytes 1024 | tf_op jit(solution)/shard_map/pallas_call | solution.py:355
  119.7 0.0 copy-start.1
  119.7 1.2 copy-done.1
  120.9 0.6 copy-done.3
  121.5 5.4 %all-to-all-done.1.refs_0_ = bf16[32,32,384]{2,1,0:T(8,128)(2,1)S(1)} async-done(((bf16[32,32,384]{2,1,0:T(8,128)(2,1)}), bf16[32,32,384]{2,1,0:T(8,128)(2,1)S(1)}, u32[]{:S(2)}, u32[]{:S(2)}) %all-to-all-start.1) | async-done | bytes 786464 | tf_op jit(solution)/shard_map/all_to_all | solution.py:481
  126.8 0.9 copy-done.4
  127.7 6.3 %shard_map.198 = (f32[4,360,384]{2,1,0:T(8,128)}, bf16[16,16,128]{2,1,0:T(8,128)(2,1)}) custom-call(bf16[32,32,384]{2,1,0:T(8,128)(2,1)} %copy-done.4, bf16[360,256]{1,0:T(8,128)(2,1)} %constant.103.clone.refs_1_, bf16[384,512]{1,0:T(8,128)(2,1)} %get-tuple-element.19.refs_2_, f32[32,360]{1,0:T(8,128)} %get-tuple-element.20.refs_3_, ...), custom_call_target="tpu_custom_call" | custom-call | flops 707788800 | bytes 9219456 | tf_op jit(solution)/shard_map/pallas_call | solution.py:355
  134.0 6.9 %all-to-all-start.2 = ((bf16[16,16,128]{2,1,0:T(8,128)(2,1)}), bf16[16,16,128]{2,1,0:T(8,128)(2,1)S(1)}, u32[]{:S(2)}, u32[]{:S(2)}) async-start(bf16[16,16,128]{2,1,0:T(8,128)(2,1)} %get-tuple-element.31.tiles_ref), calls=%async_computation.2 | async-start | bytes 131072 | tf_op jit(solution)/shard_map/all_to_all | solution.py:515
  140.9 4.4 %shard_map.199 = bf16[4,360,384]{2,1,0:T(8,128)(2,1)} custom-call(f32[4,360,384]{2,1,0:T(8,128)} %get-tuple-element.30.updated_any, bf16[16,16,128]{2,1,0:T(8,128)(2,1)} %get-tuple-element.31.tiles_ref, bf16[4,360,128]{2,1,0:T(8,128)(2,1)} %fusion.1.cell_any.cell_ref, bf16[4,360,48]{2,1,0:T(8,128)(2,1)} %compare_convert_fusion.slot_any, f32[384]{0:T(512)} %imprint_ref.1), custom_call_target="tpu_custom_call" | custom-call | flops 283115520 | bytes 3891712 | tf_op jit(solution)/shard_map/pallas_call | solution.py:355
  145.3 2.1 %all-to-all-done.2.tiles_ref = bf16[16,16,128]{2,1,0:T(8,128)(2,1)S(1)} async-done(((bf16[16,16,128]{2,1,0:T(8,128)(2,1)}), bf16[16,16,128]{2,1,0:T(8,128)(2,1)S(1)}, u32[]{:S(2)}, u32[]{:S(2)}) %all-to-all-start.2) | async-done | bytes 65568 | tf_op jit(solution)/shard_map/all_to_all | solution.py:515
  147.4 0.0 copy-done
  147.4 0.9 shard_map.200
  (26 shorter events, 0.2 us)
Async XLA Ops:
  0.6 21.6 %copy-start.6 = (bf16[1,16,76,128]{3,1,2,0:T(8,128)(2,1)S(1)}, bf16[1,16,76,128]{3,1,2,0:T(8,128)(2,1)}, u32[]{:S(2)}) copy-start(bf16[1,16,76,128]{3,1,2,0:T(8,128)(2,1)} %param.27) | copy-start | bytes 933892
  0.6 43.5 %copy-start.11 = (s32[14,1]{0,1:T(1,128)S(1)}, s32[14,1]{0,1:T(1,128)}, u32[]{:S(2)}) copy-start(s32[14,1]{0,1:T(1,128)} %param.32) | copy-start | bytes 172
  0.7 43.8 %copy-start.7 = (s32[14,128]{1,0:T(8,128)S(1)}, s32[14,128]{1,0:T(8,128)}, u32[]{:S(2)}) copy-start(s32[14,128]{1,0:T(8,128)} %param.30) | copy-start | bytes 21508
  0.7 43.9 %copy-start.9 = (s32[4,360]{1,0:T(4,128)S(1)}, s32[4,360]{1,0:T(4,128)}, u32[]{:S(2)}) copy-start(s32[4,360]{1,0:T(4,128)} %param.31) | copy-start | bytes 17284
  5.3 64.9 %copy-start.2 = (f32[128,384]{1,0:T(8,128)S(1)}, f32[128,384]{1,0:T(8,128)}, u32[]{:S(2)}) copy-start(f32[128,384]{1,0:T(8,128)} %gains_ref.1) | copy-start | bytes 589828
  5.4 64.9 %all-to-all-start = ((bf16[32,32,384]{2,1,0:T(8,128)(2,1)}), bf16[32,32,384]{2,1,0:T(8,128)(2,1)S(1)}, u32[]{:S(2)}, u32[]{:S(2)}) async-start(bf16[32,32,384]{2,1,0:T(8,128)(2,1)} %shard_map.194), calls=%async_computation | async-start | bytes 1572864 | tf_op jit(solution)/shard_map/all_to_all | solution.py:414
  22.5 38.6 %collective-permute-start = (bf16[2,76,128]{2,1,0:T(8,128)(2,1)S(1)}, bf16[2,76,128]{2,1,0:T(8,128)(2,1)S(1)}, u32[]{:S(2)}, u32[]{:S(2)}) collective-permute-start(bf16[2,76,128]{2,1,0:T(8,128)(2,1)S(1)} %bitcast.62), channel_id=1, source_target_pairs={{0,29},{1,30},{2,31},{3,0},{4,1},{5,2},{6,3},{7,4},{8,5},{9,6},{10... | collective-permute-start | bytes 116744 | tf_op jit(solution)/shard_map/ppermute | solution.py:35
  27.3 33.7 %collective-permute-start.1 = (bf16[2,76,128]{2,1,0:T(8,128)(2,1)S(1)}, bf16[2,76,128]{2,1,0:T(8,128)(2,1)S(1)}, u32[]{:S(2)}, u32[]{:S(2)}) collective-permute-start(bf16[2,76,128]{2,1,0:T(8,128)(2,1)S(1)} %bitcast.63), channel_id=1, source_target_pairs={{0,28},{1,29},{2,30},{3,31},{4,0},{5,1},{6,2},{7,3},{8,4},{9,5},{1... | collective-permute-start | bytes 116744 | tf_op jit(solution)/shard_map/ppermute | solution.py:35
  31.3 33.1 %collective-permute-start.2 = (bf16[2,76,128]{2,1,0:T(8,128)(2,1)S(1)}, bf16[2,76,128]{2,1,0:T(8,128)(2,1)S(1)}, u32[]{:S(2)}, u32[]{:S(2)}) collective-permute-start(bf16[2,76,128]{2,1,0:T(8,128)(2,1)S(1)} %bitcast.64), channel_id=1, source_target_pairs={{0,27},{1,28},{2,29},{3,30},{4,31},{5,0},{6,1},{7,2},{8,3},{9,4},{... | collective-permute-start | bytes 116744 | tf_op jit(solution)/shard_map/ppermute | solution.py:35
  37.7 26.7 %collective-permute-start.3 = (bf16[2,76,128]{2,1,0:T(8,128)(2,1)S(1)}, bf16[2,76,128]{2,1,0:T(8,128)(2,1)S(1)}, u32[]{:S(2)}, u32[]{:S(2)}) collective-permute-start(bf16[2,76,128]{2,1,0:T(8,128)(2,1)S(1)} %bitcast.65), channel_id=1, source_target_pairs={{0,26},{1,27},{2,28},{3,29},{4,30},{5,31},{6,0},{7,1},{8,2},{9,3},... | collective-permute-start | bytes 116744 | tf_op jit(solution)/shard_map/ppermute | solution.py:35
  41.7 28.5 %collective-permute-start.4 = (bf16[2,76,128]{2,1,0:T(8,128)(2,1)S(1)}, bf16[2,76,128]{2,1,0:T(8,128)(2,1)S(1)}, u32[]{:S(2)}, u32[]{:S(2)}) collective-permute-start(bf16[2,76,128]{2,1,0:T(8,128)(2,1)S(1)} %bitcast.66), channel_id=1, source_target_pairs={{0,25},{1,26},{2,27},{3,28},{4,29},{5,30},{6,31},{7,0},{8,1},{9,2}... | collective-permute-start | bytes 116744 | tf_op jit(solution)/shard_map/ppermute | solution.py:35
  44.7 37.5 %copy-start.10 = (s32[4,360]{1,0:T(4,128)S(1)}, s32[4,360]{1,0:T(4,128)}, u32[]{:S(2)}) copy-start(s32[4,360]{1,0:T(4,128)} %param.20) | copy-start | bytes 17284
  44.7 37.5 %copy-start.5 = (bf16[9,200,84]{1,2,0:T(8,128)(2,1)S(1)}, bf16[9,200,84]{1,2,0:T(8,128)(2,1)}, u32[]{:S(2)}) copy-start(bf16[9,200,84]{1,2,0:T(8,128)(2,1)} %param.28) | copy-start | bytes 907204
  70.3 14.0 %copy-start.12 = (pred[80]{0:T(512)(128)(4,1)S(1)}, pred[80]{0:T(512)(128)(4,1)}, u32[]{:S(2)}) copy-start(pred[80]{0:T(512)(128)(4,1)} %constant.98.clone.1) | copy-start | bytes 244
  72.0 18.9 %copy-start.13 = (s32[14]{0:T(128)S(1)}, s32[14]{0:T(128)}, u32[]{:S(2)}) copy-start(s32[14]{0:T(128)} %param.33) | copy-start | bytes 172
  72.0 54.8 %all-to-all-start.1 = ((bf16[32,32,384]{2,1,0:T(8,128)(2,1)}), bf16[32,32,384]{2,1,0:T(8,128)(2,1)S(1)}, u32[]{:S(2)}, u32[]{:S(2)}) async-start(bf16[32,32,384]{2,1,0:T(8,128)(2,1)} %shard_map.195), calls=%async_computation.1 | async-start | bytes 1572864 | tf_op jit(solution)/shard_map/all_to_all | solution.py:481
  83.3 14.6 %copy-start.8 = (bf16[9,200]{1,0:T(8,128)(2,1)S(1)}, bf16[9,200]{1,0:T(8,128)(2,1)}, u32[]{:S(2)}) copy-start(bf16[9,200]{1,0:T(8,128)(2,1)} %param.29) | copy-start | bytes 10804
  86.0 31.8 %collective-permute-start.5 = (bf16[2,76,128]{2,1,0:T(8,128)(2,1)S(1)}, bf16[2,76,128]{2,1,0:T(8,128)(2,1)S(1)}, u32[]{:S(2)}, u32[]{:S(2)}) collective-permute-start(bf16[2,76,128]{2,1,0:T(8,128)(2,1)S(1)} %get-tuple-element.39), channel_id=1, source_target_pairs={{0,31},{1,0},{2,1},{3,2},{4,3},{5,4},{6,5},{7,6},{8,7},{9,8},{10,9... | collective-permute-start | bytes 116744 | tf_op jit(solution)/shard_map/ppermute | solution.py:35
  86.2 31.6 %collective-permute-start.6 = (bf16[2,76,128]{2,1,0:T(8,128)(2,1)S(1)}, bf16[2,76,128]{2,1,0:T(8,128)(2,1)S(1)}, u32[]{:S(2)}, u32[]{:S(2)}) collective-permute-start(bf16[2,76,128]{2,1,0:T(8,128)(2,1)S(1)} %get-tuple-element.38), channel_id=1, source_target_pairs={{0,30},{1,31},{2,0},{3,1},{4,2},{5,3},{6,4},{7,5},{8,6},{9,7},{10,... | collective-permute-start | bytes 116744 | tf_op jit(solution)/shard_map/ppermute | solution.py:35
  119.7 1.2 copy-start.1
  120.9 0.6 copy-start.3
  126.8 0.9 copy-start.4
  134.0 13.4 %copy-start = (bf16[4,360,128]{2,1,0:T(8,128)(2,1)S(1)}, bf16[4,360,128]{2,1,0:T(8,128)(2,1)}, u32[]{:S(2)}) copy-start(bf16[4,360,128]{2,1,0:T(8,128)(2,1)} %fusion.1.cell_any.cell_ref) | copy-start | bytes 1105924
  134.0 13.4 %all-to-all-start.2 = ((bf16[16,16,128]{2,1,0:T(8,128)(2,1)}), bf16[16,16,128]{2,1,0:T(8,128)(2,1)S(1)}, u32[]{:S(2)}, u32[]{:S(2)}) async-start(bf16[16,16,128]{2,1,0:T(8,128)(2,1)} %get-tuple-element.31.tiles_ref), calls=%async_computation.2 | async-start | bytes 131072 | tf_op jit(solution)/shard_map/all_to_all | solution.py:515

commit v7 on v6

--- a/solution.py
+++ b/solution.py
@@ -468,7 +468,6 @@
     slot_rows = (
         holder[:, None, :] == jnp.arange(SLOTS, dtype=jnp.int32)[None, :, None]
     ).astype(F32)
-    gathered, *far = lax.optimization_barrier((gathered, *far))
     filtered = call(
         legendre_kernel,
         [shape((bands, chunk, channels), BF16)],

time: 149 us -> 140 us (0.940)
  starting transfers between devices: 60.4 us -> 54.8 us
  waiting for transfers between devices: 51.1 us -> 47.8 us
    ppermute x7, waiting for transfers between devices: 43.6 us -> 19.3 us  [passed_along(): lax.ppermute(value, axis, [(i, (i + by) % devices) for i in range(devices)])]
    all_to_all x1, waiting for transfers between devices: 0.01 us -> 21.1 us  [shards(): lax.all_to_all(spectra, 'space', split_axis=0, concat_axis=0, tiled=True)]
    all_to_all x1, starting transfers between devices: 10.1 us -> 4.47 us  [shards(): lax.all_to_all(filtered, 'space', split_axis=0, concat_axis=0, tiled=True)]
  transfers between devices with their start and end apart: 10 -> 10, of which waited for: 6 -> 4; matrix products, arithmetic and copies ran while one was open for 5% -> 5% of each run, Pallas kernels for 8% -> 10%
where the time goes in v7:
time: 140 us; the launch traced here: 139 us
  starting transfers between devices  54.8 us (39%)
  waiting for transfers between devices  47.8 us (34%)
  Pallas kernels  25.8 us (18%)
  local copies, waits for them, and re-layouts  5.58 us (4%)
  other arithmetic  4.27 us (3%)
    ppermute x7, starting transfers between devices, passed_along(): lax.ppermute(value, axis, [(i, (i + by) % devices) for i in range(devices)])  26.5 us
    pallas_call x7, Pallas kernels, call(): pl.pallas_call(kernel, out_shape=outs if len(outs) > 1 else outs[0], in_s...  25.8 us
    all_to_all x1, waiting for transfers between devices, shards(): lax.all_to_all(spectra, 'space', split_axis=0, concat_axis=0, tiled=True)  21.1 us
    ppermute x7, waiting for transfers between devices, passed_along(): lax.ppermute(value, axis, [(i, (i + by) % devices) for i in range(devices)])  19.3 us
    all_to_all x1, starting transfers between devices, shards(): lax.all_to_all(spectra, 'space', split_axis=0, concat_axis=0, tiled=True)  16.9 us
    all_to_all x1, starting transfers between devices, shards(): lax.all_to_all(tiles, 'member', split_axis=0, concat_axis=0, tiled=True)  6.9 us
    all_to_all x1, waiting for transfers between devices, shards(): lax.all_to_all(filtered, 'space', split_axis=0, concat_axis=0, tiled=True)  5.36 us
    all_to_all x1, starting transfers between devices, shards(): lax.all_to_all(filtered, 'space', split_axis=0, concat_axis=0, tiled=True)  4.47 us
  transfers between devices with their start and end apart: 10, of which 4 were waited for; matrix products, arithmetic and copies ran while one was open for 5% of the time, Pallas kernels for 10%

profile of v7, /device:TPU:1, one launch (start us, length us, event | category | flops | bytes accessed | tf_op | source)
XLA Modules:
  0.0 139.3 jit_solution(1903569772656261183)
XLA Ops:
  0.6 0.0 copy-start.6
  0.6 0.0 copy-start.11
  0.7 0.0 copy-start.7
  0.7 0.0 copy-start.9
  0.7 4.7 %shard_map.194 = bf16[32,32,384]{2,1,0:T(8,128)(2,1)} custom-call(bf16[4,360,384]{2,1,0:T(8,128)(2,1)} %bitcast.54, f32[384]{0:T(512)} %scale_ref.3, bf16[256,360]{1,0:T(8,128)(2,1)} %constant.102.clone.table_any), custom_call_target="tpu_custom_call" | custom-call | flops 283115520 | bytes 2078208 | tf_op jit(solution)/shard_map/pallas_call | solution.py:355
  5.3 0.0 copy-start.2
  5.4 16.9 %all-to-all-start = ((bf16[32,32,384]{2,1,0:T(8,128)(2,1)}), bf16[32,32,384]{2,1,0:T(8,128)(2,1)S(1)}, u32[]{:S(2)}, u32[]{:S(2)}) async-start(bf16[32,32,384]{2,1,0:T(8,128)(2,1)} %shard_map.194), calls=%async_computation | async-start | bytes 1572864 | tf_op jit(solution)/shard_map/all_to_all | solution.py:414
  22.3 0.0 copy-done.6
  22.3 0.2 fusion.8
  22.5 4.8 %collective-permute-start.2 = (bf16[2,76,128]{2,1,0:T(8,128)(2,1)S(1)}, bf16[2,76,128]{2,1,0:T(8,128)(2,1)S(1)}, u32[]{:S(2)}, u32[]{:S(2)}) collective-permute-start(bf16[2,76,128]{2,1,0:T(8,128)(2,1)S(1)} %bitcast.66), channel_id=1, source_target_pairs={{0,29},{1,30},{2,31},{3,0},{4,1},{5,2},{6,3},{7,4},{8,5},{9,6},{10... | collective-permute-start | bytes 116744 | tf_op jit(solution)/shard_map/ppermute | solution.py:35
  27.3 4.0 %collective-permute-start.3 = (bf16[2,76,128]{2,1,0:T(8,128)(2,1)S(1)}, bf16[2,76,128]{2,1,0:T(8,128)(2,1)S(1)}, u32[]{:S(2)}, u32[]{:S(2)}) collective-permute-start(bf16[2,76,128]{2,1,0:T(8,128)(2,1)S(1)} %bitcast.65), channel_id=1, source_target_pairs={{0,28},{1,29},{2,30},{3,31},{4,0},{5,1},{6,2},{7,3},{8,4},{9,5},{1... | collective-permute-start | bytes 116744 | tf_op jit(solution)/shard_map/ppermute | solution.py:35
  31.3 6.4 %collective-permute-start.4 = (bf16[2,76,128]{2,1,0:T(8,128)(2,1)S(1)}, bf16[2,76,128]{2,1,0:T(8,128)(2,1)S(1)}, u32[]{:S(2)}, u32[]{:S(2)}) collective-permute-start(bf16[2,76,128]{2,1,0:T(8,128)(2,1)S(1)} %bitcast.62), channel_id=1, source_target_pairs={{0,27},{1,28},{2,29},{3,30},{4,31},{5,0},{6,1},{7,2},{8,3},{9,4},{... | collective-permute-start | bytes 116744 | tf_op jit(solution)/shard_map/ppermute | solution.py:35
  37.7 4.0 %collective-permute-start.5 = (bf16[2,76,128]{2,1,0:T(8,128)(2,1)S(1)}, bf16[2,76,128]{2,1,0:T(8,128)(2,1)S(1)}, u32[]{:S(2)}, u32[]{:S(2)}) collective-permute-start(bf16[2,76,128]{2,1,0:T(8,128)(2,1)S(1)} %bitcast.63), channel_id=1, source_target_pairs={{0,26},{1,27},{2,28},{3,29},{4,30},{5,31},{6,0},{7,1},{8,2},{9,3},... | collective-permute-start | bytes 116744 | tf_op jit(solution)/shard_map/ppermute | solution.py:35
  41.7 2.4 %collective-permute-start.6 = (bf16[2,76,128]{2,1,0:T(8,128)(2,1)S(1)}, bf16[2,76,128]{2,1,0:T(8,128)(2,1)S(1)}, u32[]{:S(2)}, u32[]{:S(2)}) collective-permute-start(bf16[2,76,128]{2,1,0:T(8,128)(2,1)S(1)} %bitcast.64), channel_id=1, source_target_pairs={{0,25},{1,26},{2,27},{3,28},{4,29},{5,30},{6,31},{7,0},{8,1},{9,2}... | collective-permute-start | bytes 116744 | tf_op jit(solution)/shard_map/ppermute | solution.py:35
  44.2 0.0 copy-start.10
  44.2 0.0 copy-start.5
  44.3 0.0 copy-done.11
  44.3 0.2 select_reduce_fusion.3
  44.5 0.1 copy.40
  44.6 0.0 copy-done.7
  44.6 0.1 select_reduce_fusion
  44.7 0.0 copy-done.9
  44.7 0.1 select_reduce_fusion.1
  44.8 1.0 constant_dynamic-slice_fusion
  45.8 21.1 %all-to-all-done.x_ref = bf16[32,32,384]{2,1,0:T(8,128)(2,1)S(1)} async-done(((bf16[32,32,384]{2,1,0:T(8,128)(2,1)}), bf16[32,32,384]{2,1,0:T(8,128)(2,1)S(1)}, u32[]{:S(2)}, u32[]{:S(2)}) %all-to-all-start) | async-done | bytes 786464 | tf_op jit(solution)/shard_map/all_to_all | solution.py:414
  66.9 0.0 copy-done.2
  66.9 1.7 %shard_map.195 = bf16[32,32,384]{2,1,0:T(8,128)(2,1)} custom-call(bf16[32,32,384]{2,1,0:T(8,128)(2,1)S(1)} %all-to-all-done.x_ref, bf16[4,128,128]{2,1,0:T(8,128)(2,1)S(1)} %get-tuple-element.33.forward_ref, bf16[4,128,128]{2,1,0:T(8,128)(2,1)S(1)} %get-tuple-element.32.backward_ref, f32[128,384]{1,0:T(8,128)S(1)} %copy-done.2), custom_call_target="tpu_custom_call" | custom-call | flops 201326592 | bytes 2031616 | tf_op jit(solution)/shard_map/pallas_call | solution.py:355
  68.7 4.5 %all-to-all-start.1 = ((bf16[32,32,384]{2,1,0:T(8,128)(2,1)}), bf16[32,32,384]{2,1,0:T(8,128)(2,1)S(1)}, u32[]{:S(2)}, u32[]{:S(2)}) async-start(bf16[32,32,384]{2,1,0:T(8,128)(2,1)} %shard_map.195), calls=%async_computation.1 | async-start | bytes 1572864 | tf_op jit(solution)/shard_map/all_to_all | solution.py:480
  73.2 0.0 copy-done.10
  73.2 0.0 copy-done.5
  73.3 1.0 fusion.1.cell_any.cell_ref
  74.3 1.0 compare_convert_fusion.slot_any
  75.2 0.0 copy-done.12
  75.2 0.1 slice_select_fusion
  75.3 0.7 multiply_add_fusion.refs_7_
  76.0 0.9 fusion.refs_6_
  77.0 0.0 collective-permute-done.2.refs_3_
  77.0 0.2 collective-permute-start
  77.2 0.0 collective-permute-done.3.refs_4_
  77.2 4.7 %collective-permute-start.1 = (bf16[2,76,128]{2,1,0:T(8,128)(2,1)S(1)}, bf16[2,76,128]{2,1,0:T(8,128)(2,1)S(1)}, u32[]{:S(2)}, u32[]{:S(2)}) collective-permute-start(bf16[2,76,128]{2,1,0:T(8,128)(2,1)S(1)} %get-tuple-element.26), channel_id=1, source_target_pairs={{0,30},{1,31},{2,0},{3,1},{4,2},{5,3},{6,4},{7,5},{8,6},{9,7},{10,... | collective-permute-start | bytes 116744 | tf_op jit(solution)/shard_map/ppermute | solution.py:35
  81.9 0.0 copy-done.13
  81.9 0.1 select_reduce_fusion.2.depth_ref
  82.1 5.9 %shard_map.196 = (f32[4,360,384]{2,1,0:T(8,128)}, f32[32,360]{1,0:T(8,128)}, bf16[384,512]{1,0:T(8,128)(2,1)}) custom-call(bf16[4,360,384]{2,1,0:T(8,128)(2,1)} %bitcast.55, f32[384]{0:T(512)} %scale_ref.3, bf16[384,384]{1,0:T(8,128)(2,1)} %bypass_ref.1, bf16[384,384]{1,0:T(8,128)(2,1)} %exit_ref.1, bf16[8,384]{1,0:T(8,128)(2,1)} %bitcast.69), custom_call_target="tpu_custom_call" | custom-call | flops 1024 | bytes 1024 | tf_op jit(solution)/shard_map/pallas_call | solution.py:355
  88.0 0.2 copy.47.refs_8_
  88.2 0.7 copy.48.refs_8_
  88.9 0.0 copy-done.8
  88.9 0.6 pad.9.refs_10_
  89.5 0.0 collective-permute-done.4.refs_5_
  89.5 0.0 collective-permute-done.5.refs_6_
  89.5 0.0 collective-permute-done.6.refs_7_
  89.5 19.2 %collective-permute-done.refs_1_ = bf16[2,76,128]{2,1,0:T(8,128)(2,1)S(1)} collective-permute-done((bf16[2,76,128]{2,1,0:T(8,128)(2,1)S(1)}, bf16[2,76,128]{2,1,0:T(8,128)(2,1)S(1)}, u32[]{:S(2)}, u32[]{:S(2)}) %collective-permute-start) | collective-permute-done | bytes 38944 | tf_op jit(solution)/shard_map/ppermute | solution.py:35
  108.8 0.0 collective-permute-done.1.refs_2_
  108.8 1.9 %shard_map.197 = (f32[200,2048]{1,0:T(8,128)S(1)}, f32[1,2048]{1,0:T(1,128)S(1)}) custom-call(s32[16]{0:T(128)S(1)} %select_reduce_fusion.2.depth_ref, bf16[2,76,128]{2,1,0:T(8,128)(2,1)S(1)} %bitcast.53, bf16[2,76,128]{2,1,0:T(8,128)(2,1)S(1)} %collective-permute-done.refs_1_, bf16[2,76,128]{2,1,0:T(8,128)(2,1)S(1)} %collective-permute-done.1.refs_2_, ...), custom_call_target="tpu_custom_call" | custom-call | flops 1024 | bytes 1024 | tf_op jit(solution)/shard_map/pallas_call | solution.py:355
  110.7 0.0 copy-start.1
  110.7 1.2 copy-done.1
  111.9 0.6 copy-done.3
  112.4 5.4 %all-to-all-done.1.refs_0_ = bf16[32,32,384]{2,1,0:T(8,128)(2,1)S(1)} async-done(((bf16[32,32,384]{2,1,0:T(8,128)(2,1)}), bf16[32,32,384]{2,1,0:T(8,128)(2,1)S(1)}, u32[]{:S(2)}, u32[]{:S(2)}) %all-to-all-start.1) | async-done | bytes 786464 | tf_op jit(solution)/shard_map/all_to_all | solution.py:480
  117.8 0.9 copy-done.4
  118.7 6.3 %shard_map.198 = (f32[4,360,384]{2,1,0:T(8,128)}, bf16[16,16,128]{2,1,0:T(8,128)(2,1)}) custom-call(bf16[32,32,384]{2,1,0:T(8,128)(2,1)} %copy-done.4, bf16[360,256]{1,0:T(8,128)(2,1)} %constant.103.clone.refs_1_, bf16[384,512]{1,0:T(8,128)(2,1)} %get-tuple-element.12.refs_2_, f32[32,360]{1,0:T(8,128)} %get-tuple-element.13.refs_3_, ...), custom_call_target="tpu_custom_call" | custom-call | flops 707788800 | bytes 9219456 | tf_op jit(solution)/shard_map/pallas_call | solution.py:355
  125.0 0.0 copy-start
  125.0 6.9 %all-to-all-start.2 = ((bf16[16,16,128]{2,1,0:T(8,128)(2,1)}), bf16[16,16,128]{2,1,0:T(8,128)(2,1)S(1)}, u32[]{:S(2)}, u32[]{:S(2)}) async-start(bf16[16,16,128]{2,1,0:T(8,128)(2,1)} %get-tuple-element.19.tiles_ref), calls=%async_computation.2 | async-start | bytes 131072 | tf_op jit(solution)/shard_map/all_to_all | solution.py:514
  131.9 4.4 %shard_map.199 = bf16[4,360,384]{2,1,0:T(8,128)(2,1)} custom-call(f32[4,360,384]{2,1,0:T(8,128)} %get-tuple-element.18.updated_any, bf16[16,16,128]{2,1,0:T(8,128)(2,1)} %get-tuple-element.19.tiles_ref, bf16[4,360,128]{2,1,0:T(8,128)(2,1)} %fusion.1.cell_any.cell_ref, bf16[4,360,48]{2,1,0:T(8,128)(2,1)} %compare_convert_fusion.slot_any, f32[384]{0:T(512)} %imprint_ref.1), custom_call_target="tpu_custom_call" | custom-call | flops 283115520 | bytes 3891712 | tf_op jit(solution)/shard_map/pallas_call | solution.py:355
  136.3 2.1 %all-to-all-done.2.tiles_ref = bf16[16,16,128]{2,1,0:T(8,128)(2,1)S(1)} async-done(((bf16[16,16,128]{2,1,0:T(8,128)(2,1)}), bf16[16,16,128]{2,1,0:T(8,128)(2,1)S(1)}, u32[]{:S(2)}, u32[]{:S(2)}) %all-to-all-start.2) | async-done | bytes 65568 | tf_op jit(solution)/shard_map/all_to_all | solution.py:514
  138.4 0.9 shard_map.200
  (26 shorter events, 0.2 us)
Async XLA Ops:
  0.6 21.6 %copy-start.6 = (bf16[1,16,76,128]{3,1,2,0:T(8,128)(2,1)S(1)}, bf16[1,16,76,128]{3,1,2,0:T(8,128)(2,1)}, u32[]{:S(2)}) copy-start(bf16[1,16,76,128]{3,1,2,0:T(8,128)(2,1)} %param.27) | copy-start | bytes 933892
  0.6 43.6 %copy-start.11 = (s32[14,1]{0,1:T(1,128)S(1)}, s32[14,1]{0,1:T(1,128)}, u32[]{:S(2)}) copy-start(s32[14,1]{0,1:T(1,128)} %param.32) | copy-start | bytes 172
  0.7 43.9 %copy-start.7 = (s32[14,128]{1,0:T(8,128)S(1)}, s32[14,128]{1,0:T(8,128)}, u32[]{:S(2)}) copy-start(s32[14,128]{1,0:T(8,128)} %param.30) | copy-start | bytes 21508
  0.7 44.0 %copy-start.9 = (s32[4,360]{1,0:T(4,128)S(1)}, s32[4,360]{1,0:T(4,128)}, u32[]{:S(2)}) copy-start(s32[4,360]{1,0:T(4,128)} %param.31) | copy-start | bytes 17284
  5.3 61.6 %copy-start.2 = (f32[128,384]{1,0:T(8,128)S(1)}, f32[128,384]{1,0:T(8,128)}, u32[]{:S(2)}) copy-start(f32[128,384]{1,0:T(8,128)} %gains_ref.1) | copy-start | bytes 589828
  5.4 61.6 %all-to-all-start = ((bf16[32,32,384]{2,1,0:T(8,128)(2,1)}), bf16[32,32,384]{2,1,0:T(8,128)(2,1)S(1)}, u32[]{:S(2)}, u32[]{:S(2)}) async-start(bf16[32,32,384]{2,1,0:T(8,128)(2,1)} %shard_map.194), calls=%async_computation | async-start | bytes 1572864 | tf_op jit(solution)/shard_map/all_to_all | solution.py:414
  22.5 54.5 %collective-permute-start.2 = (bf16[2,76,128]{2,1,0:T(8,128)(2,1)S(1)}, bf16[2,76,128]{2,1,0:T(8,128)(2,1)S(1)}, u32[]{:S(2)}, u32[]{:S(2)}) collective-permute-start(bf16[2,76,128]{2,1,0:T(8,128)(2,1)S(1)} %bitcast.66), channel_id=1, source_target_pairs={{0,29},{1,30},{2,31},{3,0},{4,1},{5,2},{6,3},{7,4},{8,5},{9,6},{10... | collective-permute-start | bytes 116744 | tf_op jit(solution)/shard_map/ppermute | solution.py:35
  27.3 49.9 %collective-permute-start.3 = (bf16[2,76,128]{2,1,0:T(8,128)(2,1)S(1)}, bf16[2,76,128]{2,1,0:T(8,128)(2,1)S(1)}, u32[]{:S(2)}, u32[]{:S(2)}) collective-permute-start(bf16[2,76,128]{2,1,0:T(8,128)(2,1)S(1)} %bitcast.65), channel_id=1, source_target_pairs={{0,28},{1,29},{2,30},{3,31},{4,0},{5,1},{6,2},{7,3},{8,4},{9,5},{1... | collective-permute-start | bytes 116744 | tf_op jit(solution)/shard_map/ppermute | solution.py:35
  31.3 58.2 %collective-permute-start.4 = (bf16[2,76,128]{2,1,0:T(8,128)(2,1)S(1)}, bf16[2,76,128]{2,1,0:T(8,128)(2,1)S(1)}, u32[]{:S(2)}, u32[]{:S(2)}) collective-permute-start(bf16[2,76,128]{2,1,0:T(8,128)(2,1)S(1)} %bitcast.62), channel_id=1, source_target_pairs={{0,27},{1,28},{2,29},{3,30},{4,31},{5,0},{6,1},{7,2},{8,3},{9,4},{... | collective-permute-start | bytes 116744 | tf_op jit(solution)/shard_map/ppermute | solution.py:35
  37.7 51.8 %collective-permute-start.5 = (bf16[2,76,128]{2,1,0:T(8,128)(2,1)S(1)}, bf16[2,76,128]{2,1,0:T(8,128)(2,1)S(1)}, u32[]{:S(2)}, u32[]{:S(2)}) collective-permute-start(bf16[2,76,128]{2,1,0:T(8,128)(2,1)S(1)} %bitcast.63), channel_id=1, source_target_pairs={{0,26},{1,27},{2,28},{3,29},{4,30},{5,31},{6,0},{7,1},{8,2},{9,3},... | collective-permute-start | bytes 116744 | tf_op jit(solution)/shard_map/ppermute | solution.py:35
  41.7 47.8 %collective-permute-start.6 = (bf16[2,76,128]{2,1,0:T(8,128)(2,1)S(1)}, bf16[2,76,128]{2,1,0:T(8,128)(2,1)S(1)}, u32[]{:S(2)}, u32[]{:S(2)}) collective-permute-start(bf16[2,76,128]{2,1,0:T(8,128)(2,1)S(1)} %bitcast.64), channel_id=1, source_target_pairs={{0,25},{1,26},{2,27},{3,28},{4,29},{5,30},{6,31},{7,0},{8,1},{9,2}... | collective-permute-start | bytes 116744 | tf_op jit(solution)/shard_map/ppermute | solution.py:35
  44.2 29.0 %copy-start.10 = (s32[4,360]{1,0:T(4,128)S(1)}, s32[4,360]{1,0:T(4,128)}, u32[]{:S(2)}) copy-start(s32[4,360]{1,0:T(4,128)} %param.20) | copy-start | bytes 17284
  44.2 29.0 %copy-start.5 = (bf16[9,200,84]{1,2,0:T(8,128)(2,1)S(1)}, bf16[9,200,84]{1,2,0:T(8,128)(2,1)}, u32[]{:S(2)}) copy-start(bf16[9,200,84]{1,2,0:T(8,128)(2,1)} %param.28) | copy-start | bytes 907204
  66.9 8.3 %copy-start.12 = (pred[80]{0:T(512)(128)(4,1)S(1)}, pred[80]{0:T(512)(128)(4,1)}, u32[]{:S(2)}) copy-start(pred[80]{0:T(512)(128)(4,1)} %constant.98.clone.1) | copy-start | bytes 244
  68.7 13.3 %copy-start.13 = (s32[14]{0:T(128)S(1)}, s32[14]{0:T(128)}, u32[]{:S(2)}) copy-start(s32[14]{0:T(128)} %param.33) | copy-start | bytes 172
  68.7 49.1 %all-to-all-start.1 = ((bf16[32,32,384]{2,1,0:T(8,128)(2,1)}), bf16[32,32,384]{2,1,0:T(8,128)(2,1)S(1)}, u32[]{:S(2)}, u32[]{:S(2)}) async-start(bf16[32,32,384]{2,1,0:T(8,128)(2,1)} %shard_map.195), calls=%async_computation.1 | async-start | bytes 1572864 | tf_op jit(solution)/shard_map/all_to_all | solution.py:480
  74.2 14.7 %copy-start.8 = (bf16[9,200]{1,0:T(8,128)(2,1)S(1)}, bf16[9,200]{1,0:T(8,128)(2,1)}, u32[]{:S(2)}) copy-start(bf16[9,200]{1,0:T(8,128)(2,1)} %param.29) | copy-start | bytes 10804
  77.0 31.8 %collective-permute-start = (bf16[2,76,128]{2,1,0:T(8,128)(2,1)S(1)}, bf16[2,76,128]{2,1,0:T(8,128)(2,1)S(1)}, u32[]{:S(2)}, u32[]{:S(2)}) collective-permute-start(bf16[2,76,128]{2,1,0:T(8,128)(2,1)S(1)} %get-tuple-element.27), channel_id=1, source_target_pairs={{0,31},{1,0},{2,1},{3,2},{4,3},{5,4},{6,5},{7,6},{8,7},{9,8},{10,9... | collective-permute-start | bytes 116744 | tf_op jit(solution)/shard_map/ppermute | solution.py:35
  77.2 31.5 %collective-permute-start.1 = (bf16[2,76,128]{2,1,0:T(8,128)(2,1)S(1)}, bf16[2,76,128]{2,1,0:T(8,128)(2,1)S(1)}, u32[]{:S(2)}, u32[]{:S(2)}) collective-permute-start(bf16[2,76,128]{2,1,0:T(8,128)(2,1)S(1)} %get-tuple-element.26), channel_id=1, source_target_pairs={{0,30},{1,31},{2,0},{3,1},{4,2},{5,3},{6,4},{7,5},{8,6},{9,7},{10,... | collective-permute-start | bytes 116744 | tf_op jit(solution)/shard_map/ppermute | solution.py:35
  110.7 1.2 copy-start.1
  111.9 0.6 copy-start.3
  117.8 0.9 copy-start.4
  125.0 13.4 %copy-start = (bf16[4,360,128]{2,1,0:T(8,128)(2,1)S(1)}, bf16[4,360,128]{2,1,0:T(8,128)(2,1)}, u32[]{:S(2)}) copy-start(bf16[4,360,128]{2,1,0:T(8,128)(2,1)} %fusion.1.cell_any.cell_ref) | copy-start | bytes 1105924
  125.0 13.4 %all-to-all-start.2 = ((bf16[16,16,128]{2,1,0:T(8,128)(2,1)}), bf16[16,16,128]{2,1,0:T(8,128)(2,1)S(1)}, u32[]{:S(2)}, u32[]{:S(2)}) async-start(bf16[16,16,128]{2,1,0:T(8,128)(2,1)} %get-tuple-element.19.tiles_ref), calls=%async_computation.2 | async-start | bytes 131072 | tf_op jit(solution)/shard_map/all_to_all | solution.py:514

commit v8 on v7

--- a/solution.py
+++ b/solution.py
@@ -1,3 +1,4 @@
+import functools
 import math
 
 import jax
@@ -207,21 +208,22 @@
         out_ref[:, :, lanes] = work[third].reshape(groups, chunk, 128).astype(BF16)
 
 
-def ocean_kernel(depth_ref, *refs):
-    pieces, (weight_ref, out_ref, top_ref, columns) = refs[:NEAR], refs[NEAR:]
+def ocean_kernel(first, depth_ref, *refs):
+    pieces, (weight_ref, out_ref, columns) = refs[:-3], refs[-3:]
     masks = tap_masks(CELLS)
     level = lax.broadcasted_iota(jnp.int32, (OCH, CELLS), 0) % LEV
-    for slot in range(SLOTS):
+    hidden_channels = weight_ref.shape[0]
+    for slot in range(CAP * len(pieces)):
         lanes = slice(CELLS * slot, CELLS * (slot + 1))
         state = pieces[slot // CAP][slot % CAP].astype(F32)
-        top_ref[:, lanes] = state[0:1]
-        state = jnp.where(level < depth_ref[slot], state, 0.0)
+        out_ref[hidden_channels:, lanes] = jnp.broadcast_to(state[0:1], (8, CELLS))
+        state = jnp.where(level < depth_ref[first + slot], state, 0.0)
         state = jnp.concatenate([state, jnp.zeros((OCH_PAD - OCH, CELLS), F32)], axis=0)
         for q, tap in enumerate(TAPS):
             moved = shifted(state, tap, masks[q]).astype(BF16)
             columns[OCH_PAD * q : OCH_PAD * (q + 1), lanes] = moved
-    for at in range(0, SPAN, 512):
-        out_ref[:, at : at + 512] = jnp.dot(
+    for at in range(0, out_ref.shape[1], 512):
+        out_ref[:hidden_channels, at : at + 512] = jnp.dot(
             weight_ref[...], columns[:, at : at + 512], preferred_element_type=F32
         )
 
@@ -235,7 +237,7 @@
     leaving = []
     (
         rows_ref, synthesis_ref, wide_ref, air_flux_ref, skip_ref, air_ref, place_ref, group_ref,
-        forcing_weight_ref, wet_ref, decode_ref, top_ref,
+        forcing_weight_ref, decode_ref, far_ref, near_ref,
     ) = held
     moves = list(zip(sources, held))
     ordered = moves[:4]
@@ -284,14 +286,23 @@
     columns = jnp.concatenate(
         [shifted(forcing, tap, masks[q]) for q, tap in enumerate(TAPS)], axis=0
     ).astype(BF16)
-    hidden = gelu(
-        wet_ref[...] + jnp.dot(forcing_weight_ref[...], columns, preferred_element_type=F32)
-    ).astype(BF16)
-    partial = jnp.dot(decode_ref[...], hidden, preferred_element_type=F32)
+    hidden_channels = forcing_weight_ref.shape[0]
+    split = far_ref.shape[1]
+    partials = []
+    for wet_ref, lanes in ((far_ref, slice(0, split)), (near_ref, slice(split, SPAN))):
+        hidden = gelu(
+            wet_ref[:hidden_channels, :]
+            + jnp.dot(forcing_weight_ref[...], columns[:, lanes], preferred_element_type=F32)
+        ).astype(BF16)
+        partials.append(jnp.dot(decode_ref[...], hidden, preferred_element_type=F32))
+    partial = jnp.concatenate(partials, axis=1)
+    surface = jnp.concatenate(
+        [ref[hidden_channels : hidden_channels + 1, :] for ref in (far_ref, near_ref)], axis=1
+    )
     change = jnp.zeros((1, SPAN), F32)
     for q, tap in enumerate(TAPS):
         change = change + shifted(partial[q : q + 1, :], tap, masks[q])
-    surface = top_ref[...] + change
+    surface = surface + change
     for slot in range(SLOTS):
         sst[slot : slot + 1, :] = surface[:, CELLS * slot : CELLS * (slot + 1)]
     tiles = sst[...].astype(BF16)
@@ -437,7 +448,8 @@
     offsets = patch_holder_shift[:, 0]
     earlier = jnp.tril(jnp.ones((HOME_DEV, HOME_DEV), jnp.int32), -1)
     positions = jnp.sum((offsets[:, None] == offsets[None, :]).astype(jnp.int32) * earlier, axis=1)
-    targets = offsets * CAP + positions
+    places = jnp.where(offsets >= EARLY, offsets - EARLY + 1, offsets + NEAR - EARLY)
+    targets = jnp.where(offsets == 0, 0, places) * CAP + positions
     selected = targets[None, :] == jnp.arange(SLOTS, dtype=jnp.int32)[:, None]
     depths = jnp.sum(jnp.where(selected, wet_depth_layers[None, :], 0), axis=1)
     kernel = jnp.transpose(input_to_hidden_kernel, (1, 0, 2))
@@ -482,18 +494,23 @@
         passed_along(late[at : at + CAP], "space", -(1 + at // CAP))
         for at in range(0, late.shape[0], CAP)
     ]
-    wet, top = call(
-        ocean_kernel,
-        [shape((hidden_channels, SPAN), F32), shape((1, SPAN), F32)],
-        [depths, slots[:CAP], *near, *far, state_weight],
-        SMALL,
-        [pltpu.VMEM((len(TAPS) * OCH_PAD, SPAN), BF16)],
-        limit=32,
-        specs=[pl.BlockSpec(memory_space=pltpu.SMEM)] + [WHOLE] * (NEAR + 1),
-    )
+    def wet(first, parts):
+        width = CAP * CELLS * len(parts)
+        return call(
+            functools.partial(ocean_kernel, first),
+            [shape((hidden_channels + 8, width), F32)],
+            [depths, *parts, state_weight],
+            SMALL,
+            [pltpu.VMEM((len(TAPS) * OCH_PAD, width), BF16)],
+            limit=32,
+            specs=[pl.BlockSpec(memory_space=pltpu.SMEM)] + [WHOLE] * (len(parts) + 1),
+        )
+
+    wet_far = wet(0, [slots[:CAP], *far])
+    wet_near = wet(CAP * (len(far) + 1), near)
     operands = [
-        returned, synthesis, wide, air_flux, skip, air, place, group, forcing_weight, wet,
-        decode_weight, top,
+        returned, synthesis, wide, air_flux, skip, air, place, group, forcing_weight,
+        decode_weight, wet_far, wet_near,
     ]
     updated, tiles = call(
         surface_kernel,

time: 140 us -> 140 us (level)
    ppermute x7, waiting for transfers between devices: 19.3 us -> 16.7 us  [passed_along(): lax.ppermute(value, axis, [(i, (i + by) % devices) for i in range(devices)])]
    all_to_all x1, waiting for transfers between devices: 5.36 us -> 7.2 us  [shards(): lax.all_to_all(filtered, 'space', split_axis=0, concat_axis=0, tiled=True)]
    pallas_call x7 -> x8, Pallas kernels: 25.8 us -> 26.5 us  [call(): pl.pallas_call(kernel, out_shape=outs if len(outs) > 1 else outs[0], in_s...]
where the time goes in v8:
time: 140 us; the launch traced here: 139 us
  starting transfers between devices  54.8 us (39%)
  waiting for transfers between devices  47.1 us (34%)
  Pallas kernels  26.5 us (19%)
  local copies, waits for them, and re-layouts  5.68 us (4%)
  other arithmetic  4.27 us (3%)
    ppermute x7, starting transfers between devices, passed_along(): lax.ppermute(value, axis, [(i, (i + by) % devices) for i in range(devices)])  26.5 us
    pallas_call x8, Pallas kernels, call(): pl.pallas_call(kernel, out_shape=outs if len(outs) > 1 else outs[0], in_s...  26.5 us
    all_to_all x1, waiting for transfers between devices, shards(): lax.all_to_all(spectra, 'space', split_axis=0, concat_axis=0, tiled=True)  21.1 us
    all_to_all x1, starting transfers between devices, shards(): lax.all_to_all(spectra, 'space', split_axis=0, concat_axis=0, tiled=True)  16.9 us
    ppermute x7, waiting for transfers between devices, passed_along(): lax.ppermute(value, axis, [(i, (i + by) % devices) for i in range(devices)])  16.7 us
    all_to_all x1, waiting for transfers between devices, shards(): lax.all_to_all(filtered, 'space', split_axis=0, concat_axis=0, tiled=True)  7.2 us
    all_to_all x1, starting transfers between devices, shards(): lax.all_to_all(tiles, 'member', split_axis=0, concat_axis=0, tiled=True)  6.9 us
    all_to_all x1, starting transfers between devices, shards(): lax.all_to_all(filtered, 'space', split_axis=0, concat_axis=0, tiled=True)  4.47 us
  transfers between devices with their start and end apart: 10, of which 4 were waited for; matrix products, arithmetic and copies ran while one was open for 5% of the time, Pallas kernels for 10%

profile of v8, /device:TPU:1, one launch (start us, length us, event | category | flops | bytes accessed | tf_op | source)
XLA Modules:
  0.0 139.4 jit_solution(1221631017125195809)
XLA Ops:
  0.6 0.0 copy-start.6
  0.6 0.0 copy-start.11
  0.7 0.0 copy-start.7
  0.7 0.0 copy-start.9
  0.7 4.7 %shard_map.194 = bf16[32,32,384]{2,1,0:T(8,128)(2,1)} custom-call(bf16[4,360,384]{2,1,0:T(8,128)(2,1)} %bitcast.54, f32[384]{0:T(512)} %scale_ref.3, bf16[256,360]{1,0:T(8,128)(2,1)} %constant.115.clone.table_any), custom_call_target="tpu_custom_call" | custom-call | flops 283115520 | bytes 2078208 | tf_op jit(solution)/shard_map/pallas_call | solution.py:366
  5.3 0.0 copy-start.3
  5.4 16.9 %all-to-all-start = ((bf16[32,32,384]{2,1,0:T(8,128)(2,1)}), bf16[32,32,384]{2,1,0:T(8,128)(2,1)S(1)}, u32[]{:S(2)}, u32[]{:S(2)}) async-start(bf16[32,32,384]{2,1,0:T(8,128)(2,1)} %shard_map.194), calls=%async_computation | async-start | bytes 1572864 | tf_op jit(solution)/shard_map/all_to_all | solution.py:425
  22.3 0.0 copy-done.6
  22.3 0.2 fusion.10
  22.5 4.8 %collective-permute-start = (bf16[2,76,128]{2,1,0:T(8,128)(2,1)S(1)}, bf16[2,76,128]{2,1,0:T(8,128)(2,1)S(1)}, u32[]{:S(2)}, u32[]{:S(2)}) collective-permute-start(bf16[2,76,128]{2,1,0:T(8,128)(2,1)S(1)} %bitcast.66), channel_id=1, source_target_pairs={{0,29},{1,30},{2,31},{3,0},{4,1},{5,2},{6,3},{7,4},{8,5},{9,6},{10... | collective-permute-start | bytes 116744 | tf_op jit(solution)/shard_map/ppermute | solution.py:36
  27.3 4.0 %collective-permute-start.1 = (bf16[2,76,128]{2,1,0:T(8,128)(2,1)S(1)}, bf16[2,76,128]{2,1,0:T(8,128)(2,1)S(1)}, u32[]{:S(2)}, u32[]{:S(2)}) collective-permute-start(bf16[2,76,128]{2,1,0:T(8,128)(2,1)S(1)} %bitcast.65), channel_id=1, source_target_pairs={{0,28},{1,29},{2,30},{3,31},{4,0},{5,1},{6,2},{7,3},{8,4},{9,5},{1... | collective-permute-start | bytes 116744 | tf_op jit(solution)/shard_map/ppermute | solution.py:36
  31.3 6.4 %collective-permute-start.2 = (bf16[2,76,128]{2,1,0:T(8,128)(2,1)S(1)}, bf16[2,76,128]{2,1,0:T(8,128)(2,1)S(1)}, u32[]{:S(2)}, u32[]{:S(2)}) collective-permute-start(bf16[2,76,128]{2,1,0:T(8,128)(2,1)S(1)} %bitcast.62), channel_id=1, source_target_pairs={{0,27},{1,28},{2,29},{3,30},{4,31},{5,0},{6,1},{7,2},{8,3},{9,4},{... | collective-permute-start | bytes 116744 | tf_op jit(solution)/shard_map/ppermute | solution.py:36
  37.7 4.0 %collective-permute-start.3 = (bf16[2,76,128]{2,1,0:T(8,128)(2,1)S(1)}, bf16[2,76,128]{2,1,0:T(8,128)(2,1)S(1)}, u32[]{:S(2)}, u32[]{:S(2)}) collective-permute-start(bf16[2,76,128]{2,1,0:T(8,128)(2,1)S(1)} %bitcast.63), channel_id=1, source_target_pairs={{0,26},{1,27},{2,28},{3,29},{4,30},{5,31},{6,0},{7,1},{8,2},{9,3},... | collective-permute-start | bytes 116744 | tf_op jit(solution)/shard_map/ppermute | solution.py:36
  41.7 2.4 %collective-permute-start.4 = (bf16[2,76,128]{2,1,0:T(8,128)(2,1)S(1)}, bf16[2,76,128]{2,1,0:T(8,128)(2,1)S(1)}, u32[]{:S(2)}, u32[]{:S(2)}) collective-permute-start(bf16[2,76,128]{2,1,0:T(8,128)(2,1)S(1)} %bitcast.64), channel_id=1, source_target_pairs={{0,25},{1,26},{2,27},{3,28},{4,29},{5,30},{6,31},{7,0},{8,1},{9,2}... | collective-permute-start | bytes 116744 | tf_op jit(solution)/shard_map/ppermute | solution.py:36
  44.2 0.0 copy-start.10
  44.2 0.0 copy-start.5
  44.3 0.0 copy-done.11
  44.3 0.2 select_reduce_fusion.3
  44.5 0.1 copy.41
  44.6 0.0 copy-done.7
  44.6 0.1 select_reduce_fusion
  44.7 0.0 copy-done.9
  44.7 0.1 select_reduce_fusion.1
  44.8 1.0 constant_dynamic-slice_fusion
  45.8 21.1 %all-to-all-done.x_ref = bf16[32,32,384]{2,1,0:T(8,128)(2,1)S(1)} async-done(((bf16[32,32,384]{2,1,0:T(8,128)(2,1)}), bf16[32,32,384]{2,1,0:T(8,128)(2,1)S(1)}, u32[]{:S(2)}, u32[]{:S(2)}) %all-to-all-start) | async-done | bytes 786464 | tf_op jit(solution)/shard_map/all_to_all | solution.py:425
  66.9 0.0 copy-done.3
  66.9 1.8 %shard_map.195 = bf16[32,32,384]{2,1,0:T(8,128)(2,1)} custom-call(bf16[32,32,384]{2,1,0:T(8,128)(2,1)S(1)} %all-to-all-done.x_ref, bf16[4,128,128]{2,1,0:T(8,128)(2,1)S(1)} %get-tuple-element.29.forward_ref, bf16[4,128,128]{2,1,0:T(8,128)(2,1)S(1)} %get-tuple-element.28.backward_ref, f32[128,384]{1,0:T(8,128)S(1)} %copy-done.3), custom_call_target="tpu_custom_call" | custom-call | flops 201326592 | bytes 2031616 | tf_op jit(solution)/shard_map/pallas_call | solution.py:366
  68.7 4.5 %all-to-all-start.1 = ((bf16[32,32,384]{2,1,0:T(8,128)(2,1)}), bf16[32,32,384]{2,1,0:T(8,128)(2,1)S(1)}, u32[]{:S(2)}, u32[]{:S(2)}) async-start(bf16[32,32,384]{2,1,0:T(8,128)(2,1)} %shard_map.195), calls=%async_computation.1 | async-start | bytes 1572864 | tf_op jit(solution)/shard_map/all_to_all | solution.py:492
  73.2 0.0 copy-done.10
  73.2 0.0 copy-done.5
  73.3 1.0 fusion.1.cell_any.cell_ref
  74.2 1.0 compare_convert_fusion.slot_any
  75.2 0.0 copy-done.12
  75.2 0.1 slice_select_fusion
  75.4 0.7 multiply_add_fusion.refs_7_
  76.0 0.9 fusion.refs_6_
  77.0 0.0 collective-permute-done.refs_1_
  77.0 0.2 collective-permute-start.5
  77.2 0.0 collective-permute-done.1.refs_2_
  77.2 4.7 %collective-permute-start.6 = (bf16[2,76,128]{2,1,0:T(8,128)(2,1)S(1)}, bf16[2,76,128]{2,1,0:T(8,128)(2,1)S(1)}, u32[]{:S(2)}, u32[]{:S(2)}) collective-permute-start(bf16[2,76,128]{2,1,0:T(8,128)(2,1)S(1)} %get-tuple-element.22), channel_id=1, source_target_pairs={{0,30},{1,31},{2,0},{3,1},{4,2},{5,3},{6,4},{7,5},{8,6},{9,7},{10,... | collective-permute-start | bytes 116744 | tf_op jit(solution)/shard_map/ppermute | solution.py:36
  81.9 0.0 copy-done.13
  81.9 0.1 select_reduce_fusion.2.depth_ref
  82.0 5.9 %shard_map.196 = (f32[4,360,384]{2,1,0:T(8,128)}, f32[32,360]{1,0:T(8,128)}, bf16[384,512]{1,0:T(8,128)(2,1)}) custom-call(bf16[4,360,384]{2,1,0:T(8,128)(2,1)} %bitcast.55, f32[384]{0:T(512)} %scale_ref.3, bf16[384,384]{1,0:T(8,128)(2,1)} %bypass_ref.1, bf16[384,384]{1,0:T(8,128)(2,1)} %exit_ref.1, bf16[8,384]{1,0:T(8,128)(2,1)} %bitcast.69), custom_call_target="tpu_custom_call" | custom-call | flops 1024 | bytes 1024 | tf_op jit(solution)/shard_map/pallas_call | solution.py:366
  88.0 0.2 copy.48.refs_6_.refs_2_
  88.2 0.7 copy.50.refs_8_
  88.9 0.0 copy-done.8
  88.9 0.6 pad.8.refs_9_
  89.5 0.0 collective-permute-done.2.refs_3_
  89.5 0.0 collective-permute-done.3.refs_4_
  89.5 0.0 collective-permute-done.4.refs_5_
  89.5 1.5 %shard_map.197.refs_10_ = f32[208,1536]{1,0:T(8,128)S(1)} custom-call(s32[16]{0:T(128)S(1)} %select_reduce_fusion.2.depth_ref, bf16[2,76,128]{2,1,0:T(8,128)(2,1)S(1)} %bitcast.53, bf16[2,76,128]{2,1,0:T(8,128)(2,1)S(1)} %collective-permute-done.refs_1_, bf16[2,76,128]{2,1,0:T(8,128)(2,1)S(1)} %collective-permute-done.1.refs_2_, ...), custom_call_target="tpu_custom_call" | custom-call | flops 1024 | bytes 1024 | tf_op jit(solution)/shard_map/pallas_call | solution.py:366
  91.0 0.0 copy-start
  91.0 1.1 copy-done
  92.1 16.7 %collective-permute-done.5.refs_0_ = bf16[2,76,128]{2,1,0:T(8,128)(2,1)S(1)} collective-permute-done((bf16[2,76,128]{2,1,0:T(8,128)(2,1)S(1)}, bf16[2,76,128]{2,1,0:T(8,128)(2,1)S(1)}, u32[]{:S(2)}, u32[]{:S(2)}) %collective-permute-start.5) | collective-permute-done | bytes 38944 | tf_op jit(solution)/shard_map/ppermute | solution.py:36
  108.8 0.0 collective-permute-done.6.refs_1_
  108.8 1.1 shard_map.198.refs_11_
  109.8 0.8 copy-done.2
  110.6 7.2 %all-to-all-done.1.refs_0_ = bf16[32,32,384]{2,1,0:T(8,128)(2,1)S(1)} async-done(((bf16[32,32,384]{2,1,0:T(8,128)(2,1)}), bf16[32,32,384]{2,1,0:T(8,128)(2,1)S(1)}, u32[]{:S(2)}, u32[]{:S(2)}) %all-to-all-start.1) | async-done | bytes 786464 | tf_op jit(solution)/shard_map/all_to_all | solution.py:492
  117.8 0.9 copy-done.4
  118.7 6.4 %shard_map.199 = (f32[4,360,384]{2,1,0:T(8,128)}, bf16[16,16,128]{2,1,0:T(8,128)(2,1)}) custom-call(bf16[32,32,384]{2,1,0:T(8,128)(2,1)} %copy-done.4, bf16[360,256]{1,0:T(8,128)(2,1)} %constant.116.clone.refs_1_, bf16[384,512]{1,0:T(8,128)(2,1)} %get-tuple-element.10.refs_2_, f32[32,360]{1,0:T(8,128)} %get-tuple-element.11.refs_3_, ...), custom_call_target="tpu_custom_call" | custom-call | flops 707788800 | bytes 9276800 | tf_op jit(solution)/shard_map/pallas_call | solution.py:366
  125.1 6.9 %all-to-all-start.2 = ((bf16[16,16,128]{2,1,0:T(8,128)(2,1)}), bf16[16,16,128]{2,1,0:T(8,128)(2,1)S(1)}, u32[]{:S(2)}, u32[]{:S(2)}) async-start(bf16[16,16,128]{2,1,0:T(8,128)(2,1)} %get-tuple-element.15.tiles_ref), calls=%async_computation.2 | async-start | bytes 131072 | tf_op jit(solution)/shard_map/all_to_all | solution.py:531
  132.0 4.4 %shard_map.200 = bf16[4,360,384]{2,1,0:T(8,128)(2,1)} custom-call(f32[4,360,384]{2,1,0:T(8,128)} %get-tuple-element.14.updated_any, bf16[16,16,128]{2,1,0:T(8,128)(2,1)} %get-tuple-element.15.tiles_ref, bf16[4,360,128]{2,1,0:T(8,128)(2,1)} %fusion.1.cell_any.cell_ref, bf16[4,360,48]{2,1,0:T(8,128)(2,1)} %compare_convert_fusion.slot_any, f32[384]{0:T(512)} %imprint_ref.1), custom_call_target="tpu_custom_call" | custom-call | flops 283115520 | bytes 3891712 | tf_op jit(solution)/shard_map/pallas_call | solution.py:366
  136.4 2.1 %all-to-all-done.2.tiles_ref = bf16[16,16,128]{2,1,0:T(8,128)(2,1)S(1)} async-done(((bf16[16,16,128]{2,1,0:T(8,128)(2,1)}), bf16[16,16,128]{2,1,0:T(8,128)(2,1)S(1)}, u32[]{:S(2)}, u32[]{:S(2)}) %all-to-all-start.2) | async-done | bytes 65568 | tf_op jit(solution)/shard_map/all_to_all | solution.py:531
  138.5 0.9 shard_map.201
  (27 shorter events, 0.2 us)
Async XLA Ops:
  0.6 21.6 %copy-start.6 = (bf16[1,16,76,128]{3,1,2,0:T(8,128)(2,1)S(1)}, bf16[1,16,76,128]{3,1,2,0:T(8,128)(2,1)}, u32[]{:S(2)}) copy-start(bf16[1,16,76,128]{3,1,2,0:T(8,128)(2,1)} %param.27) | copy-start | bytes 933892
  0.6 43.6 %copy-start.11 = (s32[14,1]{0,1:T(1,128)S(1)}, s32[14,1]{0,1:T(1,128)}, u32[]{:S(2)}) copy-start(s32[14,1]{0,1:T(1,128)} %param.32) | copy-start | bytes 172
  0.7 43.9 %copy-start.7 = (s32[14,128]{1,0:T(8,128)S(1)}, s32[14,128]{1,0:T(8,128)}, u32[]{:S(2)}) copy-start(s32[14,128]{1,0:T(8,128)} %param.30) | copy-start | bytes 21508
  0.7 44.0 %copy-start.9 = (s32[4,360]{1,0:T(4,128)S(1)}, s32[4,360]{1,0:T(4,128)}, u32[]{:S(2)}) copy-start(s32[4,360]{1,0:T(4,128)} %param.31) | copy-start | bytes 17284
  5.3 61.6 %copy-start.3 = (f32[128,384]{1,0:T(8,128)S(1)}, f32[128,384]{1,0:T(8,128)}, u32[]{:S(2)}) copy-start(f32[128,384]{1,0:T(8,128)} %gains_ref.1) | copy-start | bytes 589828
  5.4 61.6 %all-to-all-start = ((bf16[32,32,384]{2,1,0:T(8,128)(2,1)}), bf16[32,32,384]{2,1,0:T(8,128)(2,1)S(1)}, u32[]{:S(2)}, u32[]{:S(2)}) async-start(bf16[32,32,384]{2,1,0:T(8,128)(2,1)} %shard_map.194), calls=%async_computation | async-start | bytes 1572864 | tf_op jit(solution)/shard_map/all_to_all | solution.py:425
  22.5 54.5 %collective-permute-start = (bf16[2,76,128]{2,1,0:T(8,128)(2,1)S(1)}, bf16[2,76,128]{2,1,0:T(8,128)(2,1)S(1)}, u32[]{:S(2)}, u32[]{:S(2)}) collective-permute-start(bf16[2,76,128]{2,1,0:T(8,128)(2,1)S(1)} %bitcast.66), channel_id=1, source_target_pairs={{0,29},{1,30},{2,31},{3,0},{4,1},{5,2},{6,3},{7,4},{8,5},{9,6},{10... | collective-permute-start | bytes 116744 | tf_op jit(solution)/shard_map/ppermute | solution.py:36
  27.3 49.9 %collective-permute-start.1 = (bf16[2,76,128]{2,1,0:T(8,128)(2,1)S(1)}, bf16[2,76,128]{2,1,0:T(8,128)(2,1)S(1)}, u32[]{:S(2)}, u32[]{:S(2)}) collective-permute-start(bf16[2,76,128]{2,1,0:T(8,128)(2,1)S(1)} %bitcast.65), channel_id=1, source_target_pairs={{0,28},{1,29},{2,30},{3,31},{4,0},{5,1},{6,2},{7,3},{8,4},{9,5},{1... | collective-permute-start | bytes 116744 | tf_op jit(solution)/shard_map/ppermute | solution.py:36
  31.3 58.2 %collective-permute-start.2 = (bf16[2,76,128]{2,1,0:T(8,128)(2,1)S(1)}, bf16[2,76,128]{2,1,0:T(8,128)(2,1)S(1)}, u32[]{:S(2)}, u32[]{:S(2)}) collective-permute-start(bf16[2,76,128]{2,1,0:T(8,128)(2,1)S(1)} %bitcast.62), channel_id=1, source_target_pairs={{0,27},{1,28},{2,29},{3,30},{4,31},{5,0},{6,1},{7,2},{8,3},{9,4},{... | collective-permute-start | bytes 116744 | tf_op jit(solution)/shard_map/ppermute | solution.py:36
  37.7 51.8 %collective-permute-start.3 = (bf16[2,76,128]{2,1,0:T(8,128)(2,1)S(1)}, bf16[2,76,128]{2,1,0:T(8,128)(2,1)S(1)}, u32[]{:S(2)}, u32[]{:S(2)}) collective-permute-start(bf16[2,76,128]{2,1,0:T(8,128)(2,1)S(1)} %bitcast.63), channel_id=1, source_target_pairs={{0,26},{1,27},{2,28},{3,29},{4,30},{5,31},{6,0},{7,1},{8,2},{9,3},... | collective-permute-start | bytes 116744 | tf_op jit(solution)/shard_map/ppermute | solution.py:36
  41.7 47.8 %collective-permute-start.4 = (bf16[2,76,128]{2,1,0:T(8,128)(2,1)S(1)}, bf16[2,76,128]{2,1,0:T(8,128)(2,1)S(1)}, u32[]{:S(2)}, u32[]{:S(2)}) collective-permute-start(bf16[2,76,128]{2,1,0:T(8,128)(2,1)S(1)} %bitcast.64), channel_id=1, source_target_pairs={{0,25},{1,26},{2,27},{3,28},{4,29},{5,30},{6,31},{7,0},{8,1},{9,2}... | collective-permute-start | bytes 116744 | tf_op jit(solution)/shard_map/ppermute | solution.py:36
  44.2 29.0 %copy-start.10 = (s32[4,360]{1,0:T(4,128)S(1)}, s32[4,360]{1,0:T(4,128)}, u32[]{:S(2)}) copy-start(s32[4,360]{1,0:T(4,128)} %param.20) | copy-start | bytes 17284
  44.2 29.0 %copy-start.5 = (bf16[9,200,84]{1,2,0:T(8,128)(2,1)S(1)}, bf16[9,200,84]{1,2,0:T(8,128)(2,1)}, u32[]{:S(2)}) copy-start(bf16[9,200,84]{1,2,0:T(8,128)(2,1)} %param.28) | copy-start | bytes 907204
  66.9 8.3 %copy-start.12 = (pred[80]{0:T(512)(128)(4,1)S(1)}, pred[80]{0:T(512)(128)(4,1)}, u32[]{:S(2)}) copy-start(pred[80]{0:T(512)(128)(4,1)} %constant.112.clone.1) | copy-start | bytes 244
  68.7 13.3 %copy-start.13 = (s32[14]{0:T(128)S(1)}, s32[14]{0:T(128)}, u32[]{:S(2)}) copy-start(s32[14]{0:T(128)} %param.33) | copy-start | bytes 172
  68.7 49.1 %all-to-all-start.1 = ((bf16[32,32,384]{2,1,0:T(8,128)(2,1)}), bf16[32,32,384]{2,1,0:T(8,128)(2,1)S(1)}, u32[]{:S(2)}, u32[]{:S(2)}) async-start(bf16[32,32,384]{2,1,0:T(8,128)(2,1)} %shard_map.195), calls=%async_computation.1 | async-start | bytes 1572864 | tf_op jit(solution)/shard_map/all_to_all | solution.py:492
  74.2 14.6 %copy-start.8 = (bf16[9,200]{1,0:T(8,128)(2,1)S(1)}, bf16[9,200]{1,0:T(8,128)(2,1)}, u32[]{:S(2)}) copy-start(bf16[9,200]{1,0:T(8,128)(2,1)} %param.29) | copy-start | bytes 10804
  77.0 31.8 %collective-permute-start.5 = (bf16[2,76,128]{2,1,0:T(8,128)(2,1)S(1)}, bf16[2,76,128]{2,1,0:T(8,128)(2,1)S(1)}, u32[]{:S(2)}, u32[]{:S(2)}) collective-permute-start(bf16[2,76,128]{2,1,0:T(8,128)(2,1)S(1)} %get-tuple-element.23), channel_id=1, source_target_pairs={{0,31},{1,0},{2,1},{3,2},{4,3},{5,4},{6,5},{7,6},{8,7},{9,8},{10,9... | collective-permute-start | bytes 116744 | tf_op jit(solution)/shard_map/ppermute | solution.py:36
  77.2 31.6 %collective-permute-start.6 = (bf16[2,76,128]{2,1,0:T(8,128)(2,1)S(1)}, bf16[2,76,128]{2,1,0:T(8,128)(2,1)S(1)}, u32[]{:S(2)}, u32[]{:S(2)}) collective-permute-start(bf16[2,76,128]{2,1,0:T(8,128)(2,1)S(1)} %get-tuple-element.22), channel_id=1, source_target_pairs={{0,30},{1,31},{2,0},{3,1},{4,2},{5,3},{6,4},{7,5},{8,6},{9,7},{10,... | collective-permute-start | bytes 116744 | tf_op jit(solution)/shard_map/ppermute | solution.py:36
  91.0 1.1 copy-start
  109.8 0.8 copy-start.2
  117.8 0.9 copy-start.4
  125.1 13.4 %copy-start.1 = (bf16[4,360,128]{2,1,0:T(8,128)(2,1)S(1)}, bf16[4,360,128]{2,1,0:T(8,128)(2,1)}, u32[]{:S(2)}) copy-start(bf16[4,360,128]{2,1,0:T(8,128)(2,1)} %fusion.1.cell_any.cell_ref) | copy-start | bytes 1105924
  125.1 13.4 %all-to-all-start.2 = ((bf16[16,16,128]{2,1,0:T(8,128)(2,1)}), bf16[16,16,128]{2,1,0:T(8,128)(2,1)S(1)}, u32[]{:S(2)}, u32[]{:S(2)}) async-start(bf16[16,16,128]{2,1,0:T(8,128)(2,1)} %get-tuple-element.15.tiles_ref), calls=%async_computation.2 | async-start | bytes 131072 | tf_op jit(solution)/shard_map/all_to_all | solution.py:531

commit v9 on v8

--- a/solution.py
+++ b/solution.py
@@ -159,8 +159,8 @@
 
 
 def local_kernel(
-    air_any, scale_ref, bypass_ref, exit_ref, exchange_ref, skip_ref, flux_ref, wide_ref,
-    air_ref, sems,
+    air_any, scale_ref, bypass_ref, exit_ref, exchange_ref, synthesis_ref, place_ref,
+    skip_ref, pack_ref, air_ref, sems,
 ):
     rows = air_ref.shape[0]
     copies = begin([(air_any.at[j], air_ref.at[j]) for j in range(rows)], sems)
@@ -172,16 +172,23 @@
     )
     high = through.astype(BF16)
     low = (through - high.astype(F32)).astype(BF16)
-    wide_ref[:, :channels] = exit_ref[...]
-    wide_ref[:, channels:] = jnp.concatenate(
+    pack_ref[:384, :channels] = exit_ref[...]
+    pack_ref[:384, channels:] = jnp.concatenate(
         [high.astype(F32), low.astype(F32), jnp.zeros((channels, 128 - 2 * FC), F32)], axis=1
     ).astype(BF16)
+    pack_ref[384:768, :] = jnp.zeros((384, 512), BF16)
+    longitudes, orders = synthesis_ref.shape
+    pack_ref[384 : 384 + longitudes, :orders] = synthesis_ref[...]
+    for block in range(SPAN // 512):
+        pack_ref[768 + 128 * block : 896 + 128 * block, :] = place_ref[
+            :, 512 * block : 512 * (block + 1)
+        ]
     for j in range(rows):
         copies[j].wait()
         own = air_ref[j]
         normed = normalised(own.astype(F32), scale)
         skip_ref[j] = jnp.dot(normed, bypass_ref[...], preferred_element_type=F32)
-        flux_ref[FC * j : FC * (j + 1), :] = lax.dot_general(
+        skip_ref[rows, FC * j : FC * (j + 1), :longitudes] = lax.dot_general(
             exchange_ref[...], own, dims, preferred_element_type=F32
         )
 
@@ -228,38 +235,43 @@
         )
 
 
-def surface_kernel(*refs):
-    count = 12
+def surface_kernel(rows_ref, *refs):
+    count = 8
     sources, (updated_any, tiles_ref), held, (updated_ref, flux, sst, sems, out_sems) = (
         refs[:count], refs[count : count + 2], refs[count + 2 : 2 * count + 2],
         refs[2 * count + 2 :],
     )
     leaving = []
     (
-        rows_ref, synthesis_ref, wide_ref, air_flux_ref, skip_ref, air_ref, place_ref, group_ref,
-        forcing_weight_ref, decode_ref, far_ref, near_ref,
+        pack_ref, skip_ref, air_ref, group_ref, forcing_weight_ref, decode_ref, far_ref, near_ref,
     ) = held
-    moves = list(zip(sources, held))
-    ordered = moves[:4]
-    for j in range(air_ref.shape[0]):
-        ordered += [(source.at[j], target.at[j]) for source, target in moves[4:6]]
-    copies = begin(ordered + moves[6:], sems)
-    after = len(ordered)
+    pack_any, skip_any, air_any = sources[:3]
+    rows = air_ref.shape[0]
+    tables, places, fluxes = pl.ds(0, 768), pl.ds(768, 512), pl.ds(0, FC * rows)
+    ordered = [
+        (pack_any.at[tables], pack_ref.at[tables]),
+        (skip_any.at[rows, fluxes], skip_ref.at[rows, fluxes]),
+    ]
+    for j in range(rows):
+        ordered += [(skip_any.at[j], skip_ref.at[j]), (air_any.at[j], air_ref.at[j])]
+    ordered.append((pack_any.at[places], pack_ref.at[places]))
+    copies = begin(ordered + list(zip(sources, held))[3:], sems)
+    after = 2 + 2 * rows
     latitude_rows, longitudes, channels = air_ref.shape
     groups = rows_ref.shape[0]
     pairs = []
-    copies[0].wait()
     for pair in range(latitude_rows // 2):
         both = rows_ref[:, 16 * pair : 16 * (pair + 1), :].astype(F32)
         pairs.extend([both[:, :8], both[:, 8:]])
-    copies[1].wait()
+    for one in copies[:2]:
+        one.wait()
     for j in range(latitude_rows):
         own = pairs[j].reshape(8 * groups, channels).astype(BF16)
-        spectral = jnp.dot(synthesis_ref[...], own, preferred_element_type=F32)
-        for one in copies[2:6] if j == 0 else copies[4 + 2 * j : 6 + 2 * j]:
+        spectral = jnp.dot(pack_ref[384 : 384 + longitudes, : 8 * groups], own, preferred_element_type=F32)
+        for one in copies[2 + 2 * j : 4 + 2 * j]:
             one.wait()
         mixed = gelu(spectral + skip_ref[j]).astype(BF16)
-        wide = jnp.dot(mixed, wide_ref[...], preferred_element_type=F32)
+        wide = jnp.dot(mixed, pack_ref[:384, :], preferred_element_type=F32)
         updated_ref[j] = air_ref[j].astype(F32) + wide[:, :channels]
         leave = pltpu.make_async_copy(updated_ref.at[j], updated_any.at[j], out_sems.at[j])
         leave.start()
@@ -269,7 +281,11 @@
         )
         turned = jnp.transpose(narrow)
         extra = jnp.concatenate(
-            [air_flux_ref[FC * j : FC * (j + 1), :], jnp.zeros((FC, 384 - longitudes), F32)], axis=1
+            [
+                skip_ref[latitude_rows, FC * j : FC * (j + 1), :longitudes],
+                jnp.zeros((FC, 384 - longitudes), F32),
+            ],
+            axis=1,
         )
         total = turned[:FC] + turned[FC : 2 * FC] + extra
         for part in range(3):
@@ -277,7 +293,16 @@
             flux[at : at + FC, :] = total[:, 128 * part : 128 * (part + 1)]
     for one in copies[after:]:
         one.wait()
-    spread = jnp.dot(flux[...].astype(BF16), place_ref[...], preferred_element_type=F32)
+    points = flux[...].astype(BF16)
+    spread = jnp.concatenate(
+        [
+            jnp.dot(
+                points, pack_ref[768 + at : 896 + at, :], preferred_element_type=F32
+            )
+            for at in range(0, SPAN // 4, 128)
+        ],
+        axis=1,
+    )
     group = group_ref[...]
     forcing = jnp.zeros((FC, SPAN), F32)
     for at in range(3 * latitude_rows):
@@ -433,18 +458,6 @@
     first = lax.axis_index("space") * per_device
     forward = lax.dynamic_slice_in_dim(forward, first, per_device, 0)
     backward = lax.dynamic_slice_in_dim(backward, first, per_device, 0)
-    skip, air_flux, wide = call(
-        local_kernel,
-        [
-            shape(air.shape, F32),
-            shape((FC * latitude_rows, longitudes), F32),
-            shape((channels, channels + 128), BF16),
-        ],
-        [air, layernorm_scaling, bypass_factor, core_exit_factor, air_to_exchange_factor.T],
-        SMALL,
-        held([air]) + [pltpu.SemaphoreType.DMA((latitude_rows,))],
-        specs=[FAR] + [WHOLE] * 4,
-    )
     offsets = patch_holder_shift[:, 0]
     earlier = jnp.tril(jnp.ones((HOME_DEV, HOME_DEV), jnp.int32), -1)
     positions = jnp.sum((offsets[:, None] == offsets[None, :]).astype(jnp.int32) * earlier, axis=1)
@@ -463,6 +476,17 @@
     line, column = picks // longitudes, picks % longitudes
     group = column // 128 * latitude_rows + line
     place = (column % 128 == jnp.arange(128, dtype=jnp.int32)[:, None]).astype(BF16)
+    skip, pack = call(
+        local_kernel,
+        [shape((latitude_rows + 1, longitudes, channels), F32), shape((1280, 512), BF16)],
+        [
+            air, layernorm_scaling, bypass_factor, core_exit_factor, air_to_exchange_factor.T,
+            synthesis, place,
+        ],
+        SMALL,
+        held([air]) + [pltpu.SemaphoreType.DMA((latitude_rows,))],
+        specs=[FAR] + [WHOLE] * 6,
+    )
     tile = node_sea_pick // CELLS
     holder = jnp.sum(
         jnp.where(
@@ -508,24 +532,22 @@
 
     wet_far = wet(0, [slots[:CAP], *far])
     wet_near = wet(CAP * (len(far) + 1), near)
-    operands = [
-        returned, synthesis, wide, air_flux, skip, air, place, group, forcing_weight,
-        decode_weight, wet_far, wet_near,
-    ]
+    operands = [pack, skip, air, group, forcing_weight, decode_weight, wet_far, wet_near]
     updated, tiles = call(
         surface_kernel,
         [shape(air.shape, F32), shape((members, SLOTS, CELLS), BF16)],
-        operands,
+        [returned] + operands,
         2 * latitude_rows * longitudes * channels * (channels + 2 * MMAX),
         held(operands)
         + [
             pltpu.VMEM(air.shape, F32),
             pltpu.VMEM((3 * FC * latitude_rows, 128), F32),
             pltpu.VMEM((SLOTS, CELLS), F32),
-            pltpu.SemaphoreType.DMA((len(operands) + 2 * latitude_rows,)),
+            pltpu.SemaphoreType.DMA((len(operands) + 2 * latitude_rows + 1,)),
             pltpu.SemaphoreType.DMA((latitude_rows,)),
         ],
-        specs=[FAR] * len(operands),
+        limit=52,
+        specs=[WHOLE] + [FAR] * len(operands),
         out_specs=[FAR, WHOLE],
     )
     everyone = lax.all_to_all(tiles, "member", split_axis=0, concat_axis=0, tiled=True)

time: 140 us -> 139 us (level)
  local copies, waits for them, and re-layouts: 5.68 us -> 2.78 us
  waiting for transfers between devices: 47.1 us -> 49.3 us
    unnamed x35 -> x31, local copies, waits for them, and re-layouts: 2.85 us -> 1.16 us
    ppermute x7, waiting for transfers between devices: 16.7 us -> 18.1 us  [passed_along(): lax.ppermute(value, axis, [(i, (i + by) % devices) for i in range(devices)])]
  transfers between devices with their start and end apart: 10 -> 10, of which waited for: 4 -> 4; matrix products, arithmetic and copies ran while one was open for 5% -> 4% of each run, Pallas kernels for 10% -> 11%
where the time goes in v9:
time: 139 us; the launch traced here: 138 us
  starting transfers between devices  54.5 us (39%)
  waiting for transfers between devices  49.3 us (35%)
  Pallas kernels  26.6 us (19%)
  other arithmetic  3.72 us (3%)
  local copies, waits for them, and re-layouts  2.78 us (2%)
    pallas_call x8, Pallas kernels, call(): pl.pallas_call(kernel, out_shape=outs if len(outs) > 1 else outs[0], in_s...  26.6 us
    ppermute x7, starting transfers between devices, passed_along(): lax.ppermute(value, axis, [(i, (i + by) % devices) for i in range(devices)])  26.5 us
    all_to_all x1, waiting for transfers between devices, shards(): lax.all_to_all(spectra, 'space', split_axis=0, concat_axis=0, tiled=True)  21.1 us
    ppermute x7, waiting for transfers between devices, passed_along(): lax.ppermute(value, axis, [(i, (i + by) % devices) for i in range(devices)])  18.1 us
    all_to_all x1, starting transfers between devices, shards(): lax.all_to_all(spectra, 'space', split_axis=0, concat_axis=0, tiled=True)  16.8 us
    all_to_all x1, waiting for transfers between devices, shards(): lax.all_to_all(filtered, 'space', split_axis=0, concat_axis=0, tiled=True)  7.97 us
    all_to_all x1, starting transfers between devices, shards(): lax.all_to_all(tiles, 'member', split_axis=0, concat_axis=0, tiled=True)  6.9 us
    all_to_all x1, starting transfers between devices, shards(): lax.all_to_all(filtered, 'space', split_axis=0, concat_axis=0, tiled=True)  4.34 us
  transfers between devices with their start and end apart: 10, of which 4 were waited for; matrix products, arithmetic and copies ran while one was open for 4% of the time, Pallas kernels for 11%

profile of v9, /device:TPU:1, one launch (start us, length us, event | category | flops | bytes accessed | tf_op | source)
XLA Modules:
  0.0 138.1 jit_solution(8101476807334525130)
XLA Ops:
  0.6 0.0 copy-start.4
  0.6 0.0 copy-start.9
  0.7 0.0 copy-start.5
  0.7 0.0 copy-start.7
  0.7 0.0 copy-start.2
  0.7 4.7 %shard_map.194 = bf16[32,32,384]{2,1,0:T(8,128)(2,1)} custom-call(bf16[4,360,384]{2,1,0:T(8,128)(2,1)} %bitcast.54, f32[384]{0:T(512)} %scale_ref.3, bf16[256,360]{1,0:T(8,128)(2,1)} %constant.115.clone.table_any), custom_call_target="tpu_custom_call" | custom-call | flops 283115520 | bytes 2078208 | tf_op jit(solution)/shard_map/pallas_call | solution.py:391
  5.4 16.8 %all-to-all-start = ((bf16[32,32,384]{2,1,0:T(8,128)(2,1)}), bf16[32,32,384]{2,1,0:T(8,128)(2,1)S(1)}, u32[]{:S(2)}, u32[]{:S(2)}) async-start(bf16[32,32,384]{2,1,0:T(8,128)(2,1)} %shard_map.194), calls=%async_computation | async-start | bytes 1572864 | tf_op jit(solution)/shard_map/all_to_all | solution.py:450
  22.1 0.0 copy-done.4
  22.1 0.0 copy-start.8
  22.2 0.0 copy-start.3
  22.2 0.2 fusion.10
  22.4 4.8 %collective-permute-start = (bf16[2,76,128]{2,1,0:T(8,128)(2,1)S(1)}, bf16[2,76,128]{2,1,0:T(8,128)(2,1)S(1)}, u32[]{:S(2)}, u32[]{:S(2)}) collective-permute-start(bf16[2,76,128]{2,1,0:T(8,128)(2,1)S(1)} %bitcast.66), channel_id=1, source_target_pairs={{0,29},{1,30},{2,31},{3,0},{4,1},{5,2},{6,3},{7,4},{8,5},{9,6},{10... | collective-permute-start | bytes 116744 | tf_op jit(solution)/shard_map/ppermute | solution.py:36
  27.2 4.0 %collective-permute-start.1 = (bf16[2,76,128]{2,1,0:T(8,128)(2,1)S(1)}, bf16[2,76,128]{2,1,0:T(8,128)(2,1)S(1)}, u32[]{:S(2)}, u32[]{:S(2)}) collective-permute-start(bf16[2,76,128]{2,1,0:T(8,128)(2,1)S(1)} %bitcast.65), channel_id=1, source_target_pairs={{0,28},{1,29},{2,30},{3,31},{4,0},{5,1},{6,2},{7,3},{8,4},{9,5},{1... | collective-permute-start | bytes 116744 | tf_op jit(solution)/shard_map/ppermute | solution.py:36
  31.2 6.4 %collective-permute-start.2 = (bf16[2,76,128]{2,1,0:T(8,128)(2,1)S(1)}, bf16[2,76,128]{2,1,0:T(8,128)(2,1)S(1)}, u32[]{:S(2)}, u32[]{:S(2)}) collective-permute-start(bf16[2,76,128]{2,1,0:T(8,128)(2,1)S(1)} %bitcast.62), channel_id=1, source_target_pairs={{0,27},{1,28},{2,29},{3,30},{4,31},{5,0},{6,1},{7,2},{8,3},{9,4},{... | collective-permute-start | bytes 116744 | tf_op jit(solution)/shard_map/ppermute | solution.py:36
  37.6 0.0 copy-start.10
  37.6 4.0 %collective-permute-start.3 = (bf16[2,76,128]{2,1,0:T(8,128)(2,1)S(1)}, bf16[2,76,128]{2,1,0:T(8,128)(2,1)S(1)}, u32[]{:S(2)}, u32[]{:S(2)}) collective-permute-start(bf16[2,76,128]{2,1,0:T(8,128)(2,1)S(1)} %bitcast.63), channel_id=1, source_target_pairs={{0,26},{1,27},{2,28},{3,29},{4,30},{5,31},{6,0},{7,1},{8,2},{9,3},... | collective-permute-start | bytes 116744 | tf_op jit(solution)/shard_map/ppermute | solution.py:36
  41.7 2.4 %collective-permute-start.4 = (bf16[2,76,128]{2,1,0:T(8,128)(2,1)S(1)}, bf16[2,76,128]{2,1,0:T(8,128)(2,1)S(1)}, u32[]{:S(2)}, u32[]{:S(2)}) collective-permute-start(bf16[2,76,128]{2,1,0:T(8,128)(2,1)S(1)} %bitcast.64), channel_id=1, source_target_pairs={{0,25},{1,26},{2,27},{3,28},{4,29},{5,30},{6,31},{7,0},{8,1},{9,2}... | collective-permute-start | bytes 116744 | tf_op jit(solution)/shard_map/ppermute | solution.py:36
  44.2 0.0 copy-done.9
  44.2 0.2 select_reduce_fusion.3
  44.4 0.1 copy.41
  44.5 0.0 copy-done.5
  44.5 0.1 select_reduce_fusion
  44.6 0.0 copy-done.7
  44.6 0.1 select_reduce_fusion.1
  44.7 1.0 constant_dynamic-slice_fusion
  45.7 21.1 %all-to-all-done.x_ref = bf16[32,32,384]{2,1,0:T(8,128)(2,1)S(1)} async-done(((bf16[32,32,384]{2,1,0:T(8,128)(2,1)}), bf16[32,32,384]{2,1,0:T(8,128)(2,1)S(1)}, u32[]{:S(2)}, u32[]{:S(2)}) %all-to-all-start) | async-done | bytes 786464 | tf_op jit(solution)/shard_map/all_to_all | solution.py:450
  66.8 0.0 copy-done.2
  66.8 1.7 %shard_map.195 = bf16[32,32,384]{2,1,0:T(8,128)(2,1)} custom-call(bf16[32,32,384]{2,1,0:T(8,128)(2,1)S(1)} %all-to-all-done.x_ref, bf16[4,128,128]{2,1,0:T(8,128)(2,1)S(1)} %get-tuple-element.27.forward_ref, bf16[4,128,128]{2,1,0:T(8,128)(2,1)S(1)} %get-tuple-element.26.backward_ref, f32[128,384]{1,0:T(8,128)S(1)} %copy-done.2), custom_call_target="tpu_custom_call" | custom-call | flops 201326592 | bytes 2031616 | tf_op jit(solution)/shard_map/pallas_call | solution.py:391
  68.5 4.3 %all-to-all-start.1 = ((bf16[32,32,384]{2,1,0:T(8,128)(2,1)}), bf16[32,32,384]{2,1,0:T(8,128)(2,1)S(1)}, u32[]{:S(2)}, u32[]{:S(2)}) async-start(bf16[32,32,384]{2,1,0:T(8,128)(2,1)} %shard_map.195), calls=%async_computation.1 | async-start | bytes 1572864 | tf_op jit(solution)/shard_map/all_to_all | solution.py:516
  72.9 0.0 copy-done.8
  73.0 0.0 copy-done.3
  73.0 0.0 copy-start.6
  73.0 1.0 fusion.1.cell_any.cell_ref
  74.0 1.1 compare_convert_fusion.slot_any
  75.1 0.0 copy-done.10
  75.1 0.1 slice_select_fusion
  75.2 0.1 multiply_add_fusion.refs_3_
  75.3 0.9 fusion.place_ref
  76.2 0.0 collective-permute-done.refs_1_
  76.2 0.2 collective-permute-start.5
  76.4 0.0 collective-permute-done.1.refs_2_
  76.4 4.7 %collective-permute-start.6 = (bf16[2,76,128]{2,1,0:T(8,128)(2,1)S(1)}, bf16[2,76,128]{2,1,0:T(8,128)(2,1)S(1)}, u32[]{:S(2)}, u32[]{:S(2)}) collective-permute-start(bf16[2,76,128]{2,1,0:T(8,128)(2,1)S(1)} %get-tuple-element.20), channel_id=1, source_target_pairs={{0,30},{1,31},{2,0},{3,1},{4,2},{5,3},{6,4},{7,5},{8,6},{9,7},{10,... | collective-permute-start | bytes 116744 | tf_op jit(solution)/shard_map/ppermute | solution.py:36
  81.1 0.0 copy-done.11
  81.2 0.1 select_reduce_fusion.2.depth_ref
  81.3 6.3 %shard_map.196 = (f32[5,360,384]{2,1,0:T(8,128)}, bf16[1280,512]{1,0:T(8,128)(2,1)}) custom-call(bf16[4,360,384]{2,1,0:T(8,128)(2,1)} %bitcast.55, f32[384]{0:T(512)} %scale_ref.3, bf16[384,384]{1,0:T(8,128)(2,1)} %bypass_ref.1, bf16[384,384]{1,0:T(8,128)(2,1)} %exit_ref.1, bf16[8,384]{1,0:T(8,128)(2,1)} %bitcast.69, ...), custom_call_target="tpu_custom_call" | custom-call | flops 1024 | bytes 1024 | tf_op jit(solution)/shard_map/pallas_call | solution.py:391
  87.5 0.2 copy.48.refs_6_.refs_2_
  87.7 0.1 copy.50.refs_4_
  87.8 0.0 copy-done.6
  87.8 0.0 collective-permute-done.2.refs_3_
  87.9 0.0 collective-permute-done.3.refs_4_
  87.9 0.0 collective-permute-done.4.refs_5_
  87.9 1.5 %shard_map.197.refs_6_ = f32[208,1536]{1,0:T(8,128)S(1)} custom-call(s32[16]{0:T(128)S(1)} %select_reduce_fusion.2.depth_ref, bf16[2,76,128]{2,1,0:T(8,128)(2,1)S(1)} %bitcast.53, bf16[2,76,128]{2,1,0:T(8,128)(2,1)S(1)} %collective-permute-done.refs_1_, bf16[2,76,128]{2,1,0:T(8,128)(2,1)S(1)} %collective-permute-done.1.refs_2_, ...), custom_call_target="tpu_custom_call" | custom-call | flops 1024 | bytes 1024 | tf_op jit(solution)/shard_map/pallas_call | solution.py:391
  89.4 0.0 copy-start
  89.4 1.0 copy-done
  90.4 18.1 %collective-permute-done.5.refs_0_ = bf16[2,76,128]{2,1,0:T(8,128)(2,1)S(1)} collective-permute-done((bf16[2,76,128]{2,1,0:T(8,128)(2,1)S(1)}, bf16[2,76,128]{2,1,0:T(8,128)(2,1)S(1)}, u32[]{:S(2)}, u32[]{:S(2)}) %collective-permute-start.5) | collective-permute-done | bytes 38944 | tf_op jit(solution)/shard_map/ppermute | solution.py:36
  108.5 0.0 collective-permute-done.6.refs_1_
  108.5 1.1 shard_map.198.refs_7_
  109.6 8.0 %all-to-all-done.1.rows_ref = bf16[32,32,384]{2,1,0:T(8,128)(2,1)S(1)} async-done(((bf16[32,32,384]{2,1,0:T(8,128)(2,1)}), bf16[32,32,384]{2,1,0:T(8,128)(2,1)S(1)}, u32[]{:S(2)}, u32[]{:S(2)}) %all-to-all-start.1) | async-done | bytes 786464 | tf_op jit(solution)/shard_map/all_to_all | solution.py:516
  117.6 6.2 %shard_map.199 = (f32[4,360,384]{2,1,0:T(8,128)}, bf16[16,16,128]{2,1,0:T(8,128)(2,1)}) custom-call(bf16[32,32,384]{2,1,0:T(8,128)(2,1)S(1)} %all-to-all-done.1.rows_ref, bf16[1280,512]{1,0:T(8,128)(2,1)} %get-tuple-element.9.refs_0_, f32[5,360,384]{2,1,0:T(8,128)} %get-tuple-element.10.refs_1_, bf16[4,360,384]{2,1,0:T(8,128)(2,1)} %bitcast.56, ...), custom_call_target="tpu_custom_call" | custom-call | flops 707788800 | bytes 9992576 | tf_op jit(solution)/shard_map/pallas_call | solution.py:391
  123.7 0.0 copy-start.1
  123.8 6.9 %all-to-all-start.2 = ((bf16[16,16,128]{2,1,0:T(8,128)(2,1)}), bf16[16,16,128]{2,1,0:T(8,128)(2,1)S(1)}, u32[]{:S(2)}, u32[]{:S(2)}) async-start(bf16[16,16,128]{2,1,0:T(8,128)(2,1)} %get-tuple-element.13.tiles_ref), calls=%async_computation.2 | async-start | bytes 131072 | tf_op jit(solution)/shard_map/all_to_all | solution.py:553
  130.7 4.4 %shard_map.200 = bf16[4,360,384]{2,1,0:T(8,128)(2,1)} custom-call(f32[4,360,384]{2,1,0:T(8,128)} %get-tuple-element.12.updated_any, bf16[16,16,128]{2,1,0:T(8,128)(2,1)} %get-tuple-element.13.tiles_ref, bf16[4,360,128]{2,1,0:T(8,128)(2,1)} %fusion.1.cell_any.cell_ref, bf16[4,360,48]{2,1,0:T(8,128)(2,1)} %compare_convert_fusion.slot_any, f32[384]{0:T(512)} %imprint_ref.1), custom_call_target="tpu_custom_call" | custom-call | flops 283115520 | bytes 3891712 | tf_op jit(solution)/shard_map/pallas_call | solution.py:391
  135.1 2.1 %all-to-all-done.2.tiles_ref = bf16[16,16,128]{2,1,0:T(8,128)(2,1)S(1)} async-done(((bf16[16,16,128]{2,1,0:T(8,128)(2,1)}), bf16[16,16,128]{2,1,0:T(8,128)(2,1)S(1)}, u32[]{:S(2)}, u32[]{:S(2)}) %all-to-all-start.2) | async-done | bytes 65568 | tf_op jit(solution)/shard_map/all_to_all | solution.py:553
  137.2 0.9 shard_map.201
  (23 shorter events, 0.2 us)
Async XLA Ops:
  0.6 21.5 %copy-start.4 = (bf16[1,16,76,128]{3,1,2,0:T(8,128)(2,1)S(1)}, bf16[1,16,76,128]{3,1,2,0:T(8,128)(2,1)}, u32[]{:S(2)}) copy-start(bf16[1,16,76,128]{3,1,2,0:T(8,128)(2,1)} %param.27) | copy-start | bytes 933892
  0.6 43.5 %copy-start.9 = (s32[14,1]{0,1:T(1,128)S(1)}, s32[14,1]{0,1:T(1,128)}, u32[]{:S(2)}) copy-start(s32[14,1]{0,1:T(1,128)} %param.32) | copy-start | bytes 172
  0.7 43.8 %copy-start.5 = (s32[14,128]{1,0:T(8,128)S(1)}, s32[14,128]{1,0:T(8,128)}, u32[]{:S(2)}) copy-start(s32[14,128]{1,0:T(8,128)} %param.30) | copy-start | bytes 21508
  0.7 43.9 %copy-start.7 = (s32[4,360]{1,0:T(4,128)S(1)}, s32[4,360]{1,0:T(4,128)}, u32[]{:S(2)}) copy-start(s32[4,360]{1,0:T(4,128)} %param.31) | copy-start | bytes 17284
  0.7 66.1 %copy-start.2 = (f32[128,384]{1,0:T(8,128)S(1)}, f32[128,384]{1,0:T(8,128)}, u32[]{:S(2)}) copy-start(f32[128,384]{1,0:T(8,128)} %gains_ref.1) | copy-start | bytes 589828
  5.4 61.4 %all-to-all-start = ((bf16[32,32,384]{2,1,0:T(8,128)(2,1)}), bf16[32,32,384]{2,1,0:T(8,128)(2,1)S(1)}, u32[]{:S(2)}, u32[]{:S(2)}) async-start(bf16[32,32,384]{2,1,0:T(8,128)(2,1)} %shard_map.194), calls=%async_computation | async-start | bytes 1572864 | tf_op jit(solution)/shard_map/all_to_all | solution.py:450
  22.1 50.8 %copy-start.8 = (s32[4,360]{1,0:T(4,128)S(1)}, s32[4,360]{1,0:T(4,128)}, u32[]{:S(2)}) copy-start(s32[4,360]{1,0:T(4,128)} %param.20) | copy-start | bytes 17284
  22.2 50.8 %copy-start.3 = (bf16[9,200,84]{1,2,0:T(8,128)(2,1)S(1)}, bf16[9,200,84]{1,2,0:T(8,128)(2,1)}, u32[]{:S(2)}) copy-start(bf16[9,200,84]{1,2,0:T(8,128)(2,1)} %param.28) | copy-start | bytes 907204
  22.4 53.8 %collective-permute-start = (bf16[2,76,128]{2,1,0:T(8,128)(2,1)S(1)}, bf16[2,76,128]{2,1,0:T(8,128)(2,1)S(1)}, u32[]{:S(2)}, u32[]{:S(2)}) collective-permute-start(bf16[2,76,128]{2,1,0:T(8,128)(2,1)S(1)} %bitcast.66), channel_id=1, source_target_pairs={{0,29},{1,30},{2,31},{3,0},{4,1},{5,2},{6,3},{7,4},{8,5},{9,6},{10... | collective-permute-start | bytes 116744 | tf_op jit(solution)/shard_map/ppermute | solution.py:36
  27.2 49.2 %collective-permute-start.1 = (bf16[2,76,128]{2,1,0:T(8,128)(2,1)S(1)}, bf16[2,76,128]{2,1,0:T(8,128)(2,1)S(1)}, u32[]{:S(2)}, u32[]{:S(2)}) collective-permute-start(bf16[2,76,128]{2,1,0:T(8,128)(2,1)S(1)} %bitcast.65), channel_id=1, source_target_pairs={{0,28},{1,29},{2,30},{3,31},{4,0},{5,1},{6,2},{7,3},{8,4},{9,5},{1... | collective-permute-start | bytes 116744 | tf_op jit(solution)/shard_map/ppermute | solution.py:36
  31.2 56.6 %collective-permute-start.2 = (bf16[2,76,128]{2,1,0:T(8,128)(2,1)S(1)}, bf16[2,76,128]{2,1,0:T(8,128)(2,1)S(1)}, u32[]{:S(2)}, u32[]{:S(2)}) collective-permute-start(bf16[2,76,128]{2,1,0:T(8,128)(2,1)S(1)} %bitcast.62), channel_id=1, source_target_pairs={{0,27},{1,28},{2,29},{3,30},{4,31},{5,0},{6,1},{7,2},{8,3},{9,4},{... | collective-permute-start | bytes 116744 | tf_op jit(solution)/shard_map/ppermute | solution.py:36
  37.6 37.5 %copy-start.10 = (pred[80]{0:T(512)(128)(4,1)S(1)}, pred[80]{0:T(512)(128)(4,1)}, u32[]{:S(2)}) copy-start(pred[80]{0:T(512)(128)(4,1)} %constant.112.clone.1) | copy-start | bytes 244
  37.6 50.2 %collective-permute-start.3 = (bf16[2,76,128]{2,1,0:T(8,128)(2,1)S(1)}, bf16[2,76,128]{2,1,0:T(8,128)(2,1)S(1)}, u32[]{:S(2)}, u32[]{:S(2)}) collective-permute-start(bf16[2,76,128]{2,1,0:T(8,128)(2,1)S(1)} %bitcast.63), channel_id=1, source_target_pairs={{0,26},{1,27},{2,28},{3,29},{4,30},{5,31},{6,0},{7,1},{8,2},{9,3},... | collective-permute-start | bytes 116744 | tf_op jit(solution)/shard_map/ppermute | solution.py:36
  41.7 46.2 %collective-permute-start.4 = (bf16[2,76,128]{2,1,0:T(8,128)(2,1)S(1)}, bf16[2,76,128]{2,1,0:T(8,128)(2,1)S(1)}, u32[]{:S(2)}, u32[]{:S(2)}) collective-permute-start(bf16[2,76,128]{2,1,0:T(8,128)(2,1)S(1)} %bitcast.64), channel_id=1, source_target_pairs={{0,25},{1,26},{2,27},{3,28},{4,29},{5,30},{6,31},{7,0},{8,1},{9,2}... | collective-permute-start | bytes 116744 | tf_op jit(solution)/shard_map/ppermute | solution.py:36
  66.8 14.3 %copy-start.11 = (s32[14]{0:T(128)S(1)}, s32[14]{0:T(128)}, u32[]{:S(2)}) copy-start(s32[14]{0:T(128)} %param.33) | copy-start | bytes 172
  68.5 49.0 %all-to-all-start.1 = ((bf16[32,32,384]{2,1,0:T(8,128)(2,1)}), bf16[32,32,384]{2,1,0:T(8,128)(2,1)S(1)}, u32[]{:S(2)}, u32[]{:S(2)}) async-start(bf16[32,32,384]{2,1,0:T(8,128)(2,1)} %shard_map.195), calls=%async_computation.1 | async-start | bytes 1572864 | tf_op jit(solution)/shard_map/all_to_all | solution.py:516
  73.0 14.8 %copy-start.6 = (bf16[9,200]{1,0:T(8,128)(2,1)S(1)}, bf16[9,200]{1,0:T(8,128)(2,1)}, u32[]{:S(2)}) copy-start(bf16[9,200]{1,0:T(8,128)(2,1)} %param.29) | copy-start | bytes 10804
  76.2 32.3 %collective-permute-start.5 = (bf16[2,76,128]{2,1,0:T(8,128)(2,1)S(1)}, bf16[2,76,128]{2,1,0:T(8,128)(2,1)S(1)}, u32[]{:S(2)}, u32[]{:S(2)}) collective-permute-start(bf16[2,76,128]{2,1,0:T(8,128)(2,1)S(1)} %get-tuple-element.21), channel_id=1, source_target_pairs={{0,31},{1,0},{2,1},{3,2},{4,3},{5,4},{6,5},{7,6},{8,7},{9,8},{10,9... | collective-permute-start | bytes 116744 | tf_op jit(solution)/shard_map/ppermute | solution.py:36
  76.4 32.1 %collective-permute-start.6 = (bf16[2,76,128]{2,1,0:T(8,128)(2,1)S(1)}, bf16[2,76,128]{2,1,0:T(8,128)(2,1)S(1)}, u32[]{:S(2)}, u32[]{:S(2)}) collective-permute-start(bf16[2,76,128]{2,1,0:T(8,128)(2,1)S(1)} %get-tuple-element.20), channel_id=1, source_target_pairs={{0,30},{1,31},{2,0},{3,1},{4,2},{5,3},{6,4},{7,5},{8,6},{9,7},{10,... | collective-permute-start | bytes 116744 | tf_op jit(solution)/shard_map/ppermute | solution.py:36
  89.4 1.1 copy-start
  123.7 13.4 %copy-start.1 = (bf16[4,360,128]{2,1,0:T(8,128)(2,1)S(1)}, bf16[4,360,128]{2,1,0:T(8,128)(2,1)}, u32[]{:S(2)}) copy-start(bf16[4,360,128]{2,1,0:T(8,128)(2,1)} %fusion.1.cell_any.cell_ref) | copy-start | bytes 1105924
  123.8 13.4 %all-to-all-start.2 = ((bf16[16,16,128]{2,1,0:T(8,128)(2,1)}), bf16[16,16,128]{2,1,0:T(8,128)(2,1)S(1)}, u32[]{:S(2)}, u32[]{:S(2)}) async-start(bf16[16,16,128]{2,1,0:T(8,128)(2,1)} %get-tuple-element.13.tiles_ref), calls=%async_computation.2 | async-start | bytes 131072 | tf_op jit(solution)/shard_map/all_to_all | solution.py:553

commit v10 on v9

--- a/solution.py
+++ b/solution.py
@@ -82,8 +82,10 @@
 
 
 def gelu(x):
-    inner = math.sqrt(2.0 / math.pi) * (x + 0.044715 * (x * x * x))
-    return 0.5 * x * (1.0 + jnp.tanh(inner))
+    scale = math.sqrt(2.0 / math.pi)
+    inner = x * (scale + (0.044715 * scale) * (x * x))
+    half = 0.5 * x
+    return half * jnp.tanh(inner) + half
 
 
 def tap_masks(width):
@@ -193,8 +195,11 @@
         )
 
 
-def legendre_kernel(x_ref, forward_ref, backward_ref, gains_ref, out_ref, work):
+def legendre_kernel(
+    x_ref, forward_ref, backward_ref, gains_ref, out_any, work, out_ref, out_sems
+):
     groups, chunk, channels = x_ref.shape
+    leaving = []
     total = groups * chunk
     latitudes = total // 8
     for third in range(channels // 128):
@@ -213,6 +218,13 @@
             work[third, real, :] = back[:, :128]
             work[third, imaginary, :] = back[:, 128:]
         out_ref[:, :, lanes] = work[third].reshape(groups, chunk, 128).astype(BF16)
+        leave = pltpu.make_async_copy(
+            out_ref.at[:, :, lanes], out_any.at[:, :, lanes], out_sems.at[third]
+        )
+        leave.start()
+        leaving.append(leave)
+    for one in leaving:
+        one.wait()
 
 
 def ocean_kernel(first, depth_ref, *refs):
@@ -247,28 +259,30 @@
     ) = held
     pack_any, skip_any, air_any = sources[:3]
     rows = air_ref.shape[0]
-    tables, places, fluxes = pl.ds(0, 768), pl.ds(768, 512), pl.ds(0, FC * rows)
-    ordered = [
-        (pack_any.at[tables], pack_ref.at[tables]),
-        (skip_any.at[rows, fluxes], skip_ref.at[rows, fluxes]),
-    ]
+    places, fluxes = pl.ds(768, 512), pl.ds(0, FC * rows)
+    leaves, enters = pl.ds(0, 384), pl.ds(384, 384)
+    ordered = [(pack_any.at[enters], pack_ref.at[enters])]
     for j in range(rows):
         ordered += [(skip_any.at[j], skip_ref.at[j]), (air_any.at[j], air_ref.at[j])]
+        if j == 0:
+            ordered += [
+                (pack_any.at[leaves], pack_ref.at[leaves]),
+                (skip_any.at[rows, fluxes], skip_ref.at[rows, fluxes]),
+            ]
     ordered.append((pack_any.at[places], pack_ref.at[places]))
     copies = begin(ordered + list(zip(sources, held))[3:], sems)
-    after = 2 + 2 * rows
+    after = 3 + 2 * rows
     latitude_rows, longitudes, channels = air_ref.shape
     groups = rows_ref.shape[0]
     pairs = []
     for pair in range(latitude_rows // 2):
         both = rows_ref[:, 16 * pair : 16 * (pair + 1), :].astype(F32)
         pairs.extend([both[:, :8], both[:, 8:]])
-    for one in copies[:2]:
-        one.wait()
+    copies[0].wait()
     for j in range(latitude_rows):
         own = pairs[j].reshape(8 * groups, channels).astype(BF16)
         spectral = jnp.dot(pack_ref[384 : 384 + longitudes, : 8 * groups], own, preferred_element_type=F32)
-        for one in copies[2 + 2 * j : 4 + 2 * j]:
+        for one in copies[1:5] if j == 0 else copies[3 + 2 * j : 5 + 2 * j]:
             one.wait()
         mixed = gelu(spectral + skip_ref[j]).astype(BF16)
         wide = jnp.dot(mixed, pack_ref[:384, :], preferred_element_type=F32)
@@ -509,8 +523,13 @@
         [shape((bands, chunk, channels), BF16)],
         [gathered, forward, backward, harmonic_damping_factor],
         2 * 2 * 2 * per_device * LMAX * latitudes * channels,
-        [pltpu.VMEM((channels // 128, bands * chunk, 128), F32)],
+        [
+            pltpu.VMEM((channels // 128, bands * chunk, 128), F32),
+            pltpu.VMEM((bands, chunk, channels), BF16),
+            pltpu.SemaphoreType.DMA((channels // 128,)),
+        ],
         limit=32,
+        out_specs=FAR,
     )
     filtered, late = lax.optimization_barrier((filtered, slots[CAP : EARLY * CAP]))
     returned = lax.all_to_all(filtered, "space", split_axis=0, concat_axis=0, tiled=True)

time: 139 us -> 139 us (level)
  no operation moved by 1% of the time
where the time goes in v10:
time: 139 us; the launch traced here: 138 us
  starting transfers between devices  54.6 us (39%)
  waiting for transfers between devices  49.3 us (35%)
  Pallas kernels  26.5 us (19%)
  other arithmetic  3.72 us (3%)
  local copies, waits for them, and re-layouts  2.78 us (2%)
    ppermute x7, starting transfers between devices, passed_along(): lax.ppermute(value, axis, [(i, (i + by) % devices) for i in range(devices)])  26.5 us
    pallas_call x8, Pallas kernels, call(): pl.pallas_call(kernel, out_shape=outs if len(outs) > 1 else outs[0], in_s...  26.5 us
    all_to_all x1, waiting for transfers between devices, shards(): lax.all_to_all(spectra, 'space', split_axis=0, concat_axis=0, tiled=True)  21.1 us
    ppermute x7, waiting for transfers between devices, passed_along(): lax.ppermute(value, axis, [(i, (i + by) % devices) for i in range(devices)])  18.1 us
    all_to_all x1, starting transfers between devices, shards(): lax.all_to_all(spectra, 'space', split_axis=0, concat_axis=0, tiled=True)  16.8 us
    all_to_all x1, waiting for transfers between devices, shards(): lax.all_to_all(filtered, 'space', split_axis=0, concat_axis=0, tiled=True)  7.97 us
    all_to_all x1, starting transfers between devices, shards(): lax.all_to_all(tiles, 'member', split_axis=0, concat_axis=0, tiled=True)  6.9 us
    all_to_all x1, starting transfers between devices, shards(): lax.all_to_all(filtered, 'space', split_axis=0, concat_axis=0, tiled=True)  4.35 us
  transfers between devices with their start and end apart: 10, of which 4 were waited for; matrix products, arithmetic and copies ran while one was open for 4% of the time, Pallas kernels for 11%

profile of v10, /device:TPU:1, one launch (start us, length us, event | category | flops | bytes accessed | tf_op | source)
XLA Modules:
  0.0 137.9 jit_solution(16942114892768540711)
XLA Ops:
  0.6 0.0 copy-start.4
  0.6 0.0 copy-start.9
  0.7 0.0 copy-start.5
  0.7 0.0 copy-start.7
  0.7 0.0 copy-start.2
  0.7 4.7 %shard_map.194 = bf16[32,32,384]{2,1,0:T(8,128)(2,1)} custom-call(bf16[4,360,384]{2,1,0:T(8,128)(2,1)} %bitcast.54, f32[384]{0:T(512)} %scale_ref.3, bf16[256,360]{1,0:T(8,128)(2,1)} %constant.115.clone.table_any), custom_call_target="tpu_custom_call" | custom-call | flops 283115520 | bytes 2078208 | tf_op jit(solution)/shard_map/pallas_call | solution.py:405
  5.4 16.8 %all-to-all-start = ((bf16[32,32,384]{2,1,0:T(8,128)(2,1)}), bf16[32,32,384]{2,1,0:T(8,128)(2,1)S(1)}, u32[]{:S(2)}, u32[]{:S(2)}) async-start(bf16[32,32,384]{2,1,0:T(8,128)(2,1)} %shard_map.194), calls=%async_computation | async-start | bytes 1572864 | tf_op jit(solution)/shard_map/all_to_all | solution.py:464
  22.1 0.0 copy-done.4
  22.1 0.0 copy-start.8
  22.2 0.0 copy-start.3
  22.2 0.2 fusion.10
  22.4 4.8 %collective-permute-start = (bf16[2,76,128]{2,1,0:T(8,128)(2,1)S(1)}, bf16[2,76,128]{2,1,0:T(8,128)(2,1)S(1)}, u32[]{:S(2)}, u32[]{:S(2)}) collective-permute-start(bf16[2,76,128]{2,1,0:T(8,128)(2,1)S(1)} %bitcast.66), channel_id=1, source_target_pairs={{0,29},{1,30},{2,31},{3,0},{4,1},{5,2},{6,3},{7,4},{8,5},{9,6},{10... | collective-permute-start | bytes 116744 | tf_op jit(solution)/shard_map/ppermute | solution.py:36
  27.2 4.0 %collective-permute-start.1 = (bf16[2,76,128]{2,1,0:T(8,128)(2,1)S(1)}, bf16[2,76,128]{2,1,0:T(8,128)(2,1)S(1)}, u32[]{:S(2)}, u32[]{:S(2)}) collective-permute-start(bf16[2,76,128]{2,1,0:T(8,128)(2,1)S(1)} %bitcast.65), channel_id=1, source_target_pairs={{0,28},{1,29},{2,30},{3,31},{4,0},{5,1},{6,2},{7,3},{8,4},{9,5},{1... | collective-permute-start | bytes 116744 | tf_op jit(solution)/shard_map/ppermute | solution.py:36
  31.2 6.4 %collective-permute-start.2 = (bf16[2,76,128]{2,1,0:T(8,128)(2,1)S(1)}, bf16[2,76,128]{2,1,0:T(8,128)(2,1)S(1)}, u32[]{:S(2)}, u32[]{:S(2)}) collective-permute-start(bf16[2,76,128]{2,1,0:T(8,128)(2,1)S(1)} %bitcast.62), channel_id=1, source_target_pairs={{0,27},{1,28},{2,29},{3,30},{4,31},{5,0},{6,1},{7,2},{8,3},{9,4},{... | collective-permute-start | bytes 116744 | tf_op jit(solution)/shard_map/ppermute | solution.py:36
  37.6 0.0 copy-start.10
  37.6 4.0 %collective-permute-start.3 = (bf16[2,76,128]{2,1,0:T(8,128)(2,1)S(1)}, bf16[2,76,128]{2,1,0:T(8,128)(2,1)S(1)}, u32[]{:S(2)}, u32[]{:S(2)}) collective-permute-start(bf16[2,76,128]{2,1,0:T(8,128)(2,1)S(1)} %bitcast.63), channel_id=1, source_target_pairs={{0,26},{1,27},{2,28},{3,29},{4,30},{5,31},{6,0},{7,1},{8,2},{9,3},... | collective-permute-start | bytes 116744 | tf_op jit(solution)/shard_map/ppermute | solution.py:36
  41.7 2.4 %collective-permute-start.4 = (bf16[2,76,128]{2,1,0:T(8,128)(2,1)S(1)}, bf16[2,76,128]{2,1,0:T(8,128)(2,1)S(1)}, u32[]{:S(2)}, u32[]{:S(2)}) collective-permute-start(bf16[2,76,128]{2,1,0:T(8,128)(2,1)S(1)} %bitcast.64), channel_id=1, source_target_pairs={{0,25},{1,26},{2,27},{3,28},{4,29},{5,30},{6,31},{7,0},{8,1},{9,2}... | collective-permute-start | bytes 116744 | tf_op jit(solution)/shard_map/ppermute | solution.py:36
  44.2 0.0 copy-done.9
  44.2 0.2 select_reduce_fusion.3
  44.4 0.1 copy.41
  44.5 0.0 copy-done.5
  44.5 0.1 select_reduce_fusion
  44.6 0.0 copy-done.7
  44.6 0.1 select_reduce_fusion.1
  44.7 1.0 constant_dynamic-slice_fusion
  45.7 21.1 %all-to-all-done.x_ref = bf16[32,32,384]{2,1,0:T(8,128)(2,1)S(1)} async-done(((bf16[32,32,384]{2,1,0:T(8,128)(2,1)}), bf16[32,32,384]{2,1,0:T(8,128)(2,1)S(1)}, u32[]{:S(2)}, u32[]{:S(2)}) %all-to-all-start) | async-done | bytes 786464 | tf_op jit(solution)/shard_map/all_to_all | solution.py:464
  66.8 0.0 copy-done.2
  66.8 1.6 %shard_map.195 = bf16[32,32,384]{2,1,0:T(8,128)(2,1)} custom-call(bf16[32,32,384]{2,1,0:T(8,128)(2,1)S(1)} %all-to-all-done.x_ref, bf16[4,128,128]{2,1,0:T(8,128)(2,1)S(1)} %get-tuple-element.27.forward_ref, bf16[4,128,128]{2,1,0:T(8,128)(2,1)S(1)} %get-tuple-element.26.backward_ref, f32[128,384]{1,0:T(8,128)S(1)} %copy-done.2), custom_call_target="tpu_custom_call" | custom-call | flops 201326592 | bytes 2031616 | tf_op jit(solution)/shard_map/pallas_call | solution.py:405
  68.4 4.3 %all-to-all-start.1 = ((bf16[32,32,384]{2,1,0:T(8,128)(2,1)}), bf16[32,32,384]{2,1,0:T(8,128)(2,1)S(1)}, u32[]{:S(2)}, u32[]{:S(2)}) async-start(bf16[32,32,384]{2,1,0:T(8,128)(2,1)} %shard_map.195), calls=%async_computation.1 | async-start | bytes 1572864 | tf_op jit(solution)/shard_map/all_to_all | solution.py:535
  72.8 0.0 copy-done.8
  72.8 0.0 copy-done.3
  72.8 0.0 copy-start.6
  72.9 1.0 fusion.1.cell_any.cell_ref
  73.9 1.1 compare_convert_fusion.slot_any
  74.9 0.0 copy-done.10
  74.9 0.1 slice_select_fusion
  75.0 0.1 multiply_add_fusion.refs_3_
  75.1 0.9 fusion.place_ref
  76.0 0.0 collective-permute-done.refs_1_
  76.0 0.2 collective-permute-start.5
  76.3 0.0 collective-permute-done.1.refs_2_
  76.3 4.7 %collective-permute-start.6 = (bf16[2,76,128]{2,1,0:T(8,128)(2,1)S(1)}, bf16[2,76,128]{2,1,0:T(8,128)(2,1)S(1)}, u32[]{:S(2)}, u32[]{:S(2)}) collective-permute-start(bf16[2,76,128]{2,1,0:T(8,128)(2,1)S(1)} %get-tuple-element.20), channel_id=1, source_target_pairs={{0,30},{1,31},{2,0},{3,1},{4,2},{5,3},{6,4},{7,5},{8,6},{9,7},{10,... | collective-permute-start | bytes 116744 | tf_op jit(solution)/shard_map/ppermute | solution.py:36
  81.0 0.0 copy-done.11
  81.0 0.1 select_reduce_fusion.2.depth_ref
  81.1 6.2 %shard_map.196 = (f32[5,360,384]{2,1,0:T(8,128)}, bf16[1280,512]{1,0:T(8,128)(2,1)}) custom-call(bf16[4,360,384]{2,1,0:T(8,128)(2,1)} %bitcast.55, f32[384]{0:T(512)} %scale_ref.3, bf16[384,384]{1,0:T(8,128)(2,1)} %bypass_ref.1, bf16[384,384]{1,0:T(8,128)(2,1)} %exit_ref.1, bf16[8,384]{1,0:T(8,128)(2,1)} %bitcast.69, ...), custom_call_target="tpu_custom_call" | custom-call | flops 1024 | bytes 1024 | tf_op jit(solution)/shard_map/pallas_call | solution.py:405
  87.4 0.2 copy.48.refs_6_.refs_2_
  87.6 0.1 copy.50.refs_4_
  87.7 0.0 copy-done.6
  87.7 0.0 collective-permute-done.2.refs_3_
  87.7 0.0 collective-permute-done.3.refs_4_
  87.7 0.0 collective-permute-done.4.refs_5_
  87.7 1.5 %shard_map.197.refs_6_ = f32[208,1536]{1,0:T(8,128)S(1)} custom-call(s32[16]{0:T(128)S(1)} %select_reduce_fusion.2.depth_ref, bf16[2,76,128]{2,1,0:T(8,128)(2,1)S(1)} %bitcast.53, bf16[2,76,128]{2,1,0:T(8,128)(2,1)S(1)} %collective-permute-done.refs_1_, bf16[2,76,128]{2,1,0:T(8,128)(2,1)S(1)} %collective-permute-done.1.refs_2_, ...), custom_call_target="tpu_custom_call" | custom-call | flops 1024 | bytes 1024 | tf_op jit(solution)/shard_map/pallas_call | solution.py:405
  89.2 0.0 copy-start
  89.2 1.0 copy-done
  90.3 18.1 %collective-permute-done.5.refs_0_ = bf16[2,76,128]{2,1,0:T(8,128)(2,1)S(1)} collective-permute-done((bf16[2,76,128]{2,1,0:T(8,128)(2,1)S(1)}, bf16[2,76,128]{2,1,0:T(8,128)(2,1)S(1)}, u32[]{:S(2)}, u32[]{:S(2)}) %collective-permute-start.5) | collective-permute-done | bytes 38944 | tf_op jit(solution)/shard_map/ppermute | solution.py:36
  108.4 0.0 collective-permute-done.6.refs_1_
  108.4 1.1 shard_map.198.refs_7_
  109.4 8.0 %all-to-all-done.1.rows_ref = bf16[32,32,384]{2,1,0:T(8,128)(2,1)S(1)} async-done(((bf16[32,32,384]{2,1,0:T(8,128)(2,1)}), bf16[32,32,384]{2,1,0:T(8,128)(2,1)S(1)}, u32[]{:S(2)}, u32[]{:S(2)}) %all-to-all-start.1) | async-done | bytes 786464 | tf_op jit(solution)/shard_map/all_to_all | solution.py:535
  117.4 6.2 %shard_map.199 = (f32[4,360,384]{2,1,0:T(8,128)}, bf16[16,16,128]{2,1,0:T(8,128)(2,1)}) custom-call(bf16[32,32,384]{2,1,0:T(8,128)(2,1)S(1)} %all-to-all-done.1.rows_ref, bf16[1280,512]{1,0:T(8,128)(2,1)} %get-tuple-element.9.refs_0_, f32[5,360,384]{2,1,0:T(8,128)} %get-tuple-element.10.refs_1_, bf16[4,360,384]{2,1,0:T(8,128)(2,1)} %bitcast.56, ...), custom_call_target="tpu_custom_call" | custom-call | flops 707788800 | bytes 9992576 | tf_op jit(solution)/shard_map/pallas_call | solution.py:405
  123.6 0.0 copy-start.1
  123.6 6.9 %all-to-all-start.2 = ((bf16[16,16,128]{2,1,0:T(8,128)(2,1)}), bf16[16,16,128]{2,1,0:T(8,128)(2,1)S(1)}, u32[]{:S(2)}, u32[]{:S(2)}) async-start(bf16[16,16,128]{2,1,0:T(8,128)(2,1)} %get-tuple-element.13.tiles_ref), calls=%async_computation.2 | async-start | bytes 131072 | tf_op jit(solution)/shard_map/all_to_all | solution.py:572
  130.6 4.4 %shard_map.200 = bf16[4,360,384]{2,1,0:T(8,128)(2,1)} custom-call(f32[4,360,384]{2,1,0:T(8,128)} %get-tuple-element.12.updated_any, bf16[16,16,128]{2,1,0:T(8,128)(2,1)} %get-tuple-element.13.tiles_ref, bf16[4,360,128]{2,1,0:T(8,128)(2,1)} %fusion.1.cell_any.cell_ref, bf16[4,360,48]{2,1,0:T(8,128)(2,1)} %compare_convert_fusion.slot_any, f32[384]{0:T(512)} %imprint_ref.1), custom_call_target="tpu_custom_call" | custom-call | flops 283115520 | bytes 3891712 | tf_op jit(solution)/shard_map/pallas_call | solution.py:405
  134.9 2.1 %all-to-all-done.2.tiles_ref = bf16[16,16,128]{2,1,0:T(8,128)(2,1)S(1)} async-done(((bf16[16,16,128]{2,1,0:T(8,128)(2,1)}), bf16[16,16,128]{2,1,0:T(8,128)(2,1)S(1)}, u32[]{:S(2)}, u32[]{:S(2)}) %all-to-all-start.2) | async-done | bytes 65568 | tf_op jit(solution)/shard_map/all_to_all | solution.py:572
  137.1 0.9 shard_map.201
  (23 shorter events, 0.2 us)
Async XLA Ops:
  0.6 21.5 %copy-start.4 = (bf16[1,16,76,128]{3,1,2,0:T(8,128)(2,1)S(1)}, bf16[1,16,76,128]{3,1,2,0:T(8,128)(2,1)}, u32[]{:S(2)}) copy-start(bf16[1,16,76,128]{3,1,2,0:T(8,128)(2,1)} %param.27) | copy-start | bytes 933892
  0.6 43.5 %copy-start.9 = (s32[14,1]{0,1:T(1,128)S(1)}, s32[14,1]{0,1:T(1,128)}, u32[]{:S(2)}) copy-start(s32[14,1]{0,1:T(1,128)} %param.32) | copy-start | bytes 172
  0.7 43.8 %copy-start.5 = (s32[14,128]{1,0:T(8,128)S(1)}, s32[14,128]{1,0:T(8,128)}, u32[]{:S(2)}) copy-start(s32[14,128]{1,0:T(8,128)} %param.30) | copy-start | bytes 21508
  0.7 43.9 %copy-start.7 = (s32[4,360]{1,0:T(4,128)S(1)}, s32[4,360]{1,0:T(4,128)}, u32[]{:S(2)}) copy-start(s32[4,360]{1,0:T(4,128)} %param.31) | copy-start | bytes 17284
  0.7 66.1 %copy-start.2 = (f32[128,384]{1,0:T(8,128)S(1)}, f32[128,384]{1,0:T(8,128)}, u32[]{:S(2)}) copy-start(f32[128,384]{1,0:T(8,128)} %gains_ref.1) | copy-start | bytes 589828
  5.4 61.4 %all-to-all-start = ((bf16[32,32,384]{2,1,0:T(8,128)(2,1)}), bf16[32,32,384]{2,1,0:T(8,128)(2,1)S(1)}, u32[]{:S(2)}, u32[]{:S(2)}) async-start(bf16[32,32,384]{2,1,0:T(8,128)(2,1)} %shard_map.194), calls=%async_computation | async-start | bytes 1572864 | tf_op jit(solution)/shard_map/all_to_all | solution.py:464
  22.1 50.6 %copy-start.8 = (s32[4,360]{1,0:T(4,128)S(1)}, s32[4,360]{1,0:T(4,128)}, u32[]{:S(2)}) copy-start(s32[4,360]{1,0:T(4,128)} %param.20) | copy-start | bytes 17284
  22.2 50.7 %copy-start.3 = (bf16[9,200,84]{1,2,0:T(8,128)(2,1)S(1)}, bf16[9,200,84]{1,2,0:T(8,128)(2,1)}, u32[]{:S(2)}) copy-start(bf16[9,200,84]{1,2,0:T(8,128)(2,1)} %param.28) | copy-start | bytes 907204
  22.4 53.7 %collective-permute-start = (bf16[2,76,128]{2,1,0:T(8,128)(2,1)S(1)}, bf16[2,76,128]{2,1,0:T(8,128)(2,1)S(1)}, u32[]{:S(2)}, u32[]{:S(2)}) collective-permute-start(bf16[2,76,128]{2,1,0:T(8,128)(2,1)S(1)} %bitcast.66), channel_id=1, source_target_pairs={{0,29},{1,30},{2,31},{3,0},{4,1},{5,2},{6,3},{7,4},{8,5},{9,6},{10... | collective-permute-start | bytes 116744 | tf_op jit(solution)/shard_map/ppermute | solution.py:36
  27.2 49.0 %collective-permute-start.1 = (bf16[2,76,128]{2,1,0:T(8,128)(2,1)S(1)}, bf16[2,76,128]{2,1,0:T(8,128)(2,1)S(1)}, u32[]{:S(2)}, u32[]{:S(2)}) collective-permute-start(bf16[2,76,128]{2,1,0:T(8,128)(2,1)S(1)} %bitcast.65), channel_id=1, source_target_pairs={{0,28},{1,29},{2,30},{3,31},{4,0},{5,1},{6,2},{7,3},{8,4},{9,5},{1... | collective-permute-start | bytes 116744 | tf_op jit(solution)/shard_map/ppermute | solution.py:36
  31.2 56.5 %collective-permute-start.2 = (bf16[2,76,128]{2,1,0:T(8,128)(2,1)S(1)}, bf16[2,76,128]{2,1,0:T(8,128)(2,1)S(1)}, u32[]{:S(2)}, u32[]{:S(2)}) collective-permute-start(bf16[2,76,128]{2,1,0:T(8,128)(2,1)S(1)} %bitcast.62), channel_id=1, source_target_pairs={{0,27},{1,28},{2,29},{3,30},{4,31},{5,0},{6,1},{7,2},{8,3},{9,4},{... | collective-permute-start | bytes 116744 | tf_op jit(solution)/shard_map/ppermute | solution.py:36
  37.6 37.3 %copy-start.10 = (pred[80]{0:T(512)(128)(4,1)S(1)}, pred[80]{0:T(512)(128)(4,1)}, u32[]{:S(2)}) copy-start(pred[80]{0:T(512)(128)(4,1)} %constant.112.clone.1) | copy-start | bytes 244
  37.6 50.1 %collective-permute-start.3 = (bf16[2,76,128]{2,1,0:T(8,128)(2,1)S(1)}, bf16[2,76,128]{2,1,0:T(8,128)(2,1)S(1)}, u32[]{:S(2)}, u32[]{:S(2)}) collective-permute-start(bf16[2,76,128]{2,1,0:T(8,128)(2,1)S(1)} %bitcast.63), channel_id=1, source_target_pairs={{0,26},{1,27},{2,28},{3,29},{4,30},{5,31},{6,0},{7,1},{8,2},{9,3},... | collective-permute-start | bytes 116744 | tf_op jit(solution)/shard_map/ppermute | solution.py:36
  41.7 46.1 %collective-permute-start.4 = (bf16[2,76,128]{2,1,0:T(8,128)(2,1)S(1)}, bf16[2,76,128]{2,1,0:T(8,128)(2,1)S(1)}, u32[]{:S(2)}, u32[]{:S(2)}) collective-permute-start(bf16[2,76,128]{2,1,0:T(8,128)(2,1)S(1)} %bitcast.64), channel_id=1, source_target_pairs={{0,25},{1,26},{2,27},{3,28},{4,29},{5,30},{6,31},{7,0},{8,1},{9,2}... | collective-permute-start | bytes 116744 | tf_op jit(solution)/shard_map/ppermute | solution.py:36
  66.8 14.2 %copy-start.11 = (s32[14]{0:T(128)S(1)}, s32[14]{0:T(128)}, u32[]{:S(2)}) copy-start(s32[14]{0:T(128)} %param.33) | copy-start | bytes 172
  68.4 49.0 %all-to-all-start.1 = ((bf16[32,32,384]{2,1,0:T(8,128)(2,1)}), bf16[32,32,384]{2,1,0:T(8,128)(2,1)S(1)}, u32[]{:S(2)}, u32[]{:S(2)}) async-start(bf16[32,32,384]{2,1,0:T(8,128)(2,1)} %shard_map.195), calls=%async_computation.1 | async-start | bytes 1572864 | tf_op jit(solution)/shard_map/all_to_all | solution.py:535
  72.8 14.8 %copy-start.6 = (bf16[9,200]{1,0:T(8,128)(2,1)S(1)}, bf16[9,200]{1,0:T(8,128)(2,1)}, u32[]{:S(2)}) copy-start(bf16[9,200]{1,0:T(8,128)(2,1)} %param.29) | copy-start | bytes 10804
  76.0 32.3 %collective-permute-start.5 = (bf16[2,76,128]{2,1,0:T(8,128)(2,1)S(1)}, bf16[2,76,128]{2,1,0:T(8,128)(2,1)S(1)}, u32[]{:S(2)}, u32[]{:S(2)}) collective-permute-start(bf16[2,76,128]{2,1,0:T(8,128)(2,1)S(1)} %get-tuple-element.21), channel_id=1, source_target_pairs={{0,31},{1,0},{2,1},{3,2},{4,3},{5,4},{6,5},{7,6},{8,7},{9,8},{10,9... | collective-permute-start | bytes 116744 | tf_op jit(solution)/shard_map/ppermute | solution.py:36
  76.3 32.1 %collective-permute-start.6 = (bf16[2,76,128]{2,1,0:T(8,128)(2,1)S(1)}, bf16[2,76,128]{2,1,0:T(8,128)(2,1)S(1)}, u32[]{:S(2)}, u32[]{:S(2)}) collective-permute-start(bf16[2,76,128]{2,1,0:T(8,128)(2,1)S(1)} %get-tuple-element.20), channel_id=1, source_target_pairs={{0,30},{1,31},{2,0},{3,1},{4,2},{5,3},{6,4},{7,5},{8,6},{9,7},{10,... | collective-permute-start | bytes 116744 | tf_op jit(solution)/shard_map/ppermute | solution.py:36
  89.2 1.1 copy-start
  123.6 13.4 %copy-start.1 = (bf16[4,360,128]{2,1,0:T(8,128)(2,1)S(1)}, bf16[4,360,128]{2,1,0:T(8,128)(2,1)}, u32[]{:S(2)}) copy-start(bf16[4,360,128]{2,1,0:T(8,128)(2,1)} %fusion.1.cell_any.cell_ref) | copy-start | bytes 1105924
  123.6 13.4 %all-to-all-start.2 = ((bf16[16,16,128]{2,1,0:T(8,128)(2,1)}), bf16[16,16,128]{2,1,0:T(8,128)(2,1)S(1)}, u32[]{:S(2)}, u32[]{:S(2)}) async-start(bf16[16,16,128]{2,1,0:T(8,128)(2,1)} %get-tuple-element.13.tiles_ref), calls=%async_computation.2 | async-start | bytes 131072 | tf_op jit(solution)/shard_map/all_to_all | solution.py:572

commit v11 on v9

--- a/solution.py
+++ b/solution.py
@@ -23,7 +23,7 @@
 OCH = 76
 OCH_PAD = 80
 TAPS = [(row, col) for row in (-1, 0, 1) for col in (-1, 0, 1)]
-EARLY = 3
+EARLY = 4
 SMALL = 1024
 BF16 = jnp.bfloat16
 F32 = jnp.float32
@@ -229,9 +229,9 @@
         for q, tap in enumerate(TAPS):
             moved = shifted(state, tap, masks[q]).astype(BF16)
             columns[OCH_PAD * q : OCH_PAD * (q + 1), lanes] = moved
-    for at in range(0, out_ref.shape[1], 512):
-        out_ref[:hidden_channels, at : at + 512] = jnp.dot(
-            weight_ref[...], columns[:, at : at + 512], preferred_element_type=F32
+    for at in range(0, out_ref.shape[1], 256):
+        out_ref[:hidden_channels, at : at + 256] = jnp.dot(
+            weight_ref[...], columns[:, at : at + 256], preferred_element_type=F32
         )
 
 

time: 139 us -> 139 us (level)
  starting transfers between devices: 54.5 us -> 57.1 us
  waiting for transfers between devices: 49.3 us -> 47.5 us
    all_to_all x1, waiting for transfers between devices: 7.97 us -> 5.24 us  [shards(): lax.all_to_all(filtered, 'space', split_axis=0, concat_axis=0, tiled=True)]
    all_to_all x1, waiting for transfers between devices: 21.1 us -> 23.6 us  [shards(): lax.all_to_all(spectra, 'space', split_axis=0, concat_axis=0, tiled=True)]
    ppermute x7, starting transfers between devices: 26.5 us -> 28.5 us  [passed_along(): lax.ppermute(value, axis, [(i, (i + by) % devices) for i in range(devices)])]
    ppermute x7, waiting for transfers between devices: 18.1 us -> 16.5 us  [passed_along(): lax.ppermute(value, axis, [(i, (i + by) % devices) for i in range(devices)])]
  transfers between devices with their start and end apart: 10 -> 10, of which waited for: 4 -> 5; matrix products, arithmetic and copies ran while one was open for 4% -> 4% of each run, Pallas kernels for 11% -> 11%
where the time goes in v11:
time: 139 us
  starting transfers between devices  57.1 us (41%)
  waiting for transfers between devices  47.5 us (34%)
  Pallas kernels  26.5 us (19%)
  other arithmetic  3.69 us (3%)
  local copies, waits for them, and re-layouts  2.67 us (2%)
    ppermute x7, starting transfers between devices, passed_along(): lax.ppermute(value, axis, [(i, (i + by) % devices) for i in range(devices)])  28.5 us
    pallas_call x8, Pallas kernels, call(): pl.pallas_call(kernel, out_shape=outs if len(outs) > 1 else outs[0], in_s...  26.5 us
    all_to_all x1, waiting for transfers between devices, shards(): lax.all_to_all(spectra, 'space', split_axis=0, concat_axis=0, tiled=True)  23.6 us
    all_to_all x1, starting transfers between devices, shards(): lax.all_to_all(spectra, 'space', split_axis=0, concat_axis=0, tiled=True)  16.8 us
    ppermute x7, waiting for transfers between devices, passed_along(): lax.ppermute(value, axis, [(i, (i + by) % devices) for i in range(devices)])  16.5 us
    all_to_all x1, starting transfers between devices, shards(): lax.all_to_all(tiles, 'member', split_axis=0, concat_axis=0, tiled=True)  6.9 us
    all_to_all x1, waiting for transfers between devices, shards(): lax.all_to_all(filtered, 'space', split_axis=0, concat_axis=0, tiled=True)  5.24 us
    all_to_all x1, starting transfers between devices, shards(): lax.all_to_all(filtered, 'space', split_axis=0, concat_axis=0, tiled=True)  4.87 us
  transfers between devices with their start and end apart: 10, of which 5 were waited for; matrix products, arithmetic and copies ran while one was open for 4% of the time, Pallas kernels for 11%

profile of v11, /device:TPU:1, one launch (start us, length us, event | category | flops | bytes accessed | tf_op | source)
XLA Modules:
  0.0 138.5 jit_solution(5887829851343762894)
XLA Ops:
  0.6 0.0 copy-start.4
  0.6 0.0 copy-start.9
  0.7 0.0 copy-start.5
  0.7 0.0 copy-start.7
  0.7 0.0 copy-start.2
  0.7 4.7 %shard_map.194 = bf16[32,32,384]{2,1,0:T(8,128)(2,1)} custom-call(bf16[4,360,384]{2,1,0:T(8,128)(2,1)} %bitcast.51, f32[384]{0:T(512)} %scale_ref.3, bf16[256,360]{1,0:T(8,128)(2,1)} %constant.113.clone.table_any), custom_call_target="tpu_custom_call" | custom-call | flops 283115520 | bytes 2078208 | tf_op jit(solution)/shard_map/pallas_call | solution.py:391
  5.4 16.8 %all-to-all-start = ((bf16[32,32,384]{2,1,0:T(8,128)(2,1)}), bf16[32,32,384]{2,1,0:T(8,128)(2,1)S(1)}, u32[]{:S(2)}, u32[]{:S(2)}) async-start(bf16[32,32,384]{2,1,0:T(8,128)(2,1)} %shard_map.194), calls=%async_computation | async-start | bytes 1572864 | tf_op jit(solution)/shard_map/all_to_all | solution.py:450
  22.1 0.0 copy-done.4
  22.1 0.0 copy-start.8
  22.2 0.0 copy-start.3
  22.2 0.1 fusion.10
  22.3 5.5 %collective-permute-start = (bf16[2,76,128]{2,1,0:T(8,128)(2,1)S(1)}, bf16[2,76,128]{2,1,0:T(8,128)(2,1)S(1)}, u32[]{:S(2)}, u32[]{:S(2)}) collective-permute-start(bf16[2,76,128]{2,1,0:T(8,128)(2,1)S(1)} %bitcast.62), channel_id=1, source_target_pairs={{0,28},{1,29},{2,30},{3,31},{4,0},{5,1},{6,2},{7,3},{8,4},{9,5},{1... | collective-permute-start | bytes 116744 | tf_op jit(solution)/shard_map/ppermute | solution.py:36
  27.8 4.5 %collective-permute-start.1 = (bf16[2,76,128]{2,1,0:T(8,128)(2,1)S(1)}, bf16[2,76,128]{2,1,0:T(8,128)(2,1)S(1)}, u32[]{:S(2)}, u32[]{:S(2)}) collective-permute-start(bf16[2,76,128]{2,1,0:T(8,128)(2,1)S(1)} %bitcast.61), channel_id=1, source_target_pairs={{0,27},{1,28},{2,29},{3,30},{4,31},{5,0},{6,1},{7,2},{8,3},{9,4},{... | collective-permute-start | bytes 116744 | tf_op jit(solution)/shard_map/ppermute | solution.py:36
  32.4 6.1 %collective-permute-start.2 = (bf16[2,76,128]{2,1,0:T(8,128)(2,1)S(1)}, bf16[2,76,128]{2,1,0:T(8,128)(2,1)S(1)}, u32[]{:S(2)}, u32[]{:S(2)}) collective-permute-start(bf16[2,76,128]{2,1,0:T(8,128)(2,1)S(1)} %bitcast.59), channel_id=1, source_target_pairs={{0,26},{1,27},{2,28},{3,29},{4,30},{5,31},{6,0},{7,1},{8,2},{9,3},... | collective-permute-start | bytes 116744 | tf_op jit(solution)/shard_map/ppermute | solution.py:36
  38.4 3.1 %collective-permute-start.3 = (bf16[2,76,128]{2,1,0:T(8,128)(2,1)S(1)}, bf16[2,76,128]{2,1,0:T(8,128)(2,1)S(1)}, u32[]{:S(2)}, u32[]{:S(2)}) collective-permute-start(bf16[2,76,128]{2,1,0:T(8,128)(2,1)S(1)} %bitcast.60), channel_id=1, source_target_pairs={{0,25},{1,26},{2,27},{3,28},{4,29},{5,30},{6,31},{7,0},{8,1},{9,2}... | collective-permute-start | bytes 116744 | tf_op jit(solution)/shard_map/ppermute | solution.py:36
  41.6 0.0 copy-start.10
  41.7 0.0 copy-done.9
  41.7 0.2 select_reduce_fusion.3
  41.9 0.1 copy.39
  42.0 0.0 copy-done.5
  42.0 0.1 select_reduce_fusion
  42.1 0.0 copy-done.7
  42.1 0.1 select_reduce_fusion.1
  42.2 1.0 constant_dynamic-slice_fusion
  43.2 23.6 %all-to-all-done.x_ref = bf16[32,32,384]{2,1,0:T(8,128)(2,1)S(1)} async-done(((bf16[32,32,384]{2,1,0:T(8,128)(2,1)}), bf16[32,32,384]{2,1,0:T(8,128)(2,1)S(1)}, u32[]{:S(2)}, u32[]{:S(2)}) %all-to-all-start) | async-done | bytes 786464 | tf_op jit(solution)/shard_map/all_to_all | solution.py:450
  66.8 0.0 copy-done.2
  66.8 1.8 %shard_map.195 = bf16[32,32,384]{2,1,0:T(8,128)(2,1)} custom-call(bf16[32,32,384]{2,1,0:T(8,128)(2,1)S(1)} %all-to-all-done.x_ref, bf16[4,128,128]{2,1,0:T(8,128)(2,1)S(1)} %get-tuple-element.27.forward_ref, bf16[4,128,128]{2,1,0:T(8,128)(2,1)S(1)} %get-tuple-element.26.backward_ref, f32[128,384]{1,0:T(8,128)S(1)} %copy-done.2), custom_call_target="tpu_custom_call" | custom-call | flops 201326592 | bytes 2031616 | tf_op jit(solution)/shard_map/pallas_call | solution.py:391
  68.6 4.9 %all-to-all-start.1 = ((bf16[32,32,384]{2,1,0:T(8,128)(2,1)}), bf16[32,32,384]{2,1,0:T(8,128)(2,1)S(1)}, u32[]{:S(2)}, u32[]{:S(2)}) async-start(bf16[32,32,384]{2,1,0:T(8,128)(2,1)} %shard_map.195), calls=%async_computation.1 | async-start | bytes 1572864 | tf_op jit(solution)/shard_map/all_to_all | solution.py:516
  73.5 0.0 copy-done.8
  73.5 0.0 copy-done.3
  73.6 0.0 copy-start.6
  73.6 1.0 fusion.1.cell_any.cell_ref
  74.6 1.0 compare_convert_fusion.slot_any
  75.6 0.0 copy-done.10
  75.6 0.1 slice_select_fusion
  75.7 0.1 multiply_add_fusion.refs_3_
  75.8 0.9 fusion.place_ref
  76.7 0.2 collective-permute-start.4
  76.9 0.0 collective-permute-done.refs_1_
  77.0 4.7 %collective-permute-start.5 = (bf16[2,76,128]{2,1,0:T(8,128)(2,1)S(1)}, bf16[2,76,128]{2,1,0:T(8,128)(2,1)S(1)}, u32[]{:S(2)}, u32[]{:S(2)}) collective-permute-start(bf16[2,76,128]{2,1,0:T(8,128)(2,1)S(1)} %get-tuple-element.20), channel_id=1, source_target_pairs={{0,30},{1,31},{2,0},{3,1},{4,2},{5,3},{6,4},{7,5},{8,6},{9,7},{10,... | collective-permute-start | bytes 116744 | tf_op jit(solution)/shard_map/ppermute | solution.py:36
  81.7 0.0 collective-permute-done.1.refs_2_
  81.7 4.4 %collective-permute-start.6 = (bf16[2,76,128]{2,1,0:T(8,128)(2,1)S(1)}, bf16[2,76,128]{2,1,0:T(8,128)(2,1)S(1)}, u32[]{:S(2)}, u32[]{:S(2)}) collective-permute-start(bf16[2,76,128]{2,1,0:T(8,128)(2,1)S(1)} %get-tuple-element.19), channel_id=1, source_target_pairs={{0,29},{1,30},{2,31},{3,0},{4,1},{5,2},{6,3},{7,4},{8,5},{9,6},{10... | collective-permute-start | bytes 116744 | tf_op jit(solution)/shard_map/ppermute | solution.py:36
  86.1 0.0 copy-done.11
  86.1 0.1 select_reduce_fusion.2.depth_ref
  86.3 6.3 %shard_map.196 = (f32[5,360,384]{2,1,0:T(8,128)}, bf16[1280,512]{1,0:T(8,128)(2,1)}) custom-call(bf16[4,360,384]{2,1,0:T(8,128)(2,1)} %bitcast.52, f32[384]{0:T(512)} %scale_ref.3, bf16[384,384]{1,0:T(8,128)(2,1)} %bypass_ref.1, bf16[384,384]{1,0:T(8,128)(2,1)} %exit_ref.1, bf16[8,384]{1,0:T(8,128)(2,1)} %bitcast.65, ...), custom_call_target="tpu_custom_call" | custom-call | flops 1024 | bytes 1024 | tf_op jit(solution)/shard_map/pallas_call | solution.py:391
  92.5 0.2 copy.45.refs_5_.refs_3_
  92.7 0.1 copy.47.refs_4_
  92.8 0.0 copy-done.6
  92.8 0.0 collective-permute-done.2.refs_3_
  92.9 0.0 collective-permute-done.3.refs_4_
  92.9 1.3 shard_map.197.refs_6_
  94.2 0.0 copy-start
  94.2 1.0 copy-done
  95.2 14.7 %collective-permute-done.4.refs_0_ = bf16[2,76,128]{2,1,0:T(8,128)(2,1)S(1)} collective-permute-done((bf16[2,76,128]{2,1,0:T(8,128)(2,1)S(1)}, bf16[2,76,128]{2,1,0:T(8,128)(2,1)S(1)}, u32[]{:S(2)}, u32[]{:S(2)}) %collective-permute-start.4) | collective-permute-done | bytes 38944 | tf_op jit(solution)/shard_map/ppermute | solution.py:36
  109.8 0.0 collective-permute-done.5.refs_1_
  109.8 1.9 %collective-permute-done.6.refs_2_ = bf16[2,76,128]{2,1,0:T(8,128)(2,1)S(1)} collective-permute-done((bf16[2,76,128]{2,1,0:T(8,128)(2,1)S(1)}, bf16[2,76,128]{2,1,0:T(8,128)(2,1)S(1)}, u32[]{:S(2)}, u32[]{:S(2)}) %collective-permute-start.6) | collective-permute-done | bytes 38944 | tf_op jit(solution)/shard_map/ppermute | solution.py:36
  111.7 1.1 shard_map.198.refs_7_
  112.9 5.2 %all-to-all-done.1.rows_ref = bf16[32,32,384]{2,1,0:T(8,128)(2,1)S(1)} async-done(((bf16[32,32,384]{2,1,0:T(8,128)(2,1)}), bf16[32,32,384]{2,1,0:T(8,128)(2,1)S(1)}, u32[]{:S(2)}, u32[]{:S(2)}) %all-to-all-start.1) | async-done | bytes 786464 | tf_op jit(solution)/shard_map/all_to_all | solution.py:516
  118.1 6.1 %shard_map.199 = (f32[4,360,384]{2,1,0:T(8,128)}, bf16[16,16,128]{2,1,0:T(8,128)(2,1)}) custom-call(bf16[32,32,384]{2,1,0:T(8,128)(2,1)S(1)} %all-to-all-done.1.rows_ref, bf16[1280,512]{1,0:T(8,128)(2,1)} %get-tuple-element.9.refs_0_, f32[5,360,384]{2,1,0:T(8,128)} %get-tuple-element.10.refs_1_, bf16[4,360,384]{2,1,0:T(8,128)(2,1)} %bitcast.53, ...), custom_call_target="tpu_custom_call" | custom-call | flops 707788800 | bytes 9992576 | tf_op jit(solution)/shard_map/pallas_call | solution.py:391
  124.2 0.0 copy-start.1
  124.2 6.9 %all-to-all-start.2 = ((bf16[16,16,128]{2,1,0:T(8,128)(2,1)}), bf16[16,16,128]{2,1,0:T(8,128)(2,1)S(1)}, u32[]{:S(2)}, u32[]{:S(2)}) async-start(bf16[16,16,128]{2,1,0:T(8,128)(2,1)} %get-tuple-element.13.tiles_ref), calls=%async_computation.2 | async-start | bytes 131072 | tf_op jit(solution)/shard_map/all_to_all | solution.py:553
  131.2 4.4 %shard_map.200 = bf16[4,360,384]{2,1,0:T(8,128)(2,1)} custom-call(f32[4,360,384]{2,1,0:T(8,128)} %get-tuple-element.12.updated_any, bf16[16,16,128]{2,1,0:T(8,128)(2,1)} %get-tuple-element.13.tiles_ref, bf16[4,360,128]{2,1,0:T(8,128)(2,1)} %fusion.1.cell_any.cell_ref, bf16[4,360,48]{2,1,0:T(8,128)(2,1)} %compare_convert_fusion.slot_any, f32[384]{0:T(512)} %imprint_ref.1), custom_call_target="tpu_custom_call" | custom-call | flops 283115520 | bytes 3891712 | tf_op jit(solution)/shard_map/pallas_call | solution.py:391
  135.5 2.1 %all-to-all-done.2.tiles_ref = bf16[16,16,128]{2,1,0:T(8,128)(2,1)S(1)} async-done(((bf16[16,16,128]{2,1,0:T(8,128)(2,1)}), bf16[16,16,128]{2,1,0:T(8,128)(2,1)S(1)}, u32[]{:S(2)}, u32[]{:S(2)}) %all-to-all-start.2) | async-done | bytes 65568 | tf_op jit(solution)/shard_map/all_to_all | solution.py:553
  137.7 0.9 shard_map.201
  (22 shorter events, 0.2 us)
Async XLA Ops:
  0.6 21.5 %copy-start.4 = (bf16[1,16,76,128]{3,1,2,0:T(8,128)(2,1)S(1)}, bf16[1,16,76,128]{3,1,2,0:T(8,128)(2,1)}, u32[]{:S(2)}) copy-start(bf16[1,16,76,128]{3,1,2,0:T(8,128)(2,1)} %param.27) | copy-start | bytes 933892
  0.6 41.0 %copy-start.9 = (s32[14,1]{0,1:T(1,128)S(1)}, s32[14,1]{0,1:T(1,128)}, u32[]{:S(2)}) copy-start(s32[14,1]{0,1:T(1,128)} %param.32) | copy-start | bytes 172
  0.7 41.3 %copy-start.5 = (s32[14,128]{1,0:T(8,128)S(1)}, s32[14,128]{1,0:T(8,128)}, u32[]{:S(2)}) copy-start(s32[14,128]{1,0:T(8,128)} %param.30) | copy-start | bytes 21508
  0.7 41.4 %copy-start.7 = (s32[4,360]{1,0:T(4,128)S(1)}, s32[4,360]{1,0:T(4,128)}, u32[]{:S(2)}) copy-start(s32[4,360]{1,0:T(4,128)} %param.31) | copy-start | bytes 17284
  0.7 66.1 %copy-start.2 = (f32[128,384]{1,0:T(8,128)S(1)}, f32[128,384]{1,0:T(8,128)}, u32[]{:S(2)}) copy-start(f32[128,384]{1,0:T(8,128)} %gains_ref.1) | copy-start | bytes 589828
  5.4 61.4 %all-to-all-start = ((bf16[32,32,384]{2,1,0:T(8,128)(2,1)}), bf16[32,32,384]{2,1,0:T(8,128)(2,1)S(1)}, u32[]{:S(2)}, u32[]{:S(2)}) async-start(bf16[32,32,384]{2,1,0:T(8,128)(2,1)} %shard_map.194), calls=%async_computation | async-start | bytes 1572864 | tf_op jit(solution)/shard_map/all_to_all | solution.py:450
  22.1 51.3 %copy-start.8 = (s32[4,360]{1,0:T(4,128)S(1)}, s32[4,360]{1,0:T(4,128)}, u32[]{:S(2)}) copy-start(s32[4,360]{1,0:T(4,128)} %param.20) | copy-start | bytes 17284
  22.2 51.4 %copy-start.3 = (bf16[9,200,84]{1,2,0:T(8,128)(2,1)S(1)}, bf16[9,200,84]{1,2,0:T(8,128)(2,1)}, u32[]{:S(2)}) copy-start(bf16[9,200,84]{1,2,0:T(8,128)(2,1)} %param.28) | copy-start | bytes 907204
  22.3 54.6 %collective-permute-start = (bf16[2,76,128]{2,1,0:T(8,128)(2,1)S(1)}, bf16[2,76,128]{2,1,0:T(8,128)(2,1)S(1)}, u32[]{:S(2)}, u32[]{:S(2)}) collective-permute-start(bf16[2,76,128]{2,1,0:T(8,128)(2,1)S(1)} %bitcast.62), channel_id=1, source_target_pairs={{0,28},{1,29},{2,30},{3,31},{4,0},{5,1},{6,2},{7,3},{8,4},{9,5},{1... | collective-permute-start | bytes 116744 | tf_op jit(solution)/shard_map/ppermute | solution.py:36
  27.8 53.8 %collective-permute-start.1 = (bf16[2,76,128]{2,1,0:T(8,128)(2,1)S(1)}, bf16[2,76,128]{2,1,0:T(8,128)(2,1)S(1)}, u32[]{:S(2)}, u32[]{:S(2)}) collective-permute-start(bf16[2,76,128]{2,1,0:T(8,128)(2,1)S(1)} %bitcast.61), channel_id=1, source_target_pairs={{0,27},{1,28},{2,29},{3,30},{4,31},{5,0},{6,1},{7,2},{8,3},{9,4},{... | collective-permute-start | bytes 116744 | tf_op jit(solution)/shard_map/ppermute | solution.py:36
  32.4 60.5 %collective-permute-start.2 = (bf16[2,76,128]{2,1,0:T(8,128)(2,1)S(1)}, bf16[2,76,128]{2,1,0:T(8,128)(2,1)S(1)}, u32[]{:S(2)}, u32[]{:S(2)}) collective-permute-start(bf16[2,76,128]{2,1,0:T(8,128)(2,1)S(1)} %bitcast.59), channel_id=1, source_target_pairs={{0,26},{1,27},{2,28},{3,29},{4,30},{5,31},{6,0},{7,1},{8,2},{9,3},... | collective-permute-start | bytes 116744 | tf_op jit(solution)/shard_map/ppermute | solution.py:36
  38.4 54.4 %collective-permute-start.3 = (bf16[2,76,128]{2,1,0:T(8,128)(2,1)S(1)}, bf16[2,76,128]{2,1,0:T(8,128)(2,1)S(1)}, u32[]{:S(2)}, u32[]{:S(2)}) collective-permute-start(bf16[2,76,128]{2,1,0:T(8,128)(2,1)S(1)} %bitcast.60), channel_id=1, source_target_pairs={{0,25},{1,26},{2,27},{3,28},{4,29},{5,30},{6,31},{7,0},{8,1},{9,2}... | collective-permute-start | bytes 116744 | tf_op jit(solution)/shard_map/ppermute | solution.py:36
  41.6 34.0 %copy-start.10 = (pred[80]{0:T(512)(128)(4,1)S(1)}, pred[80]{0:T(512)(128)(4,1)}, u32[]{:S(2)}) copy-start(pred[80]{0:T(512)(128)(4,1)} %constant.110.clone.1) | copy-start | bytes 244
  66.8 19.3 %copy-start.11 = (s32[14]{0:T(128)S(1)}, s32[14]{0:T(128)}, u32[]{:S(2)}) copy-start(s32[14]{0:T(128)} %param.33) | copy-start | bytes 172
  68.6 49.5 %all-to-all-start.1 = ((bf16[32,32,384]{2,1,0:T(8,128)(2,1)}), bf16[32,32,384]{2,1,0:T(8,128)(2,1)S(1)}, u32[]{:S(2)}, u32[]{:S(2)}) async-start(bf16[32,32,384]{2,1,0:T(8,128)(2,1)} %shard_map.195), calls=%async_computation.1 | async-start | bytes 1572864 | tf_op jit(solution)/shard_map/all_to_all | solution.py:516
  73.6 19.3 %copy-start.6 = (bf16[9,200]{1,0:T(8,128)(2,1)S(1)}, bf16[9,200]{1,0:T(8,128)(2,1)}, u32[]{:S(2)}) copy-start(bf16[9,200]{1,0:T(8,128)(2,1)} %param.29) | copy-start | bytes 10804
  76.7 33.1 %collective-permute-start.4 = (bf16[2,76,128]{2,1,0:T(8,128)(2,1)S(1)}, bf16[2,76,128]{2,1,0:T(8,128)(2,1)S(1)}, u32[]{:S(2)}, u32[]{:S(2)}) collective-permute-start(bf16[2,76,128]{2,1,0:T(8,128)(2,1)S(1)} %get-tuple-element.21), channel_id=1, source_target_pairs={{0,31},{1,0},{2,1},{3,2},{4,3},{5,4},{6,5},{7,6},{8,7},{9,8},{10,9... | collective-permute-start | bytes 116744 | tf_op jit(solution)/shard_map/ppermute | solution.py:36
  77.0 32.9 %collective-permute-start.5 = (bf16[2,76,128]{2,1,0:T(8,128)(2,1)S(1)}, bf16[2,76,128]{2,1,0:T(8,128)(2,1)S(1)}, u32[]{:S(2)}, u32[]{:S(2)}) collective-permute-start(bf16[2,76,128]{2,1,0:T(8,128)(2,1)S(1)} %get-tuple-element.20), channel_id=1, source_target_pairs={{0,30},{1,31},{2,0},{3,1},{4,2},{5,3},{6,4},{7,5},{8,6},{9,7},{10,... | collective-permute-start | bytes 116744 | tf_op jit(solution)/shard_map/ppermute | solution.py:36
  81.7 30.0 %collective-permute-start.6 = (bf16[2,76,128]{2,1,0:T(8,128)(2,1)S(1)}, bf16[2,76,128]{2,1,0:T(8,128)(2,1)S(1)}, u32[]{:S(2)}, u32[]{:S(2)}) collective-permute-start(bf16[2,76,128]{2,1,0:T(8,128)(2,1)S(1)} %get-tuple-element.19), channel_id=1, source_target_pairs={{0,29},{1,30},{2,31},{3,0},{4,1},{5,2},{6,3},{7,4},{8,5},{9,6},{10... | collective-permute-start | bytes 116744 | tf_op jit(solution)/shard_map/ppermute | solution.py:36
  94.2 1.0 copy-start
  124.2 13.4 %copy-start.1 = (bf16[4,360,128]{2,1,0:T(8,128)(2,1)S(1)}, bf16[4,360,128]{2,1,0:T(8,128)(2,1)}, u32[]{:S(2)}) copy-start(bf16[4,360,128]{2,1,0:T(8,128)(2,1)} %fusion.1.cell_any.cell_ref) | copy-start | bytes 1105924
  124.2 13.4 %all-to-all-start.2 = ((bf16[16,16,128]{2,1,0:T(8,128)(2,1)}), bf16[16,16,128]{2,1,0:T(8,128)(2,1)S(1)}, u32[]{:S(2)}, u32[]{:S(2)}) async-start(bf16[16,16,128]{2,1,0:T(8,128)(2,1)} %get-tuple-element.13.tiles_ref), calls=%async_computation.2 | async-start | bytes 131072 | tf_op jit(solution)/shard_map/all_to_all | solution.py:553
